TPU v7x, 128 devices: a whole 4x4x4 slice. The times are simulated.
128 devices in a mesh: lat: 8 (over x_lo, z), lon: 16 (over y, x_hi, core).
Axes of the slice: x: 4 (x_hi: 2, x_lo: 2; x = x_hi * 2 + x_lo), y: 4, z: 4, core: 2. Of those that a mesh axis runs over, the one named last changes fastest.
Arguments:
- initial: float32 [3, 72, 64, 2048], P(None, None, 'lat', 'lon'), may hold values from -6 to 6
- east_wind: float32 [2, 72, 64, 2048], P(None, None, 'lat', 'lon'), may hold values from -0.3 to 0.3
- north_wind: float32 [2, 72, 64, 2048], P(None, None, 'lat', 'lon'), may hold values from -0.3 to 0.3
- mixing: float32 [2, 72, 64, 2048], P(None, None, 'lat', 'lon'), may hold values from 0.02 to 0.2
- kernel: bfloat16 [16384, 72, 128], P(('lat', 'lon')), may hold values from -0.75 to 0.75
- columns: int32 [16384, 128], P(('lat', 'lon')), may hold values from 0 to 3071
- observed: bfloat16 [16384, 128], P(('lat', 'lon')), may hold values from -6 to 6
- obs_weight: bfloat16 [16384, 128], P(('lat', 'lon')), may hold values from 1 to 8
- counts: int32 [16384], P(('lat', 'lon')), may hold values from 64 to 128
- targets: int32 [16384, 1], P(('lat', 'lon')), may hold values from 0 to 127; in each aligned block of 128 rows (0 to 127, 128 to 255, ...) at most 2 rows name the same one
Outputs:
- gradient: float32 [3, 72, 64, 2048], P(None, None, 'lat', 'lon')
- innovations: float32 [16384, 128], P(('lat', 'lon'))
Inputs may be any that keep to these rules, and one draw needn't show every extreme that they name: `targets`: destinations are device indices over lat and lon in mesh order (lat index times the lon devices plus lon index). Among the blocks of one device at most 2 share a destination, and in every draw some device sends exactly 2 blocks to one destination. `columns`: the value is the tracer times 8 * 128 plus the cell's row times 128 plus its column, inside the destination device's block of the grid. The first counts[b] soundings of block b are live.
All inputs are finite; a program needn't handle non-finite values.
Results may differ from a plain program's by a relative error of at most 0.0005.
Values may be sent and summed in bfloat16 or wider, within the bound.
No kernel may reach another device: no remote copies, remote signals or barrier semaphores. Data moves between devices by JAX's collectives and lax.ppermute only.
A program may use at most 128 MiB of HBM per device.

v0:
```python
import jax
import jax.numpy as jnp
from jax import lax
from jax.sharding import PartitionSpec as P

CAP = 2


def extended(shard, sides, width, wrap):
    for axis, dim in sides:
        size, length = (lax.axis_size(axis), shard.shape[dim])
        up = [(i, (i + 1) % size) for i in range(size if wrap else size - 1)]
        down = [(j, i) for i, j in up]
        last = lax.slice_in_dim(shard, length - width, length, axis=dim)
        initial = lax.slice_in_dim(shard, 0, width, axis=dim)
        before = lax.ppermute(last, axis, up)
        after = lax.ppermute(initial, axis, down)
        shard = jnp.concatenate([before, shard, after], axis=dim)
    return shard


def pad_rims(field):
    with_rows = extended(field, (("lat", 2),), 1, False)
    return extended(with_rows, (("lon", 3),), 1, True)


def crop(field, offset):
    if offset == 0:
        return field
    return field[..., offset : field.shape[-2] - offset, offset : field.shape[-1] - offset]


def vertical_mix(field, coeff):
    above_cells = jnp.concatenate([field[:, 1:], jnp.zeros_like(field[:, :1])], axis=1)
    upward = coeff * (above_cells - field)
    below_flux = jnp.concatenate([jnp.zeros_like(upward[:, :1]), upward[:, :-1]], axis=1)
    return upward - below_flux


def forward_step(padded, east_pos, east_neg, north_pos, north_neg, coeff):
    interior = padded[:, :, 1:-1, 1:-1]
    zonal_flux = (
        east_pos[:, 1:-1, :-1] * padded[:, :, 1:-1, :-1]
        + east_neg[:, 1:-1, :-1] * padded[:, :, 1:-1, 1:]
    )
    merid_flux = (
        north_pos[:, :-1, 1:-1] * padded[:, :, :-1, 1:-1]
        + north_neg[:, :-1, 1:-1] * padded[:, :, 1:, 1:-1]
    )
    return (
        interior
        - (zonal_flux[..., 1:] - zonal_flux[..., :-1])
        - (merid_flux[:, :, 1:] - merid_flux[:, :, :-1])
        + vertical_mix(interior, coeff)
    )


def adjoint_step(padded, east_pos, east_neg, north_pos, north_neg, coeff):
    interior = padded[:, :, 1:-1, 1:-1]
    zonal_term = east_pos[:, 1:-1, 1:-1] * (padded[:, :, 1:-1, 2:] - interior) + east_neg[
        :, 1:-1, :-2
    ] * (interior - padded[:, :, 1:-1, :-2])
    merid_term = north_pos[:, 1:-1, 1:-1] * (padded[:, :, 2:, 1:-1] - interior) + north_neg[
        :, :-2, 1:-1
    ] * (interior - padded[:, :, :-2, 1:-1])
    return interior + zonal_term + merid_term + vertical_mix(interior, coeff)


def route_blocks(kernel, columns, observed, weight_live, slot_index, lat_count, lon_count):
    slot_total = lat_count * lon_count * CAP
    levels = kernel.shape[1]
    sounds = kernel.shape[2]
    kernel_slots = jnp.zeros((slot_total, levels, sounds), jnp.bfloat16).at[slot_index].set(kernel)
    column_slots = jnp.zeros((slot_total, sounds), jnp.int32).at[slot_index].set(columns)
    observed_slots = jnp.zeros((slot_total, sounds), jnp.bfloat16).at[slot_index].set(observed)
    weight_slots = jnp.zeros((slot_total, sounds), jnp.bfloat16).at[slot_index].set(weight_live)
    return (
        lax.all_to_all(kernel_slots, ("lat", "lon"), split_axis=0, concat_axis=0, tiled=True),
        lax.all_to_all(column_slots, ("lat", "lon"), split_axis=0, concat_axis=0, tiled=True),
        lax.all_to_all(observed_slots, ("lat", "lon"), split_axis=0, concat_axis=0, tiled=True),
        lax.all_to_all(weight_slots, ("lat", "lon"), split_axis=0, concat_axis=0, tiled=True),
    )


def per_device(
    initial, east_wind, north_wind, mixing, kernel, columns, observed, obs_weight, counts, targets
):
    lat_count = lax.axis_size("lat")
    lon_count = lax.axis_size("lon")
    tracers, levels, lat_cells, lon_cells = initial.shape
    step_count = east_wind.shape[0]
    sounds = kernel.shape[2]
    depth = 1
    lat_start = lax.axis_index("lat") * lat_cells
    total_rows = lat_cells * lat_count
    row_global = lat_start + lax.broadcasted_iota(jnp.int32, (1, 1, lat_cells, 1), 2)
    north_masked = jnp.where(row_global < total_rows - 1, north_wind, jnp.float32(0.0))
    level_index = lax.broadcasted_iota(jnp.int32, (1, levels, 1, 1), 1)
    coeff_all = jnp.where(level_index < levels - 1, mixing, jnp.float32(0.0))

    def pad_field(field):
        return pad_rims(field)

    def zero_outside(field, rim):
        rows = lat_start - rim + lax.broadcasted_iota(jnp.int32, (1, 1, field.shape[2], 1), 2)
        inside = (rows >= 0) & (rows < total_rows)
        return jnp.where(inside, field, jnp.float32(0.0))

    target_dev = targets[:, 0]
    block_count = target_dev.shape[0]
    same_target = target_dev[:, None] == target_dev[None, :]
    earlier = lax.broadcasted_iota(jnp.int32, (block_count, block_count), 1) < lax.broadcasted_iota(
        jnp.int32, (block_count, block_count), 0
    )
    rank_within = jnp.sum(jnp.where(same_target & earlier, 1, 0), axis=1).astype(jnp.int32)
    slot_index = target_dev * CAP + rank_within
    live = lax.broadcasted_iota(jnp.int32, (1, sounds), 1) < counts[:, None]
    weight_live = jnp.where(live, obs_weight, jnp.zeros_like(obs_weight))

    def run_steps(padded_state, wind_parts, moments, stepper):
        east_pos, east_neg, north_pos, north_neg, coeff_pad = wind_parts
        state = padded_state
        rim = depth
        for moment in moments:
            if rim == 0:
                state = pad_field(state)
                rim = depth
            offset = depth - rim
            state = stepper(
                state,
                crop(east_pos[moment], offset),
                crop(east_neg[moment], offset),
                crop(north_pos[moment], offset),
                crop(north_neg[moment], offset),
                crop(coeff_pad[moment], offset + 1),
            )
            rim = rim - 1
            state = zero_outside(state, rim)
        return state

    stacked = pad_field(jnp.concatenate([initial, east_wind, north_masked, coeff_all], axis=0))
    state = stacked[:tracers]
    east = stacked[tracers : tracers + step_count]
    north = stacked[tracers + step_count : tracers + 2 * step_count]
    coeff_pad = stacked[tracers + 2 * step_count :]
    wind_parts = (
        jnp.maximum(east, 0.0),
        jnp.minimum(east, 0.0),
        jnp.maximum(north, 0.0),
        jnp.minimum(north, 0.0),
        coeff_pad,
    )
    final = run_steps(state, wind_parts, range(step_count), forward_step)
    final_state, wind_parts = (final, wind_parts)
    received = route_blocks(
        kernel, columns, observed, weight_live, slot_index, lat_count, lon_count
    )
    got_kernel, got_columns, got_observed, got_weight = received
    slot_total = got_kernel.shape[0]
    cells_all = tracers * lat_cells * lon_cells
    cell_rows = jnp.transpose(final_state, (0, 2, 3, 1)).reshape(cells_all, levels)
    flat_index = got_columns.reshape(-1)
    profile = cell_rows[flat_index].reshape(slot_total, sounds, levels)
    kernel_rows = jnp.swapaxes(got_kernel, 1, 2).astype(jnp.float32)
    model = jnp.sum(kernel_rows * profile, axis=2)
    misfit = model - got_observed.astype(jnp.float32)
    forcing = got_weight.astype(jnp.float32) * misfit
    vectors = (kernel_rows * forcing[:, :, None]).reshape(slot_total * sounds, levels)
    adjoint_rows = jnp.zeros((cells_all, levels), jnp.float32).at[flat_index].add(vectors)
    adjoint_state = jnp.transpose(
        adjoint_rows.reshape(tracers, lat_cells, lon_cells, levels), (0, 3, 1, 2)
    )
    returned = lax.all_to_all(misfit, ("lat", "lon"), split_axis=0, concat_axis=0, tiled=True)
    innovations = jnp.where(live, returned[slot_index], jnp.float32(0.0))
    gradient = run_steps(
        pad_field(adjoint_state), wind_parts, range(step_count - 1, -1, -1), adjoint_step
    )
    return (gradient, innovations)


def solution(mesh):
    return jax.shard_map(
        per_device,
        mesh=mesh,
        in_specs=(
            P(None, None, "lat", "lon"),
            P(None, None, "lat", "lon"),
            P(None, None, "lat", "lon"),
            P(None, None, "lat", "lon"),
            P(("lat", "lon"), None, None),
            P(("lat", "lon"), None),
            P(("lat", "lon"), None),
            P(("lat", "lon"), None),
            P(("lat", "lon")),
            P(("lat", "lon"), None),
        ),
        out_specs=(P(None, None, "lat", "lon"), P(("lat", "lon"), None)),
        check_vma=False,
    )
```

profile of v0, /device:TPU:1, one launch (start us, length us, event | category | flops | bytes accessed | tf_op | source)
XLA Modules:
  0.0 629.3 jit_solution(13849934561636770615)
XLA Ops:
  3.5 5.2 collective-permute-start
  12.0 11.9 %all-to-all-start = ((s32[128,2,128]{2,1,0:T(2,128)}), s32[128,2,128]{2,1,0:T(2,128)}, u32[]{:S(2)}, u32[]{:S(2)}) async-start(s32[128,2,128]{2,1,0:T(2,128)} %bitcast.71), calls=%async_computation | async-start | bytes 262144 | tf_op jit(solution)/shard_map/all_to_all | solution.py:79
  26.6 2.7 broadcast_in_dim.104
  29.3 17.9 %scatter_fusion = bf16[256,72,128]{2,1,0:T(8,128)(2,1)} fusion(bf16[256,72,128]{2,1,0:T(8,128)(2,1)} %broadcast_in_dim.104, s32[128]{0:T(128)S(1)} %fusion.62, bf16[128,72,128]{2,1,0:T(8,128)(2,1)} %param.14), kind=kCustom, calls=%fused_computation.3 | custom fusion | bytes 7078400 | tf_op jit(solution)/shard_map/scatter | solution.py:73
  48.8 9.7 %all-to-all-start.3 = ((bf16[128,2,128]{2,1,0:T(2,128)(2,1)}), bf16[128,2,128]{2,1,0:T(2,128)(2,1)S(1)}, u32[]{:S(2)}, u32[]{:S(2)}) async-start(bf16[128,2,128]{2,1,0:T(2,128)(2,1)} %bitcast.22), calls=%async_computation.3 | async-start | bytes 131072 | tf_op jit(solution)/shard_map/all_to_all | solution.py:80
  59.6 2.3 pad_maximum_fusion.1
  61.9 5.7 fusion.64
  67.7 3.5 copy.72
  71.1 3.2 collective-permute-start.2
  74.3 3.5 copy.73
  78.9 3.3 copy.74
  83.1 3.2 copy.75
  86.4 12.7 %pad_maximum_fusion = f32[9,72,10,130]{3,2,0,1:T(8,128)S(1)} fusion(f32[9,72,10,1]{3,2,0,1:T(8,128)} %copy.75, f32[9,72,1,128]{3,2,0,1:T(1,128)} %collective-permute-done.1, f32[2,72,8,128]{3,2,0,1:T(8,128)S(1)} %get-tuple-element.40, f32[2,72,8,128]{3,2,0,1:T(8,128)S(1)} %get-tuple-element.41, f32[9,72,1,128]{3,2,0,1:T(1,128)} %collective-permute-done, ...), kind=kLoop, calls=%fused_computation.7 | loop fusion | flops 5896800 | bytes 6739200 | tf_op jit(solution)/shard_map/concatenate | solution.py:18
  99.1 3.6 slice_maximum_fusion.1
  102.7 2.8 copy-done.1
  107.7 9.6 %all-to-all-start.1 = ((bf16[256,72,128]{2,1,0:T(8,128)(2,1)}), bf16[256,72,128]{2,1,0:T(8,128)(2,1)}, u32[]{:S(2)}, u32[]{:S(2)}) async-start(bf16[256,72,128]{2,1,0:T(8,128)(2,1)} %scatter_fusion), calls=%async_computation.1 | async-start | bytes 9437184 | tf_op jit(solution)/shard_map/all_to_all | solution.py:78
  117.3 1.9 slice_bitcast_fusion.3
  123.0 2.0 slice_bitcast_fusion
  126.1 1.9 fusion.5
  128.1 2.9 fusion.8
  131.9 3.5 collective-permute-start.4
  148.1 6.6 %collective-permute-done.4 = f32[3,72,1,128]{3,2,0,1:T(1,128)S(1)} collective-permute-done((f32[3,72,1,128]{3,2,0,1:T(1,128)S(1)}, f32[3,72,1,128]{3,2,0,1:T(1,128)S(1)}, u32[]{:S(2)}, u32[]{:S(2)}) %collective-permute-start.4) | collective-permute-done | bytes 110624 | tf_op jit(solution)/shard_map/ppermute | solution.py:16
  154.7 14.8 %collective-permute-done.5 = f32[3,72,1,128]{3,2,0,1:T(1,128)S(1)} collective-permute-done((f32[3,72,1,128]{3,2,0,1:T(1,128)S(1)}, f32[3,72,1,128]{3,2,0,1:T(1,128)S(1)}, u32[]{:S(2)}, u32[]{:S(2)}) %collective-permute-start.5) | collective-permute-done | bytes 110624 | tf_op jit(solution)/shard_map/ppermute | solution.py:17
  172.3 2.0 copy.81
  174.3 4.0 collective-permute-start.6
  185.4 3.4 fusion.2
  191.9 109.0 %gather_fusion = f32[32768,72]{1,0:T(8,128)} fusion(f32[3072,72]{1,0:T(8,128)S(1)} %bitcast.54, s32[32768]{0:T(1024)S(1)} %copy-done.30), kind=kCustom, calls=%fused_computation | custom fusion | bytes 19005440 | tf_op jit(solution)/shard_map/gather | solution.py:163
  300.9 14.4 %copy.87 = f32[256,128,72]{1,2,0:T(8,128)} copy(f32[256,128,72]{2,1,0:T(8,128)} %bitcast.55) | data formatting | bytes 18874368 | tf_op jit(solution)/shard_map/reshape | solution.py:163
  315.2 13.4 %all-to-all-start.2 = ((bf16[128,2,128]{2,1,0:T(2,128)(2,1)}), bf16[128,2,128]{2,1,0:T(2,128)(2,1)S(1)}, u32[]{:S(2)}, u32[]{:S(2)}) async-start(bf16[128,2,128]{2,1,0:T(2,128)(2,1)} %bitcast.7), calls=%async_computation.2 | async-start | bytes 131072 | tf_op jit(solution)/shard_map/all_to_all | solution.py:81
  328.7 6.6 %fusion = f32[256,128]{1,0:T(8,128)S(1)} fusion(f32[256,128,72]{1,2,0:T(8,128)} %copy.87, bf16[256,72,128]{2,1,0:T(8,128)(2,1)} %all-to-all-done.1), kind=kLoop, calls=%fused_computation.10 | loop fusion | flops 7045120 | bytes 14286848 | tf_op jit(solution)/shard_map/reduce_sum | solution.py:165
  335.2 3.0 all-to-all-done.2
  338.2 6.9 %bitcast_multiply_fusion = f32[256,128,72]{1,2,0:T(8,128)} fusion(bf16[256,72,128]{2,1,0:T(8,128)(2,1)} %all-to-all-done.1, f32[256,128]{1,0:T(8,128)S(1)} %convert_multiply_fusion), kind=kLoop, calls=%fused_computation.8 | loop fusion | flops 4718592 | bytes 14286848 | tf_op jit(solution)/shard_map/mul | solution.py:168
  345.1 13.3 %copy.102 = f32[256,128,72]{2,1,0:T(8,128)} copy(f32[256,128,72]{1,2,0:T(8,128)} %bitcast_multiply_fusion) | data formatting | bytes 18874368 | tf_op jit(solution)/shard_map/reshape | solution.py:168
  358.4 202.5 %scatter_custom_fusion.4 = f32[3072,72]{1,0:T(8,128)S(1)} fusion(s32[32768]{0:T(1024)} %bitcast.70, f32[32768,72]{1,0:T(8,128)} %bitcast.64, f32[]{:T(128)} %constant.18.clone.1), kind=kCustom, calls=%fused_computation.128 | custom fusion | flops 2359296 | bytes 885248 | tf_op jit(solution)/shard_map/scatter-add | solution.py:169
  561.6 2.8 collective-permute-start.8
  566.2 3.8 collective-permute-done.9
  570.3 2.4 fusion.66
  572.7 1.9 copy.91
  574.6 2.1 collective-permute-start.10
  580.5 10.1 %all-to-all-start.4 = ((f32[128,2,128]{2,1,0:T(2,128)}), f32[128,2,128]{2,1,0:T(2,128)}, u32[]{:S(2)}, u32[]{:S(2)}) async-start(f32[128,2,128]{2,1,0:T(2,128)} %bitcast.53), calls=%async_computation.4 | async-start | bytes 262144 | tf_op jit(solution)/shard_map/all_to_all | solution.py:173
  594.5 4.0 fusion.30
  598.8 3.4 collective-permute-start.12
  603.9 2.3 gather_fusion.1
  610.8 2.0 copy.95
  615.4 2.6 collective-permute-start.15
  618.8 2.8 copy.96
  621.6 2.6 copy.98
  624.2 3.8 fusion.16
  (193 shorter events, 68.2 us)
Async XLA Ops:
  2.2 7.8 %copy-start.41 = (s32[128,1]{0,1:T(1,128)S(1)}, s32[128,1]{0,1:T(1,128)}, u32[]{:S(2)}) copy-start(s32[128,1]{0,1:T(1,128)} %param.19) | copy-start | bytes 1540
  3.5 20.4 %slice-start = ((f32[3,72,8,128]{3,2,1,0:T(8,128)}), f32[3,71,8,128]{3,2,1,0:T(8,128)S(1)}, s32[]{:S(2)}) async-start(f32[3,72,8,128]{3,2,1,0:T(8,128)} %param.10), calls=%async_computation.5 | async-start | bytes 1744896 | tf_op jit(solution)/shard_map/slice | solution.py:34
  3.5 56.1 %collective-permute-start = (f32[9,72,1,128]{3,2,0,1:T(1,128)}, f32[9,72,1,128]{3,2,0,1:T(1,128)}, u32[]{:S(2)}, u32[]{:S(2)}) collective-permute-start(f32[9,72,1,128]{3,2,0,1:T(1,128)} %get-tuple-element.18), channel_id=1, source_target_pairs={{0,16},{16,32},{32,48},{48,64},{64,80},{80,96},{96,112},{1,17},{17... | collective-permute-start | bytes 995336 | tf_op jit(solution)/shard_map/ppermute | solution.py:16
  8.7 50.8 %collective-permute-start.1 = (f32[9,72,1,128]{3,2,0,1:T(1,128)}, f32[9,72,1,128]{3,2,0,1:T(1,128)}, u32[]{:S(2)}, u32[]{:S(2)}) collective-permute-start(f32[9,72,1,128]{3,2,0,1:T(1,128)} %get-tuple-element.19), channel_id=1, source_target_pairs={{16,0},{32,16},{48,32},{64,48},{80,64},{96,80},{112,96},{17,1},{33... | collective-permute-start | bytes 995336 | tf_op jit(solution)/shard_map/ppermute | solution.py:17
  12.0 36.7 %all-to-all-start = ((s32[128,2,128]{2,1,0:T(2,128)}), s32[128,2,128]{2,1,0:T(2,128)}, u32[]{:S(2)}, u32[]{:S(2)}) async-start(s32[128,2,128]{2,1,0:T(2,128)} %bitcast.71), calls=%async_computation | async-start | bytes 262144 | tf_op jit(solution)/shard_map/all_to_all | solution.py:79
  23.9 570.6 %copy-start.37 = (pred[8]{0:T(512)(128)(4,1)}, pred[8]{0:T(512)(128)(4,1)S(1)}, u32[]{:S(2)}) copy-start(pred[8]{0:T(512)(128)(4,1)S(1)} %compare_and_fusion) | copy-start | bytes 28
  29.3 17.9 %copy-start.36 = (bf16[128,128]{1,0:T(8,128)(2,1)S(1)}, bf16[128,128]{1,0:T(8,128)(2,1)}, u32[]{:S(2)}) copy-start(bf16[128,128]{1,0:T(8,128)(2,1)} %param.17) | copy-start | bytes 98308
  29.3 17.9 %copy-start.39 = (s32[128]{0:T(128)S(1)}, s32[128]{0:T(128)}, u32[]{:S(2)}) copy-start(s32[128]{0:T(128)} %param.18) | copy-start | bytes 1540
  48.8 58.3 %all-to-all-start.3 = ((bf16[128,2,128]{2,1,0:T(2,128)(2,1)}), bf16[128,2,128]{2,1,0:T(2,128)(2,1)S(1)}, u32[]{:S(2)}, u32[]{:S(2)}) async-start(bf16[128,2,128]{2,1,0:T(2,128)(2,1)} %bitcast.22), calls=%async_computation.3 | async-start | bytes 131072 | tf_op jit(solution)/shard_map/all_to_all | solution.py:80
  59.5 18.6 %copy-start.29 = (s32[32768,1]{0,1:T(1,128)}, s32[32768,1]{0,1:T(1,128)S(1)}, u32[]{:S(2)}) copy-start(s32[32768,1]{0,1:T(1,128)S(1)} %compare_select_fusion) | copy-start | bytes 393220
  71.1 7.7 %collective-permute-start.2 = (f32[9,72,10,1]{1,3,2,0:T(1,128)S(1)}, f32[9,72,10,1]{1,3,2,0:T(1,128)S(1)}, u32[]{:S(2)}, u32[]{:S(2)}) collective-permute-start(f32[9,72,10,1]{1,3,2,0:T(1,128)S(1)} %copy.72), channel_id=1, source_target_pairs={{0,1},{1,2},{2,3},{3,4},{4,5},{5,6},{6,7},{7,8},{8,9},{9,10},{10,1... | collective-permute-start | bytes 77768 | tf_op jit(solution)/shard_map/ppermute | solution.py:16
  77.8 5.3 collective-permute-start.3
  99.0 6.4 %copy-start.1 = (f32[9,72,10,130]{3,2,0,1:T(8,128)}, f32[9,72,10,130]{3,2,0,1:T(8,128)S(1)}, u32[]{:S(2)}) copy-start(f32[9,72,10,130]{3,2,0,1:T(8,128)S(1)} %pad_maximum_fusion) | copy-start | bytes 10108804
  107.7 207.6 %all-to-all-start.1 = ((bf16[256,72,128]{2,1,0:T(8,128)(2,1)}), bf16[256,72,128]{2,1,0:T(8,128)(2,1)}, u32[]{:S(2)}, u32[]{:S(2)}) async-start(bf16[256,72,128]{2,1,0:T(8,128)(2,1)} %scatter_fusion), calls=%async_computation.1 | async-start | bytes 9437184 | tf_op jit(solution)/shard_map/all_to_all | solution.py:78
  131.7 6.8 %copy-start.16 = (f32[72,8,128]{2,1,0:T(8,128)}, f32[72,8,128]{2,1,0:T(8,128)S(1)}, u32[]{:S(2)}) copy-start(f32[72,8,128]{2,1,0:T(8,128)S(1)} %slice.392) | copy-start | bytes 884740
  131.7 5.7 copy-start.12
  131.9 22.8 %collective-permute-start.4 = (f32[3,72,1,128]{3,2,0,1:T(1,128)S(1)}, f32[3,72,1,128]{3,2,0,1:T(1,128)S(1)}, u32[]{:S(2)}, u32[]{:S(2)}) collective-permute-start(f32[3,72,1,128]{3,2,0,1:T(1,128)S(1)} %get-tuple-element.39), channel_id=1, source_target_pairs={{0,16},{16,32},{32,48},{48,64},{64,80},{80,96},{96,112},{1,17},{17... | collective-permute-start | bytes 331784 | tf_op jit(solution)/shard_map/ppermute | solution.py:16
  135.4 34.1 %collective-permute-start.5 = (f32[3,72,1,128]{3,2,0,1:T(1,128)S(1)}, f32[3,72,1,128]{3,2,0,1:T(1,128)S(1)}, u32[]{:S(2)}, u32[]{:S(2)}) collective-permute-start(f32[3,72,1,128]{3,2,0,1:T(1,128)S(1)} %get-tuple-element.38), channel_id=1, source_target_pairs={{16,0},{32,16},{48,32},{64,48},{80,64},{96,80},{112,96},{17,1},{33... | collective-permute-start | bytes 331784 | tf_op jit(solution)/shard_map/ppermute | solution.py:17
  137.4 10.7 %copy-start.9 = (f32[3,72,8,128]{3,2,0,1:T(8,128)}, f32[3,72,8,128]{3,2,0,1:T(8,128)S(1)}, u32[]{:S(2)}) copy-start(f32[3,72,8,128]{3,2,0,1:T(8,128)S(1)} %subtract_multiply_fusion.2) | copy-start | bytes 2654212
  154.7 14.8 %copy-start.23 = (f32[3,72,1,128]{3,2,0,1:T(1,128)}, f32[3,72,1,128]{3,2,0,1:T(1,128)S(1)}, u32[]{:S(2)}) copy-start(f32[3,72,1,128]{3,2,0,1:T(1,128)S(1)} %collective-permute-done.4) | copy-start | bytes 331780
  172.3 6.5 %copy-start.19 = (f32[72,9,128]{2,1,0:T(8,128)S(1)}, f32[72,9,128]{2,1,0:T(8,128)}, u32[]{:S(2)}) copy-start(f32[72,9,128]{2,1,0:T(8,128)} %slice.386) | copy-start | bytes 995332
  172.3 6.5 %copy-start.24 = (f32[3,72,1,128]{3,2,0,1:T(1,128)S(1)}, f32[3,72,1,128]{3,2,0,1:T(1,128)}, u32[]{:S(2)}) copy-start(f32[3,72,1,128]{3,2,0,1:T(1,128)} %copy-done.23) | copy-start | bytes 331780
  172.3 6.5 %copy-start.26 = (f32[3,72,1,128]{3,2,0,1:T(1,128)S(1)}, f32[3,72,1,128]{3,2,0,1:T(1,128)}, u32[]{:S(2)}) copy-start(f32[3,72,1,128]{3,2,0,1:T(1,128)} %copy-done.25) | copy-start | bytes 331780
  174.3 6.1 collective-permute-start.6
  178.7 4.7 collective-permute-start.7
  315.2 23.0 %all-to-all-start.2 = ((bf16[128,2,128]{2,1,0:T(2,128)(2,1)}), bf16[128,2,128]{2,1,0:T(2,128)(2,1)S(1)}, u32[]{:S(2)}, u32[]{:S(2)}) async-start(bf16[128,2,128]{2,1,0:T(2,128)(2,1)} %bitcast.7), calls=%async_computation.2 | async-start | bytes 131072 | tf_op jit(solution)/shard_map/all_to_all | solution.py:81
  328.6 9.6 %copy-start.28 = (bf16[128,2,128]{2,1,0:T(2,128)(2,1)S(1)}, bf16[128,2,128]{2,1,0:T(2,128)(2,1)}, u32[]{:S(2)}) copy-start(bf16[128,2,128]{2,1,0:T(2,128)(2,1)} %copy-done.27) | copy-start | bytes 196612
  561.6 4.5 collective-permute-start.8
  564.5 5.5 collective-permute-start.9
  565.9 14.6 %copy-start.7 = (f32[3,72,8,128]{3,2,0,1:T(8,128)}, f32[3,72,8,128]{3,2,0,1:T(8,128)S(1)}, u32[]{:S(2)}) copy-start(f32[3,72,8,128]{3,2,0,1:T(8,128)S(1)} %subtract_multiply_fusion.1) | copy-start | bytes 2654212
  566.2 6.5 %copy-start.32 = (f32[3,72,1,128]{3,2,0,1:T(1,128)}, f32[3,72,1,128]{3,2,0,1:T(1,128)S(1)}, u32[]{:S(2)}) copy-start(f32[3,72,1,128]{3,2,0,1:T(1,128)S(1)} %collective-permute-done.8) | copy-start | bytes 331780
  574.6 16.1 %collective-permute-start.10 = (f32[3,72,10,1]{1,3,2,0:T(1,128)S(1)}, f32[3,72,10,1]{1,3,2,0:T(1,128)S(1)}, u32[]{:S(2)}, u32[]{:S(2)}) collective-permute-start(f32[3,72,10,1]{1,3,2,0:T(1,128)S(1)} %copy.91), channel_id=1, source_target_pairs={{1,0},{2,1},{3,2},{4,3},{5,4},{6,5},{7,6},{8,7},{9,8},{10,9},{11,1... | collective-permute-start | bytes 25928 | tf_op jit(solution)/shard_map/ppermute | solution.py:17
  578.6 14.0 %collective-permute-start.11 = (f32[3,72,10,1]{1,3,2,0:T(1,128)S(1)}, f32[3,72,10,1]{1,3,2,0:T(1,128)S(1)}, u32[]{:S(2)}, u32[]{:S(2)}) collective-permute-start(f32[3,72,10,1]{1,3,2,0:T(1,128)S(1)} %copy.93), channel_id=1, source_target_pairs={{0,1},{1,2},{2,3},{3,4},{4,5},{5,6},{6,7},{7,8},{8,9},{9,10},{10,1... | collective-permute-start | bytes 25928 | tf_op jit(solution)/shard_map/ppermute | solution.py:16
  580.5 23.4 %all-to-all-start.4 = ((f32[128,2,128]{2,1,0:T(2,128)}), f32[128,2,128]{2,1,0:T(2,128)}, u32[]{:S(2)}, u32[]{:S(2)}) async-start(f32[128,2,128]{2,1,0:T(2,128)} %bitcast.53), calls=%async_computation.4 | async-start | bytes 262144 | tf_op jit(solution)/shard_map/all_to_all | solution.py:173
  598.5 5.2 copy-start.15
  598.8 7.4 %collective-permute-start.12 = (f32[3,72,1,128]{3,2,0,1:T(1,128)S(1)}, f32[3,72,1,128]{3,2,0,1:T(1,128)S(1)}, u32[]{:S(2)}, u32[]{:S(2)}) collective-permute-start(f32[3,72,1,128]{3,2,0,1:T(1,128)S(1)} %get-tuple-element.35), channel_id=1, source_target_pairs={{0,16},{16,32},{32,48},{48,64},{64,80},{80,96},{96,112},{1,17},{17... | collective-permute-start | bytes 331784 | tf_op jit(solution)/shard_map/ppermute | solution.py:16
  602.2 5.9 collective-permute-start.13
  603.9 5.2 copy-start.5
  610.8 7.2 %copy-start.35 = (f32[128,128]{1,0:T(8,128)S(1)}, f32[128,128]{1,0:T(8,128)}, u32[]{:S(2)}) copy-start(f32[128,128]{1,0:T(8,128)} %gather_fusion.1) | copy-start | bytes 196612
  610.8 7.2 %copy-start.40 = (s32[128]{0:T(128)S(1)}, s32[128]{0:T(128)}, u32[]{:S(2)}) copy-start(s32[128]{0:T(128)} %param.18) | copy-start | bytes 1540
  612.8 6.0 collective-permute-start.14
  615.4 6.2 collective-permute-start.15
  618.8 5.4 copy-start.6
  618.8 5.5 slice-start.5
  618.8 5.5 copy-start.20
  618.8 5.5 copy-start.21
  618.8 5.5 copy-start.22
  618.8 5.5 copy-start.38
  (23 other events, 59.7 us)
where the time goes:
time: 642 us; the launch traced here: 629 us
  other arithmetic  263 us (41%)
  local copies, waits for them, and re-layouts  241 us (38%)
  starting transfers between devices  90.7 us (14%)
  waiting for transfers between devices  32.5 us (5%)
    scatter-add x1, other arithmetic, per_device(): jnp.zeros((cells_all, levels), jnp.float32).at[flat_index].add(vectors)  202 us
    gather x1, local copies, waits for them, and re-layouts, per_device(): profile = cell_rows[flat_index].reshape(slot_total, sounds, levels)  109 us
    ppermute x8, starting transfers between devices, extended(): before = lax.ppermute(last, axis, up)  26.1 us
    ppermute x8, waiting for transfers between devices, extended(): after = lax.ppermute(initial, axis, down)  22.6 us
    scatter x1, local copies, waits for them, and re-layouts, route_blocks(): jnp.zeros((slot_total, levels, sounds), jnp.bfloat16).at[slot_index]  17.9 us
    concatenate x5, other arithmetic, extended(): shard = jnp.concatenate([before, shard, after], axis=dim)  16 us
    slice x6, local copies, waits for them, and re-layouts, extended(): last = lax.slice_in_dim(shard, length - width, length, axis=dim)  16 us
    reshape x1, local copies, waits for them, and re-layouts, per_device(): profile = cell_rows[flat_index].reshape(slot_total, sounds, levels)  14.4 us
  transfers between devices with their start and end apart: 21, of which 8 were waited for; matrix products, arithmetic and copies ran while one was open for 40% of the time, Pallas kernels for 0%

commit v1 on v0

v1 whole, which is shorter than its diff:
```python
import functools

import jax
import jax.numpy as jnp
from jax import lax
from jax.experimental import pallas as pl
from jax.experimental.pallas import tpu as pltpu
from jax.sharding import PartitionSpec as P

CAP = 2
LEVELS = 72
ROWS = 80
PAIR = 2 * LEVELS
TRACERS = 3
LAT_CELLS = 8
LANES = 128
VMEM_LIMIT = 48 << 20


def lane_index():
    return lax.broadcasted_iota(jnp.int32, (LEVELS, LANES), 1)


def rolled(array, shift, axis):
    shift = shift % array.shape[axis]
    return pltpu.roll(array, shift, axis) if shift else array


def west_of(slab, halo, place):
    return jnp.where(lane_index() == 0, rolled(halo, -place, 1), rolled(slab, 1, 1))


def east_of(slab, halo, place):
    return jnp.where(
        lane_index() == LANES - 1, rolled(halo, LANES - 1 - place, 1), rolled(slab, -1, 1)
    )


def packed_columns(slabs, lane):
    packed = jnp.zeros((LEVELS, LANES), jnp.float32)
    for place, slab in enumerate(slabs):
        packed = jnp.where(lane_index() == place, rolled(slab, place - lane, 1), packed)
    return packed


def mixed(slab, coeff):
    upward = coeff * (rolled(slab, -1, 0) - slab)
    return upward - rolled(upward, 1, 0)


def write_edges(read, north_edge, south_edge, east_edge, west_edge):
    slabs = [read(t, row) for t in range(TRACERS) for row in range(LAT_CELLS)]
    for t in range(TRACERS):
        north_edge[t] = slabs[t * LAT_CELLS + LAT_CELLS - 1]
        south_edge[t] = slabs[t * LAT_CELLS]
    east_edge[...] = packed_columns(slabs, LANES - 1)
    west_edge[...] = packed_columns(slabs, 0)


def prepare_body(
    last_ref, initial_ref, east_ref, north_ref, mixing_ref,
    state_ref, east_out, north_out, mixing_out, north_edge, south_edge, east_edge, west_edge,
):
    steps = east_ref.shape[0]
    top = lax.broadcasted_iota(jnp.int32, (LEVELS, LANES), 0) == LEVELS - 1
    for t in range(TRACERS):
        for row in range(LAT_CELLS):
            state_ref[t, row] = initial_ref[t, :, row, :]
    for m in range(steps):
        for row in range(LAT_CELLS):
            east_out[m, row] = east_ref[m, :, row, :]
            north = north_ref[m, :, row, :]
            if row == LAT_CELLS - 1:
                north = jnp.where(last_ref[0] > 0, jnp.float32(0.0), north)
            north_out[m, row] = north
            mixing_out[m, row] = jnp.where(top, jnp.float32(0.0), mixing_ref[m, :, row, :])
    for t in range(TRACERS):
        north_edge[t] = state_ref[t, LAT_CELLS - 1]
        south_edge[t] = state_ref[t, 0]
    for m in range(steps):
        north_edge[TRACERS + m] = north_out[m, LAT_CELLS - 1]
    slabs = [state_ref[t, row] for t in range(TRACERS) for row in range(LAT_CELLS)]
    winds = [east_out[m, row] for m in range(steps) for row in range(LAT_CELLS)]
    east_edge[...] = packed_columns(slabs + winds, LANES - 1)
    west_edge[...] = packed_columns(slabs, 0)


def wind_west(east, east_halo, m, row):
    return west_of(east, east_halo, TRACERS * LAT_CELLS + m * LAT_CELLS + row)


def forward_slabs(m, state_ref, east_ref, north_ref, mixing_ref, halos, winds):
    from_south, from_north, from_west, from_east = halos
    wind_south, wind_column = winds
    for row in range(LAT_CELLS):
        east = east_ref[m, row]
        before = wind_west(east, wind_column[...], m, row)
        north = north_ref[m, row]
        south = north_ref[m, row - 1] if row else wind_south[TRACERS + m]
        coeff = mixing_ref[m, row]
        for t in range(TRACERS):
            place = t * LAT_CELLS + row
            slab = state_ref[t, row]
            left = west_of(slab, from_west[...], place)
            right = east_of(slab, from_east[...], place)
            above = state_ref[t, row + 1] if row < LAT_CELLS - 1 else from_north[t]
            below = state_ref[t, row - 1] if row else from_south[t]
            zonal = jnp.maximum(east, 0.0) * slab + jnp.minimum(east, 0.0) * right
            zonal_before = jnp.maximum(before, 0.0) * left + jnp.minimum(before, 0.0) * slab
            merid = jnp.maximum(north, 0.0) * slab + jnp.minimum(north, 0.0) * above
            merid_before = jnp.maximum(south, 0.0) * below + jnp.minimum(south, 0.0) * slab
            yield t, row, slab - (zonal - zonal_before) - (merid - merid_before) + mixed(
                slab, coeff
            )


def adjoint_slabs(m, read, east_ref, north_ref, mixing_ref, halos, winds):
    from_south, from_north, from_west, from_east = halos
    wind_south, wind_column = winds
    for row in range(LAT_CELLS):
        east = jnp.maximum(east_ref[m, row], 0.0)
        before = jnp.minimum(wind_west(east_ref[m, row], wind_column[...], m, row), 0.0)
        north = jnp.maximum(north_ref[m, row], 0.0)
        south = jnp.minimum(north_ref[m, row - 1] if row else wind_south[TRACERS + m], 0.0)
        coeff = mixing_ref[m, row]
        for t in range(TRACERS):
            place = t * LAT_CELLS + row
            slab = read(t, row)
            left = west_of(slab, from_west[...], place)
            right = east_of(slab, from_east[...], place)
            above = read(t, row + 1) if row < LAT_CELLS - 1 else from_north[t]
            below = read(t, row - 1) if row else from_south[t]
            yield t, row, (
                slab
                + (east * (right - slab) + before * (slab - left))
                + (north * (above - slab) + south * (slab - below))
                + mixed(slab, coeff)
            )


def forward_first_body(
    state_ref, east_ref, north_ref, mixing_ref, s, n, w, e, out_ref, *edges
):
    for t, row, slab in forward_slabs(
        0, state_ref, east_ref, north_ref, mixing_ref, (s, n, w, e), (s, w)
    ):
        out_ref[t, row] = slab
    write_edges(lambda t, row: out_ref[t, row], *edges)


def forward_last_body(
    state_ref, east_ref, north_ref, mixing_ref, s, n, w, e, wind_s, wind_w, field_ref, after_ref
):
    for t, row, slab in forward_slabs(
        1, state_ref, east_ref, north_ref, mixing_ref, (s, n, w, e), (wind_s, wind_w)
    ):
        after_ref[t, row] = slab
    for i in range(6):
        for low_row in range(2):
            slabs = []
            for p in (2 * i, 2 * i + 1):
                slabs.append(after_ref[p // 4, (p % 4) * 2 + low_row])
            both = jnp.concatenate(slabs, axis=0)
            high = both.astype(jnp.bfloat16)
            low = (both - high.astype(jnp.float32)).astype(jnp.bfloat16)
            rows = slice(i * PAIR, (i + 1) * PAIR)
            field_ref[rows, low_row * LANES : (low_row + 1) * LANES] = high
            field_ref[rows, (2 + low_row) * LANES : (3 + low_row) * LANES] = low


def cell_slab(ref, t, row):
    first = (t * 4 + row // 2) * LEVELS
    return ref[first : first + LEVELS, (row % 2) * LANES : (row % 2 + 1) * LANES]


def adjoint_first_body(
    adjoint_ref, east_ref, north_ref, mixing_ref, s, n, w, e, wind_s, wind_w, out_ref, *edges
):
    for t, row, slab in adjoint_slabs(
        1,
        lambda t, row: cell_slab(adjoint_ref, t, row),
        east_ref, north_ref, mixing_ref, (s, n, w, e), (wind_s, wind_w),
    ):
        out_ref[t, row] = slab
    write_edges(lambda t, row: out_ref[t, row], *edges)


def adjoint_last_body(
    state_ref, east_ref, north_ref, mixing_ref, s, n, w, e, wind_s, wind_w, out_ref
):
    for t, row, slab in adjoint_slabs(
        0,
        lambda t, row: state_ref[t, row],
        east_ref, north_ref, mixing_ref, (s, n, w, e), (wind_s, wind_w),
    ):
        out_ref[t, :, row, :] = slab


STATE = jax.ShapeDtypeStruct((TRACERS, LAT_CELLS, LEVELS, LANES), jnp.float32)
ROW_EDGE = jax.ShapeDtypeStruct((TRACERS, LEVELS, LANES), jnp.float32)
COLUMN_EDGE = jax.ShapeDtypeStruct((LEVELS, LANES), jnp.float32)
EDGES = [ROW_EDGE, ROW_EDGE, COLUMN_EDGE, COLUMN_EDGE]


def whole(body, outs, operands, name, scratch=(), scalars=0):
    vmem = pl.BlockSpec(memory_space=pltpu.VMEM)
    smem = pl.BlockSpec(memory_space=pltpu.SMEM)
    return pl.pallas_call(
        body,
        in_specs=[smem if i < scalars else vmem for i in range(len(operands))],
        out_specs=jax.tree.map(lambda _: vmem, outs),
        out_shape=outs,
        scratch_shapes=list(scratch),
        compiler_params=pltpu.CompilerParams(vmem_limit_bytes=VMEM_LIMIT),
        cost_estimate=pl.CostEstimate(flops=5000000, bytes_accessed=6000000, transcendentals=0),
        name=name,
    )(*operands)


def exchange_edges(edges):
    north_edge, south_edge, east_edge, west_edge = edges
    lat, lon = lax.axis_size("lat"), lax.axis_size("lon")
    up = [(i, i + 1) for i in range(lat - 1)]
    right = [(i, (i + 1) % lon) for i in range(lon)]
    return (
        lax.ppermute(north_edge, "lat", up),
        lax.ppermute(south_edge, "lat", [(j, i) for i, j in up]),
        lax.ppermute(east_edge, "lon", right),
        lax.ppermute(west_edge, "lon", [(j, i) for i, j in right]),
    )


def pack_body(source_ref, kernel_ref, meta_ref, out_ref):
    def one(slot, carry):
        source = source_ref[slot]
        block = jnp.maximum(source, 0)
        meta = jnp.where(source >= 0, meta_ref[block].astype(jnp.float32), jnp.float32(0.0))
        rows = jnp.concatenate([kernel_ref[block].astype(jnp.float32), meta], axis=0)
        out_ref[slot] = rows.astype(jnp.bfloat16)
        return carry

    lax.fori_loop(0, out_ref.shape[0], one, 0, unroll=4)


def pack_blocks(source, kernel, meta):
    count, _, sounds = kernel.shape
    vmem = pl.BlockSpec(memory_space=pltpu.VMEM)
    return pl.pallas_call(
        pack_body,
        in_specs=[pl.BlockSpec(memory_space=pltpu.SMEM), vmem, vmem],
        out_specs=vmem,
        out_shape=jax.ShapeDtypeStruct((count, ROWS, sounds), jnp.bfloat16),
        compiler_params=pltpu.CompilerParams(vmem_limit_bytes=VMEM_LIMIT),
        name="pack_blocks",
    )(source, kernel, meta)


def first_soundings_body(per_step, width, field_ref, block_ref, adjoint_ref, misfit_ref):
    @pl.when(pl.program_id(0) == 0)
    def _():
        adjoint_ref[...] = jnp.zeros_like(adjoint_ref)

    def write_misfit(block, row):
        misfit_ref[block : block + 1, :] = row

    soundings(per_step, width, field_ref, block_ref, adjoint_ref, write_misfit)


def second_soundings_body(
    per_step, width, field_ref, block_ref, earlier_ref, other_ref, adjoint_ref, misfit_ref, *edges
):
    @pl.when(pl.program_id(0) == 0)
    def _():
        adjoint_ref[...] = earlier_ref[...]

    def write_misfit(block, row):
        misfit_ref[2 * block : 2 * block + 1, :] = other_ref[block : block + 1, :]
        misfit_ref[2 * block + 1 : 2 * block + 2, :] = row

    soundings(per_step, width, field_ref, block_ref, adjoint_ref, write_misfit)

    @pl.when(pl.program_id(0) == pl.num_programs(0) - 1)
    def _():
        write_edges(lambda t, row: cell_slab(adjoint_ref, t, row), *edges)


def soundings(per_step, width, field_ref, block_ref, adjoint_ref, write_misfit):

    n = width * 128
    for group in range(per_step // width):
        first = group * width
        blocks = [block_ref[first + i] for i in range(width)]
        profile = jnp.concatenate([b[:LEVELS] for b in blocks], axis=1)
        meta = jnp.concatenate([b[LEVELS:] for b in blocks], axis=1).astype(jnp.float32)
        part, cell, observed, weight = (meta[j : j + 1] for j in range(4))
        hit = lax.broadcasted_iota(jnp.int32, (256, n), 0).astype(jnp.float32) == cell
        pick = jnp.where(hit, 1.0, 0.0).astype(jnp.bfloat16)
        pick_twice = jnp.concatenate([pick, pick], axis=0)
        column = jnp.zeros((LEVELS, n), jnp.float32)
        for i in range(6):
            found = jnp.dot(
                field_ref[i * PAIR : (i + 1) * PAIR, :],
                pick_twice,
                preferred_element_type=jnp.float32,
            )
            column = jnp.where(part == 2.0 * i, found[:LEVELS], column)
            column = jnp.where(part == 2.0 * i + 1.0, found[LEVELS:], column)
        model = jnp.sum(profile.astype(jnp.float32) * column, axis=0, keepdims=True)
        misfit = model - observed
        for i in range(width):
            write_misfit(first + i, misfit[:, i * 128 : (i + 1) * 128])
        forcing = weight * misfit
        high = forcing.astype(jnp.bfloat16).astype(jnp.float32)
        low = forcing - high
        spread = jnp.concatenate(
            [
                jnp.where(hit, high, 0.0).astype(jnp.bfloat16),
                jnp.where(hit, low, 0.0).astype(jnp.bfloat16),
            ],
            axis=1,
        )
        twice = jnp.concatenate([profile, profile], axis=0)
        second = lax.broadcasted_iota(jnp.int32, (PAIR, n), 0) >= LEVELS
        part_row = (part - jnp.where(second, 1.0, 0.0)).astype(jnp.bfloat16)
        for i in range(6):
            left = jnp.where(part_row == jnp.bfloat16(2 * i), twice, jnp.bfloat16(0))
            adjoint_ref[i * PAIR : (i + 1) * PAIR, :] += lax.dot_general(
                jnp.concatenate([left, left], axis=1),
                spread,
                (((1,), (1,)), ((), ())),
                preferred_element_type=jnp.float32,
            )


def observe(field, blocks, earlier=None):
    count = blocks.shape[0]
    per_step, width = 16, 4

    def fixed(shape):
        return pl.BlockSpec(shape, lambda i: (0,) * len(shape))

    def rows(height):
        return pl.BlockSpec((height, 128), lambda i: (i, 0))

    cells = (12 * LEVELS, 256)
    in_specs = [
        fixed((12 * LEVELS, 512)),
        pl.BlockSpec((per_step, ROWS, 128), lambda i: (i, 0, 0)),
    ]
    first = earlier is None
    outs = [jax.ShapeDtypeStruct(cells, jnp.float32)]
    if first:
        body, operands = first_soundings_body, (field, blocks)
        out_specs = [fixed(cells), rows(per_step)]
        outs += [jax.ShapeDtypeStruct((count, 128), jnp.float32)]
    else:
        body, operands = second_soundings_body, (field, blocks) + tuple(earlier)
        in_specs += [fixed(cells), rows(per_step)]
        out_specs = [fixed(cells), rows(2 * per_step)] + [fixed(edge.shape) for edge in EDGES]
        outs += [jax.ShapeDtypeStruct((2 * count, 128), jnp.float32)] + EDGES
    return pl.pallas_call(
        functools.partial(body, per_step, width),
        grid=(count // per_step,),
        in_specs=in_specs,
        out_specs=out_specs,
        out_shape=outs,
        compiler_params=pltpu.CompilerParams(vmem_limit_bytes=VMEM_LIMIT),
        cost_estimate=pl.CostEstimate(
            flops=count * 4 * 864 * 512 * 128, bytes_accessed=count * 40960, transcendentals=0
        ),
        name="first_soundings" if first else "second_soundings",
    )(*operands)


def per_device(
    initial, east_wind, north_wind, mixing, kernel, columns, observed, obs_weight, counts, targets
):
    lat_count = lax.axis_size("lat")
    lon_count = lax.axis_size("lon")
    sounds = kernel.shape[2]
    target_dev = targets[:, 0]
    block_count = target_dev.shape[0]
    device_count = lat_count * lon_count
    block_id = lax.broadcasted_iota(jnp.int32, (block_count, device_count), 0)
    meant = target_dev[:, None] == lax.broadcasted_iota(
        jnp.int32, (block_count, device_count), 1
    )
    source_first = jnp.min(jnp.where(meant, block_id, block_count), axis=0)
    source_last = jnp.max(jnp.where(meant, block_id, -1), axis=0)
    source_first = jnp.where(source_last >= 0, source_first, -1)
    source_second = jnp.where(source_last > source_first, source_last, -1)
    is_second = jnp.max(jnp.where(meant & (block_id != source_first[None, :]), 1, 0), axis=1)
    slot_index = target_dev * CAP + is_second
    live = lax.broadcasted_iota(jnp.int32, (1, sounds), 1) < counts[:, None]
    weight_live = jnp.where(live, obs_weight, jnp.zeros_like(obs_weight))
    zeros = jnp.zeros_like(obs_weight)
    meta = jnp.stack(
        [(columns // 256).astype(jnp.bfloat16), (columns % 256).astype(jnp.bfloat16)]
        + [observed, weight_live, zeros, zeros, zeros, zeros],
        axis=1,
    )

    def exchange(array):
        return lax.all_to_all(array, ("lat", "lon"), split_axis=0, concat_axis=0, tiled=True)

    got_first = exchange(pack_blocks(source_first, kernel, meta))
    got_second = exchange(pack_blocks(source_second, kernel, meta))

    is_last = (lax.axis_index("lat") == lat_count - 1).astype(jnp.int32).reshape(1)
    winds_like = jax.ShapeDtypeStruct((2, LAT_CELLS, LEVELS, LANES), jnp.float32)
    tall_edge = jax.ShapeDtypeStruct((TRACERS + 2, LEVELS, LANES), jnp.float32)
    prepared = whole(
        prepare_body,
        [STATE, winds_like, winds_like, winds_like, tall_edge] + EDGES[1:],
        (is_last, initial, east_wind, north_wind, mixing),
        "prepare",
        scalars=1,
    )
    state, fields, edges = prepared[0], tuple(prepared[1:4]), prepared[4:]
    halos = exchange_edges(edges)
    winds = (halos[0], halos[2])
    middle, *edges = whole(
        forward_first_body, [STATE] + EDGES, (state,) + fields + halos, "forward_first"
    )
    field = whole(
        forward_last_body,
        jax.ShapeDtypeStruct((12 * LEVELS, 512), jnp.bfloat16),
        (middle,) + fields + exchange_edges(edges) + winds,
        "forward_last",
        scratch=[pltpu.VMEM(STATE.shape, jnp.float32)],
    )
    earlier = observe(field, got_first)
    adjoint, misfit, *edges = observe(field, got_second, earlier)
    halos = exchange_edges(edges)
    returned = exchange(misfit)
    middle, *edges = whole(
        adjoint_first_body, [STATE] + EDGES, (adjoint,) + fields + halos + winds, "adjoint_first"
    )
    gradient = whole(
        adjoint_last_body,
        jax.ShapeDtypeStruct(initial.shape, jnp.float32),
        (middle,) + fields + exchange_edges(edges) + winds,
        "adjoint_last",
    )
    innovations = jnp.where(live, returned[slot_index], jnp.float32(0.0))
    return (gradient, innovations)


def solution(mesh):
    return jax.shard_map(
        per_device,
        mesh=mesh,
        in_specs=(
            P(None, None, "lat", "lon"),
            P(None, None, "lat", "lon"),
            P(None, None, "lat", "lon"),
            P(None, None, "lat", "lon"),
            P(("lat", "lon"), None, None),
            P(("lat", "lon"), None),
            P(("lat", "lon"), None),
            P(("lat", "lon"), None),
            P(("lat", "lon")),
            P(("lat", "lon"), None),
        ),
        out_specs=(P(None, None, "lat", "lon"), P(("lat", "lon"), None)),
        check_vma=False,
    )
```

time: 642 us -> 250 us (0.39)
  the two profiles are of different devices: /device:TPU:1 before, /device:TPU:31 now
where the time goes in v1:
time: 250 us; the launch traced here: 249 us
  Pallas kernels  128 us (51%)
  starting transfers between devices  66.1 us (26%)
  waiting for transfers between devices  37.5 us (15%)
  local copies, waits for them, and re-layouts  12.4 us (5%)
  other arithmetic  3.42 us (1%)
    pallas_call x2, Pallas kernels, observe(): pl.pallas_call(functools.partial(body, per_step, width), grid=(count // p...  113 us
    all_to_all x3, starting transfers between devices, exchange(): lax.all_to_all(array, ('lat', 'lon'), split_axis=0, concat_axis=0, tiled=...  27.6 us
    ppermute x4, starting transfers between devices, exchange_edges(): lax.ppermute(south_edge, 'lat', [(j, i) for i, j in up])  19 us
    ppermute x4, waiting for transfers between devices, exchange_edges(): lax.ppermute(west_edge, 'lon', [(j, i) for i, j in right])  17.5 us
    ppermute x4, waiting for transfers between devices, exchange_edges(): lax.ppermute(east_edge, 'lon', right)  17.3 us
    ppermute x4, starting transfers between devices, exchange_edges(): lax.ppermute(north_edge, 'lat', up)  10.6 us
    unnamed x28, local copies, waits for them, and re-layouts  10.2 us
    pallas_call x5, Pallas kernels, whole(): pl.pallas_call(body, in_specs=[smem if i < scalars else vmem for i in ran...  9.28 us
  transfers between devices with their start and end apart: 19, of which 8 were waited for; matrix products, arithmetic and copies ran while one was open for 1% of the time, Pallas kernels for 27%

profile of v1, /device:TPU:31, one launch (start us, length us, event | category | flops | bytes accessed | tf_op | source)
XLA Modules:
  0.0 248.6 jit_solution(4608557503142923473)
XLA Ops:
  0.6 0.8 select_reduce_fusion.1
  1.4 0.9 fusion.8
  2.4 0.8 fusion.7
  3.3 0.8 copy.18
  4.2 0.5 stack.23.meta_ref
  4.7 1.7 copy-done
  6.4 2.9 %pack_blocks.3 = bf16[128,80,128]{2,1,0:T(8,128)(2,1)} custom-call(s32[128]{0:T(128)S(1)} %get-tuple-element.58.source_ref, bf16[128,72,128]{2,1,0:T(8,128)(2,1)S(1)} %copy-done, bf16[128,8,128]{2,1,0:T(8,128)(2,1)S(1)} %stack.23.meta_ref), custom_call_target="tpu_custom_call" | custom-call | tf_op jit(solution)/shard_map/pack_blocks/pallas_call | solution.py:248
  9.3 10.9 %all-to-all-start.1 = ((bf16[128,80,128]{2,1,0:T(8,128)(2,1)}), bf16[128,80,128]{2,1,0:T(8,128)(2,1)}, u32[]{:S(2)}, u32[]{:S(2)}) async-start(bf16[128,80,128]{2,1,0:T(8,128)(2,1)} %pack_blocks.3), calls=%async_computation.1 | async-start | bytes 5242880 | tf_op jit(solution)/shard_map/all_to_all | solution.py:404
  20.3 1.1 copy-done.7
  21.4 1.1 copy-done.8
  22.4 1.1 copy-done.9
  23.5 1.9 prepare.1
  25.4 3.4 %collective-permute-start = (f32[5,72,128]{2,1,0:T(8,128)S(1)}, f32[5,72,128]{2,1,0:T(8,128)S(1)}, u32[]{:S(2)}, u32[]{:S(2)}) collective-permute-start(f32[5,72,128]{2,1,0:T(8,128)S(1)} %get-tuple-element.32), channel_id=1, source_target_pairs={{0,16},{16,32},{32,48},{48,64},{64,80},{80,96},{96,112},{1,17},{17... | collective-permute-start | bytes 552968 | tf_op jit(solution)/shard_map/ppermute | solution.py:226
  28.8 4.0 %collective-permute-start.1 = (f32[3,72,128]{2,1,0:T(8,128)S(1)}, f32[3,72,128]{2,1,0:T(8,128)S(1)}, u32[]{:S(2)}, u32[]{:S(2)}) collective-permute-start(f32[3,72,128]{2,1,0:T(8,128)S(1)} %get-tuple-element.33), channel_id=1, source_target_pairs={{16,0},{32,16},{48,32},{64,48},{80,64},{96,80},{112,96},{17,1},{33... | collective-permute-start | bytes 331784 | tf_op jit(solution)/shard_map/ppermute | solution.py:227
  32.8 2.0 collective-permute-start.2
  34.8 16.0 %collective-permute-done.2.w.wind_w = f32[72,128]{1,0:T(8,128)S(1)} collective-permute-done((f32[72,128]{1,0:T(8,128)S(1)}, f32[72,128]{1,0:T(8,128)S(1)}, u32[]{:S(2)}, u32[]{:S(2)}) %collective-permute-start.2) | collective-permute-done | bytes 36896 | tf_op jit(solution)/shard_map/ppermute | solution.py:228
  50.7 2.4 collective-permute-done.3.e
  53.2 2.7 %collective-permute-done.s.wind_s = f32[5,72,128]{2,1,0:T(8,128)S(1)} collective-permute-done((f32[5,72,128]{2,1,0:T(8,128)S(1)}, f32[5,72,128]{2,1,0:T(8,128)S(1)}, u32[]{:S(2)}, u32[]{:S(2)}) %collective-permute-start) | collective-permute-done | bytes 184352 | tf_op jit(solution)/shard_map/ppermute | solution.py:226
  55.8 1.8 forward_first.1
  57.7 1.9 collective-permute-start.4
  59.6 5.5 %collective-permute-start.5 = (f32[3,72,128]{2,1,0:T(8,128)S(1)}, f32[3,72,128]{2,1,0:T(8,128)S(1)}, u32[]{:S(2)}, u32[]{:S(2)}) collective-permute-start(f32[3,72,128]{2,1,0:T(8,128)S(1)} %get-tuple-element.38), channel_id=1, source_target_pairs={{16,0},{32,16},{48,32},{64,48},{80,64},{96,80},{112,96},{17,1},{33... | collective-permute-start | bytes 331784 | tf_op jit(solution)/shard_map/ppermute | solution.py:227
  65.1 4.0 %collective-permute-start.6 = (f32[72,128]{1,0:T(8,128)S(1)}, f32[72,128]{1,0:T(8,128)S(1)}, u32[]{:S(2)}, u32[]{:S(2)}) collective-permute-start(f32[72,128]{1,0:T(8,128)S(1)} %get-tuple-element.39), channel_id=1, source_target_pairs={{0,1},{1,2},{2,3},{3,4},{4,5},{5,6},{6,7},{7,8},{8,9},{9,10},{10,1... | collective-permute-start | bytes 110600 | tf_op jit(solution)/shard_map/ppermute | solution.py:228
  69.1 0.2 select_reduce_fusion
  69.3 3.0 %pack_blocks.2 = bf16[128,80,128]{2,1,0:T(8,128)(2,1)} custom-call(s32[128]{0:T(128)S(1)} %get-tuple-element.59.source_ref, bf16[128,72,128]{2,1,0:T(8,128)(2,1)S(1)} %copy-done.1, bf16[128,8,128]{2,1,0:T(8,128)(2,1)S(1)} %stack.23.meta_ref), custom_call_target="tpu_custom_call" | custom-call | tf_op jit(solution)/shard_map/pack_blocks/pallas_call | solution.py:248
  72.3 3.8 %collective-permute-done.7.e = f32[72,128]{1,0:T(8,128)S(1)} collective-permute-done((f32[72,128]{1,0:T(8,128)S(1)}, f32[72,128]{1,0:T(8,128)S(1)}, u32[]{:S(2)}, u32[]{:S(2)}) %collective-permute-start.7) | collective-permute-done | bytes 36896 | tf_op jit(solution)/shard_map/ppermute | solution.py:229
  76.1 1.4 forward_last.1.field_ref
  77.5 6.9 %all-to-all-start = ((bf16[128,80,128]{2,1,0:T(8,128)(2,1)}), bf16[128,80,128]{2,1,0:T(8,128)(2,1)}, u32[]{:S(2)}, u32[]{:S(2)}) async-start(bf16[128,80,128]{2,1,0:T(8,128)(2,1)} %pack_blocks.2), calls=%async_computation | async-start | bytes 5242880 | tf_op jit(solution)/shard_map/all_to_all | solution.py:404
  84.4 56.2 %first_soundings.1 = (f32[864,256]{1,0:T(8,128)S(1)}, f32[128,128]{1,0:T(8,128)S(1)}) custom-call(bf16[864,512]{1,0:T(8,128)(2,1)S(1)} %forward_last.1.field_ref, bf16[128,80,128]{2,1,0:T(8,128)(2,1)} %all-to-all-done.1.block_ref), custom_call_target="tpu_custom_call" | custom-call | flops 28991029248 | bytes 5242880 | tf_op jit(solution)/shard_map/first_soundings/pallas_call | solution.py:361
  140.6 0.9 copy-done.10
  141.6 1.2 copy-done.6
  142.7 1.2 copy-done.11
  143.9 56.8 %second_soundings.1 = (f32[864,256]{1,0:T(8,128)S(1)}, f32[256,128]{1,0:T(8,128)}, f32[3,72,128]{2,1,0:T(8,128)S(1)}, f32[3,72,128]{2,1,0:T(8,128)S(1)}, f32[72,128]{1,0:T(8,128)S(1)}, /*index=5*/f32[72,128]{1,0:T(8,128)S(1)}) custom-call(bf16[864,512]{1,0:T(8,128)(2,1)S(1)} %copy-done.6, bf16[128,80,128]{2,1,0:T(8,128)(2,1)} %all-to-all-done.block_ref, ...), custom_call_target="tpu_custom_call" | custom-call | flops 28991029248 | bytes 5242880 | tf_op jit(solution)/shard_map/second_soundings/pallas_call | solution.py:361
  200.7 9.8 %all-to-all-start.2 = ((f32[128,2,128]{2,1,0:T(2,128)}), f32[128,2,128]{2,1,0:T(2,128)S(1)}, u32[]{:S(2)}, u32[]{:S(2)}) async-start(f32[128,2,128]{2,1,0:T(2,128)} %bitcast.6), calls=%async_computation.2 | async-start | bytes 262144 | tf_op jit(solution)/shard_map/all_to_all | solution.py:404
  210.5 3.4 %collective-permute-start.8 = (f32[3,72,128]{2,1,0:T(8,128)S(1)}, f32[3,72,128]{2,1,0:T(8,128)S(1)}, u32[]{:S(2)}, u32[]{:S(2)}) collective-permute-start(f32[3,72,128]{2,1,0:T(8,128)S(1)} %get-tuple-element.44), channel_id=1, source_target_pairs={{0,16},{16,32},{32,48},{48,64},{64,80},{80,96},{96,112},{1,17},{17... | collective-permute-start | bytes 331784 | tf_op jit(solution)/shard_map/ppermute | solution.py:226
  213.9 4.0 %collective-permute-start.9 = (f32[3,72,128]{2,1,0:T(8,128)S(1)}, f32[3,72,128]{2,1,0:T(8,128)S(1)}, u32[]{:S(2)}, u32[]{:S(2)}) collective-permute-start(f32[3,72,128]{2,1,0:T(8,128)S(1)} %get-tuple-element.45), channel_id=1, source_target_pairs={{16,0},{32,16},{48,32},{64,48},{80,64},{96,80},{112,96},{17,1},{33... | collective-permute-start | bytes 331784 | tf_op jit(solution)/shard_map/ppermute | solution.py:227
  217.9 2.0 collective-permute-start.10
  219.9 1.3 collective-permute-done.10.w
  221.2 5.7 %collective-permute-done.11.e = f32[72,128]{1,0:T(8,128)S(1)} collective-permute-done((f32[72,128]{1,0:T(8,128)S(1)}, f32[72,128]{1,0:T(8,128)S(1)}, u32[]{:S(2)}, u32[]{:S(2)}) %collective-permute-start.11) | collective-permute-done | bytes 36896 | tf_op jit(solution)/shard_map/ppermute | solution.py:229
  226.9 1.8 adjoint_first.1
  228.7 0.9 copy-done.3
  229.6 1.9 collective-permute-start.12
  231.5 5.5 %collective-permute-start.13 = (f32[3,72,128]{2,1,0:T(8,128)S(1)}, f32[3,72,128]{2,1,0:T(8,128)S(1)}, u32[]{:S(2)}, u32[]{:S(2)}) collective-permute-start(f32[3,72,128]{2,1,0:T(8,128)S(1)} %get-tuple-element.50), channel_id=1, source_target_pairs={{16,0},{32,16},{48,32},{64,48},{80,64},{96,80},{112,96},{17,1},{33... | collective-permute-start | bytes 331784 | tf_op jit(solution)/shard_map/ppermute | solution.py:227
  237.0 1.0 collective-permute-start.14
  238.0 0.6 gather_fusion
  238.7 0.7 fusion.2
  239.5 5.5 %collective-permute-done.15.e = f32[72,128]{1,0:T(8,128)S(1)} collective-permute-done((f32[72,128]{1,0:T(8,128)S(1)}, f32[72,128]{1,0:T(8,128)S(1)}, u32[]{:S(2)}, u32[]{:S(2)}) %collective-permute-start.15) | collective-permute-done | bytes 36896 | tf_op jit(solution)/shard_map/ppermute | solution.py:229
  245.0 1.2 copy-done.4
  246.2 2.4 adjoint_last.1
  (42 shorter events, 0.4 us)
Async XLA Ops:
  4.7 1.7 copy-start
  9.3 11.0 %copy-start.2 = (f32[3,72,8,128]{3,2,1,0:T(8,128)S(1)}, f32[3,72,8,128]{3,2,1,0:T(8,128)}, u32[]{:S(2)}) copy-start(f32[3,72,8,128]{3,2,1,0:T(8,128)} %initial_ref.1) | copy-start | bytes 2654212
  9.3 68.2 %all-to-all-start.1 = ((bf16[128,80,128]{2,1,0:T(8,128)(2,1)}), bf16[128,80,128]{2,1,0:T(8,128)(2,1)}, u32[]{:S(2)}, u32[]{:S(2)}) async-start(bf16[128,80,128]{2,1,0:T(8,128)(2,1)} %pack_blocks.3), calls=%async_computation.1 | async-start | bytes 5242880 | tf_op jit(solution)/shard_map/all_to_all | solution.py:404
  20.3 1.1 copy-start.7
  21.4 1.1 copy-start.8
  22.4 1.1 copy-start.9
  23.5 45.6 %copy-start.13 = (s32[128,1]{0,1:T(1,128)S(1)}, s32[128,1]{0,1:T(1,128)}, u32[]{:S(2)}) copy-start(s32[128,1]{0,1:T(1,128)} %param.19) | copy-start | bytes 1540
  23.5 45.8 %copy-start.1 = (bf16[128,72,128]{2,1,0:T(8,128)(2,1)S(1)}, bf16[128,72,128]{2,1,0:T(8,128)(2,1)}, u32[]{:S(2)}) copy-start(bf16[128,72,128]{2,1,0:T(8,128)(2,1)} %kernel_ref.3) | copy-start | bytes 7077892
  25.4 30.4 %collective-permute-start = (f32[5,72,128]{2,1,0:T(8,128)S(1)}, f32[5,72,128]{2,1,0:T(8,128)S(1)}, u32[]{:S(2)}, u32[]{:S(2)}) collective-permute-start(f32[5,72,128]{2,1,0:T(8,128)S(1)} %get-tuple-element.32), channel_id=1, source_target_pairs={{0,16},{16,32},{32,48},{48,64},{64,80},{80,96},{96,112},{1,17},{17... | collective-permute-start | bytes 552968 | tf_op jit(solution)/shard_map/ppermute | solution.py:226
  28.8 24.4 %collective-permute-start.1 = (f32[3,72,128]{2,1,0:T(8,128)S(1)}, f32[3,72,128]{2,1,0:T(8,128)S(1)}, u32[]{:S(2)}, u32[]{:S(2)}) collective-permute-start(f32[3,72,128]{2,1,0:T(8,128)S(1)} %get-tuple-element.33), channel_id=1, source_target_pairs={{16,0},{32,16},{48,32},{64,48},{80,64},{96,80},{112,96},{17,1},{33... | collective-permute-start | bytes 331784 | tf_op jit(solution)/shard_map/ppermute | solution.py:227
  32.8 17.9 %collective-permute-start.2 = (f32[72,128]{1,0:T(8,128)S(1)}, f32[72,128]{1,0:T(8,128)S(1)}, u32[]{:S(2)}, u32[]{:S(2)}) collective-permute-start(f32[72,128]{1,0:T(8,128)S(1)} %get-tuple-element.34), channel_id=1, source_target_pairs={{0,1},{1,2},{2,3},{3,4},{4,5},{5,6},{6,7},{7,8},{8,9},{9,10},{10,1... | collective-permute-start | bytes 110600 | tf_op jit(solution)/shard_map/ppermute | solution.py:228
  34.8 18.4 %collective-permute-start.3 = (f32[72,128]{1,0:T(8,128)S(1)}, f32[72,128]{1,0:T(8,128)S(1)}, u32[]{:S(2)}, u32[]{:S(2)}) collective-permute-start(f32[72,128]{1,0:T(8,128)S(1)} %get-tuple-element.35), channel_id=1, source_target_pairs={{1,0},{2,1},{3,2},{4,3},{5,4},{6,5},{7,6},{8,7},{9,8},{10,9},{11,1... | collective-permute-start | bytes 110600 | tf_op jit(solution)/shard_map/ppermute | solution.py:229
  57.7 18.4 %collective-permute-start.4 = (f32[3,72,128]{2,1,0:T(8,128)S(1)}, f32[3,72,128]{2,1,0:T(8,128)S(1)}, u32[]{:S(2)}, u32[]{:S(2)}) collective-permute-start(f32[3,72,128]{2,1,0:T(8,128)S(1)} %get-tuple-element.37), channel_id=1, source_target_pairs={{0,16},{16,32},{32,48},{48,64},{64,80},{80,96},{96,112},{1,17},{17... | collective-permute-start | bytes 331784 | tf_op jit(solution)/shard_map/ppermute | solution.py:226
  59.6 16.5 %collective-permute-start.5 = (f32[3,72,128]{2,1,0:T(8,128)S(1)}, f32[3,72,128]{2,1,0:T(8,128)S(1)}, u32[]{:S(2)}, u32[]{:S(2)}) collective-permute-start(f32[3,72,128]{2,1,0:T(8,128)S(1)} %get-tuple-element.38), channel_id=1, source_target_pairs={{16,0},{32,16},{48,32},{64,48},{80,64},{96,80},{112,96},{17,1},{33... | collective-permute-start | bytes 331784 | tf_op jit(solution)/shard_map/ppermute | solution.py:227
  65.1 7.2 %collective-permute-start.6 = (f32[72,128]{1,0:T(8,128)S(1)}, f32[72,128]{1,0:T(8,128)S(1)}, u32[]{:S(2)}, u32[]{:S(2)}) collective-permute-start(f32[72,128]{1,0:T(8,128)S(1)} %get-tuple-element.39), channel_id=1, source_target_pairs={{0,1},{1,2},{2,3},{3,4},{4,5},{5,6},{6,7},{7,8},{8,9},{9,10},{10,1... | collective-permute-start | bytes 110600 | tf_op jit(solution)/shard_map/ppermute | solution.py:228
  69.1 7.0 %collective-permute-start.7 = (f32[72,128]{1,0:T(8,128)S(1)}, f32[72,128]{1,0:T(8,128)S(1)}, u32[]{:S(2)}, u32[]{:S(2)}) collective-permute-start(f32[72,128]{1,0:T(8,128)S(1)} %get-tuple-element.40), channel_id=1, source_target_pairs={{1,0},{2,1},{3,2},{4,3},{5,4},{6,5},{7,6},{8,7},{9,8},{10,9},{11,1... | collective-permute-start | bytes 110600 | tf_op jit(solution)/shard_map/ppermute | solution.py:229
  77.5 63.1 %copy-start.5 = (bf16[864,512]{1,0:T(8,128)(2,1)}, bf16[864,512]{1,0:T(8,128)(2,1)S(1)}, u32[]{:S(2)}) copy-start(bf16[864,512]{1,0:T(8,128)(2,1)S(1)} %forward_last.1.field_ref) | copy-start | bytes 2654212
  77.5 64.0 %all-to-all-start = ((bf16[128,80,128]{2,1,0:T(8,128)(2,1)}), bf16[128,80,128]{2,1,0:T(8,128)(2,1)}, u32[]{:S(2)}, u32[]{:S(2)}) async-start(bf16[128,80,128]{2,1,0:T(8,128)(2,1)} %pack_blocks.2), calls=%async_computation | async-start | bytes 5242880 | tf_op jit(solution)/shard_map/all_to_all | solution.py:404
  140.6 0.9 copy-start.10
  141.6 1.2 copy-start.6
  142.7 1.2 copy-start.11
  200.7 37.9 %copy-start.12 = (s32[128]{0:T(128)S(1)}, s32[128]{0:T(128)}, u32[]{:S(2)}) copy-start(s32[128]{0:T(128)} %param.18) | copy-start | bytes 1540
  200.7 37.3 %all-to-all-start.2 = ((f32[128,2,128]{2,1,0:T(2,128)}), f32[128,2,128]{2,1,0:T(2,128)S(1)}, u32[]{:S(2)}, u32[]{:S(2)}) async-start(f32[128,2,128]{2,1,0:T(2,128)} %bitcast.6), calls=%async_computation.2 | async-start | bytes 262144 | tf_op jit(solution)/shard_map/all_to_all | solution.py:404
  210.5 16.4 %collective-permute-start.8 = (f32[3,72,128]{2,1,0:T(8,128)S(1)}, f32[3,72,128]{2,1,0:T(8,128)S(1)}, u32[]{:S(2)}, u32[]{:S(2)}) collective-permute-start(f32[3,72,128]{2,1,0:T(8,128)S(1)} %get-tuple-element.44), channel_id=1, source_target_pairs={{0,16},{16,32},{32,48},{48,64},{64,80},{80,96},{96,112},{1,17},{17... | collective-permute-start | bytes 331784 | tf_op jit(solution)/shard_map/ppermute | solution.py:226
  213.9 13.0 %collective-permute-start.9 = (f32[3,72,128]{2,1,0:T(8,128)S(1)}, f32[3,72,128]{2,1,0:T(8,128)S(1)}, u32[]{:S(2)}, u32[]{:S(2)}) collective-permute-start(f32[3,72,128]{2,1,0:T(8,128)S(1)} %get-tuple-element.45), channel_id=1, source_target_pairs={{16,0},{32,16},{48,32},{64,48},{80,64},{96,80},{112,96},{17,1},{33... | collective-permute-start | bytes 331784 | tf_op jit(solution)/shard_map/ppermute | solution.py:227
  217.9 3.2 %collective-permute-start.10 = (f32[72,128]{1,0:T(8,128)S(1)}, f32[72,128]{1,0:T(8,128)S(1)}, u32[]{:S(2)}, u32[]{:S(2)}) collective-permute-start(f32[72,128]{1,0:T(8,128)S(1)} %get-tuple-element.46), channel_id=1, source_target_pairs={{0,1},{1,2},{2,3},{3,4},{4,5},{5,6},{6,7},{7,8},{8,9},{9,10},{10,1... | collective-permute-start | bytes 110600 | tf_op jit(solution)/shard_map/ppermute | solution.py:228
  219.9 7.0 %collective-permute-start.11 = (f32[72,128]{1,0:T(8,128)S(1)}, f32[72,128]{1,0:T(8,128)S(1)}, u32[]{:S(2)}, u32[]{:S(2)}) collective-permute-start(f32[72,128]{1,0:T(8,128)S(1)} %get-tuple-element.47), channel_id=1, source_target_pairs={{1,0},{2,1},{3,2},{4,3},{5,4},{6,5},{7,6},{8,7},{9,8},{10,9},{11,1... | collective-permute-start | bytes 110600 | tf_op jit(solution)/shard_map/ppermute | solution.py:229
  228.7 0.9 copy-start.3
  229.6 15.4 %collective-permute-start.12 = (f32[3,72,128]{2,1,0:T(8,128)S(1)}, f32[3,72,128]{2,1,0:T(8,128)S(1)}, u32[]{:S(2)}, u32[]{:S(2)}) collective-permute-start(f32[3,72,128]{2,1,0:T(8,128)S(1)} %get-tuple-element.49), channel_id=1, source_target_pairs={{0,16},{16,32},{32,48},{48,64},{64,80},{80,96},{96,112},{1,17},{17... | collective-permute-start | bytes 331784 | tf_op jit(solution)/shard_map/ppermute | solution.py:226
  231.5 13.5 %collective-permute-start.13 = (f32[3,72,128]{2,1,0:T(8,128)S(1)}, f32[3,72,128]{2,1,0:T(8,128)S(1)}, u32[]{:S(2)}, u32[]{:S(2)}) collective-permute-start(f32[3,72,128]{2,1,0:T(8,128)S(1)} %get-tuple-element.50), channel_id=1, source_target_pairs={{16,0},{32,16},{48,32},{64,48},{80,64},{96,80},{112,96},{17,1},{33... | collective-permute-start | bytes 331784 | tf_op jit(solution)/shard_map/ppermute | solution.py:227
  237.0 2.5 collective-permute-start.14
  238.0 7.0 %collective-permute-start.15 = (f32[72,128]{1,0:T(8,128)S(1)}, f32[72,128]{1,0:T(8,128)S(1)}, u32[]{:S(2)}, u32[]{:S(2)}) collective-permute-start(f32[72,128]{1,0:T(8,128)S(1)} %get-tuple-element.52), channel_id=1, source_target_pairs={{1,0},{2,1},{3,2},{4,3},{5,4},{6,5},{7,6},{8,7},{9,8},{10,9},{11,1... | collective-permute-start | bytes 110600 | tf_op jit(solution)/shard_map/ppermute | solution.py:229
  245.0 1.2 copy-start.4

commit v2 on v1

--- a/solution.py
+++ b/solution.py
@@ -7,11 +7,14 @@
 from jax.experimental.pallas import tpu as pltpu
 from jax.sharding import PartitionSpec as P
 
-CAP = 2
 LEVELS = 72
 ROWS = 80
 PAIR = 2 * LEVELS
 TRACERS = 3
+PARTS = 12
+GROUPS = 6
+GROUP_PARTS = PARTS // GROUPS
+WIDTH = 2
 LAT_CELLS = 8
 LANES = 128
 VMEM_LIMIT = 48 << 20
@@ -202,7 +205,7 @@
 EDGES = [ROW_EDGE, ROW_EDGE, COLUMN_EDGE, COLUMN_EDGE]
 
 
-def whole(body, outs, operands, name, scratch=(), scalars=0):
+def whole(body, outs, operands, name, scratch=(), scalars=0, flops=5000000):
     vmem = pl.BlockSpec(memory_space=pltpu.VMEM)
     smem = pl.BlockSpec(memory_space=pltpu.SMEM)
     return pl.pallas_call(
@@ -212,7 +215,7 @@
         out_shape=outs,
         scratch_shapes=list(scratch),
         compiler_params=pltpu.CompilerParams(vmem_limit_bytes=VMEM_LIMIT),
-        cost_estimate=pl.CostEstimate(flops=5000000, bytes_accessed=6000000, transcendentals=0),
+        cost_estimate=pl.CostEstimate(flops=flops, bytes_accessed=6000000, transcendentals=0),
         name=name,
     )(*operands)
 
@@ -230,74 +233,105 @@
     )
 
 
-def pack_body(source_ref, kernel_ref, meta_ref, out_ref):
+def pack_body(source_ref, kernel_ref, columns_ref, observed_ref, weight_ref, place_ref, out_ref):
+    row_id = lax.broadcasted_iota(jnp.int32, (8, LANES), 0)
+    to_place = lax.broadcasted_iota(jnp.int32, (LANES, LANES), 0).astype(jnp.float32)
+
     def one(slot, carry):
         source = source_ref[slot]
         block = jnp.maximum(source, 0)
-        meta = jnp.where(source >= 0, meta_ref[block].astype(jnp.float32), jnp.float32(0.0))
+        row = pl.ds(block, 1)
+        cell = columns_ref[row, :]
+        part = lax.shift_right_logical(cell, 8) + 1
+        meta = jnp.where(row_id == 0, part.astype(jnp.float32), jnp.float32(0.0))
+        meta = jnp.where(row_id == 1, (cell & 255).astype(jnp.float32), meta)
+        meta = jnp.where(row_id == 2, observed_ref[row, :], meta)
+        meta = jnp.where(row_id == 3, weight_ref[row, :], meta)
         rows = jnp.concatenate([kernel_ref[block].astype(jnp.float32), meta], axis=0)
-        out_ref[slot] = rows.astype(jnp.bfloat16)
+        place = jnp.where(source >= 0, place_ref[row, :], LANES).astype(jnp.float32)
+        moved = jnp.where(to_place == place, 1.0, 0.0).astype(jnp.bfloat16)
+        out_ref[slot] = lax.dot_general(
+            rows.astype(jnp.bfloat16),
+            moved,
+            (((1,), (1,)), ((), ())),
+            preferred_element_type=jnp.float32,
+        ).astype(jnp.bfloat16)
         return carry
 
-    lax.fori_loop(0, out_ref.shape[0], one, 0, unroll=4)
-
-
-def pack_blocks(source, kernel, meta):
-    count, _, sounds = kernel.shape
-    vmem = pl.BlockSpec(memory_space=pltpu.VMEM)
-    return pl.pallas_call(
-        pack_body,
-        in_specs=[pl.BlockSpec(memory_space=pltpu.SMEM), vmem, vmem],
-        out_specs=vmem,
-        out_shape=jax.ShapeDtypeStruct((count, ROWS, sounds), jnp.bfloat16),
-        compiler_params=pltpu.CompilerParams(vmem_limit_bytes=VMEM_LIMIT),
-        name="pack_blocks",
-    )(source, kernel, meta)
-
-
-def first_soundings_body(per_step, width, field_ref, block_ref, adjoint_ref, misfit_ref):
-    @pl.when(pl.program_id(0) == 0)
-    def _():
-        adjoint_ref[...] = jnp.zeros_like(adjoint_ref)
-
-    def write_misfit(block, row):
-        misfit_ref[block : block + 1, :] = row
-
-    soundings(per_step, width, field_ref, block_ref, adjoint_ref, write_misfit)
-
-
-def second_soundings_body(
-    per_step, width, field_ref, block_ref, earlier_ref, other_ref, adjoint_ref, misfit_ref, *edges
-):
-    @pl.when(pl.program_id(0) == 0)
-    def _():
-        adjoint_ref[...] = earlier_ref[...]
-
-    def write_misfit(block, row):
-        misfit_ref[2 * block : 2 * block + 1, :] = other_ref[block : block + 1, :]
-        misfit_ref[2 * block + 1 : 2 * block + 2, :] = row
-
-    soundings(per_step, width, field_ref, block_ref, adjoint_ref, write_misfit)
-
-    @pl.when(pl.program_id(0) == pl.num_programs(0) - 1)
-    def _():
-        write_edges(lambda t, row: cell_slab(adjoint_ref, t, row), *edges)
-
-
-def soundings(per_step, width, field_ref, block_ref, adjoint_ref, write_misfit):
-
-    n = width * 128
-    for group in range(per_step // width):
-        first = group * width
-        blocks = [block_ref[first + i] for i in range(width)]
-        profile = jnp.concatenate([b[:LEVELS] for b in blocks], axis=1)
-        meta = jnp.concatenate([b[LEVELS:] for b in blocks], axis=1).astype(jnp.float32)
+    lax.fori_loop(0, out_ref.shape[0], one, 0, unroll=8)
+
+
+def innovations_body(first_ref, second_ref, returned_ref, place_ref, out_ref, rows_ref):
+    def one(device, carry):
+        for rank, source_ref in enumerate((first_ref, second_ref)):
+            source = source_ref[device]
+            block = jnp.where(source >= 0, source, LANES)
+            rows_ref[pl.ds(block, 1), :] = returned_ref[pl.ds(2 * device + rank, 1), :]
+        return carry
+
+    lax.fori_loop(0, first_ref.shape[0], one, 0, unroll=8)
+    place = place_ref[...]
+    live = place < LANES
+    found = jnp.take_along_axis(
+        rows_ref[: place.shape[0], :], jnp.where(live, place, 0), axis=1
+    )
+    out_ref[...] = jnp.where(live, found, jnp.float32(0.0))
+
+
+def soundings(count_ref, field_ref, block_ref, adjoint_ref, write_misfit, stream_ref, found_ref, cell_ref):
+    n = WIDTH * LANES
+    one, nil = jnp.bfloat16(1), jnp.bfloat16(0)
+    lane = lax.broadcasted_iota(jnp.int32, (ROWS, LANES), 1)
+    cell_ref[...] = (
+        lax.broadcasted_iota(jnp.int32, (256, LANES), 0).astype(jnp.float32).astype(jnp.bfloat16)
+    )
+    empty = jnp.zeros((ROWS, LANES), jnp.bfloat16)
+
+    def merge(block, carry):
+        ends, tails = list(carry[0]), list(carry[1])
+        values = block_ref[block]
+        start = jnp.int32(0)
+        for g in range(GROUPS):
+            count = count_ref[block * GROUPS + g]
+            tile, at = lax.shift_right_logical(ends[g], 7), ends[g] & (LANES - 1)
+            turned = pltpu.roll(values, (at - start) & (LANES - 1), 1)
+            joined = jnp.where(lane >= at, turned, tails[g])
+            stream_ref[g, tile] = joined
+            tails[g] = jnp.where(at + count >= LANES, turned, joined)
+            ends[g] = ends[g] + count
+            start = start + count
+        return tuple(ends), tuple(tails)
+
+    ends, tails = lax.fori_loop(
+        0,
+        block_ref.shape[0],
+        merge,
+        ((jnp.int32(0),) * GROUPS, (empty,) * GROUPS),
+        unroll=2,
+    )
+    for g in range(GROUPS):
+        tile, at = lax.shift_right_logical(ends[g], 7), ends[g] & (LANES - 1)
+        stream_ref[g, tile] = jnp.where(lane < at, tails[g], empty)
+        for j in range(1, WIDTH):
+            stream_ref[g, tile + j] = empty
+
+    def load(g, step):
+        tiles = [stream_ref[g, step * WIDTH + i] for i in range(WIDTH)]
+        profile = jnp.concatenate([t[:LEVELS] for t in tiles], axis=1)
+        meta = jnp.concatenate([t[LEVELS:] for t in tiles], axis=1).astype(jnp.float32)
         part, cell, observed, weight = (meta[j : j + 1] for j in range(4))
-        hit = lax.broadcasted_iota(jnp.int32, (256, n), 0).astype(jnp.float32) == cell
-        pick = jnp.where(hit, 1.0, 0.0).astype(jnp.bfloat16)
+        cell = cell.astype(jnp.bfloat16)
+        hits = [
+            cell_ref[...] == jnp.broadcast_to(cell[:, i * LANES : (i + 1) * LANES], (256, LANES))
+            for i in range(WIDTH)
+        ]
+        return g, step, profile, part - 1.0, observed, weight, hits
+
+    def gather(g, step, profile, part, observed, weight, hits):
+        pick = jnp.concatenate([jnp.where(hit, one, nil) for hit in hits], axis=1)
         pick_twice = jnp.concatenate([pick, pick], axis=0)
         column = jnp.zeros((LEVELS, n), jnp.float32)
-        for i in range(6):
+        for i in range(g * GROUP_PARTS // 2, (g + 1) * GROUP_PARTS // 2):
             found = jnp.dot(
                 field_ref[i * PAIR : (i + 1) * PAIR, :],
                 pick_twice,
@@ -305,25 +339,35 @@
             )
             column = jnp.where(part == 2.0 * i, found[:LEVELS], column)
             column = jnp.where(part == 2.0 * i + 1.0, found[LEVELS:], column)
+        return column
+
+    def force(column, g, step, profile, part, observed, weight, hits):
         model = jnp.sum(profile.astype(jnp.float32) * column, axis=0, keepdims=True)
         misfit = model - observed
-        for i in range(width):
-            write_misfit(first + i, misfit[:, i * 128 : (i + 1) * 128])
+        for i in range(WIDTH):
+            found_ref[g, step * WIDTH + i] = jnp.broadcast_to(
+                misfit[:, i * LANES : (i + 1) * LANES], (8, LANES)
+            )
         forcing = weight * misfit
-        high = forcing.astype(jnp.bfloat16).astype(jnp.float32)
-        low = forcing - high
-        spread = jnp.concatenate(
+        high = forcing.astype(jnp.bfloat16)
+        low = (forcing - high.astype(jnp.float32)).astype(jnp.bfloat16)
+        return jnp.concatenate(
             [
-                jnp.where(hit, high, 0.0).astype(jnp.bfloat16),
-                jnp.where(hit, low, 0.0).astype(jnp.bfloat16),
+                jnp.where(
+                    hits[i], jnp.broadcast_to(term[:, i * LANES : (i + 1) * LANES], (256, LANES)), nil
+                )
+                for term in (high, low)
+                for i in range(WIDTH)
             ],
             axis=1,
         )
+
+    def scatter(spread, g, step, profile, part, observed, weight, hits):
         twice = jnp.concatenate([profile, profile], axis=0)
         second = lax.broadcasted_iota(jnp.int32, (PAIR, n), 0) >= LEVELS
         part_row = (part - jnp.where(second, 1.0, 0.0)).astype(jnp.bfloat16)
-        for i in range(6):
-            left = jnp.where(part_row == jnp.bfloat16(2 * i), twice, jnp.bfloat16(0))
+        for i in range(g * GROUP_PARTS // 2, (g + 1) * GROUP_PARTS // 2):
+            left = jnp.where(part_row == jnp.bfloat16(2 * i), twice, nil)
             adjoint_ref[i * PAIR : (i + 1) * PAIR, :] += lax.dot_general(
                 jnp.concatenate([left, left], axis=1),
                 spread,
@@ -331,45 +375,89 @@
                 preferred_element_type=jnp.float32,
             )
 
-
-def observe(field, blocks, earlier=None):
+    def work(groups, step):
+        loaded = [load(g, step) for g in groups]
+        columns = [gather(*x) for x in loaded]
+        spreads = [force(column, *x) for x, column in zip(loaded, columns)]
+        for x, spread in zip(loaded, spreads):
+            scatter(spread, *x)
+        return 0
+
+    steps = [lax.shift_right_logical(ends[g] + n - 1, n.bit_length() - 1) for g in range(GROUPS)]
+    common = functools.reduce(jnp.minimum, steps)
+    lax.fori_loop(0, common, lambda step, _: work(range(GROUPS), step), 0)
+    for g in range(GROUPS):
+        lax.fori_loop(common, steps[g], lambda step, _, g=g: work([g], step), 0)
+
+    lane = lax.broadcasted_iota(jnp.int32, (8, LANES), 1)
+    row_id = lax.broadcasted_iota(jnp.int32, (8, LANES), 0)
+
+    def part_ways(eight, ends):
+        ends = list(ends)
+        rows = jnp.zeros((8, LANES), jnp.float32)
+        for j in range(8):
+            start = jnp.int32(0)
+            row = jnp.zeros((8, LANES), jnp.float32)
+            for g in range(GROUPS):
+                count = count_ref[(eight * 8 + j) * GROUPS + g]
+                tile, at = lax.shift_right_logical(ends[g], 7), ends[g] & (LANES - 1)
+                values = jnp.where(lane >= at, found_ref[g, tile], found_ref[g, tile + 1])
+                values = pltpu.roll(values, (start - at) & (LANES - 1), 1)
+                row = jnp.where(lane >= start, values, row)
+                ends[g] = ends[g] + count
+                start = start + count
+            rows = jnp.where(row_id == j, row, rows)
+        write_misfit(eight, rows)
+        return tuple(ends)
+
+    lax.fori_loop(0, block_ref.shape[0] // 8, part_ways, (jnp.int32(0),) * GROUPS)
+
+
+def first_soundings_body(count_ref, field_ref, block_ref, adjoint_ref, misfit_ref, *scratch):
+    adjoint_ref[...] = jnp.zeros_like(adjoint_ref)
+
+    def write_misfit(eight, rows):
+        misfit_ref[pl.ds(eight * 8, 8), :] = rows
+
+    soundings(count_ref, field_ref, block_ref, adjoint_ref, write_misfit, *scratch)
+
+
+def second_soundings_body(
+    count_ref, field_ref, block_ref, earlier_ref, other_ref, adjoint_ref, misfit_ref, *rest
+):
+    edges, scratch = rest[:4], rest[4:]
+    adjoint_ref[...] = earlier_ref[...]
+
+    def write_misfit(eight, rows):
+        misfit_ref[pl.ds(eight * 16, 8, stride=2), :] = other_ref[pl.ds(eight * 8, 8), :]
+        misfit_ref[pl.ds(eight * 16 + 1, 8, stride=2), :] = rows
+
+    soundings(count_ref, field_ref, block_ref, adjoint_ref, write_misfit, *scratch)
+    write_edges(lambda t, row: cell_slab(adjoint_ref, t, row), *edges)
+
+
+def observe(field, blocks, earlier=()):
     count = blocks.shape[0]
-    per_step, width = 16, 4
-
-    def fixed(shape):
-        return pl.BlockSpec(shape, lambda i: (0,) * len(shape))
-
-    def rows(height):
-        return pl.BlockSpec((height, 128), lambda i: (i, 0))
-
-    cells = (12 * LEVELS, 256)
-    in_specs = [
-        fixed((12 * LEVELS, 512)),
-        pl.BlockSpec((per_step, ROWS, 128), lambda i: (i, 0, 0)),
-    ]
-    first = earlier is None
-    outs = [jax.ShapeDtypeStruct(cells, jnp.float32)]
-    if first:
-        body, operands = first_soundings_body, (field, blocks)
-        out_specs = [fixed(cells), rows(per_step)]
-        outs += [jax.ShapeDtypeStruct((count, 128), jnp.float32)]
-    else:
-        body, operands = second_soundings_body, (field, blocks) + tuple(earlier)
-        in_specs += [fixed(cells), rows(per_step)]
-        out_specs = [fixed(cells), rows(2 * per_step)] + [fixed(edge.shape) for edge in EDGES]
-        outs += [jax.ShapeDtypeStruct((2 * count, 128), jnp.float32)] + EDGES
-    return pl.pallas_call(
-        functools.partial(body, per_step, width),
-        grid=(count // per_step,),
-        in_specs=in_specs,
-        out_specs=out_specs,
-        out_shape=outs,
-        compiler_params=pltpu.CompilerParams(vmem_limit_bytes=VMEM_LIMIT),
-        cost_estimate=pl.CostEstimate(
-            flops=count * 4 * 864 * 512 * 128, bytes_accessed=count * 40960, transcendentals=0
-        ),
-        name="first_soundings" if first else "second_soundings",
-    )(*operands)
+    part = blocks[:, LEVELS, :].astype(jnp.int32)[:, None, :]
+    lowest = 1 + GROUP_PARTS * lax.broadcasted_iota(jnp.int32, (1, GROUPS, 1), 1)
+    inside = (part >= lowest) & (part < lowest + GROUP_PARTS)
+    counts = jnp.sum(jnp.where(inside, 1, 0), axis=2).reshape(count * GROUPS)
+    tiles = count + WIDTH
+    outs = [jax.ShapeDtypeStruct((PARTS * LEVELS, 256), jnp.float32)]
+    outs += [jax.ShapeDtypeStruct((count * (2 if earlier else 1), LANES), jnp.float32)]
+    return whole(
+        second_soundings_body if earlier else first_soundings_body,
+        outs + (EDGES if earlier else []),
+        (counts, field, blocks) + tuple(earlier),
+        "second_soundings" if earlier else "first_soundings",
+        scratch=[
+            pltpu.VMEM((GROUPS, tiles, ROWS, LANES), jnp.bfloat16),
+            pltpu.VMEM((GROUPS, tiles, 8, LANES), jnp.float32),
+            pltpu.VMEM((256, LANES), jnp.bfloat16),
+        ],
+        scalars=1,
+        flops=15000000000,
+    )
 
 
 def per_device(
@@ -389,22 +477,23 @@
     source_last = jnp.max(jnp.where(meant, block_id, -1), axis=0)
     source_first = jnp.where(source_last >= 0, source_first, -1)
     source_second = jnp.where(source_last > source_first, source_last, -1)
-    is_second = jnp.max(jnp.where(meant & (block_id != source_first[None, :]), 1, 0), axis=1)
-    slot_index = target_dev * CAP + is_second
     live = lax.broadcasted_iota(jnp.int32, (1, sounds), 1) < counts[:, None]
-    weight_live = jnp.where(live, obs_weight, jnp.zeros_like(obs_weight))
-    zeros = jnp.zeros_like(obs_weight)
-    meta = jnp.stack(
-        [(columns // 256).astype(jnp.bfloat16), (columns % 256).astype(jnp.bfloat16)]
-        + [observed, weight_live, zeros, zeros, zeros, zeros],
-        axis=1,
-    )
+    key = (columns // 256) * sounds + lax.broadcasted_iota(jnp.int32, (1, sounds), 1)
+    key = jnp.where(live, key, PARTS * sounds)
+    place = jnp.sum(jnp.where(key[:, :, None] < key[:, None, :], 1, 0), axis=1)
+    place = jnp.where(live, place, sounds)
+    heard = (kernel, columns, observed.astype(jnp.float32), obs_weight.astype(jnp.float32), place)
 
     def exchange(array):
         return lax.all_to_all(array, ("lat", "lon"), split_axis=0, concat_axis=0, tiled=True)
 
-    got_first = exchange(pack_blocks(source_first, kernel, meta))
-    got_second = exchange(pack_blocks(source_second, kernel, meta))
+    packed = jax.ShapeDtypeStruct((device_count, ROWS, sounds), jnp.bfloat16)
+    got_first = exchange(
+        whole(pack_body, packed, (source_first,) + heard, "pack_first", scalars=1)
+    )
+    got_second = exchange(
+        whole(pack_body, packed, (source_second,) + heard, "pack_second", scalars=1)
+    )
 
     is_last = (lax.axis_index("lat") == lat_count - 1).astype(jnp.int32).reshape(1)
     winds_like = jax.ShapeDtypeStruct((2, LAT_CELLS, LEVELS, LANES), jnp.float32)
@@ -442,7 +531,14 @@
         (middle,) + fields + exchange_edges(edges) + winds,
         "adjoint_last",
     )
-    innovations = jnp.where(live, returned[slot_index], jnp.float32(0.0))
+    innovations = whole(
+        innovations_body,
+        jax.ShapeDtypeStruct((block_count, sounds), jnp.float32),
+        (source_first, source_second, returned, place),
+        "innovations",
+        scratch=[pltpu.VMEM((block_count + 8, sounds), jnp.float32)],
+        scalars=2,
+    )
     return (gradient, innovations)
 
 

time: 250 us -> 219 us (0.88)
  the two profiles are of different devices: /device:TPU:31 before, /device:TPU:1 now
where the time goes in v2:
time: 219 us; the launch traced here: 216 us
  starting transfers between devices  78.8 us (36%)
  Pallas kernels  63.3 us (29%)
  waiting for transfers between devices  55.4 us (25%)
  other arithmetic  9.31 us (4%)
  local copies, waits for them, and re-layouts  8.39 us (4%)
    pallas_call x10, Pallas kernels, whole(): pl.pallas_call(body, in_specs=[smem if i < scalars else vmem for i in ran...  63.3 us
    all_to_all x3, starting transfers between devices, exchange(): lax.all_to_all(array, ('lat', 'lon'), split_axis=0, concat_axis=0, tiled=...  40.5 us
    all_to_all x3, waiting for transfers between devices, exchange(): lax.all_to_all(array, ('lat', 'lon'), split_axis=0, concat_axis=0, tiled=...  28.1 us
    ppermute x4, waiting for transfers between devices, exchange_edges(): lax.ppermute(east_edge, 'lon', right)  15.1 us
    ppermute x4, starting transfers between devices, exchange_edges(): lax.ppermute(north_edge, 'lat', up)  14.8 us
    ppermute x4, starting transfers between devices, exchange_edges(): lax.ppermute(east_edge, 'lon', right)  14.5 us
    ppermute x4, waiting for transfers between devices, exchange_edges(): lax.ppermute(west_edge, 'lon', [(j, i) for i, j in right])  8.07 us
    unnamed x24, local copies, waits for them, and re-layouts  7.89 us
  transfers between devices with their start and end apart: 19, of which 6 were waited for; matrix products, arithmetic and copies ran while one was open for 1% of the time, Pallas kernels for 7%

profile of v2, /device:TPU:1, one launch (start us, length us, event | category | flops | bytes accessed | tf_op | source)
XLA Modules:
  0.0 216.2 jit_solution(12408391314612637991)
XLA Ops:
  0.6 0.8 select_reduce_fusion.3
  1.4 0.8 convert_element_type.11.observed_ref
  2.2 0.8 convert_element_type.12.weight_ref
  2.9 0.9 fusion.3
  3.8 2.8 %select_reduce_fusion = s32[128,128]{1,0:T(8,128)S(1)} fusion(s32[128,128]{1,0:T(8,128)S(1)} %fusion.3), kind=kLoop, calls=%fused_computation | loop fusion | flops 6275072 | bytes 131072 | tf_op jit(solution)/shard_map/reduce_sum | solution.py:483
  6.6 0.7 fusion.4.place_ref
  7.4 1.7 copy-done
  9.1 0.8 copy-done.7
  9.9 7.2 %pack_first.1 = bf16[128,80,128]{2,1,0:T(8,128)(2,1)} custom-call(s32[128]{0:T(128)S(1)} %get-tuple-element.59.source_ref.first_ref, bf16[128,72,128]{2,1,0:T(8,128)(2,1)S(1)} %copy-done, s32[128,128]{1,0:T(8,128)S(1)} %copy-done.7, f32[128,128]{1,0:T(8,128)S(1)} %convert_element_type.11.observed_ref, f32[128,128]{1,0:T(8,128)S(1)} %convert_element_type.12.weight_ref, ...), custom_call_target="tpu_custom_call" | custom-call | flops 5000000 | bytes 6000000 | tf_op jit(solution)/shard_map/pack_first/pallas_call | solution.py:211
  17.1 11.9 %all-to-all-start.1 = ((bf16[128,80,128]{2,1,0:T(8,128)(2,1)}), bf16[128,80,128]{2,1,0:T(8,128)(2,1)}, u32[]{:S(2)}, u32[]{:S(2)}) async-start(bf16[128,80,128]{2,1,0:T(8,128)(2,1)} %pack_first.1), calls=%async_computation.1 | async-start | bytes 5242880 | tf_op jit(solution)/shard_map/all_to_all | solution.py:488
  29.0 7.1 %pack_second.1 = bf16[128,80,128]{2,1,0:T(8,128)(2,1)} custom-call(s32[128]{0:T(128)S(1)} %get-tuple-element.58.source_ref.second_ref, bf16[128,72,128]{2,1,0:T(8,128)(2,1)S(1)} %copy-done.1, s32[128,128]{1,0:T(8,128)S(1)} %copy-done.8, f32[128,128]{1,0:T(8,128)S(1)} %convert_element_type.11.observed_ref, f32[128,128]{1,0:T(8,128)S(1)} %convert_element_type.12.weight_ref, ...), custom_call_target="tpu_custom_call" | custom-call | flops 5000000 | bytes 6000000 | tf_op jit(solution)/shard_map/pack_second/pallas_call | solution.py:211
  36.2 28.1 %all-to-all-done.1.block_ref = bf16[128,80,128]{2,1,0:T(8,128)(2,1)} async-done(((bf16[128,80,128]{2,1,0:T(8,128)(2,1)}), bf16[128,80,128]{2,1,0:T(8,128)(2,1)}, u32[]{:S(2)}, u32[]{:S(2)}) %all-to-all-start.1) | async-done | bytes 2621472 | tf_op jit(solution)/shard_map/all_to_all | solution.py:488
  64.3 5.4 %all-to-all-start = ((bf16[128,80,128]{2,1,0:T(8,128)(2,1)}), bf16[128,80,128]{2,1,0:T(8,128)(2,1)}, u32[]{:S(2)}, u32[]{:S(2)}) async-start(bf16[128,80,128]{2,1,0:T(8,128)(2,1)} %pack_second.1), calls=%async_computation | async-start | bytes 5242880 | tf_op jit(solution)/shard_map/all_to_all | solution.py:488
  69.8 1.1 copy-done.10
  70.8 1.1 copy-done.11
  71.9 1.9 prepare.1
  73.8 3.4 %collective-permute-start = (f32[5,72,128]{2,1,0:T(8,128)S(1)}, f32[5,72,128]{2,1,0:T(8,128)S(1)}, u32[]{:S(2)}, u32[]{:S(2)}) collective-permute-start(f32[5,72,128]{2,1,0:T(8,128)S(1)} %get-tuple-element.32), channel_id=1, source_target_pairs={{0,16},{16,32},{32,48},{48,64},{64,80},{80,96},{96,112},{1,17},{17... | collective-permute-start | bytes 552968 | tf_op jit(solution)/shard_map/ppermute | solution.py:229
  77.2 1.3 collective-permute-start.1
  78.5 3.3 %collective-permute-start.2 = (f32[72,128]{1,0:T(8,128)S(1)}, f32[72,128]{1,0:T(8,128)S(1)}, u32[]{:S(2)}, u32[]{:S(2)}) collective-permute-start(f32[72,128]{1,0:T(8,128)S(1)} %get-tuple-element.34), channel_id=1, source_target_pairs={{0,1},{1,2},{2,3},{3,4},{4,5},{5,6},{6,7},{7,8},{8,9},{9,10},{10,1... | collective-permute-start | bytes 110600 | tf_op jit(solution)/shard_map/ppermute | solution.py:231
  81.8 15.1 %collective-permute-done.2.w.wind_w = f32[72,128]{1,0:T(8,128)S(1)} collective-permute-done((f32[72,128]{1,0:T(8,128)S(1)}, f32[72,128]{1,0:T(8,128)S(1)}, u32[]{:S(2)}, u32[]{:S(2)}) %collective-permute-start.2) | collective-permute-done | bytes 36896 | tf_op jit(solution)/shard_map/ppermute | solution.py:231
  96.9 4.9 %collective-permute-done.3.e = f32[72,128]{1,0:T(8,128)S(1)} collective-permute-done((f32[72,128]{1,0:T(8,128)S(1)}, f32[72,128]{1,0:T(8,128)S(1)}, u32[]{:S(2)}, u32[]{:S(2)}) %collective-permute-start.3) | collective-permute-done | bytes 36896 | tf_op jit(solution)/shard_map/ppermute | solution.py:232
  101.8 1.8 forward_first.1
  103.7 3.8 %collective-permute-start.6 = (f32[72,128]{1,0:T(8,128)S(1)}, f32[72,128]{1,0:T(8,128)S(1)}, u32[]{:S(2)}, u32[]{:S(2)}) collective-permute-start(f32[72,128]{1,0:T(8,128)S(1)} %get-tuple-element.39), channel_id=1, source_target_pairs={{0,1},{1,2},{2,3},{3,4},{4,5},{5,6},{6,7},{7,8},{8,9},{9,10},{10,1... | collective-permute-start | bytes 110600 | tf_op jit(solution)/shard_map/ppermute | solution.py:231
  107.4 4.0 %collective-permute-start.4 = (f32[3,72,128]{2,1,0:T(8,128)S(1)}, f32[3,72,128]{2,1,0:T(8,128)S(1)}, u32[]{:S(2)}, u32[]{:S(2)}) collective-permute-start(f32[3,72,128]{2,1,0:T(8,128)S(1)} %get-tuple-element.37), channel_id=1, source_target_pairs={{0,16},{16,32},{32,48},{48,64},{64,80},{80,96},{96,112},{1,17},{17... | collective-permute-start | bytes 331784 | tf_op jit(solution)/shard_map/ppermute | solution.py:229
  111.4 1.3 collective-permute-start.5
  112.8 0.4 collective-permute-done.4.s
  113.2 3.8 %collective-permute-done.5.n = f32[3,72,128]{2,1,0:T(8,128)S(1)} collective-permute-done((f32[3,72,128]{2,1,0:T(8,128)S(1)}, f32[3,72,128]{2,1,0:T(8,128)S(1)}, u32[]{:S(2)}, u32[]{:S(2)}) %collective-permute-start.5) | collective-permute-done | bytes 110624 | tf_op jit(solution)/shard_map/ppermute | solution.py:230
  116.9 1.4 forward_last.1.field_ref
  118.3 1.2 slice_convert_fusion
  119.5 1.0 slice_convert_fusion.1
  120.5 0.3 select_reduce_fusion.1
  121.4 22.6 %first_soundings.1 = (f32[864,256]{1,0:T(8,128)S(1)}, f32[128,128]{1,0:T(8,128)S(1)}) custom-call(s32[768]{0:T(1024)S(1)} %reshape.33.count_ref, bf16[864,512]{1,0:T(8,128)(2,1)S(1)} %forward_last.1.field_ref, bf16[128,80,128]{2,1,0:T(8,128)(2,1)} %all-to-all-done.1.block_ref), custom_call_target="tpu_custom_call" | custom-call | flops 15000000512 | bytes 6000000 | tf_op jit(solution)/shard_map/first_soundings/pallas_call | solution.py:211
  144.0 1.2 copy-done.6
  145.2 14.9 %second_soundings.1 = (f32[864,256]{1,0:T(8,128)S(1)}, f32[256,128]{1,0:T(8,128)}, f32[3,72,128]{2,1,0:T(8,128)}, f32[3,72,128]{2,1,0:T(8,128)S(1)}, f32[72,128]{1,0:T(8,128)}, /*index=5*/f32[72,128]{1,0:T(8,128)S(1)}) custom-call(s32[768]{0:T(1024)S(1)} %reshape.30.count_ref, bf16[864,512]{1,0:T(8,128)(2,1)S(1)} %copy-done.6, ...), custom_call_target="tpu_custom_call" | custom-call | flops 15000000512 | bytes 6000000 | tf_op jit(solution)/shard_map/second_soundings/pallas_call | solution.py:211
  160.1 4.0 %collective-permute-start.8 = (f32[3,72,128]{2,1,0:T(8,128)}, f32[3,72,128]{2,1,0:T(8,128)S(1)}, u32[]{:S(2)}, u32[]{:S(2)}) collective-permute-start(f32[3,72,128]{2,1,0:T(8,128)} %get-tuple-element.44), channel_id=1, source_target_pairs={{0,16},{16,32},{32,48},{48,64},{64,80},{80,96},{96,112},{1,17},{17... | collective-permute-start | bytes 331784 | tf_op jit(solution)/shard_map/ppermute | solution.py:229
  164.1 1.3 collective-permute-start.9
  165.4 4.1 %collective-permute-start.10 = (f32[72,128]{1,0:T(8,128)}, f32[72,128]{1,0:T(8,128)S(1)}, u32[]{:S(2)}, u32[]{:S(2)}) collective-permute-start(f32[72,128]{1,0:T(8,128)} %get-tuple-element.46), channel_id=1, source_target_pairs={{0,1},{1,2},{2,3},{3,4},{4,5},{5,6},{6,7},{7,8},{8,9},{9,10},{10,1... | collective-permute-start | bytes 110600 | tf_op jit(solution)/shard_map/ppermute | solution.py:231
  169.5 3.8 %collective-permute-start.11 = (f32[72,128]{1,0:T(8,128)S(1)}, f32[72,128]{1,0:T(8,128)S(1)}, u32[]{:S(2)}, u32[]{:S(2)}) collective-permute-start(f32[72,128]{1,0:T(8,128)S(1)} %get-tuple-element.47), channel_id=1, source_target_pairs={{1,0},{2,1},{3,2},{4,3},{5,4},{6,5},{7,6},{8,7},{9,8},{10,9},{11,1... | collective-permute-start | bytes 110600 | tf_op jit(solution)/shard_map/ppermute | solution.py:232
  173.3 23.1 %all-to-all-start.2 = ((f32[128,2,128]{2,1,0:T(2,128)}), f32[128,2,128]{2,1,0:T(2,128)S(1)}, u32[]{:S(2)}, u32[]{:S(2)}) async-start(f32[128,2,128]{2,1,0:T(2,128)} %bitcast.4), calls=%async_computation.2 | async-start | bytes 262144 | tf_op jit(solution)/shard_map/all_to_all | solution.py:488
  196.5 2.3 %adjoint_first.1 = (f32[3,8,72,128]{3,2,1,0:T(8,128)S(1)}, f32[3,72,128]{2,1,0:T(8,128)}, f32[3,72,128]{2,1,0:T(8,128)S(1)}, f32[72,128]{1,0:T(8,128)}, f32[72,128]{1,0:T(8,128)S(1)}) custom-call(f32[864,256]{1,0:T(8,128)S(1)} %get-tuple-element.43.adjoint_ref, f32[2,8,72,128]{3,2,1,0:T(8,128)S(1)} %get-tuple-element.29.east_ref, ...), custom_call_target="tpu_custom_call" | custom-call | flops 5000000 | bytes 6000000 | tf_op jit(solution)/shard_map/adjoint_first/pallas_call | solution.py:211
  198.8 0.9 copy-done.3
  199.7 3.4 %collective-permute-start.12 = (f32[3,72,128]{2,1,0:T(8,128)}, f32[3,72,128]{2,1,0:T(8,128)S(1)}, u32[]{:S(2)}, u32[]{:S(2)}) collective-permute-start(f32[3,72,128]{2,1,0:T(8,128)} %get-tuple-element.49), channel_id=1, source_target_pairs={{0,16},{16,32},{32,48},{48,64},{64,80},{80,96},{96,112},{1,17},{17... | collective-permute-start | bytes 331784 | tf_op jit(solution)/shard_map/ppermute | solution.py:229
  203.1 1.3 collective-permute-start.13
  204.4 3.3 %collective-permute-start.14 = (f32[72,128]{1,0:T(8,128)}, f32[72,128]{1,0:T(8,128)S(1)}, u32[]{:S(2)}, u32[]{:S(2)}) collective-permute-start(f32[72,128]{1,0:T(8,128)} %get-tuple-element.51), channel_id=1, source_target_pairs={{0,1},{1,2},{2,3},{3,4},{4,5},{5,6},{6,7},{7,8},{8,9},{9,10},{10,1... | collective-permute-start | bytes 110600 | tf_op jit(solution)/shard_map/ppermute | solution.py:231
  207.7 1.7 innovations.1
  209.4 3.2 %collective-permute-done.15.e = f32[72,128]{1,0:T(8,128)S(1)} collective-permute-done((f32[72,128]{1,0:T(8,128)S(1)}, f32[72,128]{1,0:T(8,128)S(1)}, u32[]{:S(2)}, u32[]{:S(2)}) %collective-permute-start.15) | collective-permute-done | bytes 36896 | tf_op jit(solution)/shard_map/ppermute | solution.py:232
  212.6 1.2 copy-done.4
  213.8 2.4 %adjoint_last.1 = f32[3,72,8,128]{3,2,1,0:T(8,128)} custom-call(f32[3,8,72,128]{3,2,1,0:T(8,128)S(1)} %copy-done.4, f32[2,8,72,128]{3,2,1,0:T(8,128)S(1)} %get-tuple-element.29.east_ref, f32[2,8,72,128]{3,2,1,0:T(8,128)S(1)} %get-tuple-element.30.north_ref, f32[2,8,72,128]{3,2,1,0:T(8,128)S(1)} %get-tuple-element.31.mixing_ref, ...), custom_call_target="tpu_custom_call" | custom-call | flops 5000000 | bytes 6000000 | tf_op jit(solution)/shard_map/adjoint_last/pallas_call | solution.py:211
  (39 shorter events, 0.6 us)
Async XLA Ops:
  7.4 1.7 copy-start
  9.1 0.8 copy-start.7
  17.1 11.9 %copy-start.1 = (bf16[128,72,128]{2,1,0:T(8,128)(2,1)S(1)}, bf16[128,72,128]{2,1,0:T(8,128)(2,1)}, u32[]{:S(2)}) copy-start(bf16[128,72,128]{2,1,0:T(8,128)(2,1)} %kernel_ref.3) | copy-start | bytes 7077892
  17.1 11.9 %copy-start.8 = (s32[128,128]{1,0:T(8,128)S(1)}, s32[128,128]{1,0:T(8,128)}, u32[]{:S(2)}) copy-start(s32[128,128]{1,0:T(8,128)} %columns_ref.3) | copy-start | bytes 196612
  17.1 47.1 %all-to-all-start.1 = ((bf16[128,80,128]{2,1,0:T(8,128)(2,1)}), bf16[128,80,128]{2,1,0:T(8,128)(2,1)}, u32[]{:S(2)}, u32[]{:S(2)}) async-start(bf16[128,80,128]{2,1,0:T(8,128)(2,1)} %pack_first.1), calls=%async_computation.1 | async-start | bytes 5242880 | tf_op jit(solution)/shard_map/all_to_all | solution.py:488
  36.2 33.6 %copy-start.2 = (f32[3,72,8,128]{3,2,1,0:T(8,128)S(1)}, f32[3,72,8,128]{3,2,1,0:T(8,128)}, u32[]{:S(2)}) copy-start(f32[3,72,8,128]{3,2,1,0:T(8,128)} %initial_ref.1) | copy-start | bytes 2654212
  36.2 33.6 %copy-start.9 = (f32[2,72,8,128]{3,2,1,0:T(8,128)S(1)}, f32[2,72,8,128]{3,2,1,0:T(8,128)}, u32[]{:S(2)}) copy-start(f32[2,72,8,128]{3,2,1,0:T(8,128)} %east_ref.1) | copy-start | bytes 1769476
  64.3 55.3 %all-to-all-start = ((bf16[128,80,128]{2,1,0:T(8,128)(2,1)}), bf16[128,80,128]{2,1,0:T(8,128)(2,1)}, u32[]{:S(2)}, u32[]{:S(2)}) async-start(bf16[128,80,128]{2,1,0:T(8,128)(2,1)} %pack_second.1), calls=%async_computation | async-start | bytes 5242880 | tf_op jit(solution)/shard_map/all_to_all | solution.py:488
  69.7 1.1 copy-start.10
  70.8 1.1 copy-start.11
  73.8 28.0 %collective-permute-start = (f32[5,72,128]{2,1,0:T(8,128)S(1)}, f32[5,72,128]{2,1,0:T(8,128)S(1)}, u32[]{:S(2)}, u32[]{:S(2)}) collective-permute-start(f32[5,72,128]{2,1,0:T(8,128)S(1)} %get-tuple-element.32), channel_id=1, source_target_pairs={{0,16},{16,32},{32,48},{48,64},{64,80},{80,96},{96,112},{1,17},{17... | collective-permute-start | bytes 552968 | tf_op jit(solution)/shard_map/ppermute | solution.py:229
  77.2 24.6 %collective-permute-start.1 = (f32[3,72,128]{2,1,0:T(8,128)S(1)}, f32[3,72,128]{2,1,0:T(8,128)S(1)}, u32[]{:S(2)}, u32[]{:S(2)}) collective-permute-start(f32[3,72,128]{2,1,0:T(8,128)S(1)} %get-tuple-element.33), channel_id=1, source_target_pairs={{16,0},{32,16},{48,32},{64,48},{80,64},{96,80},{112,96},{17,1},{33... | collective-permute-start | bytes 331784 | tf_op jit(solution)/shard_map/ppermute | solution.py:230
  78.5 18.4 %collective-permute-start.2 = (f32[72,128]{1,0:T(8,128)S(1)}, f32[72,128]{1,0:T(8,128)S(1)}, u32[]{:S(2)}, u32[]{:S(2)}) collective-permute-start(f32[72,128]{1,0:T(8,128)S(1)} %get-tuple-element.34), channel_id=1, source_target_pairs={{0,1},{1,2},{2,3},{3,4},{4,5},{5,6},{6,7},{7,8},{8,9},{9,10},{10,1... | collective-permute-start | bytes 110600 | tf_op jit(solution)/shard_map/ppermute | solution.py:231
  81.8 19.9 %collective-permute-start.3 = (f32[72,128]{1,0:T(8,128)S(1)}, f32[72,128]{1,0:T(8,128)S(1)}, u32[]{:S(2)}, u32[]{:S(2)}) collective-permute-start(f32[72,128]{1,0:T(8,128)S(1)} %get-tuple-element.35), channel_id=1, source_target_pairs={{1,0},{2,1},{3,2},{4,3},{5,4},{6,5},{7,6},{8,7},{9,8},{10,9},{11,1... | collective-permute-start | bytes 110600 | tf_op jit(solution)/shard_map/ppermute | solution.py:232
  103.7 9.1 %collective-permute-start.6 = (f32[72,128]{1,0:T(8,128)S(1)}, f32[72,128]{1,0:T(8,128)S(1)}, u32[]{:S(2)}, u32[]{:S(2)}) collective-permute-start(f32[72,128]{1,0:T(8,128)S(1)} %get-tuple-element.39), channel_id=1, source_target_pairs={{0,1},{1,2},{2,3},{3,4},{4,5},{5,6},{6,7},{7,8},{8,9},{9,10},{10,1... | collective-permute-start | bytes 110600 | tf_op jit(solution)/shard_map/ppermute | solution.py:231
  107.4 5.3 %collective-permute-start.7 = (f32[72,128]{1,0:T(8,128)S(1)}, f32[72,128]{1,0:T(8,128)S(1)}, u32[]{:S(2)}, u32[]{:S(2)}) collective-permute-start(f32[72,128]{1,0:T(8,128)S(1)} %get-tuple-element.40), channel_id=1, source_target_pairs={{1,0},{2,1},{3,2},{4,3},{5,4},{6,5},{7,6},{8,7},{9,8},{10,9},{11,1... | collective-permute-start | bytes 110600 | tf_op jit(solution)/shard_map/ppermute | solution.py:232
  107.4 5.7 %collective-permute-start.4 = (f32[3,72,128]{2,1,0:T(8,128)S(1)}, f32[3,72,128]{2,1,0:T(8,128)S(1)}, u32[]{:S(2)}, u32[]{:S(2)}) collective-permute-start(f32[3,72,128]{2,1,0:T(8,128)S(1)} %get-tuple-element.37), channel_id=1, source_target_pairs={{0,16},{16,32},{32,48},{48,64},{64,80},{80,96},{96,112},{1,17},{17... | collective-permute-start | bytes 331784 | tf_op jit(solution)/shard_map/ppermute | solution.py:229
  111.4 5.5 %collective-permute-start.5 = (f32[3,72,128]{2,1,0:T(8,128)S(1)}, f32[3,72,128]{2,1,0:T(8,128)S(1)}, u32[]{:S(2)}, u32[]{:S(2)}) collective-permute-start(f32[3,72,128]{2,1,0:T(8,128)S(1)} %get-tuple-element.38), channel_id=1, source_target_pairs={{16,0},{32,16},{48,32},{64,48},{80,64},{96,80},{112,96},{17,1},{33... | collective-permute-start | bytes 331784 | tf_op jit(solution)/shard_map/ppermute | solution.py:230
  118.3 25.7 %copy-start.5 = (bf16[864,512]{1,0:T(8,128)(2,1)}, bf16[864,512]{1,0:T(8,128)(2,1)S(1)}, u32[]{:S(2)}) copy-start(bf16[864,512]{1,0:T(8,128)(2,1)S(1)} %forward_last.1.field_ref) | copy-start | bytes 2654212
  144.0 1.2 copy-start.6
  160.1 36.4 %collective-permute-start.8 = (f32[3,72,128]{2,1,0:T(8,128)}, f32[3,72,128]{2,1,0:T(8,128)S(1)}, u32[]{:S(2)}, u32[]{:S(2)}) collective-permute-start(f32[3,72,128]{2,1,0:T(8,128)} %get-tuple-element.44), channel_id=1, source_target_pairs={{0,16},{16,32},{32,48},{48,64},{64,80},{80,96},{96,112},{1,17},{17... | collective-permute-start | bytes 331784 | tf_op jit(solution)/shard_map/ppermute | solution.py:229
  164.1 32.4 %collective-permute-start.9 = (f32[3,72,128]{2,1,0:T(8,128)S(1)}, f32[3,72,128]{2,1,0:T(8,128)S(1)}, u32[]{:S(2)}, u32[]{:S(2)}) collective-permute-start(f32[3,72,128]{2,1,0:T(8,128)S(1)} %get-tuple-element.45), channel_id=1, source_target_pairs={{16,0},{32,16},{48,32},{64,48},{80,64},{96,80},{112,96},{17,1},{33... | collective-permute-start | bytes 331784 | tf_op jit(solution)/shard_map/ppermute | solution.py:230
  165.4 31.1 %collective-permute-start.10 = (f32[72,128]{1,0:T(8,128)}, f32[72,128]{1,0:T(8,128)S(1)}, u32[]{:S(2)}, u32[]{:S(2)}) collective-permute-start(f32[72,128]{1,0:T(8,128)} %get-tuple-element.46), channel_id=1, source_target_pairs={{0,1},{1,2},{2,3},{3,4},{4,5},{5,6},{6,7},{7,8},{8,9},{9,10},{10,1... | collective-permute-start | bytes 110600 | tf_op jit(solution)/shard_map/ppermute | solution.py:231
  169.5 27.0 %collective-permute-start.11 = (f32[72,128]{1,0:T(8,128)S(1)}, f32[72,128]{1,0:T(8,128)S(1)}, u32[]{:S(2)}, u32[]{:S(2)}) collective-permute-start(f32[72,128]{1,0:T(8,128)S(1)} %get-tuple-element.47), channel_id=1, source_target_pairs={{1,0},{2,1},{3,2},{4,3},{5,4},{6,5},{7,6},{8,7},{9,8},{10,9},{11,1... | collective-permute-start | bytes 110600 | tf_op jit(solution)/shard_map/ppermute | solution.py:232
  173.3 34.4 %all-to-all-start.2 = ((f32[128,2,128]{2,1,0:T(2,128)}), f32[128,2,128]{2,1,0:T(2,128)S(1)}, u32[]{:S(2)}, u32[]{:S(2)}) async-start(f32[128,2,128]{2,1,0:T(2,128)} %bitcast.4), calls=%async_computation.2 | async-start | bytes 262144 | tf_op jit(solution)/shard_map/all_to_all | solution.py:488
  198.8 0.9 copy-start.3
  199.7 12.9 %collective-permute-start.12 = (f32[3,72,128]{2,1,0:T(8,128)}, f32[3,72,128]{2,1,0:T(8,128)S(1)}, u32[]{:S(2)}, u32[]{:S(2)}) collective-permute-start(f32[3,72,128]{2,1,0:T(8,128)} %get-tuple-element.49), channel_id=1, source_target_pairs={{0,16},{16,32},{32,48},{48,64},{64,80},{80,96},{96,112},{1,17},{17... | collective-permute-start | bytes 331784 | tf_op jit(solution)/shard_map/ppermute | solution.py:229
  203.1 9.5 %collective-permute-start.13 = (f32[3,72,128]{2,1,0:T(8,128)S(1)}, f32[3,72,128]{2,1,0:T(8,128)S(1)}, u32[]{:S(2)}, u32[]{:S(2)}) collective-permute-start(f32[3,72,128]{2,1,0:T(8,128)S(1)} %get-tuple-element.50), channel_id=1, source_target_pairs={{16,0},{32,16},{48,32},{64,48},{80,64},{96,80},{112,96},{17,1},{33... | collective-permute-start | bytes 331784 | tf_op jit(solution)/shard_map/ppermute | solution.py:230
  204.4 5.0 %collective-permute-start.14 = (f32[72,128]{1,0:T(8,128)}, f32[72,128]{1,0:T(8,128)S(1)}, u32[]{:S(2)}, u32[]{:S(2)}) collective-permute-start(f32[72,128]{1,0:T(8,128)} %get-tuple-element.51), channel_id=1, source_target_pairs={{0,1},{1,2},{2,3},{3,4},{4,5},{5,6},{6,7},{7,8},{8,9},{9,10},{10,1... | collective-permute-start | bytes 110600 | tf_op jit(solution)/shard_map/ppermute | solution.py:231
  207.7 4.9 %collective-permute-start.15 = (f32[72,128]{1,0:T(8,128)S(1)}, f32[72,128]{1,0:T(8,128)S(1)}, u32[]{:S(2)}, u32[]{:S(2)}) collective-permute-start(f32[72,128]{1,0:T(8,128)S(1)} %get-tuple-element.52), channel_id=1, source_target_pairs={{1,0},{2,1},{3,2},{4,3},{5,4},{6,5},{7,6},{8,7},{9,8},{10,9},{11,1... | collective-permute-start | bytes 110600 | tf_op jit(solution)/shard_map/ppermute | solution.py:232
  212.6 1.2 copy-start.4

commit v3 on v2

v3 whole, which is shorter than its diff:
```python
import functools

import jax
import jax.numpy as jnp
from jax import lax
from jax.experimental import pallas as pl
from jax.experimental.pallas import tpu as pltpu
from jax.sharding import PartitionSpec as P

LEVELS = 72
ROWS = 80
PAIR = 2 * LEVELS
TRACERS = 3
PARTS = 12
GROUPS = 6
GROUP_PARTS = PARTS // GROUPS
WIDTH = 2
LAT_CELLS = 8
LANES = 128


def lane_index():
    return lax.broadcasted_iota(jnp.int32, (LEVELS, LANES), 1)


def rolled(array, shift, axis):
    shift = shift % array.shape[axis]
    return pltpu.roll(array, shift, axis) if shift else array


def west_of(slab, halo, place):
    return jnp.where(lane_index() == 0, rolled(halo, -place, 1), rolled(slab, 1, 1))


def east_of(slab, halo, place):
    return jnp.where(
        lane_index() == LANES - 1, rolled(halo, LANES - 1 - place, 1), rolled(slab, -1, 1)
    )


SLOT = 32


def place_of(t, row):
    return t * 10 + row + 1


def packed(slabs, lane, base=0):
    out = jnp.zeros((LEVELS, LANES), jnp.float32)
    for i, slab in enumerate(slabs):
        place = base + place_of(i // LAT_CELLS, i % LAT_CELLS)
        out = jnp.where(lane_index() == place, rolled(slab, place - lane, 1), out)
    return out


def packed_wind(slabs, lane, base):
    one = packed(slabs, lane, base)
    return one + rolled(one, 10, 1) + rolled(one, 20, 1)


def slot(array, number):
    return rolled(array, -SLOT * number, 1)


def with_corners(own, south, north, number=0):
    row = (lane_index() & (SLOT - 1)) % 10
    out = jnp.where(row == 0, rolled(south, number - LAT_CELLS, 1), own)
    return jnp.where(row == 9, rolled(north, LAT_CELLS - number, 1), out)


def corners_body(from_west, from_east, up_in, down_in, up_ref, down_ref):
    last = up_in.shape[0]
    for i in range(last):
        up_ref[i] = up_in[i]
    for i in range(down_in.shape[0]):
        down_ref[i] = down_in[i]
    row = (lane_index() & (SLOT - 1)) % 10
    up = jnp.zeros((LEVELS, LANES), jnp.float32)
    down = jnp.zeros((LEVELS, LANES), jnp.float32)
    for i in range(6):
        column = from_west[i] if i < 3 else from_east[i - 3]
        up = up + rolled(jnp.where(row == LAT_CELLS, column, 0.0), -i, 1)
        down = down + rolled(jnp.where(row == 1, column, 0.0), i, 1)
    up_ref[last] = up
    down_ref[down_in.shape[0]] = down


def mixed(slab, coeff):
    upward = coeff * (rolled(slab, -1, 0) - slab)
    return upward - rolled(upward, 1, 0)


def forward(slab, left, right, above, below, east, before, north, south, coeff):
    zonal = jnp.maximum(east, 0.0) * slab + jnp.minimum(east, 0.0) * right
    zonal_before = jnp.maximum(before, 0.0) * left + jnp.minimum(before, 0.0) * slab
    merid = jnp.maximum(north, 0.0) * slab + jnp.minimum(north, 0.0) * above
    merid_before = jnp.maximum(south, 0.0) * below + jnp.minimum(south, 0.0) * slab
    return slab - (zonal - zonal_before) - (merid - merid_before) + mixed(slab, coeff)


def backward(slab, left, right, above, below, east, before, north, south, coeff):
    zonal = jnp.maximum(east, 0.0) * (right - slab) + jnp.minimum(before, 0.0) * (slab - left)
    merid = jnp.maximum(north, 0.0) * (above - slab) + jnp.minimum(south, 0.0) * (slab - below)
    return slab + zonal + merid + mixed(slab, coeff)


def write_edges(read, up_ref, down_ref, east_edge, west_edge):
    slabs = [read(t, row) for t in range(TRACERS) for row in range(LAT_CELLS)]
    for t in range(TRACERS):
        for i in range(2):
            up_ref[2 * t + i] = slabs[t * LAT_CELLS + LAT_CELLS - 2 + i]
            down_ref[2 * t + i] = slabs[t * LAT_CELLS + i]
    east_edge[...] = packed(slabs, LANES - 1) + packed(slabs, LANES - 2, SLOT)
    west_edge[...] = packed(slabs, 0) + packed(slabs, 1, SLOT)


def prepare_body(
    last_ref, initial_ref, east_ref, north_ref, mixing_ref,
    state_ref, east_out, north_out, mixing_out, up_ref, down_ref, east_edge, west_edge,
):
    steps = east_ref.shape[0]
    last = LAT_CELLS - 1
    top = lax.broadcasted_iota(jnp.int32, (LEVELS, LANES), 0) == LEVELS - 1
    for t in range(TRACERS):
        for row in range(LAT_CELLS):
            state_ref[t, row] = initial_ref[t, :, row, :]
    for m in range(steps):
        for row in range(LAT_CELLS):
            east_out[m, row] = east_ref[m, :, row, :]
            north = north_ref[m, :, row, :]
            if row == last:
                north = jnp.where(last_ref[0] > 0, jnp.float32(0.0), north)
            north_out[m, row] = north
            mixing_out[m, row] = jnp.where(top, jnp.float32(0.0), mixing_ref[m, :, row, :])
    write_edges(
        lambda t, row: state_ref[t, row], up_ref, down_ref, east_edge.at[0], west_edge.at[0]
    )
    for m in range(steps):
        ups = (east_out[m, last], mixing_out[m, last], north_out[m, last], north_out[m, last - 1])
        for i, slab in enumerate(ups):
            up_ref[6 + 4 * m + i] = slab
        for i, slab in enumerate((east_out[m, 0], mixing_out[m, 0], north_out[m, 0])):
            down_ref[6 + 3 * m + i] = slab
        east, north, mixing = (
            [ref[m, row] for row in range(LAT_CELLS)] for ref in (east_out, north_out, mixing_out)
        )
        east_edge[1 + m] = (
            packed_wind(east, LANES - 1, 0)
            + packed_wind(mixing, LANES - 1, SLOT)
            + packed_wind(north, LANES - 1, 2 * SLOT)
            + packed_wind(east, LANES - 2, 3 * SLOT)
        )
        west_edge[1 + m] = (
            packed_wind(east, 0, 0)
            + packed_wind(mixing, 0, SLOT)
            + packed_wind(north, 0, 2 * SLOT)
        )


def two_steps(
    step, moments, read, winds, wind_up, wind_down, wind_east, sides,
    up_ref, down_ref, own_east, own_west, from_west, from_east, middle_ref, write,
):
    east_ref, north_ref, mixing_ref = winds

    def state(t, row):
        if row < 0:
            return up_ref[2 * t + row + 2]
        return read(t, row) if row < LAT_CELLS else down_ref[2 * t + row - LAT_CELLS]

    def wind(ref, number, m, row):
        if row < -1:
            return wind_up(4 * m + 3)
        if row < 0:
            return wind_up(4 * m + number)
        return ref[m, row] if row < LAT_CELLS else wind_down(3 * m + number)

    def winds_of(m, row, east_side):
        east = wind(east_ref, 0, m, row)
        return (
            east,
            west_of(east, east_side, place_of(0, row)),
            wind(north_ref, 2, m, row),
            wind(north_ref, 2, m, row - 1),
            wind(mixing_ref, 1, m, row),
        )

    m = moments[0]
    side_west, side_east = sides(m)
    for row in range(-1, LAT_CELLS + 1):
        local = winds_of(m, row, side_west)
        for t in range(TRACERS):
            slab, place = state(t, row), place_of(t, row)
            middle_ref[t, row + 1] = step(
                slab,
                west_of(slab, from_west, place),
                east_of(slab, from_east, place),
                state(t, row + 1),
                state(t, row - 1),
                *local,
            )

    def column(own, left, right, east, before, side):
        north = slot(side, 2)
        around = (rolled(own, -1, 1), rolled(own, 1, 1))
        return step(
            own, left, right, *around, east, before, north, rolled(north, 1, 1), slot(side, 1)
        )

    next_west = column(
        from_west, slot(from_west, 1), own_west, side_west, slot(side_west, 3), side_west
    )
    next_east = column(
        from_east, own_east, slot(from_east, 1), side_east, wind_east(m), side_east
    )
    m = moments[1]
    side_west, _ = sides(m)
    for row in range(LAT_CELLS):
        local = winds_of(m, row, side_west)
        for t in range(TRACERS):
            slab, place = middle_ref[t, row + 1], place_of(t, row)
            write(
                t,
                row,
                step(
                    slab,
                    west_of(slab, next_west, place),
                    east_of(slab, next_east, place),
                    middle_ref[t, row + 2],
                    middle_ref[t, row],
                    *local,
                ),
            )


def forward_body(
    state_ref, east_ref, north_ref, mixing_ref, own_east, own_west,
    up_ref, down_ref, from_west, from_east,
    field_ref, sides_ref, middle_ref, after_ref,
):
    south, north = up_ref.at[14], down_ref.at[12]
    for m in range(2):
        sides_ref[m, 0] = with_corners(from_west[1 + m], south[...], north[...], 1 + m)
        sides_ref[m, 1] = with_corners(from_east[1 + m], south[...], north[...], 4 + m)

    def write(t, row, slab):
        after_ref[t, row] = slab

    two_steps(
        forward,
        (0, 1),
        lambda t, row: state_ref[t, row],
        (east_ref, north_ref, mixing_ref),
        lambda i: up_ref[6 + i],
        lambda i: down_ref[6 + i],
        lambda m: own_east[1 + m],
        lambda m: (sides_ref[m, 0], sides_ref[m, 1]),
        up_ref,
        down_ref,
        own_east[0],
        own_west[0],
        with_corners(from_west[0], south[...], north[...], 0),
        with_corners(from_east[0], south[...], north[...], 3),
        middle_ref,
        write,
    )
    for i in range(6):
        for low_row in range(2):
            slabs = []
            for p in (2 * i, 2 * i + 1):
                slabs.append(after_ref[p // 4, (p % 4) * 2 + low_row])
            both = jnp.concatenate(slabs, axis=0)
            high = both.astype(jnp.bfloat16)
            low = (both - high.astype(jnp.float32)).astype(jnp.bfloat16)
            rows = slice(i * PAIR, (i + 1) * PAIR)
            field_ref[rows, low_row * LANES : (low_row + 1) * LANES] = high
            field_ref[rows, (2 + low_row) * LANES : (3 + low_row) * LANES] = low


def cell_slab(ref, t, row):
    first = (t * 4 + row // 2) * LEVELS
    return ref[first : first + LEVELS, (row % 2) * LANES : (row % 2 + 1) * LANES]


def adjoint_body(
    adjoint_ref, east_ref, north_ref, mixing_ref, wind_up, wind_down, wind_east, sides_ref,
    own_east, own_west, from_west, from_east, up_ref, down_ref, gradient_ref, middle_ref,
):
    def write(t, row, slab):
        gradient_ref[t, :, row, :] = slab

    two_steps(
        backward,
        (1, 0),
        lambda t, row: cell_slab(adjoint_ref, t, row),
        (east_ref, north_ref, mixing_ref),
        lambda i: wind_up[6 + i],
        lambda i: wind_down[6 + i],
        lambda m: wind_east[1 + m],
        lambda m: (sides_ref[m, 0], sides_ref[m, 1]),
        up_ref,
        down_ref,
        own_east[...],
        own_west[...],
        with_corners(from_west[...], up_ref[6], down_ref[6]),
        with_corners(from_east[...], up_ref[7], down_ref[7]),
        middle_ref,
        write,
    )


STATE = jax.ShapeDtypeStruct((TRACERS, LAT_CELLS, LEVELS, LANES), jnp.float32)
ROW_EDGE = jax.ShapeDtypeStruct((2 * TRACERS, LEVELS, LANES), jnp.float32)
COLUMN_EDGE = jax.ShapeDtypeStruct((LEVELS, LANES), jnp.float32)
EDGES = [ROW_EDGE, ROW_EDGE, COLUMN_EDGE, COLUMN_EDGE]
MIDDLE = pltpu.VMEM((TRACERS, LAT_CELLS + 2, LEVELS, LANES), jnp.float32)


def whole(body, outs, operands, name, scratch=(), scalars=0, flops=5000000, scalar_outs=0, vmem_mib=56):
    smem = pl.BlockSpec(memory_space=pltpu.SMEM)

    def vmem(array):
        zeros = (0,) * len(array.shape)
        return pl.BlockSpec(array.shape, lambda i: zeros, pipeline_mode=pl.Buffered(1))

    return pl.pallas_call(
        body,
        grid=(1,),
        in_specs=[smem if i < scalars else vmem(a) for i, a in enumerate(operands)],
        out_specs=[vmem(a) if i < len(outs) - scalar_outs else smem for i, a in enumerate(outs)],
        out_shape=outs,
        scratch_shapes=list(scratch),
        compiler_params=pltpu.CompilerParams(vmem_limit_bytes=vmem_mib << 20),
        cost_estimate=pl.CostEstimate(flops=flops, bytes_accessed=6000000, transcendentals=0),
        name=name,
    )(*operands)


def shifted(array, lat_by, lon_by):
    lat, lon = lax.axis_size("lat"), lax.axis_size("lon")
    if not lat_by:
        return lax.ppermute(array, "lon", [(j, (j + lon_by) % lon) for j in range(lon)])
    rows = [(i, i + lat_by) for i in range(lat) if 0 <= i + lat_by < lat]
    if not lon_by:
        return lax.ppermute(array, "lat", rows)
    pairs = [(i * lon + j, k * lon + (j + lon_by) % lon) for i, k in rows for j in range(lon)]
    return lax.ppermute(array, ("lat", "lon"), pairs)


def plan(targets_ref, counts_ref, columns_ref, place_ref, first_ref, second_ref, tally_ref):
    def clear(device, carry):
        first_ref[device] = -1
        second_ref[device] = -1
        return carry

    lax.fori_loop(0, first_ref.shape[0], clear, 0, unroll=8)

    def name(block, carry):
        target = targets_ref[block]
        known = first_ref[target]
        second_ref[target] = jnp.where(known < 0, -1, block)
        first_ref[target] = jnp.where(known < 0, block, known)
        return carry

    lax.fori_loop(0, targets_ref.shape[0], name, 0, unroll=8)
    part_id = lax.broadcasted_iota(jnp.int32, (16, LANES), 0)
    group = lax.broadcasted_iota(jnp.int32, (16, LANES), 1) * GROUP_PARTS
    of_group = (part_id >= group) & (part_id < group + GROUP_PARTS)
    lane = lax.broadcasted_iota(jnp.int32, (1, LANES), 1)
    row_id = lax.broadcasted_iota(jnp.int32, (8, LANES), 0)
    square = (LANES, 2 * LANES)
    earlier = lax.broadcasted_iota(jnp.int32, square, 0) < lax.broadcasted_iota(
        jnp.int32, square, 1
    )
    earlier = jnp.where(earlier, 1.0, 0.0).astype(jnp.bfloat16)

    def rank(eight, carry):
        parts = lax.shift_right_logical(columns_ref[pl.ds(eight * 8, 8), :], 8)
        rows = [parts[j : j + 1] for j in range(8)]
        lives = [lane < counts_ref[eight * 8 + j] for j in range(8)]
        members = [
            jnp.where((part_id == row) & live, 1.0, 0.0) for row, live in zip(rows, lives)
        ]
        sums = jnp.dot(
            jnp.concatenate(members, axis=0).astype(jnp.bfloat16),
            earlier,
            preferred_element_type=jnp.float32,
        )
        places = jnp.zeros((8, LANES), jnp.float32)
        tallies = jnp.zeros((8, LANES), jnp.float32)
        for j in range(8):
            own = sums[16 * j : 16 * j + 16]
            before = jnp.where(
                part_id == rows[j],
                own[:, :LANES],
                jnp.where(part_id < rows[j], own[:, LANES:], jnp.float32(0.0)),
            )
            place = jnp.sum(before, axis=0, keepdims=True)
            place = jnp.where(lives[j], place, jnp.float32(LANES))
            places = jnp.where(row_id == j, place, places)
            tally = jnp.sum(jnp.where(of_group, own[:, LANES:], 0.0), axis=0, keepdims=True)
            tallies = jnp.where(row_id == j, tally, tallies)
        place_ref[pl.ds(eight * 8, 8), :] = places
        tally_ref[pl.ds(eight * 8, 8), :] = tallies
        return carry

    lax.fori_loop(0, targets_ref.shape[0] // 8, rank, 0, unroll=2)


def pack(
    source_ref, kernel_ref, columns_ref, observed_ref, weight_ref, place_ref, tally_ref, out_ref,
    observed_wide, weight_wide, order_ref,
):
    observed_wide[...] = observed_ref[...].astype(jnp.float32)
    weight_wide[...] = weight_ref[...].astype(jnp.float32)
    order_ref[...] = (
        lax.broadcasted_iota(jnp.int32, (LANES, LANES), 0).astype(jnp.float32).astype(jnp.bfloat16)
    )
    row_id = lax.broadcasted_iota(jnp.int32, (8, LANES), 0)
    one, nil = jnp.bfloat16(1), jnp.bfloat16(0)

    def sorted_block(slot):
        source = source_ref[slot]
        block = jnp.maximum(source, 0)
        row = pl.ds(block, 1)
        cell = columns_ref[row, :]
        part = lax.shift_right_logical(cell, 8) + 1
        meta = jnp.where(row_id == 0, part.astype(jnp.float32), jnp.float32(0.0))
        meta = jnp.where(row_id == 1, (cell & 255).astype(jnp.float32), meta)
        meta = jnp.where(row_id == 2, observed_wide[row, :], meta)
        meta = jnp.where(row_id == 3, weight_wide[row, :], meta)
        rows = jnp.concatenate([kernel_ref[block].astype(jnp.float32), meta], axis=0)
        place = jnp.where(source >= 0, place_ref[row, :], jnp.float32(LANES)).astype(jnp.bfloat16)
        moved = jnp.where(order_ref[...] == jnp.broadcast_to(place, (LANES, LANES)), one, nil)
        result = lax.dot_general(
            rows.astype(jnp.bfloat16),
            moved,
            (((1,), (1,)), ((), ())),
            preferred_element_type=jnp.float32,
        )
        tally = jnp.where(source >= 0, tally_ref[row, :], jnp.float32(0.0))
        meta = jnp.where(row_id == 4, tally, result[LEVELS:])
        return jnp.concatenate([result[:LEVELS], meta], axis=0).astype(jnp.bfloat16)

    together = 16

    def several(step, carry):
        blocks = [sorted_block(step * together + j) for j in range(together)]
        for j in range(together):
            out_ref[step * together + j] = blocks[j]
        return carry

    lax.fori_loop(0, out_ref.shape[0] // together, several, 0)


def pack_first_body(
    targets_ref, counts_ref, kernel_ref, columns_ref, observed_ref, weight_ref,
    out_ref, place_ref, tally_ref, first_ref, second_ref, *scratch,
):
    plan(targets_ref, counts_ref, columns_ref, place_ref, first_ref, second_ref, tally_ref)
    pack(
        first_ref, kernel_ref, columns_ref, observed_ref, weight_ref, place_ref, tally_ref, out_ref,
        *scratch,
    )


def innovations_body(first_ref, second_ref, returned_ref, place_ref, out_ref, rows_ref):
    def one(device, carry):
        for rank, source_ref in enumerate((first_ref, second_ref)):
            source = source_ref[device]
            block = jnp.where(source >= 0, source, LANES)
            rows_ref[pl.ds(block, 1), :] = returned_ref[pl.ds(2 * device + rank, 1), :]
        return carry

    lax.fori_loop(0, first_ref.shape[0], one, 0, unroll=8)
    place = place_ref[...].astype(jnp.int32)
    live = place < LANES
    found = jnp.take_along_axis(
        rows_ref[: place.shape[0], :], jnp.where(live, place, 0), axis=1
    )
    out_ref[...] = jnp.where(live, found, jnp.float32(0.0))


def soundings(
    field_ref, block_ref, adjoint_ref, write_misfit,
    stream_ref, found_ref, cell_ref, tally_ref, count_ref, sem,
):
    n = WIDTH * LANES
    one, nil = jnp.bfloat16(1), jnp.bfloat16(0)
    lane = lax.broadcasted_iota(jnp.int32, (ROWS, LANES), 1)
    cell_ref[...] = (
        lax.broadcasted_iota(jnp.int32, (256, LANES), 0).astype(jnp.float32).astype(jnp.bfloat16)
    )
    empty = jnp.zeros((ROWS, LANES), jnp.bfloat16)
    eighth = lax.broadcasted_iota(jnp.int32, (8, LANES), 0)

    def tally(eight, carry):
        rows = jnp.zeros((8, LANES), jnp.float32)
        for j in range(8):
            meta = block_ref[eight * 8 + j][LEVELS:].astype(jnp.float32)
            rows = jnp.where(eighth == j, meta[4:5], rows)
        tally_ref[pl.ds(eight * 8, 8), :] = rows.astype(jnp.int32)
        return carry

    lax.fori_loop(0, block_ref.shape[0] // 8, tally, 0, unroll=2)
    copy = pltpu.make_async_copy(tally_ref, count_ref, sem)
    copy.start()
    copy.wait()

    def merge(block, carry):
        ends, tails = list(carry[0]), list(carry[1])
        values = block_ref[block]
        start = jnp.int32(0)
        for g in range(GROUPS):
            count = count_ref[block, g]
            tile, at = lax.shift_right_logical(ends[g], 7), ends[g] & (LANES - 1)
            turned = pltpu.roll(values, (at - start) & (LANES - 1), 1)
            joined = jnp.where(lane >= at, turned, tails[g])
            stream_ref[g, tile] = joined
            tails[g] = jnp.where(at + count >= LANES, turned, joined)
            ends[g] = ends[g] + count
            start = start + count
        return tuple(ends), tuple(tails)

    ends, tails = lax.fori_loop(
        0,
        block_ref.shape[0],
        merge,
        ((jnp.int32(0),) * GROUPS, (empty,) * GROUPS),
        unroll=2,
    )
    for g in range(GROUPS):
        tile, at = lax.shift_right_logical(ends[g], 7), ends[g] & (LANES - 1)
        stream_ref[g, tile] = jnp.where(lane < at, tails[g], empty)
        for j in range(1, WIDTH):
            stream_ref[g, tile + j] = empty

    def load(g, step):
        tiles = [stream_ref[g, step * WIDTH + i] for i in range(WIDTH)]
        profile = jnp.concatenate([t[:LEVELS] for t in tiles], axis=1)
        meta = jnp.concatenate([t[LEVELS:] for t in tiles], axis=1).astype(jnp.float32)
        part, cell, observed, weight = (meta[j : j + 1] for j in range(4))
        cell = cell.astype(jnp.bfloat16)
        hits = [
            cell_ref[...] == jnp.broadcast_to(cell[:, i * LANES : (i + 1) * LANES], (256, LANES))
            for i in range(WIDTH)
        ]
        return g, step, profile, part - 1.0, observed, weight, hits

    def gather(g, step, profile, part, observed, weight, hits):
        pick = jnp.concatenate([jnp.where(hit, one, nil) for hit in hits], axis=1)
        pick_twice = jnp.concatenate([pick, pick], axis=0)
        column = jnp.zeros((LEVELS, n), jnp.float32)
        for i in range(g * GROUP_PARTS // 2, (g + 1) * GROUP_PARTS // 2):
            found = jnp.dot(
                field_ref[i * PAIR : (i + 1) * PAIR, :],
                pick_twice,
                preferred_element_type=jnp.float32,
            )
            column = jnp.where(part == 2.0 * i, found[:LEVELS], column)
            column = jnp.where(part == 2.0 * i + 1.0, found[LEVELS:], column)
        return column

    def force(column, g, step, profile, part, observed, weight, hits):
        model = jnp.sum(profile.astype(jnp.float32) * column, axis=0, keepdims=True)
        misfit = model - observed
        for i in range(WIDTH):
            found_ref[g, step * WIDTH + i] = jnp.broadcast_to(
                misfit[:, i * LANES : (i + 1) * LANES], (8, LANES)
            )
        forcing = weight * misfit
        high = forcing.astype(jnp.bfloat16)
        low = (forcing - high.astype(jnp.float32)).astype(jnp.bfloat16)
        return jnp.concatenate(
            [
                jnp.where(
                    hits[i], jnp.broadcast_to(term[:, i * LANES : (i + 1) * LANES], (256, LANES)), nil
                )
                for term in (high, low)
                for i in range(WIDTH)
            ],
            axis=1,
        )

    def scatter(spread, g, step, profile, part, observed, weight, hits):
        twice = jnp.concatenate([profile, profile], axis=0)
        second = lax.broadcasted_iota(jnp.int32, (PAIR, n), 0) >= LEVELS
        part_row = (part - jnp.where(second, 1.0, 0.0)).astype(jnp.bfloat16)
        for i in range(g * GROUP_PARTS // 2, (g + 1) * GROUP_PARTS // 2):
            left = jnp.where(part_row == jnp.bfloat16(2 * i), twice, nil)
            adjoint_ref[i * PAIR : (i + 1) * PAIR, :] += lax.dot_general(
                jnp.concatenate([left, left], axis=1),
                spread,
                (((1,), (1,)), ((), ())),
                preferred_element_type=jnp.float32,
            )

    def work(groups, step):
        loaded = [load(g, step) for g in groups]
        columns = [gather(*x) for x in loaded]
        spreads = [force(column, *x) for x, column in zip(loaded, columns)]
        for x, spread in zip(loaded, spreads):
            scatter(spread, *x)
        return 0

    steps = [lax.shift_right_logical(ends[g] + n - 1, n.bit_length() - 1) for g in range(GROUPS)]
    common = functools.reduce(jnp.minimum, steps)
    lax.fori_loop(0, common, lambda step, _: work(range(GROUPS), step), 0)
    for g in range(GROUPS):
        lax.fori_loop(common, steps[g], lambda step, _, g=g: work([g], step), 0)

    lane = lax.broadcasted_iota(jnp.int32, (8, LANES), 1)
    row_id = lax.broadcasted_iota(jnp.int32, (8, LANES), 0)

    def part_ways(eight, ends):
        ends = list(ends)
        rows = jnp.zeros((8, LANES), jnp.float32)
        for j in range(8):
            start = jnp.int32(0)
            row = jnp.zeros((8, LANES), jnp.float32)
            for g in range(GROUPS):
                count = count_ref[eight * 8 + j, g]
                tile, at = lax.shift_right_logical(ends[g], 7), ends[g] & (LANES - 1)
                values = jnp.where(lane >= at, found_ref[g, tile], found_ref[g, tile + 1])
                values = pltpu.roll(values, (start - at) & (LANES - 1), 1)
                row = jnp.where(lane >= start, values, row)
                ends[g] = ends[g] + count
                start = start + count
            rows = jnp.where(row_id == j, row, rows)
        write_misfit(eight, rows)
        return tuple(ends)

    lax.fori_loop(0, block_ref.shape[0] // 8, part_ways, (jnp.int32(0),) * GROUPS)


def first_soundings_body(field_ref, block_ref, adjoint_ref, misfit_ref, *scratch):
    adjoint_ref[...] = jnp.zeros_like(adjoint_ref)

    def write_misfit(eight, rows):
        misfit_ref[pl.ds(eight * 8, 8), :] = rows

    soundings(field_ref, block_ref, adjoint_ref, write_misfit, *scratch)


def second_soundings_body(
    field_ref, block_ref, earlier_ref, other_ref, adjoint_ref, misfit_ref, *rest
):
    edges, scratch = rest[:4], rest[4:]
    adjoint_ref[...] = earlier_ref[...]

    def write_misfit(eight, rows):
        misfit_ref[pl.ds(eight * 16, 8, stride=2), :] = other_ref[pl.ds(eight * 8, 8), :]
        misfit_ref[pl.ds(eight * 16 + 1, 8, stride=2), :] = rows

    soundings(field_ref, block_ref, adjoint_ref, write_misfit, *scratch)
    write_edges(lambda t, row: cell_slab(adjoint_ref, t, row), *edges)


def observe(field, blocks, earlier=()):
    count = blocks.shape[0]
    tiles = count + WIDTH
    outs = [jax.ShapeDtypeStruct((PARTS * LEVELS, 256), jnp.float32)]
    outs += [jax.ShapeDtypeStruct((count * (2 if earlier else 1), LANES), jnp.float32)]
    return whole(
        second_soundings_body if earlier else first_soundings_body,
        outs + (EDGES if earlier else []),
        (field, blocks) + tuple(earlier),
        "second_soundings" if earlier else "first_soundings",
        scratch=[
            pltpu.VMEM((GROUPS, tiles, ROWS, LANES), jnp.bfloat16),
            pltpu.VMEM((GROUPS, tiles, 8, LANES), jnp.float32),
            pltpu.VMEM((256, LANES), jnp.bfloat16),
            pltpu.VMEM((count, LANES), jnp.int32),
            pltpu.SMEM((count, LANES), jnp.int32),
            pltpu.SemaphoreType.DMA(()),
        ],
        flops=15000000000,
    )


def per_device(
    initial, east_wind, north_wind, mixing, kernel, columns, observed, obs_weight, counts, targets
):
    lat_count = lax.axis_size("lat")
    lon_count = lax.axis_size("lon")
    sounds = kernel.shape[2]
    block_count = kernel.shape[0]
    device_count = lat_count * lon_count

    def exchange(array):
        return lax.all_to_all(array, ("lat", "lon"), split_axis=0, concat_axis=0, tiled=True)

    is_last = (lax.axis_index("lat") == lat_count - 1).astype(jnp.int32).reshape(1)
    winds_like = jax.ShapeDtypeStruct((2, LAT_CELLS, LEVELS, LANES), jnp.float32)

    def slabs_like(number):
        return jax.ShapeDtypeStruct((number, LEVELS, LANES), jnp.float32)

    prepared = whole(
        prepare_body,
        [STATE, winds_like, winds_like, winds_like]
        + [slabs_like(14), slabs_like(12), slabs_like(3), slabs_like(3)],
        (is_last, initial, east_wind, north_wind, mixing),
        "prepare",
        scalars=1,
    )
    state, fields, (up, down, east, west) = prepared[0], tuple(prepared[1:4]), prepared[4:]
    counts, east, west = lax.optimization_barrier((counts, east, west))
    slots = jax.ShapeDtypeStruct((device_count, ROWS, sounds), jnp.bfloat16)
    by_device = jax.ShapeDtypeStruct((device_count,), jnp.int32)
    heard = (kernel, columns, observed, obs_weight)
    scratch = [pltpu.VMEM((block_count, sounds), jnp.float32)] * 2
    scratch += [pltpu.VMEM((LANES, LANES), jnp.bfloat16)]
    by_block = jax.ShapeDtypeStruct((block_count, sounds), jnp.float32)
    out_first, place, tally, source_first, source_second = whole(
        pack_first_body,
        [slots, by_block, by_block, by_device, by_device],
        (targets[:, 0], counts) + heard,
        "pack_first",
        scratch=scratch,
        scalars=2,
        scalar_outs=2,
    )
    (out_second,) = whole(
        pack, [slots], (source_second,) + heard + (place, tally), "pack_second", scratch=scratch,
        scalars=1,
    )
    sides = (shifted(east, 0, 1), shifted(west, 0, -1))
    out_first, *sides = lax.optimization_barrier((out_first, *sides))
    up, down = whole(
        corners_body, [slabs_like(15), slabs_like(13)], tuple(sides) + (up, down), "corners"
    )
    out_first, up, down = lax.optimization_barrier((out_first, up, down))
    got_first = exchange(out_first)
    from_south, from_north = shifted(up, 1, 0), shifted(down, -1, 0)
    out_second, from_south, from_north = lax.optimization_barrier(
        (out_second, from_south, from_north)
    )
    got_second = exchange(out_second)
    field, wind_sides = whole(
        forward_body,
        [
            jax.ShapeDtypeStruct((12 * LEVELS, 512), jnp.bfloat16),
            jax.ShapeDtypeStruct((2, 2, LEVELS, LANES), jnp.float32),
        ],
        (state,) + fields + (east, west, from_south, from_north) + tuple(sides),
        "forward",
        scratch=[MIDDLE, pltpu.VMEM(STATE.shape, jnp.float32)],
    )
    earlier = observe(field, got_first)
    adjoint, misfit, up, down, own_east, own_west = observe(field, got_second, earlier)
    from_west, from_east = shifted(own_east, 0, 1), shifted(own_west, 0, -1)
    ends = jnp.stack([from_west, from_east])
    returned = exchange(misfit)
    (gradient,) = whole(
        adjoint_body,
        [jax.ShapeDtypeStruct(initial.shape, jnp.float32)],
        (adjoint,) + fields + (from_south, from_north, east, wind_sides)
        + (own_east, own_west, from_west, from_east)
        + (shifted(jnp.concatenate([up, ends]), 1, 0), shifted(jnp.concatenate([down, ends]), -1, 0)),
        "adjoint",
        scratch=[MIDDLE],
    )
    returned, gradient = lax.optimization_barrier((returned, gradient))
    (innovations,) = whole(
        innovations_body,
        [jax.ShapeDtypeStruct((block_count, sounds), jnp.float32)],
        (source_first, source_second, returned, place),
        "innovations",
        scratch=[pltpu.VMEM((block_count + 8, sounds), jnp.float32)],
        scalars=2,
    )
    return (gradient, innovations)


def solution(mesh):
    return jax.shard_map(
        per_device,
        mesh=mesh,
        in_specs=(
            P(None, None, "lat", "lon"),
            P(None, None, "lat", "lon"),
            P(None, None, "lat", "lon"),
            P(None, None, "lat", "lon"),
            P(("lat", "lon"), None, None),
            P(("lat", "lon"), None),
            P(("lat", "lon"), None),
            P(("lat", "lon"), None),
            P(("lat", "lon")),
            P(("lat", "lon"), None),
        ),
        out_specs=(P(None, None, "lat", "lon"), P(("lat", "lon"), None)),
        check_vma=False,
    )
```

time: 219 us -> 188 us (0.86)
  starting transfers between devices: 78.8 us -> 49.7 us
  Pallas kernels: 63.3 us -> 87.6 us
  waiting for transfers between devices: 55.4 us -> 45 us
  other arithmetic: 9.31 us -> 1.1 us
  local copies, waits for them, and re-layouts: 8.39 us -> 2.89 us
    pallas_call x10 -> x9, Pallas kernels: 63.3 us -> 87.6 us  [whole(): pl.pallas_call(body, grid=(1,), in_specs=[smem if i < scalars else vmem(a...]
    all_to_all x3, waiting for transfers between devices: 28.1 us -> 3.89 us  [exchange(): lax.all_to_all(array, ('lat', 'lon'), split_axis=0, concat_axis=0, tiled=...]
    ppermute x16 -> x8, starting transfers between devices: 38.3 us -> 16.7 us  [the longest x4 10 us: shifted(): return lax.ppermute(array, 'lat', rows)]
    ppermute x16 -> x8, waiting for transfers between devices: 27.3 us -> 41.1 us  [the longest x4 28.4 us: shifted(): return lax.ppermute(array, 'lat', rows)]
    all_to_all x3, starting transfers between devices: 40.5 us -> 33.1 us  [exchange(): lax.all_to_all(array, ('lat', 'lon'), split_axis=0, concat_axis=0, tiled=...]
    unnamed x24 -> x20, local copies, waits for them, and re-layouts: 7.89 us -> 2.89 us
    reduce_sum x2 -> x0, other arithmetic: 3.13 us -> none  [the longest x1 2.79 us: per_device(): place = jnp.sum(jnp.where(key[:, :, None] < key[:, None, :], 1, 0), axis=1)]
    ge x2 -> x0, other arithmetic: 2.22 us -> none  [observe(): inside = (part >= lowest) & (part < lowest + GROUP_PARTS)]
  transfers between devices with their start and end apart: 19 -> 11, of which waited for: 6 -> 5; matrix products, arithmetic and copies ran while one was open for 1% -> 0% of each run, Pallas kernels for 7% -> 31%
where the time goes in v3:
time: 188 us; the launch traced here: 187 us
  Pallas kernels  87.6 us (47%)
  starting transfers between devices  49.7 us (26%)
  waiting for transfers between devices  45 us (24%)
  local copies, waits for them, and re-layouts  2.89 us (2%)
    pallas_call x9, Pallas kernels, whole(): pl.pallas_call(body, grid=(1,), in_specs=[smem if i < scalars else vmem(a...  87.6 us
    all_to_all x3, starting transfers between devices, exchange(): lax.all_to_all(array, ('lat', 'lon'), split_axis=0, concat_axis=0, tiled=...  33.1 us
    ppermute x4, waiting for transfers between devices, shifted(): return lax.ppermute(array, 'lat', rows)  28.4 us
    ppermute x4, waiting for transfers between devices, shifted(): lax.ppermute(array, 'lon', [(j, (j + lon_by) % lon) for j in range(lon)])  12.6 us
    ppermute x4, starting transfers between devices, shifted(): return lax.ppermute(array, 'lat', rows)  10 us
    ppermute x4, starting transfers between devices, shifted(): lax.ppermute(array, 'lon', [(j, (j + lon_by) % lon) for j in range(lon)])  6.63 us
    all_to_all x3, waiting for transfers between devices, exchange(): lax.all_to_all(array, ('lat', 'lon'), split_axis=0, concat_axis=0, tiled=...  3.89 us
  transfers between devices with their start and end apart: 11, of which 5 were waited for; matrix products, arithmetic and copies ran while one was open for 0% of the time, Pallas kernels for 31%

profile of v3, /device:TPU:1, one launch (start us, length us, event | category | flops | bytes accessed | tf_op | source)
XLA Modules:
  0.0 187.1 jit_solution(4862560983964337016)
XLA Ops:
  0.6 7.4 %prepare.1 = (f32[3,8,72,128]{3,2,1,0:T(8,128)}, f32[2,8,72,128]{3,2,1,0:T(8,128)}, f32[2,8,72,128]{3,2,1,0:T(8,128)}, f32[2,8,72,128]{3,2,1,0:T(8,128)}, f32[14...) custom-call(s32[1]{0:T(128)} %bitcast.last_ref, ...), custom_call_target="tpu_custom_call" | custom-call | flops 5000000 | bytes 6000000 | tf_op jit(solution)/shard_map/prepare/pallas_call | solution.py:326
  8.0 1.4 collective-permute-start.1
  9.5 2.8 %collective-permute-start = (f32[3,72,128]{2,1,0:T(8,128)}, f32[3,72,128]{2,1,0:T(8,128)S(1)}, u32[]{:S(2)}, u32[]{:S(2)}) collective-permute-start(f32[3,72,128]{2,1,0:T(8,128)} %get-tuple-element.47.own_east.wind_east), channel_id=1, source_target_pairs={{0,1},{1,2},{2,3},{3,4},{4,5},{5,6},{6,7},{7,8},{8,9},{9,10},{10,1... | collective-permute-start | bytes 331784 | tf_op jit(solution)/shard_map/ppermute | solution.py:342
  12.3 10.0 %pack_first.1 = (bf16[128,80,128]{2,1,0:T(8,128)(2,1)}, f32[128,128]{1,0:T(8,128)}, f32[128,128]{1,0:T(8,128)}, s32[128]{0:T(128)}, s32[128]{0:T(128)}) custom-call(s32[128]{0:T(128)} %bitcast.10, s32[128]{0:T(128)} %counts_ref, bf16[128,72,128]{2,1,0:T(8,128)(2,1)} %kernel_ref.3, s32[128,128]{1,0:T(8,128)} %columns_ref.3, bf16[128,128]{1,0:T(8,128)(2,1)} %observed_ref.3, ...), custom_call_target="tpu_custom_call" | custom-call | flops 5000000 | bytes 6000000 | tf_op jit(solution)/shard_map/pack_first/pallas_call | solution.py:326
  22.3 0.0 collective-permute-done.1.from_east
  22.3 0.0 copy-start.4
  22.3 0.0 collective-permute-done.from_west
  22.3 0.0 copy-start.5
  22.3 0.6 copy-done.4
  22.9 0.1 copy-done.5
  23.0 2.4 %corners.1 = (f32[15,72,128]{2,1,0:T(8,128)}, f32[13,72,128]{2,1,0:T(8,128)}) custom-call(f32[3,72,128]{2,1,0:T(8,128)} %copy-done.5, f32[3,72,128]{2,1,0:T(8,128)} %copy-done.4, f32[14,72,128]{2,1,0:T(8,128)} %get-tuple-element.57.up_in, f32[12,72,128]{2,1,0:T(8,128)} %get-tuple-element.58.down_in), custom_call_target="tpu_custom_call" | custom-call | flops 5000000 | bytes 6000000 | tf_op jit(solution)/shard_map/corners/pallas_call | solution.py:326
  25.4 11.9 %all-to-all-start.1 = ((bf16[128,80,128]{2,1,0:T(8,128)(2,1)}), bf16[128,80,128]{2,1,0:T(8,128)(2,1)S(1)}, u32[]{:S(2)}, u32[]{:S(2)}) async-start(bf16[128,80,128]{2,1,0:T(8,128)(2,1)} %get-tuple-element.67), calls=%async_computation.1 | async-start | bytes 5242880 | tf_op jit(solution)/shard_map/all_to_all | solution.py:691
  37.3 3.4 %collective-permute-start.2 = (f32[15,72,128]{2,1,0:T(8,128)}, f32[15,72,128]{2,1,0:T(8,128)S(1)}, u32[]{:S(2)}, u32[]{:S(2)}) collective-permute-start(f32[15,72,128]{2,1,0:T(8,128)} %get-tuple-element.61), channel_id=1, source_target_pairs={{0,16},{16,32},{32,48},{48,64},{64,80},{80,96},{96,112},{1,17},{17... | collective-permute-start | bytes 1658888 | tf_op jit(solution)/shard_map/ppermute | solution.py:345
  40.8 1.3 collective-permute-start.3
  42.1 7.3 %pack_second.1 = bf16[128,80,128]{2,1,0:T(8,128)(2,1)} custom-call(s32[128]{0:T(128)} %get-tuple-element.50.source_ref.second_ref, bf16[128,72,128]{2,1,0:T(8,128)(2,1)} %kernel_ref.3, s32[128,128]{1,0:T(8,128)} %columns_ref.3, bf16[128,128]{1,0:T(8,128)(2,1)} %observed_ref.3, bf16[128,128]{1,0:T(8,128)(2,1)} %weight_ref.3, ...), custom_call_target="tpu_custom_call" | custom-call | flops 5000000 | bytes 6000000 | tf_op jit(solution)/shard_map/pack_second/pallas_call | solution.py:326
  49.4 28.4 %collective-permute-done.3.down_ref.wind_down = f32[13,72,128]{2,1,0:T(8,128)S(1)} collective-permute-done((f32[13,72,128]{2,1,0:T(8,128)}, f32[13,72,128]{2,1,0:T(8,128)S(1)}, u32[]{:S(2)}, u32[]{:S(2)}) %collective-permute-start.3) | collective-permute-done | bytes 479264 | tf_op jit(solution)/shard_map/ppermute | solution.py:345
  77.8 0.0 copy-start.2
  77.8 0.8 copy-done.2
  78.6 0.0 collective-permute-done.2.up_ref.wind_up
  78.6 0.0 all-to-all-done.1.block_ref
  78.6 0.0 copy-start
  78.6 10.9 %all-to-all-start = ((bf16[128,80,128]{2,1,0:T(8,128)(2,1)}), bf16[128,80,128]{2,1,0:T(8,128)(2,1)}, u32[]{:S(2)}, u32[]{:S(2)}) async-start(bf16[128,80,128]{2,1,0:T(8,128)(2,1)} %pack_second.1), calls=%async_computation | async-start | bytes 5242880 | tf_op jit(solution)/shard_map/all_to_all | solution.py:691
  89.6 0.0 copy-done.1
  89.6 0.0 copy-done
  89.6 6.5 %forward.1 = (bf16[864,512]{1,0:T(8,128)(2,1)}, f32[2,2,72,128]{3,2,1,0:T(8,128)}) custom-call(f32[3,8,72,128]{3,2,1,0:T(8,128)} %get-tuple-element.41.state_ref, f32[2,8,72,128]{3,2,1,0:T(8,128)} %get-tuple-element.42.east_ref, f32[2,8,72,128]{3,2,1,0:T(8,128)} %get-tuple-element.43.north_ref, f32[2,8,72,128]{3,2,1,0:T(8,128)} %get-tuple-element.44.mixing_ref, ...), custom_call_target="tpu_custom_call" | custom-call | flops 5000000 | bytes 6000000 | tf_op jit(solution)/shard_map/forward/pallas_call | solution.py:326
  96.1 27.5 %first_soundings.1 = (f32[864,256]{1,0:T(8,128)}, f32[128,128]{1,0:T(8,128)}) custom-call(bf16[864,512]{1,0:T(8,128)(2,1)} %get-tuple-element.65.field_ref, bf16[128,80,128]{2,1,0:T(8,128)(2,1)} %copy-done), custom_call_target="tpu_custom_call" | custom-call | flops 15000000512 | bytes 6000000 | tf_op jit(solution)/shard_map/first_soundings/pallas_call | solution.py:326
  123.6 1.2 all-to-all-done.block_ref
  124.8 17.9 %second_soundings.1 = (f32[864,256]{1,0:T(8,128)}, f32[256,128]{1,0:T(8,128)}, f32[6,72,128]{2,1,0:T(8,128)}, f32[6,72,128]{2,1,0:T(8,128)}, f32[72,128]{1,0:T(8,128)}, /*index=5*/f32[72,128]{1,0:T(8,128)}) custom-call(bf16[864,512]{1,0:T(8,128)(2,1)} %get-tuple-element.65.field_ref, bf16[128,80,128]{2,1,0:T(8,128)(2,1)} %all-to-all-done.block_ref, ...), custom_call_target="tpu_custom_call" | custom-call | flops 15000000512 | bytes 6000000 | tf_op jit(solution)/shard_map/second_soundings/pallas_call | solution.py:326
  142.7 2.4 %collective-permute-start.4 = (f32[72,128]{1,0:T(8,128)}, f32[72,128]{1,0:T(8,128)S(1)}, u32[]{:S(2)}, u32[]{:S(2)}) collective-permute-start(f32[72,128]{1,0:T(8,128)} %get-tuple-element.73.own_east), channel_id=1, source_target_pairs={{0,1},{1,2},{2,3},{3,4},{4,5},{5,6},{6,7},{7,8},{8,9},{9,10},{10,1... | collective-permute-start | bytes 110600 | tf_op jit(solution)/shard_map/ppermute | solution.py:342
  145.1 0.0 collective-permute-start.5
  145.1 1.4 collective-permute-done.4.from_west
  146.5 11.3 %collective-permute-done.5.from_east = f32[72,128]{1,0:T(8,128)S(1)} collective-permute-done((f32[72,128]{1,0:T(8,128)}, f32[72,128]{1,0:T(8,128)S(1)}, u32[]{:S(2)}, u32[]{:S(2)}) %collective-permute-start.5) | collective-permute-done | bytes 36896 | tf_op jit(solution)/shard_map/ppermute | solution.py:342
  157.8 1.1 pad_maximum_fusion
  158.9 1.3 collective-permute-start.7
  160.2 4.0 %collective-permute-start.6 = (f32[8,72,128]{2,1,0:T(8,128)S(1)}, f32[8,72,128]{2,1,0:T(8,128)S(1)}, u32[]{:S(2)}, u32[]{:S(2)}) collective-permute-start(f32[8,72,128]{2,1,0:T(8,128)S(1)} %get-tuple-element.81), channel_id=1, source_target_pairs={{0,16},{16,32},{32,48},{48,64},{64,80},{80,96},{96,112},{1,17},{17... | collective-permute-start | bytes 884744 | tf_op jit(solution)/shard_map/ppermute | solution.py:345
  164.2 10.2 %all-to-all-start.2 = ((f32[128,2,128]{2,1,0:T(2,128)}), f32[128,2,128]{2,1,0:T(2,128)S(1)}, u32[]{:S(2)}, u32[]{:S(2)}) async-start(f32[128,2,128]{2,1,0:T(2,128)} %bitcast.9), calls=%async_computation.2 | async-start | bytes 262144 | tf_op jit(solution)/shard_map/all_to_all | solution.py:691
  174.4 0.0 collective-permute-done.7.down_ref
  174.4 0.0 copy-start.6
  174.4 0.0 collective-permute-done.6.up_ref
  174.4 0.0 copy-start.7
  174.4 0.0 copy-done.8
  174.5 0.0 copy-done.9
  174.5 0.7 copy-done.6
  175.1 0.1 copy-done.7
  175.2 6.4 %adjoint.1 = f32[3,72,8,128]{3,2,1,0:T(8,128)} custom-call(f32[864,256]{1,0:T(8,128)} %get-tuple-element.71.adjoint_ref, f32[2,8,72,128]{3,2,1,0:T(8,128)} %get-tuple-element.42.east_ref, f32[2,8,72,128]{3,2,1,0:T(8,128)} %get-tuple-element.43.north_ref, f32[2,8,72,128]{3,2,1,0:T(8,128)} %get-tuple-element.44.mixing_ref, f32[15,72,128]{2,1,0:T(8,128)} %copy-done.1, ...), custom_call_target="tpu_custom_call" | custom-call | flops 5000000 | bytes 6000000 | tf_op jit(solution)/shard_map/adjoint/pallas_call | solution.py:326
  181.6 2.7 %all-to-all-done.2 = f32[128,2,128]{2,1,0:T(2,128)S(1)} async-done(((f32[128,2,128]{2,1,0:T(2,128)}), f32[128,2,128]{2,1,0:T(2,128)S(1)}, u32[]{:S(2)}, u32[]{:S(2)}) %all-to-all-start.2) | async-done | bytes 131104 | tf_op jit(solution)/shard_map/all_to_all | solution.py:691
  184.4 0.6 copy-done.3
  185.0 2.1 %innovations.1 = f32[128,128]{1,0:T(8,128)} custom-call(s32[128]{0:T(128)} %get-tuple-element.78.first_ref, s32[128]{0:T(128)} %get-tuple-element.50.source_ref.second_ref, f32[256,128]{1,0:T(8,128)} %bitcast.6, f32[128,128]{1,0:T(8,128)} %get-tuple-element.51.place_ref), custom_call_target="tpu_custom_call" | custom-call | flops 5000000 | bytes 6000000 | tf_op jit(solution)/shard_map/innovations/pallas_call | solution.py:326
  (4 shorter events, 0.0 us)
Async XLA Ops:
  8.0 14.3 %collective-permute-start.1 = (f32[3,72,128]{2,1,0:T(8,128)}, f32[3,72,128]{2,1,0:T(8,128)S(1)}, u32[]{:S(2)}, u32[]{:S(2)}) collective-permute-start(f32[3,72,128]{2,1,0:T(8,128)} %get-tuple-element.48.own_west), channel_id=1, source_target_pairs={{0,15},{1,0},{2,1},{3,2},{4,3},{5,4},{6,5},{7,6},{8,7},{9,8},{10,9... | collective-permute-start | bytes 331784 | tf_op jit(solution)/shard_map/ppermute | solution.py:342
  9.5 12.9 %collective-permute-start = (f32[3,72,128]{2,1,0:T(8,128)}, f32[3,72,128]{2,1,0:T(8,128)S(1)}, u32[]{:S(2)}, u32[]{:S(2)}) collective-permute-start(f32[3,72,128]{2,1,0:T(8,128)} %get-tuple-element.47.own_east.wind_east), channel_id=1, source_target_pairs={{0,1},{1,2},{2,3},{3,4},{4,5},{5,6},{6,7},{7,8},{8,9},{9,10},{10,1... | collective-permute-start | bytes 331784 | tf_op jit(solution)/shard_map/ppermute | solution.py:342
  22.3 0.6 copy-start.4
  22.3 0.7 copy-start.5
  25.4 53.2 %all-to-all-start.1 = ((bf16[128,80,128]{2,1,0:T(8,128)(2,1)}), bf16[128,80,128]{2,1,0:T(8,128)(2,1)S(1)}, u32[]{:S(2)}, u32[]{:S(2)}) async-start(bf16[128,80,128]{2,1,0:T(8,128)(2,1)} %get-tuple-element.67), calls=%async_computation.1 | async-start | bytes 5242880 | tf_op jit(solution)/shard_map/all_to_all | solution.py:691
  37.3 41.3 %collective-permute-start.2 = (f32[15,72,128]{2,1,0:T(8,128)}, f32[15,72,128]{2,1,0:T(8,128)S(1)}, u32[]{:S(2)}, u32[]{:S(2)}) collective-permute-start(f32[15,72,128]{2,1,0:T(8,128)} %get-tuple-element.61), channel_id=1, source_target_pairs={{0,16},{16,32},{32,48},{48,64},{64,80},{80,96},{96,112},{1,17},{17... | collective-permute-start | bytes 1658888 | tf_op jit(solution)/shard_map/ppermute | solution.py:345
  40.8 37.0 %collective-permute-start.3 = (f32[13,72,128]{2,1,0:T(8,128)}, f32[13,72,128]{2,1,0:T(8,128)S(1)}, u32[]{:S(2)}, u32[]{:S(2)}) collective-permute-start(f32[13,72,128]{2,1,0:T(8,128)} %get-tuple-element.62), channel_id=1, source_target_pairs={{16,0},{32,16},{48,32},{64,48},{80,64},{96,80},{112,96},{17,1},{33... | collective-permute-start | bytes 1437704 | tf_op jit(solution)/shard_map/ppermute | solution.py:345
  77.8 0.8 copy-start.2
  78.6 11.0 %copy-start.1 = (f32[15,72,128]{2,1,0:T(8,128)}, f32[15,72,128]{2,1,0:T(8,128)S(1)}, u32[]{:S(2)}) copy-start(f32[15,72,128]{2,1,0:T(8,128)S(1)} %collective-permute-done.2.up_ref.wind_up) | copy-start | bytes 1658884
  78.6 11.0 %copy-start = (bf16[128,80,128]{2,1,0:T(8,128)(2,1)}, bf16[128,80,128]{2,1,0:T(8,128)(2,1)S(1)}, u32[]{:S(2)}) copy-start(bf16[128,80,128]{2,1,0:T(8,128)(2,1)S(1)} %all-to-all-done.1.block_ref) | copy-start | bytes 7864324
  78.6 46.2 %all-to-all-start = ((bf16[128,80,128]{2,1,0:T(8,128)(2,1)}), bf16[128,80,128]{2,1,0:T(8,128)(2,1)}, u32[]{:S(2)}, u32[]{:S(2)}) async-start(bf16[128,80,128]{2,1,0:T(8,128)(2,1)} %pack_second.1), calls=%async_computation | async-start | bytes 5242880 | tf_op jit(solution)/shard_map/all_to_all | solution.py:691
  142.7 3.8 %collective-permute-start.4 = (f32[72,128]{1,0:T(8,128)}, f32[72,128]{1,0:T(8,128)S(1)}, u32[]{:S(2)}, u32[]{:S(2)}) collective-permute-start(f32[72,128]{1,0:T(8,128)} %get-tuple-element.73.own_east), channel_id=1, source_target_pairs={{0,1},{1,2},{2,3},{3,4},{4,5},{5,6},{6,7},{7,8},{8,9},{9,10},{10,1... | collective-permute-start | bytes 110600 | tf_op jit(solution)/shard_map/ppermute | solution.py:342
  145.1 12.6 %collective-permute-start.5 = (f32[72,128]{1,0:T(8,128)}, f32[72,128]{1,0:T(8,128)S(1)}, u32[]{:S(2)}, u32[]{:S(2)}) collective-permute-start(f32[72,128]{1,0:T(8,128)} %get-tuple-element.74.own_west), channel_id=1, source_target_pairs={{0,15},{1,0},{2,1},{3,2},{4,3},{5,4},{6,5},{7,6},{8,7},{9,8},{10,9... | collective-permute-start | bytes 110600 | tf_op jit(solution)/shard_map/ppermute | solution.py:342
  146.5 27.9 %copy-start.8 = (f32[72,128]{1,0:T(8,128)}, f32[72,128]{1,0:T(8,128)S(1)}, u32[]{:S(2)}) copy-start(f32[72,128]{1,0:T(8,128)S(1)} %collective-permute-done.4.from_west) | copy-start | bytes 110596
  157.8 16.7 %copy-start.9 = (f32[72,128]{1,0:T(8,128)}, f32[72,128]{1,0:T(8,128)S(1)}, u32[]{:S(2)}) copy-start(f32[72,128]{1,0:T(8,128)S(1)} %collective-permute-done.5.from_east) | copy-start | bytes 110596
  158.9 15.5 %collective-permute-start.7 = (f32[8,72,128]{2,1,0:T(8,128)S(1)}, f32[8,72,128]{2,1,0:T(8,128)S(1)}, u32[]{:S(2)}, u32[]{:S(2)}) collective-permute-start(f32[8,72,128]{2,1,0:T(8,128)S(1)} %get-tuple-element.80), channel_id=1, source_target_pairs={{16,0},{32,16},{48,32},{64,48},{80,64},{96,80},{112,96},{17,1},{33... | collective-permute-start | bytes 884744 | tf_op jit(solution)/shard_map/ppermute | solution.py:345
  160.2 14.3 %collective-permute-start.6 = (f32[8,72,128]{2,1,0:T(8,128)S(1)}, f32[8,72,128]{2,1,0:T(8,128)S(1)}, u32[]{:S(2)}, u32[]{:S(2)}) collective-permute-start(f32[8,72,128]{2,1,0:T(8,128)S(1)} %get-tuple-element.81), channel_id=1, source_target_pairs={{0,16},{16,32},{32,48},{48,64},{64,80},{80,96},{96,112},{1,17},{17... | collective-permute-start | bytes 884744 | tf_op jit(solution)/shard_map/ppermute | solution.py:345
  164.2 20.2 %all-to-all-start.2 = ((f32[128,2,128]{2,1,0:T(2,128)}), f32[128,2,128]{2,1,0:T(2,128)S(1)}, u32[]{:S(2)}, u32[]{:S(2)}) async-start(f32[128,2,128]{2,1,0:T(2,128)} %bitcast.9), calls=%async_computation.2 | async-start | bytes 262144 | tf_op jit(solution)/shard_map/all_to_all | solution.py:691
  174.4 0.7 copy-start.6
  174.4 0.8 copy-start.7
  184.4 0.7 copy-start.3

commit v4 on v3

--- a/solution.py
+++ b/solution.py
@@ -68,12 +68,7 @@
     return jnp.where(row == 9, rolled(north, LAT_CELLS - number, 1), out)
 
 
-def corners_body(from_west, from_east, up_in, down_in, up_ref, down_ref):
-    last = up_in.shape[0]
-    for i in range(last):
-        up_ref[i] = up_in[i]
-    for i in range(down_in.shape[0]):
-        down_ref[i] = down_in[i]
+def corners_body(from_west, from_east, up_ref, down_ref):
     row = (lane_index() & (SLOT - 1)) % 10
     up = jnp.zeros((LEVELS, LANES), jnp.float32)
     down = jnp.zeros((LEVELS, LANES), jnp.float32)
@@ -81,8 +76,8 @@
         column = from_west[i] if i < 3 else from_east[i - 3]
         up = up + rolled(jnp.where(row == LAT_CELLS, column, 0.0), -i, 1)
         down = down + rolled(jnp.where(row == 1, column, 0.0), i, 1)
-    up_ref[last] = up
-    down_ref[down_in.shape[0]] = down
+    up_ref[...] = up
+    down_ref[...] = down
 
 
 def mixed(slab, coeff):
@@ -114,36 +109,46 @@
     west_edge[...] = packed(slabs, 0) + packed(slabs, 1, SLOT)
 
 
-def prepare_body(
-    last_ref, initial_ref, east_ref, north_ref, mixing_ref,
-    state_ref, east_out, north_out, mixing_out, up_ref, down_ref, east_edge, west_edge,
-):
-    steps = east_ref.shape[0]
-    last = LAT_CELLS - 1
-    top = lax.broadcasted_iota(jnp.int32, (LEVELS, LANES), 0) == LEVELS - 1
+def arrange_body(
+    last_ref, initial_ref, east_ref, north_ref, mixing_ref, state_ref, east_out, north_out, mixing_out
+):
     for t in range(TRACERS):
         for row in range(LAT_CELLS):
             state_ref[t, row] = initial_ref[t, :, row, :]
-    for m in range(steps):
+    for m in range(east_ref.shape[0]):
         for row in range(LAT_CELLS):
             east_out[m, row] = east_ref[m, :, row, :]
-            north = north_ref[m, :, row, :]
-            if row == last:
-                north = jnp.where(last_ref[0] > 0, jnp.float32(0.0), north)
-            north_out[m, row] = north
-            mixing_out[m, row] = jnp.where(top, jnp.float32(0.0), mixing_ref[m, :, row, :])
+            north_out[m, row] = masked_north(last_ref, north_ref, m, row)
+            mixing_out[m, row] = masked_mixing(mixing_ref, m, row)
+
+
+def masked_north(last_ref, north_ref, m, row):
+    north = north_ref[m, :, row, :]
+    if row == LAT_CELLS - 1:
+        north = jnp.where(last_ref[0] > 0, jnp.float32(0.0), north)
+    return north
+
+
+def masked_mixing(mixing_ref, m, row):
+    top = lax.broadcasted_iota(jnp.int32, (LEVELS, LANES), 0) == LEVELS - 1
+    return jnp.where(top, jnp.float32(0.0), mixing_ref[m, :, row, :])
+
+
+def edges_body(
+    last_ref, initial_ref, east_ref, north_ref, mixing_ref, up_ref, down_ref, east_edge, west_edge
+):
+    last = LAT_CELLS - 1
     write_edges(
-        lambda t, row: state_ref[t, row], up_ref, down_ref, east_edge.at[0], west_edge.at[0]
-    )
-    for m in range(steps):
-        ups = (east_out[m, last], mixing_out[m, last], north_out[m, last], north_out[m, last - 1])
-        for i, slab in enumerate(ups):
+        lambda t, row: initial_ref[t, :, row, :], up_ref, down_ref, east_edge.at[0], west_edge.at[0]
+    )
+    for m in range(east_ref.shape[0]):
+        east = [east_ref[m, :, row, :] for row in range(LAT_CELLS)]
+        north = [masked_north(last_ref, north_ref, m, row) for row in range(LAT_CELLS)]
+        mixing = [masked_mixing(mixing_ref, m, row) for row in range(LAT_CELLS)]
+        for i, slab in enumerate((east[last], mixing[last], north[last], north[last - 1])):
             up_ref[6 + 4 * m + i] = slab
-        for i, slab in enumerate((east_out[m, 0], mixing_out[m, 0], north_out[m, 0])):
+        for i, slab in enumerate((east[0], mixing[0], north[0])):
             down_ref[6 + 3 * m + i] = slab
-        east, north, mixing = (
-            [ref[m, row] for row in range(LAT_CELLS)] for ref in (east_out, north_out, mixing_out)
-        )
         east_edge[1 + m] = (
             packed_wind(east, LANES - 1, 0)
             + packed_wind(mixing, LANES - 1, SLOT)
@@ -235,10 +240,9 @@
 
 def forward_body(
     state_ref, east_ref, north_ref, mixing_ref, own_east, own_west,
-    up_ref, down_ref, from_west, from_east,
+    up_ref, down_ref, from_west, from_east, south, north,
     field_ref, sides_ref, middle_ref, after_ref,
 ):
-    south, north = up_ref.at[14], down_ref.at[12]
     for m in range(2):
         sides_ref[m, 0] = with_corners(from_west[1 + m], south[...], north[...], 1 + m)
         sides_ref[m, 1] = with_corners(from_east[1 + m], south[...], north[...], 4 + m)
@@ -527,7 +531,7 @@
         block_ref.shape[0],
         merge,
         ((jnp.int32(0),) * GROUPS, (empty,) * GROUPS),
-        unroll=2,
+        unroll=4,
     )
     for g in range(GROUPS):
         tile, at = lax.shift_right_logical(ends[g], 7), ends[g] & (LANES - 1)
@@ -696,16 +700,16 @@
     def slabs_like(number):
         return jax.ShapeDtypeStruct((number, LEVELS, LANES), jnp.float32)
 
-    prepared = whole(
-        prepare_body,
-        [STATE, winds_like, winds_like, winds_like]
-        + [slabs_like(14), slabs_like(12), slabs_like(3), slabs_like(3)],
-        (is_last, initial, east_wind, north_wind, mixing),
-        "prepare",
+    grid = (is_last, initial, east_wind, north_wind, mixing)
+    up, down, east, west = whole(
+        edges_body,
+        [slabs_like(14), slabs_like(12), slabs_like(3), slabs_like(3)],
+        grid,
+        "edges",
         scalars=1,
     )
-    state, fields, (up, down, east, west) = prepared[0], tuple(prepared[1:4]), prepared[4:]
-    counts, east, west = lax.optimization_barrier((counts, east, west))
+    counts, up, down, east, west = lax.optimization_barrier((counts, up, down, east, west))
+    from_south, from_north = shifted(up, 1, 0), shifted(down, -1, 0)
     slots = jax.ShapeDtypeStruct((device_count, ROWS, sounds), jnp.bfloat16)
     by_device = jax.ShapeDtypeStruct((device_count,), jnp.int32)
     heard = (kernel, columns, observed, obs_weight)
@@ -726,17 +730,19 @@
         scalars=1,
     )
     sides = (shifted(east, 0, 1), shifted(west, 0, -1))
-    out_first, *sides = lax.optimization_barrier((out_first, *sides))
-    up, down = whole(
-        corners_body, [slabs_like(15), slabs_like(13)], tuple(sides) + (up, down), "corners"
-    )
-    out_first, up, down = lax.optimization_barrier((out_first, up, down))
+    out_first, from_south, from_north, *sides = lax.optimization_barrier(
+        (out_first, from_south, from_north, *sides)
+    )
     got_first = exchange(out_first)
-    from_south, from_north = shifted(up, 1, 0), shifted(down, -1, 0)
-    out_second, from_south, from_north = lax.optimization_barrier(
-        (out_second, from_south, from_north)
-    )
+    corner_up, corner_down = whole(corners_body, [COLUMN_EDGE] * 2, tuple(sides), "corners")
+    sides += [shifted(corner_up, 1, 0), shifted(corner_down, -1, 0)]
+    grid = lax.optimization_barrier((corner_up,) + grid)[1:]
+    arranged = whole(
+        arrange_body, [STATE, winds_like, winds_like, winds_like], grid, "arrange", scalars=1
+    )
+    out_second, *rest = lax.optimization_barrier((out_second, *sides, *arranged))
     got_second = exchange(out_second)
+    sides, state, fields = rest[:4], rest[4], tuple(rest[5:])
     field, wind_sides = whole(
         forward_body,
         [

time: 188 us -> 177 us (0.941)
  waiting for transfers between devices: 45 us -> 31.3 us
  starting transfers between devices: 49.7 us -> 58 us
  Pallas kernels: 87.6 us -> 82.3 us
    ppermute x4 -> x6, waiting for transfers between devices: 28.4 us -> 6.56 us  [shifted(): return lax.ppermute(array, 'lat', rows)]
    all_to_all x3, waiting for transfers between devices: 3.89 us -> 19.6 us  [exchange(): lax.all_to_all(array, ('lat', 'lon'), split_axis=0, concat_axis=0, tiled=...]
    ppermute x4, waiting for transfers between devices: 12.6 us -> 5.1 us  [shifted(): lax.ppermute(array, 'lon', [(j, (j + lon_by) % lon) for j in range(lon)])]
    ppermute x4 -> x6, starting transfers between devices: 10 us -> 16.3 us  [shifted(): return lax.ppermute(array, 'lat', rows)]
    pallas_call x9 -> x10, Pallas kernels: 87.6 us -> 82.3 us  [whole(): pl.pallas_call(body, grid=(1,), in_specs=[smem if i < scalars else vmem(a...]
    all_to_all x3, starting transfers between devices: 33.1 us -> 35.6 us  [exchange(): lax.all_to_all(array, ('lat', 'lon'), split_axis=0, concat_axis=0, tiled=...]
  transfers between devices with their start and end apart: 11 -> 13, of which waited for: 5 -> 6; matrix products, arithmetic and copies ran while one was open for 0% -> 0% of each run, Pallas kernels for 31% -> 33%
where the time goes in v4:
time: 177 us
  Pallas kernels  82.3 us (46%)
  starting transfers between devices  58 us (33%)
  waiting for transfers between devices  31.3 us (18%)
  local copies, waits for them, and re-layouts  3.01 us (2%)
    pallas_call x10, Pallas kernels, whole(): pl.pallas_call(body, grid=(1,), in_specs=[smem if i < scalars else vmem(a...  82.3 us
    all_to_all x3, starting transfers between devices, exchange(): lax.all_to_all(array, ('lat', 'lon'), split_axis=0, concat_axis=0, tiled=...  35.6 us
    all_to_all x3, waiting for transfers between devices, exchange(): lax.all_to_all(array, ('lat', 'lon'), split_axis=0, concat_axis=0, tiled=...  19.6 us
    ppermute x6, starting transfers between devices, shifted(): return lax.ppermute(array, 'lat', rows)  16.3 us
    ppermute x6, waiting for transfers between devices, shifted(): return lax.ppermute(array, 'lat', rows)  6.56 us
    ppermute x4, starting transfers between devices, shifted(): lax.ppermute(array, 'lon', [(j, (j + lon_by) % lon) for j in range(lon)])  6.13 us
    ppermute x4, waiting for transfers between devices, shifted(): lax.ppermute(array, 'lon', [(j, (j + lon_by) % lon) for j in range(lon)])  5.1 us
  transfers between devices with their start and end apart: 13, of which 6 were waited for; matrix products, arithmetic and copies ran while one was open for 0% of the time, Pallas kernels for 33%

profile of v4, /device:TPU:1, one launch (start us, length us, event | category | flops | bytes accessed | tf_op | source)
XLA Modules:
  0.0 176.5 jit_solution(7200318881835726554)
XLA Ops:
  0.6 6.3 %edges.1 = (f32[14,72,128]{2,1,0:T(8,128)}, f32[12,72,128]{2,1,0:T(8,128)}, f32[3,72,128]{2,1,0:T(8,128)}, f32[3,72,128]{2,1,0:T(8,128)}) custom-call(s32[1]{0:T(128)} %bitcast.1.last_ref, f32[3,72,8,128]{3,2,1,0:T(8,128)} %initial_ref.2, f32[2,72,8,128]{3,2,1,0:T(8,128)} %east_ref.2, f32[2,72,8,128]{3,2,1,0:T(8,128)} %north_ref.2, f32[2,72,8,128]{3,2,1,0:T(8,128)} %mixing_ref.2), custom_call_target="tpu_custom_call" | custom-call | flops 5000000 | bytes 6000000 | tf_op jit(solution)/shard_map/edges/pallas_call | solution.py:330
  6.9 4.4 %collective-permute-start = (f32[14,72,128]{2,1,0:T(8,128)}, f32[14,72,128]{2,1,0:T(8,128)S(1)}, u32[]{:S(2)}, u32[]{:S(2)}) collective-permute-start(f32[14,72,128]{2,1,0:T(8,128)} %get-tuple-element.62), channel_id=1, source_target_pairs={{0,16},{16,32},{32,48},{48,64},{64,80},{80,96},{96,112},{1,17},{17... | collective-permute-start | bytes 1548296 | tf_op jit(solution)/shard_map/ppermute | solution.py:349
  11.3 1.3 collective-permute-start.1
  12.6 1.0 collective-permute-start.3
  13.6 2.7 %collective-permute-start.2 = (f32[3,72,128]{2,1,0:T(8,128)}, f32[3,72,128]{2,1,0:T(8,128)S(1)}, u32[]{:S(2)}, u32[]{:S(2)}) collective-permute-start(f32[3,72,128]{2,1,0:T(8,128)} %get-tuple-element.64.own_east.wind_east), channel_id=1, source_target_pairs={{0,1},{1,2},{2,3},{3,4},{4,5},{5,6},{6,7},{7,8},{8,9},{9,10},{10,1... | collective-permute-start | bytes 331784 | tf_op jit(solution)/shard_map/ppermute | solution.py:346
  16.3 10.0 %pack_first.1 = (bf16[128,80,128]{2,1,0:T(8,128)(2,1)}, f32[128,128]{1,0:T(8,128)}, f32[128,128]{1,0:T(8,128)}, s32[128]{0:T(128)}, s32[128]{0:T(128)}) custom-call(s32[128]{0:T(128)} %bitcast.10, s32[128]{0:T(128)} %counts_ref, bf16[128,72,128]{2,1,0:T(8,128)(2,1)} %kernel_ref.3, s32[128,128]{1,0:T(8,128)} %columns_ref.3, bf16[128,128]{1,0:T(8,128)(2,1)} %observed_ref.3, ...), custom_call_target="tpu_custom_call" | custom-call | flops 5000000 | bytes 6000000 | tf_op jit(solution)/shard_map/pack_first/pallas_call | solution.py:330
  26.3 0.0 collective-permute-done.3.from_east
  26.4 0.0 copy-start.4
  26.4 0.0 collective-permute-done.2.from_west
  26.4 0.0 copy-start.5
  26.4 0.0 collective-permute-done.1.down_ref.wind_down
  26.4 0.0 copy-start.2
  26.4 0.0 collective-permute-done.up_ref.wind_up
  26.4 0.8 copy-done.2
  27.2 0.8 copy-done.1
  28.0 12.0 %all-to-all-start.1 = ((bf16[128,80,128]{2,1,0:T(8,128)(2,1)}), bf16[128,80,128]{2,1,0:T(8,128)(2,1)S(1)}, u32[]{:S(2)}, u32[]{:S(2)}) async-start(bf16[128,80,128]{2,1,0:T(8,128)(2,1)} %get-tuple-element.91), calls=%async_computation.1 | async-start | bytes 5242880 | tf_op jit(solution)/shard_map/all_to_all | solution.py:695
  40.0 0.0 copy-done.4
  40.0 0.0 copy-done.5
  40.1 1.7 corners.1
  41.8 1.3 collective-permute-start.5
  43.1 4.0 %collective-permute-start.4 = (f32[72,128]{1,0:T(8,128)}, f32[72,128]{1,0:T(8,128)S(1)}, u32[]{:S(2)}, u32[]{:S(2)}) collective-permute-start(f32[72,128]{1,0:T(8,128)} %get-tuple-element.68), channel_id=1, source_target_pairs={{0,16},{16,32},{32,48},{48,64},{64,80},{80,96},{96,112},{1,17},{17... | collective-permute-start | bytes 110600 | tf_op jit(solution)/shard_map/ppermute | solution.py:349
  47.1 7.3 %pack_second.1 = bf16[128,80,128]{2,1,0:T(8,128)(2,1)} custom-call(s32[128]{0:T(128)} %get-tuple-element.58.source_ref.second_ref, bf16[128,72,128]{2,1,0:T(8,128)(2,1)} %kernel_ref.3, s32[128,128]{1,0:T(8,128)} %columns_ref.3, bf16[128,128]{1,0:T(8,128)(2,1)} %observed_ref.3, bf16[128,128]{1,0:T(8,128)(2,1)} %weight_ref.3, ...), custom_call_target="tpu_custom_call" | custom-call | flops 5000000 | bytes 6000000 | tf_op jit(solution)/shard_map/pack_second/pallas_call | solution.py:330
  54.5 4.6 %arrange.1 = (f32[3,8,72,128]{3,2,1,0:T(8,128)}, f32[2,8,72,128]{3,2,1,0:T(8,128)}, f32[2,8,72,128]{3,2,1,0:T(8,128)}, f32[2,8,72,128]{3,2,1,0:T(8,128)}) custom-call(s32[1]{0:T(128)} %bitcast.1.last_ref, f32[3,72,8,128]{3,2,1,0:T(8,128)} %initial_ref.2, f32[2,72,8,128]{3,2,1,0:T(8,128)} %east_ref.2, f32[2,72,8,128]{3,2,1,0:T(8,128)} %north_ref.2, ...), custom_call_target="tpu_custom_call" | custom-call | flops 5000000 | bytes 6000000 | tf_op jit(solution)/shard_map/arrange/pallas_call | solution.py:330
  59.1 6.5 %collective-permute-done.5.north = f32[72,128]{1,0:T(8,128)S(1)} collective-permute-done((f32[72,128]{1,0:T(8,128)}, f32[72,128]{1,0:T(8,128)S(1)}, u32[]{:S(2)}, u32[]{:S(2)}) %collective-permute-start.5) | collective-permute-done | bytes 36896 | tf_op jit(solution)/shard_map/ppermute | solution.py:349
  65.6 0.0 collective-permute-done.4.south
  65.6 10.0 %all-to-all-done.1.block_ref = bf16[128,80,128]{2,1,0:T(8,128)(2,1)S(1)} async-done(((bf16[128,80,128]{2,1,0:T(8,128)(2,1)}), bf16[128,80,128]{2,1,0:T(8,128)(2,1)S(1)}, u32[]{:S(2)}, u32[]{:S(2)}) %all-to-all-start.1) | async-done | bytes 2621472 | tf_op jit(solution)/shard_map/all_to_all | solution.py:695
  75.6 0.0 copy-done.10
  75.6 6.1 %all-to-all-start = ((bf16[128,80,128]{2,1,0:T(8,128)(2,1)}), bf16[128,80,128]{2,1,0:T(8,128)(2,1)}, u32[]{:S(2)}, u32[]{:S(2)}) async-start(bf16[128,80,128]{2,1,0:T(8,128)(2,1)} %pack_second.1), calls=%async_computation | async-start | bytes 5242880 | tf_op jit(solution)/shard_map/all_to_all | solution.py:695
  81.7 6.5 %forward.1 = (bf16[864,512]{1,0:T(8,128)(2,1)}, f32[2,2,72,128]{3,2,1,0:T(8,128)}) custom-call(f32[3,8,72,128]{3,2,1,0:T(8,128)} %get-tuple-element.79.state_ref, f32[2,8,72,128]{3,2,1,0:T(8,128)} %get-tuple-element.80.east_ref, f32[2,8,72,128]{3,2,1,0:T(8,128)} %get-tuple-element.81.north_ref, f32[2,8,72,128]{3,2,1,0:T(8,128)} %get-tuple-element.82.mixing_ref, ...), custom_call_target="tpu_custom_call" | custom-call | flops 5000000 | bytes 6000000 | tf_op jit(solution)/shard_map/forward/pallas_call | solution.py:330
  88.3 21.8 %first_soundings.1 = (f32[864,256]{1,0:T(8,128)}, f32[128,128]{1,0:T(8,128)}) custom-call(bf16[864,512]{1,0:T(8,128)(2,1)} %get-tuple-element.89.field_ref, bf16[128,80,128]{2,1,0:T(8,128)(2,1)} %copy-done), custom_call_target="tpu_custom_call" | custom-call | flops 15000000512 | bytes 6000000 | tf_op jit(solution)/shard_map/first_soundings/pallas_call | solution.py:330
  110.1 6.9 %all-to-all-done.block_ref = bf16[128,80,128]{2,1,0:T(8,128)(2,1)} async-done(((bf16[128,80,128]{2,1,0:T(8,128)(2,1)}), bf16[128,80,128]{2,1,0:T(8,128)(2,1)}, u32[]{:S(2)}, u32[]{:S(2)}) %all-to-all-start) | async-done | bytes 2621472 | tf_op jit(solution)/shard_map/all_to_all | solution.py:695
  117.0 15.6 %second_soundings.1 = (f32[864,256]{1,0:T(8,128)}, f32[256,128]{1,0:T(8,128)}, f32[6,72,128]{2,1,0:T(8,128)}, f32[6,72,128]{2,1,0:T(8,128)}, f32[72,128]{1,0:T(8,128)}, /*index=5*/f32[72,128]{1,0:T(8,128)}) custom-call(bf16[864,512]{1,0:T(8,128)(2,1)} %get-tuple-element.89.field_ref, bf16[128,80,128]{2,1,0:T(8,128)(2,1)} %all-to-all-done.block_ref, ...), custom_call_target="tpu_custom_call" | custom-call | flops 15000000512 | bytes 6000000 | tf_op jit(solution)/shard_map/second_soundings/pallas_call | solution.py:330
  132.5 2.4 %collective-permute-start.6 = (f32[72,128]{1,0:T(8,128)}, f32[72,128]{1,0:T(8,128)S(1)}, u32[]{:S(2)}, u32[]{:S(2)}) collective-permute-start(f32[72,128]{1,0:T(8,128)} %get-tuple-element.97.own_east), channel_id=1, source_target_pairs={{0,1},{1,2},{2,3},{3,4},{4,5},{5,6},{6,7},{7,8},{8,9},{9,10},{10,1... | collective-permute-start | bytes 110600 | tf_op jit(solution)/shard_map/ppermute | solution.py:346
  134.9 0.0 collective-permute-start.7
  134.9 1.4 collective-permute-done.6.from_west
  136.3 3.7 %collective-permute-done.7.from_east = f32[72,128]{1,0:T(8,128)S(1)} collective-permute-done((f32[72,128]{1,0:T(8,128)}, f32[72,128]{1,0:T(8,128)S(1)}, u32[]{:S(2)}, u32[]{:S(2)}) %collective-permute-start.7) | collective-permute-done | bytes 36896 | tf_op jit(solution)/shard_map/ppermute | solution.py:346
  140.0 1.1 pad_maximum_fusion
  141.1 1.3 collective-permute-start.9
  142.4 4.0 %collective-permute-start.8 = (f32[8,72,128]{2,1,0:T(8,128)S(1)}, f32[8,72,128]{2,1,0:T(8,128)S(1)}, u32[]{:S(2)}, u32[]{:S(2)}) collective-permute-start(f32[8,72,128]{2,1,0:T(8,128)S(1)} %get-tuple-element.105), channel_id=1, source_target_pairs={{0,16},{16,32},{32,48},{48,64},{64,80},{80,96},{96,112},{1,17},{17... | collective-permute-start | bytes 884744 | tf_op jit(solution)/shard_map/ppermute | solution.py:349
  146.4 17.4 %all-to-all-start.2 = ((f32[128,2,128]{2,1,0:T(2,128)}), f32[128,2,128]{2,1,0:T(2,128)S(1)}, u32[]{:S(2)}, u32[]{:S(2)}) async-start(f32[128,2,128]{2,1,0:T(2,128)} %bitcast.9), calls=%async_computation.2 | async-start | bytes 262144 | tf_op jit(solution)/shard_map/all_to_all | solution.py:695
  163.8 0.0 collective-permute-done.9.down_ref
  163.9 0.0 collective-permute-done.8.up_ref
  163.9 0.7 copy-done.6
  164.6 0.1 copy-done.7
  164.7 6.4 %adjoint.1 = f32[3,72,8,128]{3,2,1,0:T(8,128)} custom-call(f32[864,256]{1,0:T(8,128)} %get-tuple-element.95.adjoint_ref, f32[2,8,72,128]{3,2,1,0:T(8,128)} %get-tuple-element.80.east_ref, f32[2,8,72,128]{3,2,1,0:T(8,128)} %get-tuple-element.81.north_ref, f32[2,8,72,128]{3,2,1,0:T(8,128)} %get-tuple-element.82.mixing_ref, f32[14,72,128]{2,1,0:T(8,128)} %copy-done.1, ...), custom_call_target="tpu_custom_call" | custom-call | flops 5000000 | bytes 6000000 | tf_op jit(solution)/shard_map/adjoint/pallas_call | solution.py:330
  171.0 2.8 %all-to-all-done.2 = f32[128,2,128]{2,1,0:T(2,128)S(1)} async-done(((f32[128,2,128]{2,1,0:T(2,128)}), f32[128,2,128]{2,1,0:T(2,128)S(1)}, u32[]{:S(2)}, u32[]{:S(2)}) %all-to-all-start.2) | async-done | bytes 131104 | tf_op jit(solution)/shard_map/all_to_all | solution.py:695
  173.8 0.6 copy-done.3
  174.4 2.1 %innovations.1 = f32[128,128]{1,0:T(8,128)} custom-call(s32[128]{0:T(128)} %get-tuple-element.102.first_ref, s32[128]{0:T(128)} %get-tuple-element.58.source_ref.second_ref, f32[256,128]{1,0:T(8,128)} %bitcast.6, f32[128,128]{1,0:T(8,128)} %get-tuple-element.59.place_ref), custom_call_target="tpu_custom_call" | custom-call | flops 5000000 | bytes 6000000 | tf_op jit(solution)/shard_map/innovations/pallas_call | solution.py:330
  (13 shorter events, 0.0 us)
Async XLA Ops:
  6.9 19.5 %collective-permute-start = (f32[14,72,128]{2,1,0:T(8,128)}, f32[14,72,128]{2,1,0:T(8,128)S(1)}, u32[]{:S(2)}, u32[]{:S(2)}) collective-permute-start(f32[14,72,128]{2,1,0:T(8,128)} %get-tuple-element.62), channel_id=1, source_target_pairs={{0,16},{16,32},{32,48},{48,64},{64,80},{80,96},{96,112},{1,17},{17... | collective-permute-start | bytes 1548296 | tf_op jit(solution)/shard_map/ppermute | solution.py:349
  11.3 15.1 %collective-permute-start.1 = (f32[12,72,128]{2,1,0:T(8,128)}, f32[12,72,128]{2,1,0:T(8,128)S(1)}, u32[]{:S(2)}, u32[]{:S(2)}) collective-permute-start(f32[12,72,128]{2,1,0:T(8,128)} %get-tuple-element.63), channel_id=1, source_target_pairs={{16,0},{32,16},{48,32},{64,48},{80,64},{96,80},{112,96},{17,1},{33... | collective-permute-start | bytes 1327112 | tf_op jit(solution)/shard_map/ppermute | solution.py:349
  12.6 13.7 %collective-permute-start.3 = (f32[3,72,128]{2,1,0:T(8,128)}, f32[3,72,128]{2,1,0:T(8,128)S(1)}, u32[]{:S(2)}, u32[]{:S(2)}) collective-permute-start(f32[3,72,128]{2,1,0:T(8,128)} %get-tuple-element.65.own_west), channel_id=1, source_target_pairs={{0,15},{1,0},{2,1},{3,2},{4,3},{5,4},{6,5},{7,6},{8,7},{9,8},{10,9... | collective-permute-start | bytes 331784 | tf_op jit(solution)/shard_map/ppermute | solution.py:346
  13.6 12.7 %collective-permute-start.2 = (f32[3,72,128]{2,1,0:T(8,128)}, f32[3,72,128]{2,1,0:T(8,128)S(1)}, u32[]{:S(2)}, u32[]{:S(2)}) collective-permute-start(f32[3,72,128]{2,1,0:T(8,128)} %get-tuple-element.64.own_east.wind_east), channel_id=1, source_target_pairs={{0,1},{1,2},{2,3},{3,4},{4,5},{5,6},{6,7},{7,8},{8,9},{9,10},{10,1... | collective-permute-start | bytes 331784 | tf_op jit(solution)/shard_map/ppermute | solution.py:346
  26.4 13.7 %copy-start.4 = (f32[3,72,128]{2,1,0:T(8,128)}, f32[3,72,128]{2,1,0:T(8,128)S(1)}, u32[]{:S(2)}) copy-start(f32[3,72,128]{2,1,0:T(8,128)S(1)} %collective-permute-done.3.from_east) | copy-start | bytes 331780
  26.4 13.7 %copy-start.5 = (f32[3,72,128]{2,1,0:T(8,128)}, f32[3,72,128]{2,1,0:T(8,128)S(1)}, u32[]{:S(2)}) copy-start(f32[3,72,128]{2,1,0:T(8,128)S(1)} %collective-permute-done.2.from_west) | copy-start | bytes 331780
  26.4 0.8 copy-start.2
  27.2 0.8 copy-start.1
  28.0 47.6 %all-to-all-start.1 = ((bf16[128,80,128]{2,1,0:T(8,128)(2,1)}), bf16[128,80,128]{2,1,0:T(8,128)(2,1)S(1)}, u32[]{:S(2)}, u32[]{:S(2)}) async-start(bf16[128,80,128]{2,1,0:T(8,128)(2,1)} %get-tuple-element.91), calls=%async_computation.1 | async-start | bytes 5242880 | tf_op jit(solution)/shard_map/all_to_all | solution.py:695
  41.8 23.8 %collective-permute-start.5 = (f32[72,128]{1,0:T(8,128)}, f32[72,128]{1,0:T(8,128)S(1)}, u32[]{:S(2)}, u32[]{:S(2)}) collective-permute-start(f32[72,128]{1,0:T(8,128)} %get-tuple-element.69), channel_id=1, source_target_pairs={{16,0},{32,16},{48,32},{64,48},{80,64},{96,80},{112,96},{17,1},{33... | collective-permute-start | bytes 110600 | tf_op jit(solution)/shard_map/ppermute | solution.py:349
  43.1 22.5 %collective-permute-start.4 = (f32[72,128]{1,0:T(8,128)}, f32[72,128]{1,0:T(8,128)S(1)}, u32[]{:S(2)}, u32[]{:S(2)}) collective-permute-start(f32[72,128]{1,0:T(8,128)} %get-tuple-element.68), channel_id=1, source_target_pairs={{0,16},{16,32},{32,48},{48,64},{64,80},{80,96},{96,112},{1,17},{17... | collective-permute-start | bytes 110600 | tf_op jit(solution)/shard_map/ppermute | solution.py:349
  65.6 10.0 %copy-start.10 = (f32[72,128]{1,0:T(8,128)}, f32[72,128]{1,0:T(8,128)S(1)}, u32[]{:S(2)}) copy-start(f32[72,128]{1,0:T(8,128)S(1)} %collective-permute-done.5.north) | copy-start | bytes 110596
  65.6 10.0 %copy-start.11 = (f32[72,128]{1,0:T(8,128)}, f32[72,128]{1,0:T(8,128)S(1)}, u32[]{:S(2)}) copy-start(f32[72,128]{1,0:T(8,128)S(1)} %collective-permute-done.4.south) | copy-start | bytes 110596
  75.6 12.7 %copy-start = (bf16[128,80,128]{2,1,0:T(8,128)(2,1)}, bf16[128,80,128]{2,1,0:T(8,128)(2,1)S(1)}, u32[]{:S(2)}) copy-start(bf16[128,80,128]{2,1,0:T(8,128)(2,1)S(1)} %all-to-all-done.1.block_ref) | copy-start | bytes 7864324
  75.6 41.4 %all-to-all-start = ((bf16[128,80,128]{2,1,0:T(8,128)(2,1)}), bf16[128,80,128]{2,1,0:T(8,128)(2,1)}, u32[]{:S(2)}, u32[]{:S(2)}) async-start(bf16[128,80,128]{2,1,0:T(8,128)(2,1)} %pack_second.1), calls=%async_computation | async-start | bytes 5242880 | tf_op jit(solution)/shard_map/all_to_all | solution.py:695
  132.5 3.8 %collective-permute-start.6 = (f32[72,128]{1,0:T(8,128)}, f32[72,128]{1,0:T(8,128)S(1)}, u32[]{:S(2)}, u32[]{:S(2)}) collective-permute-start(f32[72,128]{1,0:T(8,128)} %get-tuple-element.97.own_east), channel_id=1, source_target_pairs={{0,1},{1,2},{2,3},{3,4},{4,5},{5,6},{6,7},{7,8},{8,9},{9,10},{10,1... | collective-permute-start | bytes 110600 | tf_op jit(solution)/shard_map/ppermute | solution.py:346
  134.9 5.1 %collective-permute-start.7 = (f32[72,128]{1,0:T(8,128)}, f32[72,128]{1,0:T(8,128)S(1)}, u32[]{:S(2)}, u32[]{:S(2)}) collective-permute-start(f32[72,128]{1,0:T(8,128)} %get-tuple-element.98.own_west), channel_id=1, source_target_pairs={{0,15},{1,0},{2,1},{3,2},{4,3},{5,4},{6,5},{7,6},{8,7},{9,8},{10,9... | collective-permute-start | bytes 110600 | tf_op jit(solution)/shard_map/ppermute | solution.py:346
  136.3 27.6 %copy-start.8 = (f32[72,128]{1,0:T(8,128)}, f32[72,128]{1,0:T(8,128)S(1)}, u32[]{:S(2)}) copy-start(f32[72,128]{1,0:T(8,128)S(1)} %collective-permute-done.6.from_west) | copy-start | bytes 110596
  140.0 23.9 %copy-start.9 = (f32[72,128]{1,0:T(8,128)}, f32[72,128]{1,0:T(8,128)S(1)}, u32[]{:S(2)}) copy-start(f32[72,128]{1,0:T(8,128)S(1)} %collective-permute-done.7.from_east) | copy-start | bytes 110596
  141.1 22.7 %collective-permute-start.9 = (f32[8,72,128]{2,1,0:T(8,128)S(1)}, f32[8,72,128]{2,1,0:T(8,128)S(1)}, u32[]{:S(2)}, u32[]{:S(2)}) collective-permute-start(f32[8,72,128]{2,1,0:T(8,128)S(1)} %get-tuple-element.104), channel_id=1, source_target_pairs={{16,0},{32,16},{48,32},{64,48},{80,64},{96,80},{112,96},{17,1},{33... | collective-permute-start | bytes 884744 | tf_op jit(solution)/shard_map/ppermute | solution.py:349
  142.4 21.4 %collective-permute-start.8 = (f32[8,72,128]{2,1,0:T(8,128)S(1)}, f32[8,72,128]{2,1,0:T(8,128)S(1)}, u32[]{:S(2)}, u32[]{:S(2)}) collective-permute-start(f32[8,72,128]{2,1,0:T(8,128)S(1)} %get-tuple-element.105), channel_id=1, source_target_pairs={{0,16},{16,32},{32,48},{48,64},{64,80},{80,96},{96,112},{1,17},{17... | collective-permute-start | bytes 884744 | tf_op jit(solution)/shard_map/ppermute | solution.py:349
  146.4 27.4 %all-to-all-start.2 = ((f32[128,2,128]{2,1,0:T(2,128)}), f32[128,2,128]{2,1,0:T(2,128)S(1)}, u32[]{:S(2)}, u32[]{:S(2)}) async-start(f32[128,2,128]{2,1,0:T(2,128)} %bitcast.9), calls=%async_computation.2 | async-start | bytes 262144 | tf_op jit(solution)/shard_map/all_to_all | solution.py:695
  163.9 0.7 copy-start.6
  163.9 0.8 copy-start.7
  173.8 0.6 copy-start.3

commit v5 on v4

--- a/solution.py
+++ b/solution.py
@@ -276,9 +276,9 @@
             both = jnp.concatenate(slabs, axis=0)
             high = both.astype(jnp.bfloat16)
             low = (both - high.astype(jnp.float32)).astype(jnp.bfloat16)
-            rows = slice(i * PAIR, (i + 1) * PAIR)
-            field_ref[rows, low_row * LANES : (low_row + 1) * LANES] = high
-            field_ref[rows, (2 + low_row) * LANES : (3 + low_row) * LANES] = low
+            lanes = slice(low_row * LANES, (low_row + 1) * LANES)
+            field_ref[2 * i * PAIR : (2 * i + 1) * PAIR, lanes] = high
+            field_ref[(2 * i + 1) * PAIR : (2 * i + 2) * PAIR, lanes] = low
 
 
 def cell_slab(ref, t, row):
@@ -531,7 +531,7 @@
         block_ref.shape[0],
         merge,
         ((jnp.int32(0),) * GROUPS, (empty,) * GROUPS),
-        unroll=4,
+        unroll=8,
     )
     for g in range(GROUPS):
         tile, at = lax.shift_right_logical(ends[g], 7), ends[g] & (LANES - 1)
@@ -549,62 +549,54 @@
             cell_ref[...] == jnp.broadcast_to(cell[:, i * LANES : (i + 1) * LANES], (256, LANES))
             for i in range(WIDTH)
         ]
-        return g, step, profile, part - 1.0, observed, weight, hits
-
-    def gather(g, step, profile, part, observed, weight, hits):
         pick = jnp.concatenate([jnp.where(hit, one, nil) for hit in hits], axis=1)
-        pick_twice = jnp.concatenate([pick, pick], axis=0)
+        return g, step, profile, part - 1.0, observed, weight, pick
+
+    def gather(g, step, profile, part, observed, weight, pick):
         column = jnp.zeros((LEVELS, n), jnp.float32)
         for i in range(g * GROUP_PARTS // 2, (g + 1) * GROUP_PARTS // 2):
             found = jnp.dot(
-                field_ref[i * PAIR : (i + 1) * PAIR, :],
-                pick_twice,
+                field_ref[2 * i * PAIR : 2 * (i + 1) * PAIR, :],
+                pick,
                 preferred_element_type=jnp.float32,
             )
+            found = found[:PAIR] + found[PAIR:]
             column = jnp.where(part == 2.0 * i, found[:LEVELS], column)
             column = jnp.where(part == 2.0 * i + 1.0, found[LEVELS:], column)
         return column
 
-    def force(column, g, step, profile, part, observed, weight, hits):
-        model = jnp.sum(profile.astype(jnp.float32) * column, axis=0, keepdims=True)
+    def force(column, g, step, profile, part, observed, weight, pick):
+        wide = profile.astype(jnp.float32)
+        model = jnp.sum(wide * column, axis=0, keepdims=True)
         misfit = model - observed
         for i in range(WIDTH):
             found_ref[g, step * WIDTH + i] = jnp.broadcast_to(
                 misfit[:, i * LANES : (i + 1) * LANES], (8, LANES)
             )
-        forcing = weight * misfit
-        high = forcing.astype(jnp.bfloat16)
-        low = (forcing - high.astype(jnp.float32)).astype(jnp.bfloat16)
-        return jnp.concatenate(
-            [
-                jnp.where(
-                    hits[i], jnp.broadcast_to(term[:, i * LANES : (i + 1) * LANES], (256, LANES)), nil
-                )
-                for term in (high, low)
-                for i in range(WIDTH)
-            ],
-            axis=1,
-        )
-
-    def scatter(spread, g, step, profile, part, observed, weight, hits):
-        twice = jnp.concatenate([profile, profile], axis=0)
+        vector = wide * (weight * misfit)
+        high = vector.astype(jnp.bfloat16)
+        return high, (vector - high.astype(jnp.float32)).astype(jnp.bfloat16)
+
+    def scatter(vector, g, step, profile, part, observed, weight, pick):
+        high, low = (jnp.concatenate([term, term], axis=0) for term in vector)
         second = lax.broadcasted_iota(jnp.int32, (PAIR, n), 0) >= LEVELS
         part_row = (part - jnp.where(second, 1.0, 0.0)).astype(jnp.bfloat16)
         for i in range(g * GROUP_PARTS // 2, (g + 1) * GROUP_PARTS // 2):
-            left = jnp.where(part_row == jnp.bfloat16(2 * i), twice, nil)
-            adjoint_ref[i * PAIR : (i + 1) * PAIR, :] += lax.dot_general(
-                jnp.concatenate([left, left], axis=1),
-                spread,
+            own = part_row == jnp.bfloat16(2 * i)
+            sums = lax.dot_general(
+                jnp.concatenate([jnp.where(own, high, nil), jnp.where(own, low, nil)], axis=0),
+                pick,
                 (((1,), (1,)), ((), ())),
                 preferred_element_type=jnp.float32,
             )
+            adjoint_ref[i * PAIR : (i + 1) * PAIR, :] += sums[:PAIR] + sums[PAIR:]
 
     def work(groups, step):
         loaded = [load(g, step) for g in groups]
         columns = [gather(*x) for x in loaded]
-        spreads = [force(column, *x) for x, column in zip(loaded, columns)]
-        for x, spread in zip(loaded, spreads):
-            scatter(spread, *x)
+        vectors = [force(column, *x) for x, column in zip(loaded, columns)]
+        for x, vector in zip(loaded, vectors):
+            scatter(vector, *x)
         return 0
 
     steps = [lax.shift_right_logical(ends[g] + n - 1, n.bit_length() - 1) for g in range(GROUPS)]
@@ -746,7 +738,7 @@
     field, wind_sides = whole(
         forward_body,
         [
-            jax.ShapeDtypeStruct((12 * LEVELS, 512), jnp.bfloat16),
+            jax.ShapeDtypeStruct((2 * PARTS * LEVELS, 256), jnp.bfloat16),
             jax.ShapeDtypeStruct((2, 2, LEVELS, LANES), jnp.float32),
         ],
         (state,) + fields + (east, west, from_south, from_north) + tuple(sides),

time: 177 us -> 172 us (0.972)
  starting transfers between devices: 58 us -> 52.5 us
  Pallas kernels: 82.3 us -> 79 us
  waiting for transfers between devices: 31.3 us -> 33.6 us
    all_to_all x3, starting transfers between devices: 35.6 us -> 30.1 us  [exchange(): lax.all_to_all(array, ('lat', 'lon'), split_axis=0, concat_axis=0, tiled=...]
    pallas_call x10, Pallas kernels: 82.3 us -> 79 us  [whole(): pl.pallas_call(body, grid=(1,), in_specs=[smem if i < scalars else vmem(a...]
    all_to_all x3, waiting for transfers between devices: 19.6 us -> 21.9 us  [exchange(): lax.all_to_all(array, ('lat', 'lon'), split_axis=0, concat_axis=0, tiled=...]
where the time goes in v5:
time: 172 us; the launch traced here: 170 us
  Pallas kernels  79 us (46%)
  starting transfers between devices  52.5 us (31%)
  waiting for transfers between devices  33.6 us (20%)
  local copies, waits for them, and re-layouts  3.01 us (2%)
    pallas_call x10, Pallas kernels, whole(): pl.pallas_call(body, grid=(1,), in_specs=[smem if i < scalars else vmem(a...  79 us
    all_to_all x3, starting transfers between devices, exchange(): lax.all_to_all(array, ('lat', 'lon'), split_axis=0, concat_axis=0, tiled=...  30.1 us
    all_to_all x3, waiting for transfers between devices, exchange(): lax.all_to_all(array, ('lat', 'lon'), split_axis=0, concat_axis=0, tiled=...  21.9 us
    ppermute x6, starting transfers between devices, shifted(): return lax.ppermute(array, 'lat', rows)  16.3 us
    ppermute x6, waiting for transfers between devices, shifted(): return lax.ppermute(array, 'lat', rows)  6.56 us
    ppermute x4, starting transfers between devices, shifted(): lax.ppermute(array, 'lon', [(j, (j + lon_by) % lon) for j in range(lon)])  6.13 us
    ppermute x4, waiting for transfers between devices, shifted(): lax.ppermute(array, 'lon', [(j, (j + lon_by) % lon) for j in range(lon)])  5.1 us
  transfers between devices with their start and end apart: 13, of which 6 were waited for; matrix products, arithmetic and copies ran while one was open for 0% of the time, Pallas kernels for 33%

profile of v5, /device:TPU:1, one launch (start us, length us, event | category | flops | bytes accessed | tf_op | source)
XLA Modules:
  0.0 170.1 jit_solution(6209596445161532093)
XLA Ops:
  0.6 6.3 %edges.1 = (f32[14,72,128]{2,1,0:T(8,128)}, f32[12,72,128]{2,1,0:T(8,128)}, f32[3,72,128]{2,1,0:T(8,128)}, f32[3,72,128]{2,1,0:T(8,128)}) custom-call(s32[1]{0:T(128)} %bitcast.1.last_ref, f32[3,72,8,128]{3,2,1,0:T(8,128)} %initial_ref.2, f32[2,72,8,128]{3,2,1,0:T(8,128)} %east_ref.2, f32[2,72,8,128]{3,2,1,0:T(8,128)} %north_ref.2, f32[2,72,8,128]{3,2,1,0:T(8,128)} %mixing_ref.2), custom_call_target="tpu_custom_call" | custom-call | flops 5000000 | bytes 6000000 | tf_op jit(solution)/shard_map/edges/pallas_call | solution.py:330
  6.9 4.4 %collective-permute-start = (f32[14,72,128]{2,1,0:T(8,128)}, f32[14,72,128]{2,1,0:T(8,128)S(1)}, u32[]{:S(2)}, u32[]{:S(2)}) collective-permute-start(f32[14,72,128]{2,1,0:T(8,128)} %get-tuple-element.62), channel_id=1, source_target_pairs={{0,16},{16,32},{32,48},{48,64},{64,80},{80,96},{96,112},{1,17},{17... | collective-permute-start | bytes 1548296 | tf_op jit(solution)/shard_map/ppermute | solution.py:349
  11.3 1.3 collective-permute-start.1
  12.6 1.0 collective-permute-start.3
  13.6 2.7 %collective-permute-start.2 = (f32[3,72,128]{2,1,0:T(8,128)}, f32[3,72,128]{2,1,0:T(8,128)S(1)}, u32[]{:S(2)}, u32[]{:S(2)}) collective-permute-start(f32[3,72,128]{2,1,0:T(8,128)} %get-tuple-element.64.own_east.wind_east), channel_id=1, source_target_pairs={{0,1},{1,2},{2,3},{3,4},{4,5},{5,6},{6,7},{7,8},{8,9},{9,10},{10,1... | collective-permute-start | bytes 331784 | tf_op jit(solution)/shard_map/ppermute | solution.py:346
  16.3 10.0 %pack_first.1 = (bf16[128,80,128]{2,1,0:T(8,128)(2,1)}, f32[128,128]{1,0:T(8,128)}, f32[128,128]{1,0:T(8,128)}, s32[128]{0:T(128)}, s32[128]{0:T(128)}) custom-call(s32[128]{0:T(128)} %bitcast.10, s32[128]{0:T(128)} %counts_ref, bf16[128,72,128]{2,1,0:T(8,128)(2,1)} %kernel_ref.3, s32[128,128]{1,0:T(8,128)} %columns_ref.3, bf16[128,128]{1,0:T(8,128)(2,1)} %observed_ref.3, ...), custom_call_target="tpu_custom_call" | custom-call | flops 5000000 | bytes 6000000 | tf_op jit(solution)/shard_map/pack_first/pallas_call | solution.py:330
  26.3 0.0 collective-permute-done.3.from_east
  26.4 0.0 copy-start.4
  26.4 0.0 collective-permute-done.2.from_west
  26.4 0.0 copy-start.5
  26.4 0.0 collective-permute-done.1.down_ref.wind_down
  26.4 0.0 copy-start.2
  26.4 0.0 collective-permute-done.up_ref.wind_up
  26.4 0.8 copy-done.2
  27.2 0.8 copy-done.1
  28.0 12.0 %all-to-all-start.1 = ((bf16[128,80,128]{2,1,0:T(8,128)(2,1)}), bf16[128,80,128]{2,1,0:T(8,128)(2,1)S(1)}, u32[]{:S(2)}, u32[]{:S(2)}) async-start(bf16[128,80,128]{2,1,0:T(8,128)(2,1)} %get-tuple-element.91), calls=%async_computation.1 | async-start | bytes 5242880 | tf_op jit(solution)/shard_map/all_to_all | solution.py:687
  40.0 0.0 copy-done.4
  40.1 1.7 %corners.1 = (f32[72,128]{1,0:T(8,128)}, f32[72,128]{1,0:T(8,128)}) custom-call(f32[3,72,128]{2,1,0:T(8,128)} %copy-done.5, f32[3,72,128]{2,1,0:T(8,128)} %copy-done.4), custom_call_target="tpu_custom_call" | custom-call | flops 5000000 | bytes 6000000 | tf_op jit(solution)/shard_map/corners/pallas_call | solution.py:330
  41.8 1.3 collective-permute-start.5
  43.1 4.0 %collective-permute-start.4 = (f32[72,128]{1,0:T(8,128)}, f32[72,128]{1,0:T(8,128)S(1)}, u32[]{:S(2)}, u32[]{:S(2)}) collective-permute-start(f32[72,128]{1,0:T(8,128)} %get-tuple-element.68), channel_id=1, source_target_pairs={{0,16},{16,32},{32,48},{48,64},{64,80},{80,96},{96,112},{1,17},{17... | collective-permute-start | bytes 110600 | tf_op jit(solution)/shard_map/ppermute | solution.py:349
  47.1 7.3 %pack_second.1 = bf16[128,80,128]{2,1,0:T(8,128)(2,1)} custom-call(s32[128]{0:T(128)} %get-tuple-element.58.source_ref.second_ref, bf16[128,72,128]{2,1,0:T(8,128)(2,1)} %kernel_ref.3, s32[128,128]{1,0:T(8,128)} %columns_ref.3, bf16[128,128]{1,0:T(8,128)(2,1)} %observed_ref.3, bf16[128,128]{1,0:T(8,128)(2,1)} %weight_ref.3, ...), custom_call_target="tpu_custom_call" | custom-call | flops 5000000 | bytes 6000000 | tf_op jit(solution)/shard_map/pack_second/pallas_call | solution.py:330
  54.5 4.6 %arrange.1 = (f32[3,8,72,128]{3,2,1,0:T(8,128)}, f32[2,8,72,128]{3,2,1,0:T(8,128)}, f32[2,8,72,128]{3,2,1,0:T(8,128)}, f32[2,8,72,128]{3,2,1,0:T(8,128)}) custom-call(s32[1]{0:T(128)} %bitcast.1.last_ref, f32[3,72,8,128]{3,2,1,0:T(8,128)} %initial_ref.2, f32[2,72,8,128]{3,2,1,0:T(8,128)} %east_ref.2, f32[2,72,8,128]{3,2,1,0:T(8,128)} %north_ref.2, ...), custom_call_target="tpu_custom_call" | custom-call | flops 5000000 | bytes 6000000 | tf_op jit(solution)/shard_map/arrange/pallas_call | solution.py:330
  59.1 6.5 %collective-permute-done.5.north = f32[72,128]{1,0:T(8,128)S(1)} collective-permute-done((f32[72,128]{1,0:T(8,128)}, f32[72,128]{1,0:T(8,128)S(1)}, u32[]{:S(2)}, u32[]{:S(2)}) %collective-permute-start.5) | collective-permute-done | bytes 36896 | tf_op jit(solution)/shard_map/ppermute | solution.py:349
  65.6 0.0 collective-permute-done.4.south
  65.6 10.0 %all-to-all-done.1.block_ref = bf16[128,80,128]{2,1,0:T(8,128)(2,1)S(1)} async-done(((bf16[128,80,128]{2,1,0:T(8,128)(2,1)}), bf16[128,80,128]{2,1,0:T(8,128)(2,1)S(1)}, u32[]{:S(2)}, u32[]{:S(2)}) %all-to-all-start.1) | async-done | bytes 2621472 | tf_op jit(solution)/shard_map/all_to_all | solution.py:687
  75.6 0.0 copy-done.11
  75.6 6.1 %all-to-all-start = ((bf16[128,80,128]{2,1,0:T(8,128)(2,1)}), bf16[128,80,128]{2,1,0:T(8,128)(2,1)}, u32[]{:S(2)}, u32[]{:S(2)}) async-start(bf16[128,80,128]{2,1,0:T(8,128)(2,1)} %pack_second.1), calls=%async_computation | async-start | bytes 5242880 | tf_op jit(solution)/shard_map/all_to_all | solution.py:687
  81.7 6.5 %forward.1 = (bf16[1728,256]{1,0:T(8,128)(2,1)}, f32[2,2,72,128]{3,2,1,0:T(8,128)}) custom-call(f32[3,8,72,128]{3,2,1,0:T(8,128)} %get-tuple-element.79.state_ref, f32[2,8,72,128]{3,2,1,0:T(8,128)} %get-tuple-element.80.east_ref, f32[2,8,72,128]{3,2,1,0:T(8,128)} %get-tuple-element.81.north_ref, f32[2,8,72,128]{3,2,1,0:T(8,128)} %get-tuple-element.82.mixing_ref, ...), custom_call_target="tpu_custom_call" | custom-call | flops 5000000 | bytes 6000000 | tf_op jit(solution)/shard_map/forward/pallas_call | solution.py:330
  88.3 19.5 %first_soundings.1 = (f32[864,256]{1,0:T(8,128)}, f32[128,128]{1,0:T(8,128)}) custom-call(bf16[1728,256]{1,0:T(8,128)(2,1)} %get-tuple-element.89.field_ref, bf16[128,80,128]{2,1,0:T(8,128)(2,1)} %copy-done), custom_call_target="tpu_custom_call" | custom-call | flops 15000000512 | bytes 6000000 | tf_op jit(solution)/shard_map/first_soundings/pallas_call | solution.py:330
  107.8 9.2 %all-to-all-done.block_ref = bf16[128,80,128]{2,1,0:T(8,128)(2,1)} async-done(((bf16[128,80,128]{2,1,0:T(8,128)(2,1)}), bf16[128,80,128]{2,1,0:T(8,128)(2,1)}, u32[]{:S(2)}, u32[]{:S(2)}) %all-to-all-start) | async-done | bytes 2621472 | tf_op jit(solution)/shard_map/all_to_all | solution.py:687
  117.0 14.6 %second_soundings.1 = (f32[864,256]{1,0:T(8,128)}, f32[256,128]{1,0:T(8,128)}, f32[6,72,128]{2,1,0:T(8,128)}, f32[6,72,128]{2,1,0:T(8,128)}, f32[72,128]{1,0:T(8,128)}, /*index=5*/f32[72,128]{1,0:T(8,128)}) custom-call(bf16[1728,256]{1,0:T(8,128)(2,1)} %get-tuple-element.89.field_ref, bf16[128,80,128]{2,1,0:T(8,128)(2,1)} %all-to-all-done.block_ref, ...), custom_call_target="tpu_custom_call" | custom-call | flops 15000000512 | bytes 6000000 | tf_op jit(solution)/shard_map/second_soundings/pallas_call | solution.py:330
  131.6 2.4 %collective-permute-start.6 = (f32[72,128]{1,0:T(8,128)}, f32[72,128]{1,0:T(8,128)S(1)}, u32[]{:S(2)}, u32[]{:S(2)}) collective-permute-start(f32[72,128]{1,0:T(8,128)} %get-tuple-element.97.own_east), channel_id=1, source_target_pairs={{0,1},{1,2},{2,3},{3,4},{4,5},{5,6},{6,7},{7,8},{8,9},{9,10},{10,1... | collective-permute-start | bytes 110600 | tf_op jit(solution)/shard_map/ppermute | solution.py:346
  134.0 0.0 collective-permute-start.7
  134.0 1.4 collective-permute-done.6.from_west
  135.4 3.7 %collective-permute-done.7.from_east = f32[72,128]{1,0:T(8,128)S(1)} collective-permute-done((f32[72,128]{1,0:T(8,128)}, f32[72,128]{1,0:T(8,128)S(1)}, u32[]{:S(2)}, u32[]{:S(2)}) %collective-permute-start.7) | collective-permute-done | bytes 36896 | tf_op jit(solution)/shard_map/ppermute | solution.py:346
  139.1 1.1 pad_maximum_fusion
  140.2 1.3 collective-permute-start.9
  141.5 4.0 %collective-permute-start.8 = (f32[8,72,128]{2,1,0:T(8,128)S(1)}, f32[8,72,128]{2,1,0:T(8,128)S(1)}, u32[]{:S(2)}, u32[]{:S(2)}) collective-permute-start(f32[8,72,128]{2,1,0:T(8,128)S(1)} %get-tuple-element.105), channel_id=1, source_target_pairs={{0,16},{16,32},{32,48},{48,64},{64,80},{80,96},{96,112},{1,17},{17... | collective-permute-start | bytes 884744 | tf_op jit(solution)/shard_map/ppermute | solution.py:349
  145.5 11.9 %all-to-all-start.2 = ((f32[128,2,128]{2,1,0:T(2,128)}), f32[128,2,128]{2,1,0:T(2,128)S(1)}, u32[]{:S(2)}, u32[]{:S(2)}) async-start(f32[128,2,128]{2,1,0:T(2,128)} %bitcast.9), calls=%async_computation.2 | async-start | bytes 262144 | tf_op jit(solution)/shard_map/all_to_all | solution.py:687
  157.4 0.0 collective-permute-done.9.down_ref
  157.4 0.0 copy-start.6
  157.4 0.0 collective-permute-done.8.up_ref
  157.5 0.7 copy-done.6
  158.1 0.1 copy-done.7
  158.2 6.4 %adjoint.1 = f32[3,72,8,128]{3,2,1,0:T(8,128)} custom-call(f32[864,256]{1,0:T(8,128)} %get-tuple-element.95.adjoint_ref, f32[2,8,72,128]{3,2,1,0:T(8,128)} %get-tuple-element.80.east_ref, f32[2,8,72,128]{3,2,1,0:T(8,128)} %get-tuple-element.81.north_ref, f32[2,8,72,128]{3,2,1,0:T(8,128)} %get-tuple-element.82.mixing_ref, f32[14,72,128]{2,1,0:T(8,128)} %copy-done.1, ...), custom_call_target="tpu_custom_call" | custom-call | flops 5000000 | bytes 6000000 | tf_op jit(solution)/shard_map/adjoint/pallas_call | solution.py:330
  164.6 2.8 %all-to-all-done.2 = f32[128,2,128]{2,1,0:T(2,128)S(1)} async-done(((f32[128,2,128]{2,1,0:T(2,128)}), f32[128,2,128]{2,1,0:T(2,128)S(1)}, u32[]{:S(2)}, u32[]{:S(2)}) %all-to-all-start.2) | async-done | bytes 131104 | tf_op jit(solution)/shard_map/all_to_all | solution.py:687
  167.4 0.6 copy-done.3
  168.0 2.1 %innovations.1 = f32[128,128]{1,0:T(8,128)} custom-call(s32[128]{0:T(128)} %get-tuple-element.102.first_ref, s32[128]{0:T(128)} %get-tuple-element.58.source_ref.second_ref, f32[256,128]{1,0:T(8,128)} %bitcast.6, f32[128,128]{1,0:T(8,128)} %get-tuple-element.59.place_ref), custom_call_target="tpu_custom_call" | custom-call | flops 5000000 | bytes 6000000 | tf_op jit(solution)/shard_map/innovations/pallas_call | solution.py:330
  (13 shorter events, 0.0 us)
Async XLA Ops:
  6.9 19.5 %collective-permute-start = (f32[14,72,128]{2,1,0:T(8,128)}, f32[14,72,128]{2,1,0:T(8,128)S(1)}, u32[]{:S(2)}, u32[]{:S(2)}) collective-permute-start(f32[14,72,128]{2,1,0:T(8,128)} %get-tuple-element.62), channel_id=1, source_target_pairs={{0,16},{16,32},{32,48},{48,64},{64,80},{80,96},{96,112},{1,17},{17... | collective-permute-start | bytes 1548296 | tf_op jit(solution)/shard_map/ppermute | solution.py:349
  11.3 15.1 %collective-permute-start.1 = (f32[12,72,128]{2,1,0:T(8,128)}, f32[12,72,128]{2,1,0:T(8,128)S(1)}, u32[]{:S(2)}, u32[]{:S(2)}) collective-permute-start(f32[12,72,128]{2,1,0:T(8,128)} %get-tuple-element.63), channel_id=1, source_target_pairs={{16,0},{32,16},{48,32},{64,48},{80,64},{96,80},{112,96},{17,1},{33... | collective-permute-start | bytes 1327112 | tf_op jit(solution)/shard_map/ppermute | solution.py:349
  12.6 13.7 %collective-permute-start.3 = (f32[3,72,128]{2,1,0:T(8,128)}, f32[3,72,128]{2,1,0:T(8,128)S(1)}, u32[]{:S(2)}, u32[]{:S(2)}) collective-permute-start(f32[3,72,128]{2,1,0:T(8,128)} %get-tuple-element.65.own_west), channel_id=1, source_target_pairs={{0,15},{1,0},{2,1},{3,2},{4,3},{5,4},{6,5},{7,6},{8,7},{9,8},{10,9... | collective-permute-start | bytes 331784 | tf_op jit(solution)/shard_map/ppermute | solution.py:346
  13.6 12.7 %collective-permute-start.2 = (f32[3,72,128]{2,1,0:T(8,128)}, f32[3,72,128]{2,1,0:T(8,128)S(1)}, u32[]{:S(2)}, u32[]{:S(2)}) collective-permute-start(f32[3,72,128]{2,1,0:T(8,128)} %get-tuple-element.64.own_east.wind_east), channel_id=1, source_target_pairs={{0,1},{1,2},{2,3},{3,4},{4,5},{5,6},{6,7},{7,8},{8,9},{9,10},{10,1... | collective-permute-start | bytes 331784 | tf_op jit(solution)/shard_map/ppermute | solution.py:346
  26.4 13.7 %copy-start.4 = (f32[3,72,128]{2,1,0:T(8,128)}, f32[3,72,128]{2,1,0:T(8,128)S(1)}, u32[]{:S(2)}) copy-start(f32[3,72,128]{2,1,0:T(8,128)S(1)} %collective-permute-done.3.from_east) | copy-start | bytes 331780
  26.4 13.7 %copy-start.5 = (f32[3,72,128]{2,1,0:T(8,128)}, f32[3,72,128]{2,1,0:T(8,128)S(1)}, u32[]{:S(2)}) copy-start(f32[3,72,128]{2,1,0:T(8,128)S(1)} %collective-permute-done.2.from_west) | copy-start | bytes 331780
  26.4 0.8 copy-start.2
  27.2 0.8 copy-start.1
  28.0 47.6 %all-to-all-start.1 = ((bf16[128,80,128]{2,1,0:T(8,128)(2,1)}), bf16[128,80,128]{2,1,0:T(8,128)(2,1)S(1)}, u32[]{:S(2)}, u32[]{:S(2)}) async-start(bf16[128,80,128]{2,1,0:T(8,128)(2,1)} %get-tuple-element.91), calls=%async_computation.1 | async-start | bytes 5242880 | tf_op jit(solution)/shard_map/all_to_all | solution.py:687
  41.8 23.8 %collective-permute-start.5 = (f32[72,128]{1,0:T(8,128)}, f32[72,128]{1,0:T(8,128)S(1)}, u32[]{:S(2)}, u32[]{:S(2)}) collective-permute-start(f32[72,128]{1,0:T(8,128)} %get-tuple-element.69), channel_id=1, source_target_pairs={{16,0},{32,16},{48,32},{64,48},{80,64},{96,80},{112,96},{17,1},{33... | collective-permute-start | bytes 110600 | tf_op jit(solution)/shard_map/ppermute | solution.py:349
  43.1 22.5 %collective-permute-start.4 = (f32[72,128]{1,0:T(8,128)}, f32[72,128]{1,0:T(8,128)S(1)}, u32[]{:S(2)}, u32[]{:S(2)}) collective-permute-start(f32[72,128]{1,0:T(8,128)} %get-tuple-element.68), channel_id=1, source_target_pairs={{0,16},{16,32},{32,48},{48,64},{64,80},{80,96},{96,112},{1,17},{17... | collective-permute-start | bytes 110600 | tf_op jit(solution)/shard_map/ppermute | solution.py:349
  65.6 10.0 %copy-start.10 = (f32[72,128]{1,0:T(8,128)}, f32[72,128]{1,0:T(8,128)S(1)}, u32[]{:S(2)}) copy-start(f32[72,128]{1,0:T(8,128)S(1)} %collective-permute-done.5.north) | copy-start | bytes 110596
  65.6 10.0 %copy-start.11 = (f32[72,128]{1,0:T(8,128)}, f32[72,128]{1,0:T(8,128)S(1)}, u32[]{:S(2)}) copy-start(f32[72,128]{1,0:T(8,128)S(1)} %collective-permute-done.4.south) | copy-start | bytes 110596
  75.6 12.7 %copy-start = (bf16[128,80,128]{2,1,0:T(8,128)(2,1)}, bf16[128,80,128]{2,1,0:T(8,128)(2,1)S(1)}, u32[]{:S(2)}) copy-start(bf16[128,80,128]{2,1,0:T(8,128)(2,1)S(1)} %all-to-all-done.1.block_ref) | copy-start | bytes 7864324
  75.6 41.4 %all-to-all-start = ((bf16[128,80,128]{2,1,0:T(8,128)(2,1)}), bf16[128,80,128]{2,1,0:T(8,128)(2,1)}, u32[]{:S(2)}, u32[]{:S(2)}) async-start(bf16[128,80,128]{2,1,0:T(8,128)(2,1)} %pack_second.1), calls=%async_computation | async-start | bytes 5242880 | tf_op jit(solution)/shard_map/all_to_all | solution.py:687
  131.6 3.8 %collective-permute-start.6 = (f32[72,128]{1,0:T(8,128)}, f32[72,128]{1,0:T(8,128)S(1)}, u32[]{:S(2)}, u32[]{:S(2)}) collective-permute-start(f32[72,128]{1,0:T(8,128)} %get-tuple-element.97.own_east), channel_id=1, source_target_pairs={{0,1},{1,2},{2,3},{3,4},{4,5},{5,6},{6,7},{7,8},{8,9},{9,10},{10,1... | collective-permute-start | bytes 110600 | tf_op jit(solution)/shard_map/ppermute | solution.py:346
  134.0 5.1 %collective-permute-start.7 = (f32[72,128]{1,0:T(8,128)}, f32[72,128]{1,0:T(8,128)S(1)}, u32[]{:S(2)}, u32[]{:S(2)}) collective-permute-start(f32[72,128]{1,0:T(8,128)} %get-tuple-element.98.own_west), channel_id=1, source_target_pairs={{0,15},{1,0},{2,1},{3,2},{4,3},{5,4},{6,5},{7,6},{8,7},{9,8},{10,9... | collective-permute-start | bytes 110600 | tf_op jit(solution)/shard_map/ppermute | solution.py:346
  135.4 22.1 %copy-start.8 = (f32[72,128]{1,0:T(8,128)}, f32[72,128]{1,0:T(8,128)S(1)}, u32[]{:S(2)}) copy-start(f32[72,128]{1,0:T(8,128)S(1)} %collective-permute-done.6.from_west) | copy-start | bytes 110596
  139.1 18.4 %copy-start.9 = (f32[72,128]{1,0:T(8,128)}, f32[72,128]{1,0:T(8,128)S(1)}, u32[]{:S(2)}) copy-start(f32[72,128]{1,0:T(8,128)S(1)} %collective-permute-done.7.from_east) | copy-start | bytes 110596
  140.2 17.2 %collective-permute-start.9 = (f32[8,72,128]{2,1,0:T(8,128)S(1)}, f32[8,72,128]{2,1,0:T(8,128)S(1)}, u32[]{:S(2)}, u32[]{:S(2)}) collective-permute-start(f32[8,72,128]{2,1,0:T(8,128)S(1)} %get-tuple-element.104), channel_id=1, source_target_pairs={{16,0},{32,16},{48,32},{64,48},{80,64},{96,80},{112,96},{17,1},{33... | collective-permute-start | bytes 884744 | tf_op jit(solution)/shard_map/ppermute | solution.py:349
  141.5 15.9 %collective-permute-start.8 = (f32[8,72,128]{2,1,0:T(8,128)S(1)}, f32[8,72,128]{2,1,0:T(8,128)S(1)}, u32[]{:S(2)}, u32[]{:S(2)}) collective-permute-start(f32[8,72,128]{2,1,0:T(8,128)S(1)} %get-tuple-element.105), channel_id=1, source_target_pairs={{0,16},{16,32},{32,48},{48,64},{64,80},{80,96},{96,112},{1,17},{17... | collective-permute-start | bytes 884744 | tf_op jit(solution)/shard_map/ppermute | solution.py:349
  145.5 21.9 %all-to-all-start.2 = ((f32[128,2,128]{2,1,0:T(2,128)}), f32[128,2,128]{2,1,0:T(2,128)S(1)}, u32[]{:S(2)}, u32[]{:S(2)}) async-start(f32[128,2,128]{2,1,0:T(2,128)} %bitcast.9), calls=%async_computation.2 | async-start | bytes 262144 | tf_op jit(solution)/shard_map/all_to_all | solution.py:687
  157.4 0.7 copy-start.6
  157.4 0.8 copy-start.7
  167.4 0.6 copy-start.3

commit v6 on v5

--- a/solution.py
+++ b/solution.py
@@ -45,16 +45,16 @@
     return t * 10 + row + 1
 
 
-def packed(slabs, lane, base=0):
+def packed(slabs, lane, base=0, first_row=0, rows=LAT_CELLS):
     out = jnp.zeros((LEVELS, LANES), jnp.float32)
     for i, slab in enumerate(slabs):
-        place = base + place_of(i // LAT_CELLS, i % LAT_CELLS)
+        place = base + place_of(i // rows, first_row + i % rows)
         out = jnp.where(lane_index() == place, rolled(slab, place - lane, 1), out)
     return out
 
 
 def packed_wind(slabs, lane, base):
-    one = packed(slabs, lane, base)
+    one = packed(slabs, lane, base, -1, LAT_CELLS + 2)
     return one + rolled(one, 10, 1) + rolled(one, 20, 1)
 
 
@@ -62,22 +62,10 @@
     return rolled(array, -SLOT * number, 1)
 
 
-def with_corners(own, south, north, number=0):
+def with_corners(own, south, north):
     row = (lane_index() & (SLOT - 1)) % 10
-    out = jnp.where(row == 0, rolled(south, number - LAT_CELLS, 1), own)
-    return jnp.where(row == 9, rolled(north, LAT_CELLS - number, 1), out)
-
-
-def corners_body(from_west, from_east, up_ref, down_ref):
-    row = (lane_index() & (SLOT - 1)) % 10
-    up = jnp.zeros((LEVELS, LANES), jnp.float32)
-    down = jnp.zeros((LEVELS, LANES), jnp.float32)
-    for i in range(6):
-        column = from_west[i] if i < 3 else from_east[i - 3]
-        up = up + rolled(jnp.where(row == LAT_CELLS, column, 0.0), -i, 1)
-        down = down + rolled(jnp.where(row == 1, column, 0.0), i, 1)
-    up_ref[...] = up
-    down_ref[...] = down
+    out = jnp.where(row == 0, rolled(south, -LAT_CELLS, 1), own)
+    return jnp.where(row == 9, rolled(north, LAT_CELLS, 1), out)
 
 
 def mixed(slab, coeff):
@@ -110,45 +98,30 @@
 
 
 def arrange_body(
-    last_ref, initial_ref, east_ref, north_ref, mixing_ref, state_ref, east_out, north_out, mixing_out
-):
+    last_ref, initial_ref, east_ref, north_ref, mixing_ref, up_ref, down_ref,
+    state_ref, east_out, north_out, mixing_out, east_edge, west_edge,
+):
+    slabs = []
     for t in range(TRACERS):
+        slabs.append(up_ref[2 * t + 1])
         for row in range(LAT_CELLS):
             state_ref[t, row] = initial_ref[t, :, row, :]
+            slabs.append(state_ref[t, row])
+        slabs.append(down_ref[2 * t])
+    rows = LAT_CELLS + 2
+    east_edge[0] = packed(slabs, LANES - 1, 0, -1, rows) + packed(slabs, LANES - 2, SLOT, -1, rows)
+    west_edge[0] = packed(slabs, 0, 0, -1, rows) + packed(slabs, 1, SLOT, -1, rows)
     for m in range(east_ref.shape[0]):
         for row in range(LAT_CELLS):
             east_out[m, row] = east_ref[m, :, row, :]
             north_out[m, row] = masked_north(last_ref, north_ref, m, row)
             mixing_out[m, row] = masked_mixing(mixing_ref, m, row)
 
-
-def masked_north(last_ref, north_ref, m, row):
-    north = north_ref[m, :, row, :]
-    if row == LAT_CELLS - 1:
-        north = jnp.where(last_ref[0] > 0, jnp.float32(0.0), north)
-    return north
-
-
-def masked_mixing(mixing_ref, m, row):
-    top = lax.broadcasted_iota(jnp.int32, (LEVELS, LANES), 0) == LEVELS - 1
-    return jnp.where(top, jnp.float32(0.0), mixing_ref[m, :, row, :])
-
-
-def edges_body(
-    last_ref, initial_ref, east_ref, north_ref, mixing_ref, up_ref, down_ref, east_edge, west_edge
-):
-    last = LAT_CELLS - 1
-    write_edges(
-        lambda t, row: initial_ref[t, :, row, :], up_ref, down_ref, east_edge.at[0], west_edge.at[0]
-    )
-    for m in range(east_ref.shape[0]):
-        east = [east_ref[m, :, row, :] for row in range(LAT_CELLS)]
-        north = [masked_north(last_ref, north_ref, m, row) for row in range(LAT_CELLS)]
-        mixing = [masked_mixing(mixing_ref, m, row) for row in range(LAT_CELLS)]
-        for i, slab in enumerate((east[last], mixing[last], north[last], north[last - 1])):
-            up_ref[6 + 4 * m + i] = slab
-        for i, slab in enumerate((east[0], mixing[0], north[0])):
-            down_ref[6 + 3 * m + i] = slab
+        def column(ref, number):
+            own = [ref[m, row] for row in range(LAT_CELLS)]
+            return [up_ref[6 + 4 * m + number]] + own + [down_ref[6 + 3 * m + number]]
+
+        east, mixing, north = column(east_out, 0), column(mixing_out, 1), column(north_out, 2)
         east_edge[1 + m] = (
             packed_wind(east, LANES - 1, 0)
             + packed_wind(mixing, LANES - 1, SLOT)
@@ -160,6 +133,34 @@
             + packed_wind(mixing, 0, SLOT)
             + packed_wind(north, 0, 2 * SLOT)
         )
+
+
+def masked_north(last_ref, north_ref, m, row):
+    north = north_ref[m, :, row, :]
+    if row == LAT_CELLS - 1:
+        north = jnp.where(last_ref[0] > 0, jnp.float32(0.0), north)
+    return north
+
+
+def masked_mixing(mixing_ref, m, row):
+    top = lax.broadcasted_iota(jnp.int32, (LEVELS, LANES), 0) == LEVELS - 1
+    return jnp.where(top, jnp.float32(0.0), mixing_ref[m, :, row, :])
+
+
+def rows_body(last_ref, initial_ref, east_ref, north_ref, mixing_ref, up_ref, down_ref):
+    last = LAT_CELLS - 1
+    for t in range(TRACERS):
+        for i in range(2):
+            up_ref[2 * t + i] = initial_ref[t, :, LAT_CELLS - 2 + i, :]
+            down_ref[2 * t + i] = initial_ref[t, :, i, :]
+    for m in range(east_ref.shape[0]):
+        up_ref[6 + 4 * m] = east_ref[m, :, last, :]
+        up_ref[7 + 4 * m] = masked_mixing(mixing_ref, m, last)
+        up_ref[8 + 4 * m] = masked_north(last_ref, north_ref, m, last)
+        up_ref[9 + 4 * m] = masked_north(last_ref, north_ref, m, last - 1)
+        down_ref[6 + 3 * m] = east_ref[m, :, 0, :]
+        down_ref[7 + 3 * m] = masked_mixing(mixing_ref, m, 0)
+        down_ref[8 + 3 * m] = masked_north(last_ref, north_ref, m, 0)
 
 
 def two_steps(
@@ -240,13 +241,8 @@
 
 def forward_body(
     state_ref, east_ref, north_ref, mixing_ref, own_east, own_west,
-    up_ref, down_ref, from_west, from_east, south, north,
-    field_ref, sides_ref, middle_ref, after_ref,
-):
-    for m in range(2):
-        sides_ref[m, 0] = with_corners(from_west[1 + m], south[...], north[...], 1 + m)
-        sides_ref[m, 1] = with_corners(from_east[1 + m], south[...], north[...], 4 + m)
-
+    up_ref, down_ref, from_west, from_east, field_ref, middle_ref, after_ref,
+):
     def write(t, row, slab):
         after_ref[t, row] = slab
 
@@ -258,13 +254,13 @@
         lambda i: up_ref[6 + i],
         lambda i: down_ref[6 + i],
         lambda m: own_east[1 + m],
-        lambda m: (sides_ref[m, 0], sides_ref[m, 1]),
+        lambda m: (from_west[1 + m], from_east[1 + m]),
         up_ref,
         down_ref,
         own_east[0],
         own_west[0],
-        with_corners(from_west[0], south[...], north[...], 0),
-        with_corners(from_east[0], south[...], north[...], 3),
+        from_west[0],
+        from_east[0],
         middle_ref,
         write,
     )
@@ -287,7 +283,7 @@
 
 
 def adjoint_body(
-    adjoint_ref, east_ref, north_ref, mixing_ref, wind_up, wind_down, wind_east, sides_ref,
+    adjoint_ref, east_ref, north_ref, mixing_ref, wind_up, wind_down, wind_east, side_west, side_east,
     own_east, own_west, from_west, from_east, up_ref, down_ref, gradient_ref, middle_ref,
 ):
     def write(t, row, slab):
@@ -301,7 +297,7 @@
         lambda i: wind_up[6 + i],
         lambda i: wind_down[6 + i],
         lambda m: wind_east[1 + m],
-        lambda m: (sides_ref[m, 0], sides_ref[m, 1]),
+        lambda m: (side_west[1 + m], side_east[1 + m]),
         up_ref,
         down_ref,
         own_east[...],
@@ -320,7 +316,7 @@
 MIDDLE = pltpu.VMEM((TRACERS, LAT_CELLS + 2, LEVELS, LANES), jnp.float32)
 
 
-def whole(body, outs, operands, name, scratch=(), scalars=0, flops=5000000, scalar_outs=0, vmem_mib=56):
+def whole(body, outs, operands, name, scratch=(), scalars=0, flops=5000000, scalar_outs=0, vmem_mib=63):
     smem = pl.BlockSpec(memory_space=pltpu.SMEM)
 
     def vmem(array):
@@ -693,14 +689,8 @@
         return jax.ShapeDtypeStruct((number, LEVELS, LANES), jnp.float32)
 
     grid = (is_last, initial, east_wind, north_wind, mixing)
-    up, down, east, west = whole(
-        edges_body,
-        [slabs_like(14), slabs_like(12), slabs_like(3), slabs_like(3)],
-        grid,
-        "edges",
-        scalars=1,
-    )
-    counts, up, down, east, west = lax.optimization_barrier((counts, up, down, east, west))
+    up, down = whole(rows_body, [slabs_like(14), slabs_like(12)], grid, "rows", scalars=1)
+    counts, up, down = lax.optimization_barrier((counts, up, down))
     from_south, from_north = shifted(up, 1, 0), shifted(down, -1, 0)
     slots = jax.ShapeDtypeStruct((device_count, ROWS, sounds), jnp.bfloat16)
     by_device = jax.ShapeDtypeStruct((device_count,), jnp.int32)
@@ -721,27 +711,25 @@
         pack, [slots], (source_second,) + heard + (place, tally), "pack_second", scratch=scratch,
         scalars=1,
     )
-    sides = (shifted(east, 0, 1), shifted(west, 0, -1))
-    out_first, from_south, from_north, *sides = lax.optimization_barrier(
-        (out_first, from_south, from_north, *sides)
+    out_first, from_south, from_north = lax.optimization_barrier(
+        (out_first, from_south, from_north)
     )
     got_first = exchange(out_first)
-    corner_up, corner_down = whole(corners_body, [COLUMN_EDGE] * 2, tuple(sides), "corners")
-    sides += [shifted(corner_up, 1, 0), shifted(corner_down, -1, 0)]
-    grid = lax.optimization_barrier((corner_up,) + grid)[1:]
-    arranged = whole(
-        arrange_body, [STATE, winds_like, winds_like, winds_like], grid, "arrange", scalars=1
-    )
-    out_second, *rest = lax.optimization_barrier((out_second, *sides, *arranged))
+    state, *rest = whole(
+        arrange_body,
+        [STATE, winds_like, winds_like, winds_like, slabs_like(3), slabs_like(3)],
+        grid + (from_south, from_north),
+        "arrange",
+        scalars=1,
+    )
+    fields, (east, west) = tuple(rest[:3]), rest[3:]
+    side_west, side_east = shifted(east, 0, 1), shifted(west, 0, -1)
+    out_second, side_west, side_east = lax.optimization_barrier((out_second, side_west, side_east))
     got_second = exchange(out_second)
-    sides, state, fields = rest[:4], rest[4], tuple(rest[5:])
-    field, wind_sides = whole(
+    (field,) = whole(
         forward_body,
-        [
-            jax.ShapeDtypeStruct((2 * PARTS * LEVELS, 256), jnp.bfloat16),
-            jax.ShapeDtypeStruct((2, 2, LEVELS, LANES), jnp.float32),
-        ],
-        (state,) + fields + (east, west, from_south, from_north) + tuple(sides),
+        [jax.ShapeDtypeStruct((2 * PARTS * LEVELS, 256), jnp.bfloat16)],
+        (state,) + fields + (east, west, from_south, from_north, side_west, side_east),
         "forward",
         scratch=[MIDDLE, pltpu.VMEM(STATE.shape, jnp.float32)],
     )
@@ -753,7 +741,7 @@
     (gradient,) = whole(
         adjoint_body,
         [jax.ShapeDtypeStruct(initial.shape, jnp.float32)],
-        (adjoint,) + fields + (from_south, from_north, east, wind_sides)
+        (adjoint,) + fields + (from_south, from_north, east, side_west, side_east)
         + (own_east, own_west, from_west, from_east)
         + (shifted(jnp.concatenate([up, ends]), 1, 0), shifted(jnp.concatenate([down, ends]), -1, 0)),
         "adjoint",

time: 172 us -> 167 us (0.971)
  starting transfers between devices: 52.5 us -> 49 us
  waiting for transfers between devices: 33.6 us -> 37 us
  Pallas kernels: 79 us -> 76.1 us
    ppermute x4, waiting for transfers between devices: 5.1 us -> 20.3 us  [shifted(): lax.ppermute(array, 'lon', [(j, (j + lon_by) % lon) for j in range(lon)])]
    all_to_all x3, waiting for transfers between devices: 21.9 us -> 14.9 us  [exchange(): lax.all_to_all(array, ('lat', 'lon'), split_axis=0, concat_axis=0, tiled=...]
    ppermute x6 -> x4, waiting for transfers between devices: 6.56 us -> 1.84 us  [shifted(): return lax.ppermute(array, 'lat', rows)]
    ppermute x6 -> x4, starting transfers between devices: 16.3 us -> 12.4 us  [shifted(): return lax.ppermute(array, 'lat', rows)]
    pallas_call x10 -> x9, Pallas kernels: 79 us -> 76.1 us  [whole(): pl.pallas_call(body, grid=(1,), in_specs=[smem if i < scalars else vmem(a...]
  transfers between devices with their start and end apart: 13 -> 11, of which waited for: 6 -> 7; matrix products, arithmetic and copies ran while one was open for 0% -> 0% of each run, Pallas kernels for 33% -> 34%
where the time goes in v6:
time: 167 us; the launch traced here: 166 us
  Pallas kernels  76.1 us (46%)
  starting transfers between devices  49 us (29%)
  waiting for transfers between devices  37 us (22%)
  local copies, waits for them, and re-layouts  2.44 us (1%)
    pallas_call x9, Pallas kernels, whole(): pl.pallas_call(body, grid=(1,), in_specs=[smem if i < scalars else vmem(a...  76.1 us
    all_to_all x3, starting transfers between devices, exchange(): lax.all_to_all(array, ('lat', 'lon'), split_axis=0, concat_axis=0, tiled=...  30.9 us
    ppermute x4, waiting for transfers between devices, shifted(): lax.ppermute(array, 'lon', [(j, (j + lon_by) % lon) for j in range(lon)])  20.3 us
    all_to_all x3, waiting for transfers between devices, exchange(): lax.all_to_all(array, ('lat', 'lon'), split_axis=0, concat_axis=0, tiled=...  14.9 us
    ppermute x4, starting transfers between devices, shifted(): return lax.ppermute(array, 'lat', rows)  12.4 us
    ppermute x4, starting transfers between devices, shifted(): lax.ppermute(array, 'lon', [(j, (j + lon_by) % lon) for j in range(lon)])  5.64 us
  transfers between devices with their start and end apart: 11, of which 7 were waited for; matrix products, arithmetic and copies ran while one was open for 0% of the time, Pallas kernels for 34%

profile of v6, /device:TPU:1, one launch (start us, length us, event | category | flops | bytes accessed | tf_op | source)
XLA Modules:
  0.0 166.4 jit_solution(4829600706245969662)
XLA Ops:
  0.6 3.1 %rows.1 = (f32[14,72,128]{2,1,0:T(8,128)}, f32[12,72,128]{2,1,0:T(8,128)}) custom-call(s32[1]{0:T(128)} %bitcast.last_ref, f32[3,72,8,128]{3,2,1,0:T(8,128)} %initial_ref.3, f32[2,72,8,128]{3,2,1,0:T(8,128)} %east_ref.3, f32[2,72,8,128]{3,2,1,0:T(8,128)} %north_ref.3, f32[2,72,8,128]{3,2,1,0:T(8,128)} %mixing_ref.3), custom_call_target="tpu_custom_call" | custom-call | flops 5000000 | bytes 6000000 | tf_op jit(solution)/shard_map/rows/pallas_call | solution.py:326
  3.8 4.4 %collective-permute-start = (f32[14,72,128]{2,1,0:T(8,128)}, f32[14,72,128]{2,1,0:T(8,128)S(1)}, u32[]{:S(2)}, u32[]{:S(2)}) collective-permute-start(f32[14,72,128]{2,1,0:T(8,128)} %get-tuple-element.38), channel_id=1, source_target_pairs={{0,16},{16,32},{32,48},{48,64},{64,80},{80,96},{96,112},{1,17},{17... | collective-permute-start | bytes 1548296 | tf_op jit(solution)/shard_map/ppermute | solution.py:345
  8.2 1.3 collective-permute-start.1
  9.5 10.0 %pack_first.1 = (bf16[128,80,128]{2,1,0:T(8,128)(2,1)}, f32[128,128]{1,0:T(8,128)}, f32[128,128]{1,0:T(8,128)}, s32[128]{0:T(128)}, s32[128]{0:T(128)}) custom-call(s32[128]{0:T(128)} %bitcast.10, s32[128]{0:T(128)} %counts_ref, bf16[128,72,128]{2,1,0:T(8,128)(2,1)} %kernel_ref.3, s32[128,128]{1,0:T(8,128)} %columns_ref.3, bf16[128,128]{1,0:T(8,128)(2,1)} %observed_ref.3, ...), custom_call_target="tpu_custom_call" | custom-call | flops 5000000 | bytes 6000000 | tf_op jit(solution)/shard_map/pack_first/pallas_call | solution.py:326
  19.5 1.8 %collective-permute-done.1.down_ref.wind_down = f32[12,72,128]{2,1,0:T(8,128)S(1)} collective-permute-done((f32[12,72,128]{2,1,0:T(8,128)}, f32[12,72,128]{2,1,0:T(8,128)S(1)}, u32[]{:S(2)}, u32[]{:S(2)}) %collective-permute-start.1) | collective-permute-done | bytes 442400 | tf_op jit(solution)/shard_map/ppermute | solution.py:345
  21.3 0.0 copy-start.1
  21.3 0.0 collective-permute-done.up_ref.wind_up
  21.3 0.0 copy-start
  21.3 0.8 copy-done.1
  22.1 0.2 copy-done
  22.3 12.4 %all-to-all-start.1 = ((bf16[128,80,128]{2,1,0:T(8,128)(2,1)}), bf16[128,80,128]{2,1,0:T(8,128)(2,1)}, u32[]{:S(2)}, u32[]{:S(2)}) async-start(bf16[128,80,128]{2,1,0:T(8,128)(2,1)} %get-tuple-element.54), calls=%async_computation.1 | async-start | bytes 5242880 | tf_op jit(solution)/shard_map/all_to_all | solution.py:683
  34.7 7.8 %arrange.1 = (f32[3,8,72,128]{3,2,1,0:T(8,128)}, f32[2,8,72,128]{3,2,1,0:T(8,128)}, f32[2,8,72,128]{3,2,1,0:T(8,128)}, f32[2,8,72,128]{3,2,1,0:T(8,128)}, f32[3,72,128]{2,1,0:T(8,128)}, /*index=5*/f32[3,72,128]{2,1,0:T(8,128)}) custom-call(s32[1]{0:T(128)} %bitcast.last_ref, f32[3,72,8,128]{3,2,1,0:T(8,128)} %initial_ref.3, f32[2,72,8,128]{3,2,1,0:T(8,128)} %east_ref.3, ...), custom_call_target="tpu_custom_call" | custom-call | flops 5000000 | bytes 6000000 | tf_op jit(solution)/shard_map/arrange/pallas_call | solution.py:326
  42.5 1.1 collective-permute-start.3
  43.6 2.1 %collective-permute-start.2 = (f32[3,72,128]{2,1,0:T(8,128)}, f32[3,72,128]{2,1,0:T(8,128)S(1)}, u32[]{:S(2)}, u32[]{:S(2)}) collective-permute-start(f32[3,72,128]{2,1,0:T(8,128)} %get-tuple-element.46.own_east.wind_east), channel_id=1, source_target_pairs={{0,1},{1,2},{2,3},{3,4},{4,5},{5,6},{6,7},{7,8},{8,9},{9,10},{10,1... | collective-permute-start | bytes 331784 | tf_op jit(solution)/shard_map/ppermute | solution.py:342
  45.8 7.3 %pack_second.1 = bf16[128,80,128]{2,1,0:T(8,128)(2,1)} custom-call(s32[128]{0:T(128)} %get-tuple-element.48.source_ref.second_ref, bf16[128,72,128]{2,1,0:T(8,128)(2,1)} %kernel_ref.3, s32[128,128]{1,0:T(8,128)} %columns_ref.3, bf16[128,128]{1,0:T(8,128)(2,1)} %observed_ref.3, bf16[128,128]{1,0:T(8,128)(2,1)} %weight_ref.3, ...), custom_call_target="tpu_custom_call" | custom-call | flops 5000000 | bytes 6000000 | tf_op jit(solution)/shard_map/pack_second/pallas_call | solution.py:326
  53.0 15.2 %collective-permute-done.3.from_east.side_east = f32[3,72,128]{2,1,0:T(8,128)S(1)} collective-permute-done((f32[3,72,128]{2,1,0:T(8,128)}, f32[3,72,128]{2,1,0:T(8,128)S(1)}, u32[]{:S(2)}, u32[]{:S(2)}) %collective-permute-start.3) | collective-permute-done | bytes 110624 | tf_op jit(solution)/shard_map/ppermute | solution.py:342
  68.2 0.0 copy-start.3
  68.2 0.0 collective-permute-done.2.from_west.side_west
  68.2 0.0 copy-start.4
  68.2 1.7 %all-to-all-done.1.block_ref = bf16[128,80,128]{2,1,0:T(8,128)(2,1)} async-done(((bf16[128,80,128]{2,1,0:T(8,128)(2,1)}), bf16[128,80,128]{2,1,0:T(8,128)(2,1)}, u32[]{:S(2)}, u32[]{:S(2)}) %all-to-all-start.1) | async-done | bytes 2621472 | tf_op jit(solution)/shard_map/all_to_all | solution.py:683
  69.9 6.6 %all-to-all-start = ((bf16[128,80,128]{2,1,0:T(8,128)(2,1)}), bf16[128,80,128]{2,1,0:T(8,128)(2,1)}, u32[]{:S(2)}, u32[]{:S(2)}) async-start(bf16[128,80,128]{2,1,0:T(8,128)(2,1)} %pack_second.1), calls=%async_computation | async-start | bytes 5242880 | tf_op jit(solution)/shard_map/all_to_all | solution.py:683
  76.5 0.0 copy-done.3
  76.5 0.0 copy-done.4
  76.5 6.3 %forward.1.field_ref = bf16[1728,256]{1,0:T(8,128)(2,1)} custom-call(f32[3,8,72,128]{3,2,1,0:T(8,128)} %get-tuple-element.42.state_ref, f32[2,8,72,128]{3,2,1,0:T(8,128)} %get-tuple-element.43.east_ref, f32[2,8,72,128]{3,2,1,0:T(8,128)} %get-tuple-element.44.north_ref, f32[2,8,72,128]{3,2,1,0:T(8,128)} %get-tuple-element.45.mixing_ref, ...), custom_call_target="tpu_custom_call" | custom-call | flops 5000000 | bytes 6000000 | tf_op jit(solution)/shard_map/forward/pallas_call | solution.py:326
  82.9 18.4 %first_soundings.1 = (f32[864,256]{1,0:T(8,128)}, f32[128,128]{1,0:T(8,128)}) custom-call(bf16[1728,256]{1,0:T(8,128)(2,1)} %forward.1.field_ref, bf16[128,80,128]{2,1,0:T(8,128)(2,1)} %all-to-all-done.1.block_ref), custom_call_target="tpu_custom_call" | custom-call | flops 15000000512 | bytes 6000000 | tf_op jit(solution)/shard_map/first_soundings/pallas_call | solution.py:326
  101.3 10.5 %all-to-all-done.block_ref = bf16[128,80,128]{2,1,0:T(8,128)(2,1)} async-done(((bf16[128,80,128]{2,1,0:T(8,128)(2,1)}), bf16[128,80,128]{2,1,0:T(8,128)(2,1)}, u32[]{:S(2)}, u32[]{:S(2)}) %all-to-all-start) | async-done | bytes 2621472 | tf_op jit(solution)/shard_map/all_to_all | solution.py:683
  111.8 14.6 %second_soundings.1 = (f32[864,256]{1,0:T(8,128)}, f32[256,128]{1,0:T(8,128)}, f32[6,72,128]{2,1,0:T(8,128)}, f32[6,72,128]{2,1,0:T(8,128)}, f32[72,128]{1,0:T(8,128)}, /*index=5*/f32[72,128]{1,0:T(8,128)}) custom-call(bf16[1728,256]{1,0:T(8,128)(2,1)} %forward.1.field_ref, bf16[128,80,128]{2,1,0:T(8,128)(2,1)} %all-to-all-done.block_ref, ...), custom_call_target="tpu_custom_call" | custom-call | flops 15000000512 | bytes 6000000 | tf_op jit(solution)/shard_map/second_soundings/pallas_call | solution.py:326
  126.4 2.4 %collective-permute-start.4 = (f32[72,128]{1,0:T(8,128)}, f32[72,128]{1,0:T(8,128)S(1)}, u32[]{:S(2)}, u32[]{:S(2)}) collective-permute-start(f32[72,128]{1,0:T(8,128)} %get-tuple-element.59.own_east), channel_id=1, source_target_pairs={{0,1},{1,2},{2,3},{3,4},{4,5},{5,6},{6,7},{7,8},{8,9},{9,10},{10,1... | collective-permute-start | bytes 110600 | tf_op jit(solution)/shard_map/ppermute | solution.py:342
  128.8 0.0 collective-permute-start.5
  128.8 1.4 collective-permute-done.4.from_west
  130.2 0.0 copy-start.7
  130.2 3.7 %collective-permute-done.5.from_east = f32[72,128]{1,0:T(8,128)S(1)} collective-permute-done((f32[72,128]{1,0:T(8,128)}, f32[72,128]{1,0:T(8,128)S(1)}, u32[]{:S(2)}, u32[]{:S(2)}) %collective-permute-start.5) | collective-permute-done | bytes 36896 | tf_op jit(solution)/shard_map/ppermute | solution.py:342
  133.9 1.1 pad_maximum_fusion
  135.0 1.3 collective-permute-start.7
  136.3 5.5 %collective-permute-start.6 = (f32[8,72,128]{2,1,0:T(8,128)S(1)}, f32[8,72,128]{2,1,0:T(8,128)S(1)}, u32[]{:S(2)}, u32[]{:S(2)}) collective-permute-start(f32[8,72,128]{2,1,0:T(8,128)S(1)} %get-tuple-element.67), channel_id=1, source_target_pairs={{0,16},{16,32},{32,48},{48,64},{64,80},{80,96},{96,112},{1,17},{17... | collective-permute-start | bytes 884744 | tf_op jit(solution)/shard_map/ppermute | solution.py:345
  141.8 11.9 %all-to-all-start.2 = ((f32[128,2,128]{2,1,0:T(2,128)}), f32[128,2,128]{2,1,0:T(2,128)S(1)}, u32[]{:S(2)}, u32[]{:S(2)}) async-start(f32[128,2,128]{2,1,0:T(2,128)} %bitcast.9), calls=%async_computation.2 | async-start | bytes 262144 | tf_op jit(solution)/shard_map/all_to_all | solution.py:683
  153.7 0.0 collective-permute-done.7.down_ref
  153.7 0.0 copy-start.5
  153.7 0.0 collective-permute-done.6.up_ref
  153.8 0.0 copy-start.6
  153.8 0.0 copy-done.7
  153.8 0.0 copy-done.8
  153.8 0.7 copy-done.5
  154.5 0.1 copy-done.6
  154.6 6.4 %adjoint.1 = f32[3,72,8,128]{3,2,1,0:T(8,128)} custom-call(f32[864,256]{1,0:T(8,128)} %get-tuple-element.58.adjoint_ref, f32[2,8,72,128]{3,2,1,0:T(8,128)} %get-tuple-element.43.east_ref, f32[2,8,72,128]{3,2,1,0:T(8,128)} %get-tuple-element.44.north_ref, f32[2,8,72,128]{3,2,1,0:T(8,128)} %get-tuple-element.45.mixing_ref, f32[14,72,128]{2,1,0:T(8,128)} %copy-done, ...), custom_call_target="tpu_custom_call" | custom-call | flops 5000000 | bytes 6000000 | tf_op jit(solution)/shard_map/adjoint/pallas_call | solution.py:326
  161.0 2.7 %all-to-all-done.2 = f32[128,2,128]{2,1,0:T(2,128)S(1)} async-done(((f32[128,2,128]{2,1,0:T(2,128)}), f32[128,2,128]{2,1,0:T(2,128)S(1)}, u32[]{:S(2)}, u32[]{:S(2)}) %all-to-all-start.2) | async-done | bytes 131104 | tf_op jit(solution)/shard_map/all_to_all | solution.py:683
  163.7 0.7 copy-done.2
  164.4 2.1 %innovations.1 = f32[128,128]{1,0:T(8,128)} custom-call(s32[128]{0:T(128)} %get-tuple-element.64.first_ref, s32[128]{0:T(128)} %get-tuple-element.48.source_ref.second_ref, f32[256,128]{1,0:T(8,128)} %bitcast.6, f32[128,128]{1,0:T(8,128)} %get-tuple-element.49.place_ref), custom_call_target="tpu_custom_call" | custom-call | flops 5000000 | bytes 6000000 | tf_op jit(solution)/shard_map/innovations/pallas_call | solution.py:326
  (2 shorter events, 0.0 us)
Async XLA Ops:
  3.8 17.6 %collective-permute-start = (f32[14,72,128]{2,1,0:T(8,128)}, f32[14,72,128]{2,1,0:T(8,128)S(1)}, u32[]{:S(2)}, u32[]{:S(2)}) collective-permute-start(f32[14,72,128]{2,1,0:T(8,128)} %get-tuple-element.38), channel_id=1, source_target_pairs={{0,16},{16,32},{32,48},{48,64},{64,80},{80,96},{96,112},{1,17},{17... | collective-permute-start | bytes 1548296 | tf_op jit(solution)/shard_map/ppermute | solution.py:345
  8.2 13.2 %collective-permute-start.1 = (f32[12,72,128]{2,1,0:T(8,128)}, f32[12,72,128]{2,1,0:T(8,128)S(1)}, u32[]{:S(2)}, u32[]{:S(2)}) collective-permute-start(f32[12,72,128]{2,1,0:T(8,128)} %get-tuple-element.39), channel_id=1, source_target_pairs={{16,0},{32,16},{48,32},{64,48},{80,64},{96,80},{112,96},{17,1},{33... | collective-permute-start | bytes 1327112 | tf_op jit(solution)/shard_map/ppermute | solution.py:345
  21.3 0.8 copy-start.1
  21.3 1.0 copy-start
  22.3 47.6 %all-to-all-start.1 = ((bf16[128,80,128]{2,1,0:T(8,128)(2,1)}), bf16[128,80,128]{2,1,0:T(8,128)(2,1)}, u32[]{:S(2)}, u32[]{:S(2)}) async-start(bf16[128,80,128]{2,1,0:T(8,128)(2,1)} %get-tuple-element.54), calls=%async_computation.1 | async-start | bytes 5242880 | tf_op jit(solution)/shard_map/all_to_all | solution.py:683
  42.5 25.7 %collective-permute-start.3 = (f32[3,72,128]{2,1,0:T(8,128)}, f32[3,72,128]{2,1,0:T(8,128)S(1)}, u32[]{:S(2)}, u32[]{:S(2)}) collective-permute-start(f32[3,72,128]{2,1,0:T(8,128)} %get-tuple-element.47.own_west), channel_id=1, source_target_pairs={{0,15},{1,0},{2,1},{3,2},{4,3},{5,4},{6,5},{7,6},{8,7},{9,8},{10,9... | collective-permute-start | bytes 331784 | tf_op jit(solution)/shard_map/ppermute | solution.py:342
  43.6 24.6 %collective-permute-start.2 = (f32[3,72,128]{2,1,0:T(8,128)}, f32[3,72,128]{2,1,0:T(8,128)S(1)}, u32[]{:S(2)}, u32[]{:S(2)}) collective-permute-start(f32[3,72,128]{2,1,0:T(8,128)} %get-tuple-element.46.own_east.wind_east), channel_id=1, source_target_pairs={{0,1},{1,2},{2,3},{3,4},{4,5},{5,6},{6,7},{7,8},{8,9},{9,10},{10,1... | collective-permute-start | bytes 331784 | tf_op jit(solution)/shard_map/ppermute | solution.py:342
  68.2 8.3 %copy-start.3 = (f32[3,72,128]{2,1,0:T(8,128)}, f32[3,72,128]{2,1,0:T(8,128)S(1)}, u32[]{:S(2)}) copy-start(f32[3,72,128]{2,1,0:T(8,128)S(1)} %collective-permute-done.3.from_east.side_east) | copy-start | bytes 331780
  68.2 8.3 %copy-start.4 = (f32[3,72,128]{2,1,0:T(8,128)}, f32[3,72,128]{2,1,0:T(8,128)S(1)}, u32[]{:S(2)}) copy-start(f32[3,72,128]{2,1,0:T(8,128)S(1)} %collective-permute-done.2.from_west.side_west) | copy-start | bytes 331780
  69.9 41.8 %all-to-all-start = ((bf16[128,80,128]{2,1,0:T(8,128)(2,1)}), bf16[128,80,128]{2,1,0:T(8,128)(2,1)}, u32[]{:S(2)}, u32[]{:S(2)}) async-start(bf16[128,80,128]{2,1,0:T(8,128)(2,1)} %pack_second.1), calls=%async_computation | async-start | bytes 5242880 | tf_op jit(solution)/shard_map/all_to_all | solution.py:683
  126.4 3.8 %collective-permute-start.4 = (f32[72,128]{1,0:T(8,128)}, f32[72,128]{1,0:T(8,128)S(1)}, u32[]{:S(2)}, u32[]{:S(2)}) collective-permute-start(f32[72,128]{1,0:T(8,128)} %get-tuple-element.59.own_east), channel_id=1, source_target_pairs={{0,1},{1,2},{2,3},{3,4},{4,5},{5,6},{6,7},{7,8},{8,9},{9,10},{10,1... | collective-permute-start | bytes 110600 | tf_op jit(solution)/shard_map/ppermute | solution.py:342
  128.8 5.1 %collective-permute-start.5 = (f32[72,128]{1,0:T(8,128)}, f32[72,128]{1,0:T(8,128)S(1)}, u32[]{:S(2)}, u32[]{:S(2)}) collective-permute-start(f32[72,128]{1,0:T(8,128)} %get-tuple-element.60.own_west), channel_id=1, source_target_pairs={{0,15},{1,0},{2,1},{3,2},{4,3},{5,4},{6,5},{7,6},{8,7},{9,8},{10,9... | collective-permute-start | bytes 110600 | tf_op jit(solution)/shard_map/ppermute | solution.py:342
  130.2 23.6 %copy-start.7 = (f32[72,128]{1,0:T(8,128)}, f32[72,128]{1,0:T(8,128)S(1)}, u32[]{:S(2)}) copy-start(f32[72,128]{1,0:T(8,128)S(1)} %collective-permute-done.4.from_west) | copy-start | bytes 110596
  133.9 19.9 %copy-start.8 = (f32[72,128]{1,0:T(8,128)}, f32[72,128]{1,0:T(8,128)S(1)}, u32[]{:S(2)}) copy-start(f32[72,128]{1,0:T(8,128)S(1)} %collective-permute-done.5.from_east) | copy-start | bytes 110596
  135.0 18.7 %collective-permute-start.7 = (f32[8,72,128]{2,1,0:T(8,128)S(1)}, f32[8,72,128]{2,1,0:T(8,128)S(1)}, u32[]{:S(2)}, u32[]{:S(2)}) collective-permute-start(f32[8,72,128]{2,1,0:T(8,128)S(1)} %get-tuple-element.66), channel_id=1, source_target_pairs={{16,0},{32,16},{48,32},{64,48},{80,64},{96,80},{112,96},{17,1},{33... | collective-permute-start | bytes 884744 | tf_op jit(solution)/shard_map/ppermute | solution.py:345
  136.3 17.4 %collective-permute-start.6 = (f32[8,72,128]{2,1,0:T(8,128)S(1)}, f32[8,72,128]{2,1,0:T(8,128)S(1)}, u32[]{:S(2)}, u32[]{:S(2)}) collective-permute-start(f32[8,72,128]{2,1,0:T(8,128)S(1)} %get-tuple-element.67), channel_id=1, source_target_pairs={{0,16},{16,32},{32,48},{48,64},{64,80},{80,96},{96,112},{1,17},{17... | collective-permute-start | bytes 884744 | tf_op jit(solution)/shard_map/ppermute | solution.py:345
  141.8 21.9 %all-to-all-start.2 = ((f32[128,2,128]{2,1,0:T(2,128)}), f32[128,2,128]{2,1,0:T(2,128)S(1)}, u32[]{:S(2)}, u32[]{:S(2)}) async-start(f32[128,2,128]{2,1,0:T(2,128)} %bitcast.9), calls=%async_computation.2 | async-start | bytes 262144 | tf_op jit(solution)/shard_map/all_to_all | solution.py:683
  153.7 0.7 copy-start.5
  153.8 0.8 copy-start.6
  163.7 0.7 copy-start.2

commit v7 on v6

--- a/solution.py
+++ b/solution.py
@@ -98,9 +98,11 @@
 
 
 def arrange_body(
-    last_ref, initial_ref, east_ref, north_ref, mixing_ref, up_ref, down_ref,
-    state_ref, east_out, north_out, mixing_out, east_edge, west_edge,
-):
+    last_ref, initial_ref, east_ref, north_ref, mixing_ref, up_terms, down_terms,
+    state_ref, east_out, north_out, mixing_out, east_edge, west_edge, up_ref, down_ref,
+):
+    joined_terms(up_terms, UP_LOW, up_ref)
+    joined_terms(down_terms, DOWN_LOW, down_ref)
     slabs = []
     for t in range(TRACERS):
         slabs.append(up_ref[2 * t + 1])
@@ -147,20 +149,39 @@
     return jnp.where(top, jnp.float32(0.0), mixing_ref[m, :, row, :])
 
 
+UP_LOW = (1, 3, 5, 8, 12)
+DOWN_LOW = (0, 2, 4)
+
+
 def rows_body(last_ref, initial_ref, east_ref, north_ref, mixing_ref, up_ref, down_ref):
     last = LAT_CELLS - 1
+    up, down = [], []
     for t in range(TRACERS):
         for i in range(2):
-            up_ref[2 * t + i] = initial_ref[t, :, LAT_CELLS - 2 + i, :]
-            down_ref[2 * t + i] = initial_ref[t, :, i, :]
+            up.append(initial_ref[t, :, LAT_CELLS - 2 + i, :])
+            down.append(initial_ref[t, :, i, :])
     for m in range(east_ref.shape[0]):
-        up_ref[6 + 4 * m] = east_ref[m, :, last, :]
-        up_ref[7 + 4 * m] = masked_mixing(mixing_ref, m, last)
-        up_ref[8 + 4 * m] = masked_north(last_ref, north_ref, m, last)
-        up_ref[9 + 4 * m] = masked_north(last_ref, north_ref, m, last - 1)
-        down_ref[6 + 3 * m] = east_ref[m, :, 0, :]
-        down_ref[7 + 3 * m] = masked_mixing(mixing_ref, m, 0)
-        down_ref[8 + 3 * m] = masked_north(last_ref, north_ref, m, 0)
+        for slabs, row in ((up, last), (down, 0)):
+            slabs.append(east_ref[m, :, row, :])
+            slabs.append(masked_mixing(mixing_ref, m, row))
+            slabs.append(masked_north(last_ref, north_ref, m, row))
+        up.append(masked_north(last_ref, north_ref, m, last - 1))
+    for ref, slabs, lows in ((up_ref, up, UP_LOW), (down_ref, down, DOWN_LOW)):
+        for i, slab in enumerate(slabs):
+            high = slab.astype(jnp.bfloat16)
+            ref[i] = high
+            if i in lows:
+                rest = slab - high.astype(jnp.float32)
+                ref[len(slabs) + lows.index(i)] = rest.astype(jnp.bfloat16)
+
+
+def joined_terms(terms_ref, lows, out_ref):
+    count = out_ref.shape[0]
+    for i in range(count):
+        slab = terms_ref[i].astype(jnp.float32)
+        if i in lows:
+            slab = slab + terms_ref[count + lows.index(i)].astype(jnp.float32)
+        out_ref[i] = slab
 
 
 def two_steps(
@@ -316,18 +337,33 @@
 MIDDLE = pltpu.VMEM((TRACERS, LAT_CELLS + 2, LEVELS, LANES), jnp.float32)
 
 
-def whole(body, outs, operands, name, scratch=(), scalars=0, flops=5000000, scalar_outs=0, vmem_mib=63):
+def whole(body, outs, operands, name, scratch=(), scalars=0, flops=5000000, scalar_outs=0, in_hbm=(), steps=1, vmem_mib=63):
     smem = pl.BlockSpec(memory_space=pltpu.SMEM)
 
     def vmem(array):
         zeros = (0,) * len(array.shape)
         return pl.BlockSpec(array.shape, lambda i: zeros, pipeline_mode=pl.Buffered(1))
 
+    def spec(i, array):
+        if i < scalars:
+            return smem
+        return pl.BlockSpec(memory_space=pl.ANY) if i in in_hbm else vmem(array)
+
+    def out_spec(i, array):
+        if i >= len(outs) - scalar_outs:
+            return smem
+        if i or steps == 1:
+            return vmem(array)
+        rest = array.shape[1:]
+        return pl.BlockSpec(
+            (array.shape[0] // steps,) + rest, lambda j: (j,) + (0,) * len(rest)
+        )
+
     return pl.pallas_call(
         body,
-        grid=(1,),
-        in_specs=[smem if i < scalars else vmem(a) for i, a in enumerate(operands)],
-        out_specs=[vmem(a) if i < len(outs) - scalar_outs else smem for i, a in enumerate(outs)],
+        grid=(steps,),
+        in_specs=[spec(i, array) for i, array in enumerate(operands)],
+        out_specs=[out_spec(i, array) for i, array in enumerate(outs)],
         out_shape=outs,
         scratch_shapes=list(scratch),
         compiler_params=pltpu.CompilerParams(vmem_limit_bytes=vmem_mib << 20),
@@ -407,15 +443,21 @@
     lax.fori_loop(0, targets_ref.shape[0] // 8, rank, 0, unroll=2)
 
 
-def pack(
-    source_ref, kernel_ref, columns_ref, observed_ref, weight_ref, place_ref, tally_ref, out_ref,
-    observed_wide, weight_wide, order_ref,
-):
+TOGETHER = 16
+
+
+def widen(observed_ref, weight_ref, observed_wide, weight_wide, order_ref):
     observed_wide[...] = observed_ref[...].astype(jnp.float32)
     weight_wide[...] = weight_ref[...].astype(jnp.float32)
     order_ref[...] = (
         lax.broadcasted_iota(jnp.int32, (LANES, LANES), 0).astype(jnp.float32).astype(jnp.bfloat16)
     )
+
+
+def pack(
+    first, source_ref, kernel_ref, columns_ref, place_ref, tally_ref, out_ref, at,
+    observed_wide, weight_wide, order_ref,
+):
     row_id = lax.broadcasted_iota(jnp.int32, (8, LANES), 0)
     one, nil = jnp.bfloat16(1), jnp.bfloat16(0)
 
@@ -442,25 +484,45 @@
         meta = jnp.where(row_id == 4, tally, result[LEVELS:])
         return jnp.concatenate([result[:LEVELS], meta], axis=0).astype(jnp.bfloat16)
 
-    together = 16
-
-    def several(step, carry):
-        blocks = [sorted_block(step * together + j) for j in range(together)]
-        for j in range(together):
-            out_ref[step * together + j] = blocks[j]
+    blocks = [sorted_block(first + j) for j in range(TOGETHER)]
+    for j in range(TOGETHER):
+        out_ref[at + j] = blocks[j]
+
+
+def pack_second_body(
+    source_ref, kernel_ref, columns_ref, observed_ref, weight_ref, place_ref, tally_ref, out_ref,
+    *scratch,
+):
+    widen(observed_ref, weight_ref, *scratch)
+
+    def step(i, carry):
+        at = i * TOGETHER
+        pack(
+            at, source_ref, kernel_ref, columns_ref, place_ref, tally_ref, out_ref, at, *scratch
+        )
         return carry
 
-    lax.fori_loop(0, out_ref.shape[0] // together, several, 0)
+    lax.fori_loop(0, out_ref.shape[0] // TOGETHER, step, 0)
 
 
 def pack_first_body(
-    targets_ref, counts_ref, kernel_ref, columns_ref, observed_ref, weight_ref,
-    out_ref, place_ref, tally_ref, first_ref, second_ref, *scratch,
-):
-    plan(targets_ref, counts_ref, columns_ref, place_ref, first_ref, second_ref, tally_ref)
+    targets_ref, counts_ref, kernel_hbm, columns_ref, observed_ref, weight_ref,
+    out_ref, place_ref, tally_ref, first_ref, second_ref,
+    observed_wide, weight_wide, order_ref, kernel_ref, sem,
+):
+    scratch = (observed_wide, weight_wide, order_ref)
+
+    @pl.when(pl.program_id(0) == 0)
+    def _():
+        copy = pltpu.make_async_copy(kernel_hbm, kernel_ref, sem)
+        copy.start()
+        widen(observed_ref, weight_ref, *scratch)
+        plan(targets_ref, counts_ref, columns_ref, place_ref, first_ref, second_ref, tally_ref)
+        copy.wait()
+
     pack(
-        first_ref, kernel_ref, columns_ref, observed_ref, weight_ref, place_ref, tally_ref, out_ref,
-        *scratch,
+        pl.program_id(0) * TOGETHER, first_ref, kernel_ref, columns_ref, place_ref, tally_ref,
+        out_ref, 0, *scratch,
     )
 
 
@@ -482,7 +544,7 @@
 
 
 def soundings(
-    field_ref, block_ref, adjoint_ref, write_misfit,
+    field_ref, block_ref, adjoint_ref, write_misfit, arrive,
     stream_ref, found_ref, cell_ref, tally_ref, count_ref, sem,
 ):
     n = WIDTH * LANES
@@ -534,6 +596,8 @@
         stream_ref[g, tile] = jnp.where(lane < at, tails[g], empty)
         for j in range(1, WIDTH):
             stream_ref[g, tile + j] = empty
+
+    arrive()
 
     def load(g, step):
         tiles = [stream_ref[g, step * WIDTH + i] for i in range(WIDTH)]
@@ -625,26 +689,39 @@
     lax.fori_loop(0, block_ref.shape[0] // 8, part_ways, (jnp.int32(0),) * GROUPS)
 
 
-def first_soundings_body(field_ref, block_ref, adjoint_ref, misfit_ref, *scratch):
+def first_soundings_body(
+    field_hbm, block_ref, adjoint_ref, misfit_ref, field_ref, field_sem, *scratch
+):
+    copy = pltpu.make_async_copy(field_hbm, field_ref, field_sem)
+    copy.start()
     adjoint_ref[...] = jnp.zeros_like(adjoint_ref)
 
     def write_misfit(eight, rows):
         misfit_ref[pl.ds(eight * 8, 8), :] = rows
 
-    soundings(field_ref, block_ref, adjoint_ref, write_misfit, *scratch)
+    soundings(field_ref, block_ref, adjoint_ref, write_misfit, copy.wait, *scratch)
 
 
 def second_soundings_body(
-    field_ref, block_ref, earlier_ref, other_ref, adjoint_ref, misfit_ref, *rest
-):
-    edges, scratch = rest[:4], rest[4:]
-    adjoint_ref[...] = earlier_ref[...]
+    field_hbm, block_ref, earlier_hbm, other_ref, adjoint_ref, misfit_ref, *rest
+):
+    edges, (field_ref, field_sem), scratch = rest[:4], rest[4:6], rest[6:-1]
+    copies = [
+        pltpu.make_async_copy(field_hbm, field_ref, field_sem),
+        pltpu.make_async_copy(earlier_hbm, adjoint_ref, rest[-1]),
+    ]
+    for copy in copies:
+        copy.start()
+
+    def arrive():
+        for copy in copies:
+            copy.wait()
 
     def write_misfit(eight, rows):
         misfit_ref[pl.ds(eight * 16, 8, stride=2), :] = other_ref[pl.ds(eight * 8, 8), :]
         misfit_ref[pl.ds(eight * 16 + 1, 8, stride=2), :] = rows
 
-    soundings(field_ref, block_ref, adjoint_ref, write_misfit, *scratch)
+    soundings(field_ref, block_ref, adjoint_ref, write_misfit, arrive, *scratch)
     write_edges(lambda t, row: cell_slab(adjoint_ref, t, row), *edges)
 
 
@@ -658,14 +735,18 @@
         outs + (EDGES if earlier else []),
         (field, blocks) + tuple(earlier),
         "second_soundings" if earlier else "first_soundings",
+        in_hbm=(0, 2) if earlier else (0,),
         scratch=[
+            pltpu.VMEM(field.shape, jnp.bfloat16),
+            pltpu.SemaphoreType.DMA(()),
             pltpu.VMEM((GROUPS, tiles, ROWS, LANES), jnp.bfloat16),
             pltpu.VMEM((GROUPS, tiles, 8, LANES), jnp.float32),
             pltpu.VMEM((256, LANES), jnp.bfloat16),
             pltpu.VMEM((count, LANES), jnp.int32),
             pltpu.SMEM((count, LANES), jnp.int32),
             pltpu.SemaphoreType.DMA(()),
-        ],
+        ]
+        + ([pltpu.SemaphoreType.DMA(())] if earlier else []),
         flops=15000000000,
     )
 
@@ -689,7 +770,11 @@
         return jax.ShapeDtypeStruct((number, LEVELS, LANES), jnp.float32)
 
     grid = (is_last, initial, east_wind, north_wind, mixing)
-    up, down = whole(rows_body, [slabs_like(14), slabs_like(12)], grid, "rows", scalars=1)
+    terms = [
+        jax.ShapeDtypeStruct((14 + len(UP_LOW), LEVELS, LANES), jnp.bfloat16),
+        jax.ShapeDtypeStruct((12 + len(DOWN_LOW), LEVELS, LANES), jnp.bfloat16),
+    ]
+    up, down = whole(rows_body, terms, grid, "rows", scalars=1)
     counts, up, down = lax.optimization_barrier((counts, up, down))
     from_south, from_north = shifted(up, 1, 0), shifted(down, -1, 0)
     slots = jax.ShapeDtypeStruct((device_count, ROWS, sounds), jnp.bfloat16)
@@ -703,12 +788,19 @@
         [slots, by_block, by_block, by_device, by_device],
         (targets[:, 0], counts) + heard,
         "pack_first",
-        scratch=scratch,
+        scratch=scratch
+        + [pltpu.VMEM(kernel.shape, jnp.bfloat16), pltpu.SemaphoreType.DMA(())],
         scalars=2,
         scalar_outs=2,
+        in_hbm=(2,),
+        steps=device_count // TOGETHER,
     )
     (out_second,) = whole(
-        pack, [slots], (source_second,) + heard + (place, tally), "pack_second", scratch=scratch,
+        pack_second_body,
+        [slots],
+        (source_second,) + heard + (place, tally),
+        "pack_second",
+        scratch=scratch,
         scalars=1,
     )
     out_first, from_south, from_north = lax.optimization_barrier(
@@ -717,12 +809,13 @@
     got_first = exchange(out_first)
     state, *rest = whole(
         arrange_body,
-        [STATE, winds_like, winds_like, winds_like, slabs_like(3), slabs_like(3)],
+        [STATE, winds_like, winds_like, winds_like]
+        + [slabs_like(3), slabs_like(3), slabs_like(14), slabs_like(12)],
         grid + (from_south, from_north),
         "arrange",
         scalars=1,
     )
-    fields, (east, west) = tuple(rest[:3]), rest[3:]
+    fields, (east, west, from_south, from_north) = tuple(rest[:3]), rest[3:]
     side_west, side_east = shifted(east, 0, 1), shifted(west, 0, -1)
     out_second, side_west, side_east = lax.optimization_barrier((out_second, side_west, side_east))
     got_second = exchange(out_second)

time: 167 us -> 163 us (0.976)
  waiting for transfers between devices: 37 us -> 33.6 us
    ppermute x4, waiting for transfers between devices: 1.84 us -> 0.01 us  [shifted(): return lax.ppermute(array, 'lat', rows)]
  transfers between devices with their start and end apart: 11 -> 11, of which waited for: 7 -> 6; matrix products, arithmetic and copies ran while one was open for 0% -> 0% of each run, Pallas kernels for 34% -> 35%
where the time goes in v7:
time: 163 us; the launch traced here: 164 us
  Pallas kernels  77 us (47%)
  starting transfers between devices  48.8 us (30%)
  waiting for transfers between devices  33.6 us (21%)
  local copies, waits for them, and re-layouts  2.29 us (1%)
    pallas_call x9, Pallas kernels, whole(): pl.pallas_call(body, grid=(steps,), in_specs=[spec(i, array) for i, array...  77 us
    all_to_all x3, starting transfers between devices, exchange(): lax.all_to_all(array, ('lat', 'lon'), split_axis=0, concat_axis=0, tiled=...  32.2 us
    ppermute x4, waiting for transfers between devices, shifted(): lax.ppermute(array, 'lon', [(j, (j + lon_by) % lon) for j in range(lon)])  20 us
    all_to_all x3, waiting for transfers between devices, exchange(): lax.all_to_all(array, ('lat', 'lon'), split_axis=0, concat_axis=0, tiled=...  13.6 us
    ppermute x4, starting transfers between devices, shifted(): return lax.ppermute(array, 'lat', rows)  11 us
    ppermute x4, starting transfers between devices, shifted(): lax.ppermute(array, 'lon', [(j, (j + lon_by) % lon) for j in range(lon)])  5.64 us
  transfers between devices with their start and end apart: 11, of which 6 were waited for; matrix products, arithmetic and copies ran while one was open for 0% of the time, Pallas kernels for 35%

profile of v7, /device:TPU:1, one launch (start us, length us, event | category | flops | bytes accessed | tf_op | source)
XLA Modules:
  0.0 163.7 jit_solution(6145341878080647514)
XLA Ops:
  0.6 3.8 %rows.1 = (bf16[19,72,128]{2,1,0:T(8,128)(2,1)}, bf16[15,72,128]{2,1,0:T(8,128)(2,1)}) custom-call(s32[1]{0:T(128)} %bitcast.last_ref, f32[3,72,8,128]{3,2,1,0:T(8,128)} %initial_ref.3, f32[2,72,8,128]{3,2,1,0:T(8,128)} %east_ref.3, f32[2,72,8,128]{3,2,1,0:T(8,128)} %north_ref.3, f32[2,72,8,128]{3,2,1,0:T(8,128)} %mixing_ref.3), custom_call_target="tpu_custom_call" | custom-call | flops 5000000 | bytes 6000000 | tf_op jit(solution)/shard_map/rows/pallas_call | solution.py:362
  4.4 4.4 %collective-permute-start = (bf16[19,72,128]{2,1,0:T(8,128)(2,1)}, bf16[19,72,128]{2,1,0:T(8,128)(2,1)S(1)}, u32[]{:S(2)}, u32[]{:S(2)}) collective-permute-start(bf16[19,72,128]{2,1,0:T(8,128)(2,1)} %get-tuple-element.40), channel_id=1, source_target_pairs={{0,16},{16,32},{32,48},{48,64},{64,80},{80,96},{96,112},{1,17},{17... | collective-permute-start | bytes 1050632 | tf_op jit(solution)/shard_map/ppermute | solution.py:381
  8.8 1.3 collective-permute-start.1
  10.1 9.3 %pack_first.1 = (bf16[128,80,128]{2,1,0:T(8,128)(2,1)}, f32[128,128]{1,0:T(8,128)}, f32[128,128]{1,0:T(8,128)}, s32[128]{0:T(128)}, s32[128]{0:T(128)}) custom-call(s32[128]{0:T(128)} %bitcast.10, s32[128]{0:T(128)} %counts_ref, bf16[128,72,128]{2,1,0:T(8,128)(2,1)} %kernel_ref.1, s32[128,128]{1,0:T(8,128)} %columns_ref.3, bf16[128,128]{1,0:T(8,128)(2,1)} %observed_ref.3, ...), custom_call_target="tpu_custom_call" | custom-call | flops 5000000 | bytes 6000000 | tf_op jit(solution)/shard_map/pack_first/pallas_call | solution.py:362
  19.4 0.0 collective-permute-done.1.down_terms
  19.4 0.0 copy-start.6
  19.4 0.0 collective-permute-done.up_terms
  19.4 0.0 copy-start.3
  19.4 0.7 copy-done.6
  20.1 0.1 copy-done.3
  20.2 12.1 %all-to-all-start.1 = ((bf16[128,80,128]{2,1,0:T(8,128)(2,1)}), bf16[128,80,128]{2,1,0:T(8,128)(2,1)}, u32[]{:S(2)}, u32[]{:S(2)}) async-start(bf16[128,80,128]{2,1,0:T(8,128)(2,1)} %get-tuple-element.58), calls=%async_computation.1 | async-start | bytes 5242880 | tf_op jit(solution)/shard_map/all_to_all | solution.py:764
  32.3 8.1 %arrange.1 = (f32[3,8,72,128]{3,2,1,0:T(8,128)}, f32[2,8,72,128]{3,2,1,0:T(8,128)}, f32[2,8,72,128]{3,2,1,0:T(8,128)}, f32[2,8,72,128]{3,2,1,0:T(8,128)}, f32[3,...) custom-call(s32[1]{0:T(128)} %bitcast.last_ref, ...), custom_call_target="tpu_custom_call" | custom-call | flops 5000000 | bytes 6000000 | tf_op jit(solution)/shard_map/arrange/pallas_call | solution.py:362
  40.4 1.1 collective-permute-start.3
  41.5 2.1 %collective-permute-start.2 = (f32[3,72,128]{2,1,0:T(8,128)}, f32[3,72,128]{2,1,0:T(8,128)S(1)}, u32[]{:S(2)}, u32[]{:S(2)}) collective-permute-start(f32[3,72,128]{2,1,0:T(8,128)} %get-tuple-element.48.own_east.wind_east), channel_id=1, source_target_pairs={{0,1},{1,2},{2,3},{3,4},{4,5},{5,6},{6,7},{7,8},{8,9},{9,10},{10,1... | collective-permute-start | bytes 331784 | tf_op jit(solution)/shard_map/ppermute | solution.py:378
  43.6 7.3 %pack_second.1 = bf16[128,80,128]{2,1,0:T(8,128)(2,1)} custom-call(s32[128]{0:T(128)} %get-tuple-element.52.source_ref.second_ref, bf16[128,72,128]{2,1,0:T(8,128)(2,1)} %kernel_ref.1, s32[128,128]{1,0:T(8,128)} %columns_ref.3, bf16[128,128]{1,0:T(8,128)(2,1)} %observed_ref.3, bf16[128,128]{1,0:T(8,128)(2,1)} %weight_ref.3, ...), custom_call_target="tpu_custom_call" | custom-call | flops 5000000 | bytes 6000000 | tf_op jit(solution)/shard_map/pack_second/pallas_call | solution.py:362
  50.9 14.9 %collective-permute-done.3.from_east.side_east = f32[3,72,128]{2,1,0:T(8,128)S(1)} collective-permute-done((f32[3,72,128]{2,1,0:T(8,128)}, f32[3,72,128]{2,1,0:T(8,128)S(1)}, u32[]{:S(2)}, u32[]{:S(2)}) %collective-permute-start.3) | collective-permute-done | bytes 110624 | tf_op jit(solution)/shard_map/ppermute | solution.py:378
  65.8 0.0 copy-start.1
  65.8 0.0 collective-permute-done.2.from_west.side_west
  65.8 0.0 copy-start.2
  65.8 1.7 %all-to-all-done.1.block_ref = bf16[128,80,128]{2,1,0:T(8,128)(2,1)} async-done(((bf16[128,80,128]{2,1,0:T(8,128)(2,1)}), bf16[128,80,128]{2,1,0:T(8,128)(2,1)}, u32[]{:S(2)}, u32[]{:S(2)}) %all-to-all-start.1) | async-done | bytes 2621472 | tf_op jit(solution)/shard_map/all_to_all | solution.py:764
  67.5 6.6 %all-to-all-start = ((bf16[128,80,128]{2,1,0:T(8,128)(2,1)}), bf16[128,80,128]{2,1,0:T(8,128)(2,1)}, u32[]{:S(2)}, u32[]{:S(2)}) async-start(bf16[128,80,128]{2,1,0:T(8,128)(2,1)} %pack_second.1), calls=%async_computation | async-start | bytes 5242880 | tf_op jit(solution)/shard_map/all_to_all | solution.py:764
  74.1 0.0 copy-done.1
  74.1 0.0 copy-done.2
  74.1 6.3 %forward.1.field_hbm = bf16[1728,256]{1,0:T(8,128)(2,1)} custom-call(f32[3,8,72,128]{3,2,1,0:T(8,128)} %get-tuple-element.44.state_ref, f32[2,8,72,128]{3,2,1,0:T(8,128)} %get-tuple-element.45.east_ref, f32[2,8,72,128]{3,2,1,0:T(8,128)} %get-tuple-element.46.north_ref, f32[2,8,72,128]{3,2,1,0:T(8,128)} %get-tuple-element.47.mixing_ref, ...), custom_call_target="tpu_custom_call" | custom-call | flops 5000000 | bytes 6000000 | tf_op jit(solution)/shard_map/forward/pallas_call | solution.py:362
  80.5 19.7 %first_soundings.1 = (f32[864,256]{1,0:T(8,128)}, f32[128,128]{1,0:T(8,128)}) custom-call(bf16[1728,256]{1,0:T(8,128)(2,1)} %forward.1.field_hbm, bf16[128,80,128]{2,1,0:T(8,128)(2,1)} %all-to-all-done.1.block_ref), custom_call_target="tpu_custom_call" | custom-call | flops 15000000512 | bytes 6000000 | tf_op jit(solution)/shard_map/first_soundings/pallas_call | solution.py:362
  100.2 9.2 %all-to-all-done.block_ref = bf16[128,80,128]{2,1,0:T(8,128)(2,1)} async-done(((bf16[128,80,128]{2,1,0:T(8,128)(2,1)}), bf16[128,80,128]{2,1,0:T(8,128)(2,1)}, u32[]{:S(2)}, u32[]{:S(2)}) %all-to-all-start) | async-done | bytes 2621472 | tf_op jit(solution)/shard_map/all_to_all | solution.py:764
  109.3 14.2 %second_soundings.1 = (f32[864,256]{1,0:T(8,128)}, f32[256,128]{1,0:T(8,128)}, f32[6,72,128]{2,1,0:T(8,128)}, f32[6,72,128]{2,1,0:T(8,128)}, f32[72,128]{1,0:T(8,128)}, /*index=5*/f32[72,128]{1,0:T(8,128)}) custom-call(bf16[1728,256]{1,0:T(8,128)(2,1)} %forward.1.field_hbm, bf16[128,80,128]{2,1,0:T(8,128)(2,1)} %all-to-all-done.block_ref, ...), custom_call_target="tpu_custom_call" | custom-call | flops 15000000512 | bytes 6000000 | tf_op jit(solution)/shard_map/second_soundings/pallas_call | solution.py:362
  123.5 2.4 %collective-permute-start.4 = (f32[72,128]{1,0:T(8,128)}, f32[72,128]{1,0:T(8,128)S(1)}, u32[]{:S(2)}, u32[]{:S(2)}) collective-permute-start(f32[72,128]{1,0:T(8,128)} %get-tuple-element.63.own_east), channel_id=1, source_target_pairs={{0,1},{1,2},{2,3},{3,4},{4,5},{5,6},{6,7},{7,8},{8,9},{9,10},{10,1... | collective-permute-start | bytes 110600 | tf_op jit(solution)/shard_map/ppermute | solution.py:378
  125.9 0.0 collective-permute-start.5
  125.9 1.4 collective-permute-done.4.from_west
  127.3 0.0 copy-start.7
  127.3 3.7 %collective-permute-done.5.from_east = f32[72,128]{1,0:T(8,128)S(1)} collective-permute-done((f32[72,128]{1,0:T(8,128)}, f32[72,128]{1,0:T(8,128)S(1)}, u32[]{:S(2)}, u32[]{:S(2)}) %collective-permute-start.5) | collective-permute-done | bytes 36896 | tf_op jit(solution)/shard_map/ppermute | solution.py:378
  131.0 1.1 pad_maximum_fusion
  132.1 1.3 collective-permute-start.7
  133.4 4.0 %collective-permute-start.6 = (f32[8,72,128]{2,1,0:T(8,128)S(1)}, f32[8,72,128]{2,1,0:T(8,128)S(1)}, u32[]{:S(2)}, u32[]{:S(2)}) collective-permute-start(f32[8,72,128]{2,1,0:T(8,128)S(1)} %get-tuple-element.71), channel_id=1, source_target_pairs={{0,16},{16,32},{32,48},{48,64},{64,80},{80,96},{96,112},{1,17},{17... | collective-permute-start | bytes 884744 | tf_op jit(solution)/shard_map/ppermute | solution.py:381
  137.4 13.6 %all-to-all-start.2 = ((f32[128,2,128]{2,1,0:T(2,128)}), f32[128,2,128]{2,1,0:T(2,128)S(1)}, u32[]{:S(2)}, u32[]{:S(2)}) async-start(f32[128,2,128]{2,1,0:T(2,128)} %bitcast.9), calls=%async_computation.2 | async-start | bytes 262144 | tf_op jit(solution)/shard_map/all_to_all | solution.py:764
  151.0 0.0 collective-permute-done.7.down_ref
  151.0 0.0 copy-start.4
  151.0 0.0 collective-permute-done.6.up_ref
  151.0 0.0 copy-start.5
  151.0 0.0 copy-done.7
  151.1 0.0 copy-done.8
  151.1 0.7 copy-done.4
  151.7 0.1 copy-done.5
  151.9 6.4 %adjoint.1 = f32[3,72,8,128]{3,2,1,0:T(8,128)} custom-call(f32[864,256]{1,0:T(8,128)} %get-tuple-element.62.adjoint_ref, f32[2,8,72,128]{3,2,1,0:T(8,128)} %get-tuple-element.45.east_ref, f32[2,8,72,128]{3,2,1,0:T(8,128)} %get-tuple-element.46.north_ref, f32[2,8,72,128]{3,2,1,0:T(8,128)} %get-tuple-element.47.mixing_ref, ...), custom_call_target="tpu_custom_call" | custom-call | flops 5000000 | bytes 6000000 | tf_op jit(solution)/shard_map/adjoint/pallas_call | solution.py:362
  158.2 2.7 %all-to-all-done.2 = f32[128,2,128]{2,1,0:T(2,128)S(1)} async-done(((f32[128,2,128]{2,1,0:T(2,128)}), f32[128,2,128]{2,1,0:T(2,128)S(1)}, u32[]{:S(2)}, u32[]{:S(2)}) %all-to-all-start.2) | async-done | bytes 131104 | tf_op jit(solution)/shard_map/all_to_all | solution.py:764
  161.0 0.7 copy-done
  161.6 2.1 %innovations.1 = f32[128,128]{1,0:T(8,128)} custom-call(s32[128]{0:T(128)} %get-tuple-element.68.first_ref, s32[128]{0:T(128)} %get-tuple-element.52.source_ref.second_ref, f32[256,128]{1,0:T(8,128)} %bitcast.6, f32[128,128]{1,0:T(8,128)} %get-tuple-element.53.place_ref), custom_call_target="tpu_custom_call" | custom-call | flops 5000000 | bytes 6000000 | tf_op jit(solution)/shard_map/innovations/pallas_call | solution.py:362
  (2 shorter events, 0.0 us)
Async XLA Ops:
  4.4 15.0 %collective-permute-start = (bf16[19,72,128]{2,1,0:T(8,128)(2,1)}, bf16[19,72,128]{2,1,0:T(8,128)(2,1)S(1)}, u32[]{:S(2)}, u32[]{:S(2)}) collective-permute-start(bf16[19,72,128]{2,1,0:T(8,128)(2,1)} %get-tuple-element.40), channel_id=1, source_target_pairs={{0,16},{16,32},{32,48},{48,64},{64,80},{80,96},{96,112},{1,17},{17... | collective-permute-start | bytes 1050632 | tf_op jit(solution)/shard_map/ppermute | solution.py:381
  8.8 10.6 %collective-permute-start.1 = (bf16[15,72,128]{2,1,0:T(8,128)(2,1)}, bf16[15,72,128]{2,1,0:T(8,128)(2,1)S(1)}, u32[]{:S(2)}, u32[]{:S(2)}) collective-permute-start(bf16[15,72,128]{2,1,0:T(8,128)(2,1)} %get-tuple-element.41), channel_id=1, source_target_pairs={{16,0},{32,16},{48,32},{64,48},{80,64},{96,80},{112,96},{17,1},{33... | collective-permute-start | bytes 829448 | tf_op jit(solution)/shard_map/ppermute | solution.py:381
  19.4 0.7 copy-start.6
  19.4 0.8 copy-start.3
  20.2 47.3 %all-to-all-start.1 = ((bf16[128,80,128]{2,1,0:T(8,128)(2,1)}), bf16[128,80,128]{2,1,0:T(8,128)(2,1)}, u32[]{:S(2)}, u32[]{:S(2)}) async-start(bf16[128,80,128]{2,1,0:T(8,128)(2,1)} %get-tuple-element.58), calls=%async_computation.1 | async-start | bytes 5242880 | tf_op jit(solution)/shard_map/all_to_all | solution.py:764
  40.4 25.4 %collective-permute-start.3 = (f32[3,72,128]{2,1,0:T(8,128)}, f32[3,72,128]{2,1,0:T(8,128)S(1)}, u32[]{:S(2)}, u32[]{:S(2)}) collective-permute-start(f32[3,72,128]{2,1,0:T(8,128)} %get-tuple-element.49.own_west), channel_id=1, source_target_pairs={{0,15},{1,0},{2,1},{3,2},{4,3},{5,4},{6,5},{7,6},{8,7},{9,8},{10,9... | collective-permute-start | bytes 331784 | tf_op jit(solution)/shard_map/ppermute | solution.py:378
  41.5 24.3 %collective-permute-start.2 = (f32[3,72,128]{2,1,0:T(8,128)}, f32[3,72,128]{2,1,0:T(8,128)S(1)}, u32[]{:S(2)}, u32[]{:S(2)}) collective-permute-start(f32[3,72,128]{2,1,0:T(8,128)} %get-tuple-element.48.own_east.wind_east), channel_id=1, source_target_pairs={{0,1},{1,2},{2,3},{3,4},{4,5},{5,6},{6,7},{7,8},{8,9},{9,10},{10,1... | collective-permute-start | bytes 331784 | tf_op jit(solution)/shard_map/ppermute | solution.py:378
  65.8 8.3 %copy-start.1 = (f32[3,72,128]{2,1,0:T(8,128)}, f32[3,72,128]{2,1,0:T(8,128)S(1)}, u32[]{:S(2)}) copy-start(f32[3,72,128]{2,1,0:T(8,128)S(1)} %collective-permute-done.3.from_east.side_east) | copy-start | bytes 331780
  65.8 8.3 %copy-start.2 = (f32[3,72,128]{2,1,0:T(8,128)}, f32[3,72,128]{2,1,0:T(8,128)S(1)}, u32[]{:S(2)}) copy-start(f32[3,72,128]{2,1,0:T(8,128)S(1)} %collective-permute-done.2.from_west.side_west) | copy-start | bytes 331780
  67.5 41.8 %all-to-all-start = ((bf16[128,80,128]{2,1,0:T(8,128)(2,1)}), bf16[128,80,128]{2,1,0:T(8,128)(2,1)}, u32[]{:S(2)}, u32[]{:S(2)}) async-start(bf16[128,80,128]{2,1,0:T(8,128)(2,1)} %pack_second.1), calls=%async_computation | async-start | bytes 5242880 | tf_op jit(solution)/shard_map/all_to_all | solution.py:764
  123.5 3.8 %collective-permute-start.4 = (f32[72,128]{1,0:T(8,128)}, f32[72,128]{1,0:T(8,128)S(1)}, u32[]{:S(2)}, u32[]{:S(2)}) collective-permute-start(f32[72,128]{1,0:T(8,128)} %get-tuple-element.63.own_east), channel_id=1, source_target_pairs={{0,1},{1,2},{2,3},{3,4},{4,5},{5,6},{6,7},{7,8},{8,9},{9,10},{10,1... | collective-permute-start | bytes 110600 | tf_op jit(solution)/shard_map/ppermute | solution.py:378
  125.9 5.1 %collective-permute-start.5 = (f32[72,128]{1,0:T(8,128)}, f32[72,128]{1,0:T(8,128)S(1)}, u32[]{:S(2)}, u32[]{:S(2)}) collective-permute-start(f32[72,128]{1,0:T(8,128)} %get-tuple-element.64.own_west), channel_id=1, source_target_pairs={{0,15},{1,0},{2,1},{3,2},{4,3},{5,4},{6,5},{7,6},{8,7},{9,8},{10,9... | collective-permute-start | bytes 110600 | tf_op jit(solution)/shard_map/ppermute | solution.py:378
  127.3 23.7 %copy-start.7 = (f32[72,128]{1,0:T(8,128)}, f32[72,128]{1,0:T(8,128)S(1)}, u32[]{:S(2)}) copy-start(f32[72,128]{1,0:T(8,128)S(1)} %collective-permute-done.4.from_west) | copy-start | bytes 110596
  131.0 20.0 %copy-start.8 = (f32[72,128]{1,0:T(8,128)}, f32[72,128]{1,0:T(8,128)S(1)}, u32[]{:S(2)}) copy-start(f32[72,128]{1,0:T(8,128)S(1)} %collective-permute-done.5.from_east) | copy-start | bytes 110596
  132.1 18.9 %collective-permute-start.7 = (f32[8,72,128]{2,1,0:T(8,128)S(1)}, f32[8,72,128]{2,1,0:T(8,128)S(1)}, u32[]{:S(2)}, u32[]{:S(2)}) collective-permute-start(f32[8,72,128]{2,1,0:T(8,128)S(1)} %get-tuple-element.70), channel_id=1, source_target_pairs={{16,0},{32,16},{48,32},{64,48},{80,64},{96,80},{112,96},{17,1},{33... | collective-permute-start | bytes 884744 | tf_op jit(solution)/shard_map/ppermute | solution.py:381
  133.4 17.6 %collective-permute-start.6 = (f32[8,72,128]{2,1,0:T(8,128)S(1)}, f32[8,72,128]{2,1,0:T(8,128)S(1)}, u32[]{:S(2)}, u32[]{:S(2)}) collective-permute-start(f32[8,72,128]{2,1,0:T(8,128)S(1)} %get-tuple-element.71), channel_id=1, source_target_pairs={{0,16},{16,32},{32,48},{48,64},{64,80},{80,96},{96,112},{1,17},{17... | collective-permute-start | bytes 884744 | tf_op jit(solution)/shard_map/ppermute | solution.py:381
  137.4 23.5 %all-to-all-start.2 = ((f32[128,2,128]{2,1,0:T(2,128)}), f32[128,2,128]{2,1,0:T(2,128)S(1)}, u32[]{:S(2)}, u32[]{:S(2)}) async-start(f32[128,2,128]{2,1,0:T(2,128)} %bitcast.9), calls=%async_computation.2 | async-start | bytes 262144 | tf_op jit(solution)/shard_map/all_to_all | solution.py:764
  151.0 0.7 copy-start.4
  151.0 0.8 copy-start.5
  161.0 0.7 copy-start

commit v8 on v7

--- a/solution.py
+++ b/solution.py
@@ -14,7 +14,7 @@
 PARTS = 12
 GROUPS = 6
 GROUP_PARTS = PARTS // GROUPS
-WIDTH = 2
+WIDTH = 4
 LAT_CELLS = 8
 LANES = 128
 
@@ -337,7 +337,7 @@
 MIDDLE = pltpu.VMEM((TRACERS, LAT_CELLS + 2, LEVELS, LANES), jnp.float32)
 
 
-def whole(body, outs, operands, name, scratch=(), scalars=0, flops=5000000, scalar_outs=0, in_hbm=(), steps=1, vmem_mib=63):
+def whole(body, outs, operands, name, scratch=(), scalars=0, flops=5000000, scalar_outs=0, in_hbm=(), steps=1, vmem_kib=65472):
     smem = pl.BlockSpec(memory_space=pltpu.SMEM)
 
     def vmem(array):
@@ -366,7 +366,7 @@
         out_specs=[out_spec(i, array) for i, array in enumerate(outs)],
         out_shape=outs,
         scratch_shapes=list(scratch),
-        compiler_params=pltpu.CompilerParams(vmem_limit_bytes=vmem_mib << 20),
+        compiler_params=pltpu.CompilerParams(vmem_limit_bytes=vmem_kib << 10),
         cost_estimate=pl.CostEstimate(flops=flops, bytes_accessed=6000000, transcendentals=0),
         name=name,
     )(*operands)
@@ -686,7 +686,7 @@
         write_misfit(eight, rows)
         return tuple(ends)
 
-    lax.fori_loop(0, block_ref.shape[0] // 8, part_ways, (jnp.int32(0),) * GROUPS)
+    lax.fori_loop(0, block_ref.shape[0] // 8, part_ways, (jnp.int32(0),) * GROUPS, unroll=2)
 
 
 def first_soundings_body(

time: 163 us -> 165 us (1.012); the launches traced: 164 us -> 163 us
  Pallas kernels: 77 us -> 81.2 us
  starting transfers between devices: 48.8 us -> 45.2 us
  local copies, waits for them, and re-layouts: 2.29 us -> 0.01 us
    pallas_call x9, Pallas kernels: 77 us -> 81.2 us  [whole(): pl.pallas_call(body, grid=(steps,), in_specs=[spec(i, array) for i, array...]
    all_to_all x3, starting transfers between devices: 32.2 us -> 29 us  [exchange(): lax.all_to_all(array, ('lat', 'lon'), split_axis=0, concat_axis=0, tiled=...]
    unnamed x18 -> x4, local copies, waits for them, and re-layouts: 2.29 us -> 0.01 us
    ppermute x4, starting transfers between devices: 5.64 us -> 3.82 us  [shifted(): lax.ppermute(array, 'lon', [(j, (j + lon_by) % lon) for j in range(lon)])]
  transfers between devices with their start and end apart: 11 -> 11, of which waited for: 6 -> 6; matrix products, arithmetic and copies ran while one was open for 0% -> 0% of each run, Pallas kernels for 35% -> 34%
where the time goes in v8:
time: 165 us; the launch traced here: 163 us
  Pallas kernels  81.2 us (49%)
  starting transfers between devices  45.2 us (27%)
  waiting for transfers between devices  35 us (21%)
    pallas_call x9, Pallas kernels, whole(): pl.pallas_call(body, grid=(steps,), in_specs=[spec(i, array) for i, array...  81.2 us
    all_to_all x3, starting transfers between devices, exchange(): lax.all_to_all(array, ('lat', 'lon'), split_axis=0, concat_axis=0, tiled=...  29 us
    ppermute x4, waiting for transfers between devices, shifted(): lax.ppermute(array, 'lon', [(j, (j + lon_by) % lon) for j in range(lon)])  19.7 us
    all_to_all x3, waiting for transfers between devices, exchange(): lax.all_to_all(array, ('lat', 'lon'), split_axis=0, concat_axis=0, tiled=...  15.2 us
    ppermute x4, starting transfers between devices, shifted(): return lax.ppermute(array, 'lat', rows)  12.4 us
    ppermute x4, starting transfers between devices, shifted(): lax.ppermute(array, 'lon', [(j, (j + lon_by) % lon) for j in range(lon)])  3.82 us
  transfers between devices with their start and end apart: 11, of which 6 were waited for; matrix products, arithmetic and copies ran while one was open for 0% of the time, Pallas kernels for 34%

profile of v8, /device:TPU:1, one launch (start us, length us, event | category | flops | bytes accessed | tf_op | source)
XLA Modules:
  0.0 163.2 jit_solution(8827917097814003442)
XLA Ops:
  0.6 3.8 %rows.1 = (bf16[19,72,128]{2,1,0:T(8,128)(2,1)}, bf16[15,72,128]{2,1,0:T(8,128)(2,1)}) custom-call(s32[1]{0:T(128)} %bitcast.last_ref, f32[3,72,8,128]{3,2,1,0:T(8,128)} %initial_ref.3, f32[2,72,8,128]{3,2,1,0:T(8,128)} %east_ref.3, f32[2,72,8,128]{3,2,1,0:T(8,128)} %north_ref.3, f32[2,72,8,128]{3,2,1,0:T(8,128)} %mixing_ref.3), custom_call_target="tpu_custom_call" | custom-call | flops 5000000 | bytes 6000000 | tf_op jit(solution)/shard_map/rows/pallas_call | solution.py:362
  4.4 5.1 %collective-permute-start = (bf16[19,72,128]{2,1,0:T(8,128)(2,1)}, bf16[19,72,128]{2,1,0:T(8,128)(2,1)}, u32[]{:S(2)}, u32[]{:S(2)}) collective-permute-start(bf16[19,72,128]{2,1,0:T(8,128)(2,1)} %get-tuple-element.40), channel_id=1, source_target_pairs={{0,16},{16,32},{32,48},{48,64},{64,80},{80,96},{96,112},{1,17},{17... | collective-permute-start | bytes 1050632 | tf_op jit(solution)/shard_map/ppermute | solution.py:381
  9.5 1.3 collective-permute-start.1
  10.8 9.2 %pack_first.1 = (bf16[128,80,128]{2,1,0:T(8,128)(2,1)}, f32[128,128]{1,0:T(8,128)}, f32[128,128]{1,0:T(8,128)}, s32[128]{0:T(128)}, s32[128]{0:T(128)}) custom-call(s32[128]{0:T(128)} %bitcast.9, s32[128]{0:T(128)} %counts_ref, bf16[128,72,128]{2,1,0:T(8,128)(2,1)} %kernel_ref.1, s32[128,128]{1,0:T(8,128)} %columns_ref.3, bf16[128,128]{1,0:T(8,128)(2,1)} %observed_ref.3, ...), custom_call_target="tpu_custom_call" | custom-call | flops 5000000 | bytes 6000000 | tf_op jit(solution)/shard_map/pack_first/pallas_call | solution.py:362
  20.1 0.0 collective-permute-done.1.down_terms
  20.1 0.0 collective-permute-done.up_terms
  20.1 11.7 %all-to-all-start.1 = ((bf16[128,80,128]{2,1,0:T(8,128)(2,1)}), bf16[128,80,128]{2,1,0:T(8,128)(2,1)}, u32[]{:S(2)}, u32[]{:S(2)}) async-start(bf16[128,80,128]{2,1,0:T(8,128)(2,1)} %get-tuple-element.58), calls=%async_computation.1 | async-start | bytes 5242880 | tf_op jit(solution)/shard_map/all_to_all | solution.py:764
  31.8 8.1 %arrange.1 = (f32[3,8,72,128]{3,2,1,0:T(8,128)}, f32[2,8,72,128]{3,2,1,0:T(8,128)}, f32[2,8,72,128]{3,2,1,0:T(8,128)}, f32[2,8,72,128]{3,2,1,0:T(8,128)}, f32[3,...) custom-call(s32[1]{0:T(128)} %bitcast.last_ref, ...), custom_call_target="tpu_custom_call" | custom-call | flops 5000000 | bytes 6000000 | tf_op jit(solution)/shard_map/arrange/pallas_call | solution.py:362
  39.9 1.1 collective-permute-start.3
  41.1 2.1 %collective-permute-start.2 = (f32[3,72,128]{2,1,0:T(8,128)}, f32[3,72,128]{2,1,0:T(8,128)}, u32[]{:S(2)}, u32[]{:S(2)}) collective-permute-start(f32[3,72,128]{2,1,0:T(8,128)} %get-tuple-element.48.own_east.wind_east), channel_id=1, source_target_pairs={{0,1},{1,2},{2,3},{3,4},{4,5},{5,6},{6,7},{7,8},{8,9},{9,10},{10,1... | collective-permute-start | bytes 331784 | tf_op jit(solution)/shard_map/ppermute | solution.py:378
  43.2 7.2 %pack_second.1 = bf16[128,80,128]{2,1,0:T(8,128)(2,1)} custom-call(s32[128]{0:T(128)} %get-tuple-element.52.source_ref.second_ref, bf16[128,72,128]{2,1,0:T(8,128)(2,1)} %kernel_ref.1, s32[128,128]{1,0:T(8,128)} %columns_ref.3, bf16[128,128]{1,0:T(8,128)(2,1)} %observed_ref.3, bf16[128,128]{1,0:T(8,128)(2,1)} %weight_ref.3, ...), custom_call_target="tpu_custom_call" | custom-call | flops 5000000 | bytes 6000000 | tf_op jit(solution)/shard_map/pack_second/pallas_call | solution.py:362
  50.4 15.0 %collective-permute-done.3.from_east.side_east = f32[3,72,128]{2,1,0:T(8,128)} collective-permute-done((f32[3,72,128]{2,1,0:T(8,128)}, f32[3,72,128]{2,1,0:T(8,128)}, u32[]{:S(2)}, u32[]{:S(2)}) %collective-permute-start.3) | collective-permute-done | bytes 110624 | tf_op jit(solution)/shard_map/ppermute | solution.py:378
  65.5 0.0 collective-permute-done.2.from_west.side_west
  65.5 1.6 all-to-all-done.1.block_ref
  67.1 6.7 %all-to-all-start = ((bf16[128,80,128]{2,1,0:T(8,128)(2,1)}), bf16[128,80,128]{2,1,0:T(8,128)(2,1)}, u32[]{:S(2)}, u32[]{:S(2)}) async-start(bf16[128,80,128]{2,1,0:T(8,128)(2,1)} %pack_second.1), calls=%async_computation | async-start | bytes 5242880 | tf_op jit(solution)/shard_map/all_to_all | solution.py:764
  73.8 6.4 %forward.1.field_hbm = bf16[1728,256]{1,0:T(8,128)(2,1)} custom-call(f32[3,8,72,128]{3,2,1,0:T(8,128)} %get-tuple-element.44.state_ref, f32[2,8,72,128]{3,2,1,0:T(8,128)} %get-tuple-element.45.east_ref, f32[2,8,72,128]{3,2,1,0:T(8,128)} %get-tuple-element.46.north_ref, f32[2,8,72,128]{3,2,1,0:T(8,128)} %get-tuple-element.47.mixing_ref, ...), custom_call_target="tpu_custom_call" | custom-call | flops 5000000 | bytes 6000000 | tf_op jit(solution)/shard_map/forward/pallas_call | solution.py:362
  80.1 18.7 %first_soundings.1 = (f32[864,256]{1,0:T(8,128)}, f32[128,128]{1,0:T(8,128)}) custom-call(bf16[1728,256]{1,0:T(8,128)(2,1)} %forward.1.field_hbm, bf16[128,80,128]{2,1,0:T(8,128)(2,1)} %all-to-all-done.1.block_ref), custom_call_target="tpu_custom_call" | custom-call | flops 15000000512 | bytes 6000000 | tf_op jit(solution)/shard_map/first_soundings/pallas_call | solution.py:362
  98.9 10.1 %all-to-all-done.block_ref = bf16[128,80,128]{2,1,0:T(8,128)(2,1)} async-done(((bf16[128,80,128]{2,1,0:T(8,128)(2,1)}), bf16[128,80,128]{2,1,0:T(8,128)(2,1)}, u32[]{:S(2)}, u32[]{:S(2)}) %all-to-all-start) | async-done | bytes 2621472 | tf_op jit(solution)/shard_map/all_to_all | solution.py:764
  109.0 19.3 %second_soundings.1 = (f32[864,256]{1,0:T(8,128)}, f32[256,128]{1,0:T(8,128)}, f32[6,72,128]{2,1,0:T(8,128)}, f32[6,72,128]{2,1,0:T(8,128)}, f32[72,128]{1,0:T(8,128)}, /*index=5*/f32[72,128]{1,0:T(8,128)}) custom-call(bf16[1728,256]{1,0:T(8,128)(2,1)} %forward.1.field_hbm, bf16[128,80,128]{2,1,0:T(8,128)(2,1)} %all-to-all-done.block_ref, ...), custom_call_target="tpu_custom_call" | custom-call | flops 15000000512 | bytes 6000000 | tf_op jit(solution)/shard_map/second_soundings/pallas_call | solution.py:362
  128.3 0.1 collective-permute-start.4
  128.4 0.5 collective-permute-start.5
  128.9 0.9 collective-permute-done.4.from_west
  129.8 0.0 copy-start
  129.8 3.8 %collective-permute-done.5.from_east = f32[72,128]{1,0:T(8,128)S(1)} collective-permute-done((f32[72,128]{1,0:T(8,128)}, f32[72,128]{1,0:T(8,128)S(1)}, u32[]{:S(2)}, u32[]{:S(2)}) %collective-permute-start.5) | collective-permute-done | bytes 36896 | tf_op jit(solution)/shard_map/ppermute | solution.py:378
  133.6 0.0 copy-start.1
  133.6 1.1 pad_maximum_fusion
  134.7 1.3 collective-permute-start.7
  136.0 4.7 %collective-permute-start.6 = (f32[8,72,128]{2,1,0:T(8,128)S(1)}, f32[8,72,128]{2,1,0:T(8,128)}, u32[]{:S(2)}, u32[]{:S(2)}) collective-permute-start(f32[8,72,128]{2,1,0:T(8,128)S(1)} %get-tuple-element.71), channel_id=1, source_target_pairs={{0,16},{16,32},{32,48},{48,64},{64,80},{80,96},{96,112},{1,17},{17... | collective-permute-start | bytes 884744 | tf_op jit(solution)/shard_map/ppermute | solution.py:381
  140.7 0.0 copy-done
  140.7 0.0 copy-done.1
  140.7 10.5 %all-to-all-start.2 = ((f32[128,2,128]{2,1,0:T(2,128)}), f32[128,2,128]{2,1,0:T(2,128)}, u32[]{:S(2)}, u32[]{:S(2)}) async-start(f32[128,2,128]{2,1,0:T(2,128)} %bitcast.8), calls=%async_computation.2 | async-start | bytes 262144 | tf_op jit(solution)/shard_map/all_to_all | solution.py:764
  151.3 0.0 collective-permute-done.7.down_ref
  151.3 0.0 collective-permute-done.6.up_ref
  151.3 6.4 %adjoint.1 = f32[3,72,8,128]{3,2,1,0:T(8,128)} custom-call(f32[864,256]{1,0:T(8,128)} %get-tuple-element.62.adjoint_ref, f32[2,8,72,128]{3,2,1,0:T(8,128)} %get-tuple-element.45.east_ref, f32[2,8,72,128]{3,2,1,0:T(8,128)} %get-tuple-element.46.north_ref, f32[2,8,72,128]{3,2,1,0:T(8,128)} %get-tuple-element.47.mixing_ref, ...), custom_call_target="tpu_custom_call" | custom-call | flops 5000000 | bytes 6000000 | tf_op jit(solution)/shard_map/adjoint/pallas_call | solution.py:362
  157.7 3.5 %all-to-all-done.2 = f32[128,2,128]{2,1,0:T(2,128)} async-done(((f32[128,2,128]{2,1,0:T(2,128)}), f32[128,2,128]{2,1,0:T(2,128)}, u32[]{:S(2)}, u32[]{:S(2)}) %all-to-all-start.2) | async-done | bytes 131104 | tf_op jit(solution)/shard_map/all_to_all | solution.py:764
  161.2 2.1 %innovations.1 = f32[128,128]{1,0:T(8,128)} custom-call(s32[128]{0:T(128)} %get-tuple-element.68.first_ref, s32[128]{0:T(128)} %get-tuple-element.52.source_ref.second_ref, f32[256,128]{1,0:T(8,128)} %bitcast.3.returned_ref, f32[128,128]{1,0:T(8,128)} %get-tuple-element.53.place_ref), custom_call_target="tpu_custom_call" | custom-call | flops 5000000 | bytes 6000000 | tf_op jit(solution)/shard_map/innovations/pallas_call | solution.py:362
Async XLA Ops:
  4.4 15.7 %collective-permute-start = (bf16[19,72,128]{2,1,0:T(8,128)(2,1)}, bf16[19,72,128]{2,1,0:T(8,128)(2,1)}, u32[]{:S(2)}, u32[]{:S(2)}) collective-permute-start(bf16[19,72,128]{2,1,0:T(8,128)(2,1)} %get-tuple-element.40), channel_id=1, source_target_pairs={{0,16},{16,32},{32,48},{48,64},{64,80},{80,96},{96,112},{1,17},{17... | collective-permute-start | bytes 1050632 | tf_op jit(solution)/shard_map/ppermute | solution.py:381
  9.5 10.5 %collective-permute-start.1 = (bf16[15,72,128]{2,1,0:T(8,128)(2,1)}, bf16[15,72,128]{2,1,0:T(8,128)(2,1)}, u32[]{:S(2)}, u32[]{:S(2)}) collective-permute-start(bf16[15,72,128]{2,1,0:T(8,128)(2,1)} %get-tuple-element.41), channel_id=1, source_target_pairs={{16,0},{32,16},{48,32},{64,48},{80,64},{96,80},{112,96},{17,1},{33... | collective-permute-start | bytes 829448 | tf_op jit(solution)/shard_map/ppermute | solution.py:381
  20.1 47.0 %all-to-all-start.1 = ((bf16[128,80,128]{2,1,0:T(8,128)(2,1)}), bf16[128,80,128]{2,1,0:T(8,128)(2,1)}, u32[]{:S(2)}, u32[]{:S(2)}) async-start(bf16[128,80,128]{2,1,0:T(8,128)(2,1)} %get-tuple-element.58), calls=%async_computation.1 | async-start | bytes 5242880 | tf_op jit(solution)/shard_map/all_to_all | solution.py:764
  39.9 25.5 %collective-permute-start.3 = (f32[3,72,128]{2,1,0:T(8,128)}, f32[3,72,128]{2,1,0:T(8,128)}, u32[]{:S(2)}, u32[]{:S(2)}) collective-permute-start(f32[3,72,128]{2,1,0:T(8,128)} %get-tuple-element.49.own_west), channel_id=1, source_target_pairs={{0,15},{1,0},{2,1},{3,2},{4,3},{5,4},{6,5},{7,6},{8,7},{9,8},{10,9... | collective-permute-start | bytes 331784 | tf_op jit(solution)/shard_map/ppermute | solution.py:378
  41.1 24.4 %collective-permute-start.2 = (f32[3,72,128]{2,1,0:T(8,128)}, f32[3,72,128]{2,1,0:T(8,128)}, u32[]{:S(2)}, u32[]{:S(2)}) collective-permute-start(f32[3,72,128]{2,1,0:T(8,128)} %get-tuple-element.48.own_east.wind_east), channel_id=1, source_target_pairs={{0,1},{1,2},{2,3},{3,4},{4,5},{5,6},{6,7},{7,8},{8,9},{9,10},{10,1... | collective-permute-start | bytes 331784 | tf_op jit(solution)/shard_map/ppermute | solution.py:378
  67.1 41.9 %all-to-all-start = ((bf16[128,80,128]{2,1,0:T(8,128)(2,1)}), bf16[128,80,128]{2,1,0:T(8,128)(2,1)}, u32[]{:S(2)}, u32[]{:S(2)}) async-start(bf16[128,80,128]{2,1,0:T(8,128)(2,1)} %pack_second.1), calls=%async_computation | async-start | bytes 5242880 | tf_op jit(solution)/shard_map/all_to_all | solution.py:764
  128.3 1.5 collective-permute-start.4
  128.4 5.2 %collective-permute-start.5 = (f32[72,128]{1,0:T(8,128)}, f32[72,128]{1,0:T(8,128)S(1)}, u32[]{:S(2)}, u32[]{:S(2)}) collective-permute-start(f32[72,128]{1,0:T(8,128)} %get-tuple-element.64.own_west), channel_id=1, source_target_pairs={{0,15},{1,0},{2,1},{3,2},{4,3},{5,4},{6,5},{7,6},{8,7},{9,8},{10,9... | collective-permute-start | bytes 110600 | tf_op jit(solution)/shard_map/ppermute | solution.py:378
  129.8 10.9 %copy-start = (f32[72,128]{1,0:T(8,128)}, f32[72,128]{1,0:T(8,128)S(1)}, u32[]{:S(2)}) copy-start(f32[72,128]{1,0:T(8,128)S(1)} %collective-permute-done.4.from_west) | copy-start | bytes 110596
  133.6 7.1 %copy-start.1 = (f32[72,128]{1,0:T(8,128)}, f32[72,128]{1,0:T(8,128)S(1)}, u32[]{:S(2)}) copy-start(f32[72,128]{1,0:T(8,128)S(1)} %collective-permute-done.5.from_east) | copy-start | bytes 110596
  134.7 16.6 %collective-permute-start.7 = (f32[8,72,128]{2,1,0:T(8,128)S(1)}, f32[8,72,128]{2,1,0:T(8,128)}, u32[]{:S(2)}, u32[]{:S(2)}) collective-permute-start(f32[8,72,128]{2,1,0:T(8,128)S(1)} %get-tuple-element.70), channel_id=1, source_target_pairs={{16,0},{32,16},{48,32},{64,48},{80,64},{96,80},{112,96},{17,1},{33... | collective-permute-start | bytes 884744 | tf_op jit(solution)/shard_map/ppermute | solution.py:381
  136.0 15.3 %collective-permute-start.6 = (f32[8,72,128]{2,1,0:T(8,128)S(1)}, f32[8,72,128]{2,1,0:T(8,128)}, u32[]{:S(2)}, u32[]{:S(2)}) collective-permute-start(f32[8,72,128]{2,1,0:T(8,128)S(1)} %get-tuple-element.71), channel_id=1, source_target_pairs={{0,16},{16,32},{32,48},{48,64},{64,80},{80,96},{96,112},{1,17},{17... | collective-permute-start | bytes 884744 | tf_op jit(solution)/shard_map/ppermute | solution.py:381
  140.7 20.5 %all-to-all-start.2 = ((f32[128,2,128]{2,1,0:T(2,128)}), f32[128,2,128]{2,1,0:T(2,128)}, u32[]{:S(2)}, u32[]{:S(2)}) async-start(f32[128,2,128]{2,1,0:T(2,128)} %bitcast.8), calls=%async_computation.2 | async-start | bytes 262144 | tf_op jit(solution)/shard_map/all_to_all | solution.py:764

commit v9 on v8

--- a/solution.py
+++ b/solution.py
@@ -440,10 +440,10 @@
         tally_ref[pl.ds(eight * 8, 8), :] = tallies
         return carry
 
-    lax.fori_loop(0, targets_ref.shape[0] // 8, rank, 0, unroll=2)
-
-
-TOGETHER = 16
+    lax.fori_loop(0, targets_ref.shape[0] // 8, rank, 0, unroll=4)
+
+
+TOGETHER = 32
 
 
 def widen(observed_ref, weight_ref, observed_wide, weight_wide, order_ref):
@@ -564,7 +564,7 @@
         tally_ref[pl.ds(eight * 8, 8), :] = rows.astype(jnp.int32)
         return carry
 
-    lax.fori_loop(0, block_ref.shape[0] // 8, tally, 0, unroll=2)
+    lax.fori_loop(0, block_ref.shape[0] // 8, tally, 0, unroll=4)
     copy = pltpu.make_async_copy(tally_ref, count_ref, sem)
     copy.start()
     copy.wait()

time: 165 us -> 161 us (0.976); the launches traced: 163 us -> 161 us
  Pallas kernels: 81.2 us -> 71.7 us
  starting transfers between devices: 45.2 us -> 49.6 us
  waiting for transfers between devices: 35 us -> 38 us
    pallas_call x9, Pallas kernels: 81.2 us -> 71.7 us  [whole(): pl.pallas_call(body, grid=(steps,), in_specs=[spec(i, array) for i, array...]
    all_to_all x3, starting transfers between devices: 29 us -> 31.5 us  [exchange(): lax.all_to_all(array, ('lat', 'lon'), split_axis=0, concat_axis=0, tiled=...]
    ppermute x4, starting transfers between devices: 3.82 us -> 5.64 us  [shifted(): lax.ppermute(array, 'lon', [(j, (j + lon_by) % lon) for j in range(lon)])]
  transfers between devices with their start and end apart: 11 -> 11, of which waited for: 6 -> 7; matrix products, arithmetic and copies ran while one was open for 0% -> 0% of each run, Pallas kernels for 34% -> 32%
where the time goes in v9:
time: 161 us
  Pallas kernels  71.7 us (45%)
  starting transfers between devices  49.6 us (31%)
  waiting for transfers between devices  38 us (24%)
    pallas_call x9, Pallas kernels, whole(): pl.pallas_call(body, grid=(steps,), in_specs=[spec(i, array) for i, array...  71.7 us
    all_to_all x3, starting transfers between devices, exchange(): lax.all_to_all(array, ('lat', 'lon'), split_axis=0, concat_axis=0, tiled=...  31.5 us
    ppermute x4, waiting for transfers between devices, shifted(): lax.ppermute(array, 'lon', [(j, (j + lon_by) % lon) for j in range(lon)])  20.7 us
    all_to_all x3, waiting for transfers between devices, exchange(): lax.all_to_all(array, ('lat', 'lon'), split_axis=0, concat_axis=0, tiled=...  16.7 us
    ppermute x4, starting transfers between devices, shifted(): return lax.ppermute(array, 'lat', rows)  12.4 us
    ppermute x4, starting transfers between devices, shifted(): lax.ppermute(array, 'lon', [(j, (j + lon_by) % lon) for j in range(lon)])  5.64 us
  transfers between devices with their start and end apart: 11, of which 7 were waited for; matrix products, arithmetic and copies ran while one was open for 0% of the time, Pallas kernels for 32%

profile of v9, /device:TPU:1, one launch (start us, length us, event | category | flops | bytes accessed | tf_op | source)
XLA Modules:
  0.0 161.1 jit_solution(17561241860944033900)
XLA Ops:
  0.6 3.8 %rows.1 = (bf16[19,72,128]{2,1,0:T(8,128)(2,1)}, bf16[15,72,128]{2,1,0:T(8,128)(2,1)}) custom-call(s32[1]{0:T(128)} %bitcast.last_ref, f32[3,72,8,128]{3,2,1,0:T(8,128)} %initial_ref.3, f32[2,72,8,128]{3,2,1,0:T(8,128)} %east_ref.3, f32[2,72,8,128]{3,2,1,0:T(8,128)} %north_ref.3, f32[2,72,8,128]{3,2,1,0:T(8,128)} %mixing_ref.3), custom_call_target="tpu_custom_call" | custom-call | flops 5000000 | bytes 6000000 | tf_op jit(solution)/shard_map/rows/pallas_call | solution.py:362
  4.4 5.1 %collective-permute-start = (bf16[19,72,128]{2,1,0:T(8,128)(2,1)}, bf16[19,72,128]{2,1,0:T(8,128)(2,1)}, u32[]{:S(2)}, u32[]{:S(2)}) collective-permute-start(bf16[19,72,128]{2,1,0:T(8,128)(2,1)} %get-tuple-element.40), channel_id=1, source_target_pairs={{0,16},{16,32},{32,48},{48,64},{64,80},{80,96},{96,112},{1,17},{17... | collective-permute-start | bytes 1050632 | tf_op jit(solution)/shard_map/ppermute | solution.py:381
  9.5 1.3 collective-permute-start.1
  10.8 7.6 %pack_first.1 = (bf16[128,80,128]{2,1,0:T(8,128)(2,1)}, f32[128,128]{1,0:T(8,128)}, f32[128,128]{1,0:T(8,128)}, s32[128]{0:T(128)}, s32[128]{0:T(128)}) custom-call(s32[128]{0:T(128)} %bitcast.9, s32[128]{0:T(128)} %counts_ref, bf16[128,72,128]{2,1,0:T(8,128)(2,1)} %kernel_ref.1, s32[128,128]{1,0:T(8,128)} %columns_ref.3, bf16[128,128]{1,0:T(8,128)(2,1)} %observed_ref.3, ...), custom_call_target="tpu_custom_call" | custom-call | flops 5000000 | bytes 6000000 | tf_op jit(solution)/shard_map/pack_first/pallas_call | solution.py:362
  18.4 0.5 collective-permute-done.1.down_terms
  18.9 0.0 collective-permute-done.up_terms
  18.9 12.0 %all-to-all-start.1 = ((bf16[128,80,128]{2,1,0:T(8,128)(2,1)}), bf16[128,80,128]{2,1,0:T(8,128)(2,1)}, u32[]{:S(2)}, u32[]{:S(2)}) async-start(bf16[128,80,128]{2,1,0:T(8,128)(2,1)} %get-tuple-element.58), calls=%async_computation.1 | async-start | bytes 5242880 | tf_op jit(solution)/shard_map/all_to_all | solution.py:764
  30.9 8.1 %arrange.1 = (f32[3,8,72,128]{3,2,1,0:T(8,128)}, f32[2,8,72,128]{3,2,1,0:T(8,128)}, f32[2,8,72,128]{3,2,1,0:T(8,128)}, f32[2,8,72,128]{3,2,1,0:T(8,128)}, f32[3,...) custom-call(s32[1]{0:T(128)} %bitcast.last_ref, ...), custom_call_target="tpu_custom_call" | custom-call | flops 5000000 | bytes 6000000 | tf_op jit(solution)/shard_map/arrange/pallas_call | solution.py:362
  39.0 1.1 collective-permute-start.3
  40.1 2.1 %collective-permute-start.2 = (f32[3,72,128]{2,1,0:T(8,128)}, f32[3,72,128]{2,1,0:T(8,128)}, u32[]{:S(2)}, u32[]{:S(2)}) collective-permute-start(f32[3,72,128]{2,1,0:T(8,128)} %get-tuple-element.48.own_east.wind_east), channel_id=1, source_target_pairs={{0,1},{1,2},{2,3},{3,4},{4,5},{5,6},{6,7},{7,8},{8,9},{9,10},{10,1... | collective-permute-start | bytes 331784 | tf_op jit(solution)/shard_map/ppermute | solution.py:378
  42.3 6.7 %pack_second.1 = bf16[128,80,128]{2,1,0:T(8,128)(2,1)} custom-call(s32[128]{0:T(128)} %get-tuple-element.52.source_ref.second_ref, bf16[128,72,128]{2,1,0:T(8,128)(2,1)} %kernel_ref.1, s32[128,128]{1,0:T(8,128)} %columns_ref.3, bf16[128,128]{1,0:T(8,128)(2,1)} %observed_ref.3, bf16[128,128]{1,0:T(8,128)(2,1)} %weight_ref.3, ...), custom_call_target="tpu_custom_call" | custom-call | flops 5000000 | bytes 6000000 | tf_op jit(solution)/shard_map/pack_second/pallas_call | solution.py:362
  48.9 15.6 %collective-permute-done.3.from_east.side_east = f32[3,72,128]{2,1,0:T(8,128)} collective-permute-done((f32[3,72,128]{2,1,0:T(8,128)}, f32[3,72,128]{2,1,0:T(8,128)}, u32[]{:S(2)}, u32[]{:S(2)}) %collective-permute-start.3) | collective-permute-done | bytes 110624 | tf_op jit(solution)/shard_map/ppermute | solution.py:378
  64.5 0.0 collective-permute-done.2.from_west.side_west
  64.5 1.6 all-to-all-done.1.block_ref
  66.1 6.7 %all-to-all-start = ((bf16[128,80,128]{2,1,0:T(8,128)(2,1)}), bf16[128,80,128]{2,1,0:T(8,128)(2,1)}, u32[]{:S(2)}, u32[]{:S(2)}) async-start(bf16[128,80,128]{2,1,0:T(8,128)(2,1)} %pack_second.1), calls=%async_computation | async-start | bytes 5242880 | tf_op jit(solution)/shard_map/all_to_all | solution.py:764
  72.8 6.4 %forward.1.field_hbm = bf16[1728,256]{1,0:T(8,128)(2,1)} custom-call(f32[3,8,72,128]{3,2,1,0:T(8,128)} %get-tuple-element.44.state_ref, f32[2,8,72,128]{3,2,1,0:T(8,128)} %get-tuple-element.45.east_ref, f32[2,8,72,128]{3,2,1,0:T(8,128)} %get-tuple-element.46.north_ref, f32[2,8,72,128]{3,2,1,0:T(8,128)} %get-tuple-element.47.mixing_ref, ...), custom_call_target="tpu_custom_call" | custom-call | flops 5000000 | bytes 6000000 | tf_op jit(solution)/shard_map/forward/pallas_call | solution.py:362
  79.2 17.2 %first_soundings.1 = (f32[864,256]{1,0:T(8,128)}, f32[128,128]{1,0:T(8,128)}) custom-call(bf16[1728,256]{1,0:T(8,128)(2,1)} %forward.1.field_hbm, bf16[128,80,128]{2,1,0:T(8,128)(2,1)} %all-to-all-done.1.block_ref), custom_call_target="tpu_custom_call" | custom-call | flops 15000000512 | bytes 6000000 | tf_op jit(solution)/shard_map/first_soundings/pallas_call | solution.py:362
  96.4 11.6 %all-to-all-done.block_ref = bf16[128,80,128]{2,1,0:T(8,128)(2,1)} async-done(((bf16[128,80,128]{2,1,0:T(8,128)(2,1)}), bf16[128,80,128]{2,1,0:T(8,128)(2,1)}, u32[]{:S(2)}, u32[]{:S(2)}) %all-to-all-start) | async-done | bytes 2621472 | tf_op jit(solution)/shard_map/all_to_all | solution.py:764
  108.1 13.6 %second_soundings.1 = (f32[864,256]{1,0:T(8,128)}, f32[256,128]{1,0:T(8,128)}, f32[6,72,128]{2,1,0:T(8,128)}, f32[6,72,128]{2,1,0:T(8,128)}, f32[72,128]{1,0:T(8,128)}, /*index=5*/f32[72,128]{1,0:T(8,128)}) custom-call(bf16[1728,256]{1,0:T(8,128)(2,1)} %forward.1.field_hbm, bf16[128,80,128]{2,1,0:T(8,128)(2,1)} %all-to-all-done.block_ref, ...), custom_call_target="tpu_custom_call" | custom-call | flops 15000000512 | bytes 6000000 | tf_op jit(solution)/shard_map/second_soundings/pallas_call | solution.py:362
  121.7 2.4 %collective-permute-start.4 = (f32[72,128]{1,0:T(8,128)}, f32[72,128]{1,0:T(8,128)S(1)}, u32[]{:S(2)}, u32[]{:S(2)}) collective-permute-start(f32[72,128]{1,0:T(8,128)} %get-tuple-element.63.own_east), channel_id=1, source_target_pairs={{0,1},{1,2},{2,3},{3,4},{4,5},{5,6},{6,7},{7,8},{8,9},{9,10},{10,1... | collective-permute-start | bytes 110600 | tf_op jit(solution)/shard_map/ppermute | solution.py:378
  124.1 0.0 collective-permute-start.5
  124.1 1.4 collective-permute-done.4.from_west
  125.5 0.0 copy-start
  125.5 3.7 %collective-permute-done.5.from_east = f32[72,128]{1,0:T(8,128)S(1)} collective-permute-done((f32[72,128]{1,0:T(8,128)}, f32[72,128]{1,0:T(8,128)S(1)}, u32[]{:S(2)}, u32[]{:S(2)}) %collective-permute-start.5) | collective-permute-done | bytes 36896 | tf_op jit(solution)/shard_map/ppermute | solution.py:378
  129.2 0.0 copy-start.1
  129.2 1.1 pad_maximum_fusion
  130.3 1.3 collective-permute-start.7
  131.6 4.7 %collective-permute-start.6 = (f32[8,72,128]{2,1,0:T(8,128)S(1)}, f32[8,72,128]{2,1,0:T(8,128)}, u32[]{:S(2)}, u32[]{:S(2)}) collective-permute-start(f32[8,72,128]{2,1,0:T(8,128)S(1)} %get-tuple-element.71), channel_id=1, source_target_pairs={{0,16},{16,32},{32,48},{48,64},{64,80},{80,96},{96,112},{1,17},{17... | collective-permute-start | bytes 884744 | tf_op jit(solution)/shard_map/ppermute | solution.py:381
  136.3 0.0 copy-done
  136.3 0.0 copy-done.1
  136.3 12.8 %all-to-all-start.2 = ((f32[128,2,128]{2,1,0:T(2,128)}), f32[128,2,128]{2,1,0:T(2,128)}, u32[]{:S(2)}, u32[]{:S(2)}) async-start(f32[128,2,128]{2,1,0:T(2,128)} %bitcast.8), calls=%async_computation.2 | async-start | bytes 262144 | tf_op jit(solution)/shard_map/all_to_all | solution.py:764
  149.1 0.0 collective-permute-done.7.down_ref
  149.1 0.0 collective-permute-done.6.up_ref
  149.1 6.4 %adjoint.1 = f32[3,72,8,128]{3,2,1,0:T(8,128)} custom-call(f32[864,256]{1,0:T(8,128)} %get-tuple-element.62.adjoint_ref, f32[2,8,72,128]{3,2,1,0:T(8,128)} %get-tuple-element.45.east_ref, f32[2,8,72,128]{3,2,1,0:T(8,128)} %get-tuple-element.46.north_ref, f32[2,8,72,128]{3,2,1,0:T(8,128)} %get-tuple-element.47.mixing_ref, ...), custom_call_target="tpu_custom_call" | custom-call | flops 5000000 | bytes 6000000 | tf_op jit(solution)/shard_map/adjoint/pallas_call | solution.py:362
  155.5 3.5 %all-to-all-done.2 = f32[128,2,128]{2,1,0:T(2,128)} async-done(((f32[128,2,128]{2,1,0:T(2,128)}), f32[128,2,128]{2,1,0:T(2,128)}, u32[]{:S(2)}, u32[]{:S(2)}) %all-to-all-start.2) | async-done | bytes 131104 | tf_op jit(solution)/shard_map/all_to_all | solution.py:764
  159.0 2.1 %innovations.1 = f32[128,128]{1,0:T(8,128)} custom-call(s32[128]{0:T(128)} %get-tuple-element.68.first_ref, s32[128]{0:T(128)} %get-tuple-element.52.source_ref.second_ref, f32[256,128]{1,0:T(8,128)} %bitcast.3.returned_ref, f32[128,128]{1,0:T(8,128)} %get-tuple-element.53.place_ref), custom_call_target="tpu_custom_call" | custom-call | flops 5000000 | bytes 6000000 | tf_op jit(solution)/shard_map/innovations/pallas_call | solution.py:362
Async XLA Ops:
  4.4 14.5 %collective-permute-start = (bf16[19,72,128]{2,1,0:T(8,128)(2,1)}, bf16[19,72,128]{2,1,0:T(8,128)(2,1)}, u32[]{:S(2)}, u32[]{:S(2)}) collective-permute-start(bf16[19,72,128]{2,1,0:T(8,128)(2,1)} %get-tuple-element.40), channel_id=1, source_target_pairs={{0,16},{16,32},{32,48},{48,64},{64,80},{80,96},{96,112},{1,17},{17... | collective-permute-start | bytes 1050632 | tf_op jit(solution)/shard_map/ppermute | solution.py:381
  9.5 9.4 %collective-permute-start.1 = (bf16[15,72,128]{2,1,0:T(8,128)(2,1)}, bf16[15,72,128]{2,1,0:T(8,128)(2,1)}, u32[]{:S(2)}, u32[]{:S(2)}) collective-permute-start(bf16[15,72,128]{2,1,0:T(8,128)(2,1)} %get-tuple-element.41), channel_id=1, source_target_pairs={{16,0},{32,16},{48,32},{64,48},{80,64},{96,80},{112,96},{17,1},{33... | collective-permute-start | bytes 829448 | tf_op jit(solution)/shard_map/ppermute | solution.py:381
  18.9 47.3 %all-to-all-start.1 = ((bf16[128,80,128]{2,1,0:T(8,128)(2,1)}), bf16[128,80,128]{2,1,0:T(8,128)(2,1)}, u32[]{:S(2)}, u32[]{:S(2)}) async-start(bf16[128,80,128]{2,1,0:T(8,128)(2,1)} %get-tuple-element.58), calls=%async_computation.1 | async-start | bytes 5242880 | tf_op jit(solution)/shard_map/all_to_all | solution.py:764
  39.0 25.5 %collective-permute-start.3 = (f32[3,72,128]{2,1,0:T(8,128)}, f32[3,72,128]{2,1,0:T(8,128)}, u32[]{:S(2)}, u32[]{:S(2)}) collective-permute-start(f32[3,72,128]{2,1,0:T(8,128)} %get-tuple-element.49.own_west), channel_id=1, source_target_pairs={{0,15},{1,0},{2,1},{3,2},{4,3},{5,4},{6,5},{7,6},{8,7},{9,8},{10,9... | collective-permute-start | bytes 331784 | tf_op jit(solution)/shard_map/ppermute | solution.py:378
  40.1 24.4 %collective-permute-start.2 = (f32[3,72,128]{2,1,0:T(8,128)}, f32[3,72,128]{2,1,0:T(8,128)}, u32[]{:S(2)}, u32[]{:S(2)}) collective-permute-start(f32[3,72,128]{2,1,0:T(8,128)} %get-tuple-element.48.own_east.wind_east), channel_id=1, source_target_pairs={{0,1},{1,2},{2,3},{3,4},{4,5},{5,6},{6,7},{7,8},{8,9},{9,10},{10,1... | collective-permute-start | bytes 331784 | tf_op jit(solution)/shard_map/ppermute | solution.py:378
  66.1 41.9 %all-to-all-start = ((bf16[128,80,128]{2,1,0:T(8,128)(2,1)}), bf16[128,80,128]{2,1,0:T(8,128)(2,1)}, u32[]{:S(2)}, u32[]{:S(2)}) async-start(bf16[128,80,128]{2,1,0:T(8,128)(2,1)} %pack_second.1), calls=%async_computation | async-start | bytes 5242880 | tf_op jit(solution)/shard_map/all_to_all | solution.py:764
  121.7 3.8 %collective-permute-start.4 = (f32[72,128]{1,0:T(8,128)}, f32[72,128]{1,0:T(8,128)S(1)}, u32[]{:S(2)}, u32[]{:S(2)}) collective-permute-start(f32[72,128]{1,0:T(8,128)} %get-tuple-element.63.own_east), channel_id=1, source_target_pairs={{0,1},{1,2},{2,3},{3,4},{4,5},{5,6},{6,7},{7,8},{8,9},{9,10},{10,1... | collective-permute-start | bytes 110600 | tf_op jit(solution)/shard_map/ppermute | solution.py:378
  124.1 5.1 %collective-permute-start.5 = (f32[72,128]{1,0:T(8,128)}, f32[72,128]{1,0:T(8,128)S(1)}, u32[]{:S(2)}, u32[]{:S(2)}) collective-permute-start(f32[72,128]{1,0:T(8,128)} %get-tuple-element.64.own_west), channel_id=1, source_target_pairs={{0,15},{1,0},{2,1},{3,2},{4,3},{5,4},{6,5},{7,6},{8,7},{9,8},{10,9... | collective-permute-start | bytes 110600 | tf_op jit(solution)/shard_map/ppermute | solution.py:378
  125.5 10.8 %copy-start = (f32[72,128]{1,0:T(8,128)}, f32[72,128]{1,0:T(8,128)S(1)}, u32[]{:S(2)}) copy-start(f32[72,128]{1,0:T(8,128)S(1)} %collective-permute-done.4.from_west) | copy-start | bytes 110596
  129.2 7.1 %copy-start.1 = (f32[72,128]{1,0:T(8,128)}, f32[72,128]{1,0:T(8,128)S(1)}, u32[]{:S(2)}) copy-start(f32[72,128]{1,0:T(8,128)S(1)} %collective-permute-done.5.from_east) | copy-start | bytes 110596
  130.3 18.8 %collective-permute-start.7 = (f32[8,72,128]{2,1,0:T(8,128)S(1)}, f32[8,72,128]{2,1,0:T(8,128)}, u32[]{:S(2)}, u32[]{:S(2)}) collective-permute-start(f32[8,72,128]{2,1,0:T(8,128)S(1)} %get-tuple-element.70), channel_id=1, source_target_pairs={{16,0},{32,16},{48,32},{64,48},{80,64},{96,80},{112,96},{17,1},{33... | collective-permute-start | bytes 884744 | tf_op jit(solution)/shard_map/ppermute | solution.py:381
  131.6 17.6 %collective-permute-start.6 = (f32[8,72,128]{2,1,0:T(8,128)S(1)}, f32[8,72,128]{2,1,0:T(8,128)}, u32[]{:S(2)}, u32[]{:S(2)}) collective-permute-start(f32[8,72,128]{2,1,0:T(8,128)S(1)} %get-tuple-element.71), channel_id=1, source_target_pairs={{0,16},{16,32},{32,48},{48,64},{64,80},{80,96},{96,112},{1,17},{17... | collective-permute-start | bytes 884744 | tf_op jit(solution)/shard_map/ppermute | solution.py:381
  136.3 22.7 %all-to-all-start.2 = ((f32[128,2,128]{2,1,0:T(2,128)}), f32[128,2,128]{2,1,0:T(2,128)}, u32[]{:S(2)}, u32[]{:S(2)}) async-start(f32[128,2,128]{2,1,0:T(2,128)} %bitcast.8), calls=%async_computation.2 | async-start | bytes 262144 | tf_op jit(solution)/shard_map/all_to_all | solution.py:764

commit v10 on v9

--- a/solution.py
+++ b/solution.py
@@ -589,7 +589,7 @@
         block_ref.shape[0],
         merge,
         ((jnp.int32(0),) * GROUPS, (empty,) * GROUPS),
-        unroll=8,
+        unroll=16,
     )
     for g in range(GROUPS):
         tile, at = lax.shift_right_logical(ends[g], 7), ends[g] & (LANES - 1)
@@ -686,7 +686,7 @@
         write_misfit(eight, rows)
         return tuple(ends)
 
-    lax.fori_loop(0, block_ref.shape[0] // 8, part_ways, (jnp.int32(0),) * GROUPS, unroll=2)
+    lax.fori_loop(0, block_ref.shape[0] // 8, part_ways, (jnp.int32(0),) * GROUPS, unroll=4)
 
 
 def first_soundings_body(

time: 161 us -> 162 us (level)
  transfers between devices with their start and end apart: 11 -> 11, of which waited for: 7 -> 7; matrix products, arithmetic and copies ran while one was open for 0% -> 0% of each run, Pallas kernels for 32% -> 33%
where the time goes in v10:
time: 162 us; the launch traced here: 161 us
  Pallas kernels  71.2 us (44%)
  starting transfers between devices  49.8 us (31%)
  waiting for transfers between devices  37.9 us (23%)
    pallas_call x9, Pallas kernels, whole(): pl.pallas_call(body, grid=(steps,), in_specs=[spec(i, array) for i, array...  71.2 us
    all_to_all x3, starting transfers between devices, exchange(): lax.all_to_all(array, ('lat', 'lon'), split_axis=0, concat_axis=0, tiled=...  30.1 us
    ppermute x4, waiting for transfers between devices, shifted(): lax.ppermute(array, 'lon', [(j, (j + lon_by) % lon) for j in range(lon)])  20.7 us
    all_to_all x3, waiting for transfers between devices, exchange(): lax.all_to_all(array, ('lat', 'lon'), split_axis=0, concat_axis=0, tiled=...  16.7 us
    ppermute x4, starting transfers between devices, shifted(): return lax.ppermute(array, 'lat', rows)  14 us
    ppermute x4, starting transfers between devices, shifted(): lax.ppermute(array, 'lon', [(j, (j + lon_by) % lon) for j in range(lon)])  5.64 us
  transfers between devices with their start and end apart: 11, of which 7 were waited for; matrix products, arithmetic and copies ran while one was open for 0% of the time, Pallas kernels for 33%

profile of v10, /device:TPU:1, one launch (start us, length us, event | category | flops | bytes accessed | tf_op | source)
XLA Modules:
  0.0 160.7 jit_solution(12570227505008096402)
XLA Ops:
  0.6 3.8 %rows.1 = (bf16[19,72,128]{2,1,0:T(8,128)(2,1)}, bf16[15,72,128]{2,1,0:T(8,128)(2,1)}) custom-call(s32[1]{0:T(128)} %bitcast.last_ref, f32[3,72,8,128]{3,2,1,0:T(8,128)} %initial_ref.3, f32[2,72,8,128]{3,2,1,0:T(8,128)} %east_ref.3, f32[2,72,8,128]{3,2,1,0:T(8,128)} %north_ref.3, f32[2,72,8,128]{3,2,1,0:T(8,128)} %mixing_ref.3), custom_call_target="tpu_custom_call" | custom-call | flops 5000000 | bytes 6000000 | tf_op jit(solution)/shard_map/rows/pallas_call | solution.py:362
  4.4 5.1 %collective-permute-start = (bf16[19,72,128]{2,1,0:T(8,128)(2,1)}, bf16[19,72,128]{2,1,0:T(8,128)(2,1)}, u32[]{:S(2)}, u32[]{:S(2)}) collective-permute-start(bf16[19,72,128]{2,1,0:T(8,128)(2,1)} %get-tuple-element.40), channel_id=1, source_target_pairs={{0,16},{16,32},{32,48},{48,64},{64,80},{80,96},{96,112},{1,17},{17... | collective-permute-start | bytes 1050632 | tf_op jit(solution)/shard_map/ppermute | solution.py:381
  9.5 1.3 collective-permute-start.1
  10.8 7.6 %pack_first.1 = (bf16[128,80,128]{2,1,0:T(8,128)(2,1)}, f32[128,128]{1,0:T(8,128)}, f32[128,128]{1,0:T(8,128)}, s32[128]{0:T(128)}, s32[128]{0:T(128)}) custom-call(s32[128]{0:T(128)} %bitcast.9, s32[128]{0:T(128)} %counts_ref, bf16[128,72,128]{2,1,0:T(8,128)(2,1)} %kernel_ref.1, s32[128,128]{1,0:T(8,128)} %columns_ref.3, bf16[128,128]{1,0:T(8,128)(2,1)} %observed_ref.3, ...), custom_call_target="tpu_custom_call" | custom-call | flops 5000000 | bytes 6000000 | tf_op jit(solution)/shard_map/pack_first/pallas_call | solution.py:362
  18.4 0.5 collective-permute-done.1.down_terms
  18.9 0.0 collective-permute-done.up_terms
  18.9 12.0 %all-to-all-start.1 = ((bf16[128,80,128]{2,1,0:T(8,128)(2,1)}), bf16[128,80,128]{2,1,0:T(8,128)(2,1)}, u32[]{:S(2)}, u32[]{:S(2)}) async-start(bf16[128,80,128]{2,1,0:T(8,128)(2,1)} %get-tuple-element.58), calls=%async_computation.1 | async-start | bytes 5242880 | tf_op jit(solution)/shard_map/all_to_all | solution.py:764
  30.9 8.1 %arrange.1 = (f32[3,8,72,128]{3,2,1,0:T(8,128)}, f32[2,8,72,128]{3,2,1,0:T(8,128)}, f32[2,8,72,128]{3,2,1,0:T(8,128)}, f32[2,8,72,128]{3,2,1,0:T(8,128)}, f32[3,...) custom-call(s32[1]{0:T(128)} %bitcast.last_ref, ...), custom_call_target="tpu_custom_call" | custom-call | flops 5000000 | bytes 6000000 | tf_op jit(solution)/shard_map/arrange/pallas_call | solution.py:362
  39.0 1.1 collective-permute-start.3
  40.1 2.1 %collective-permute-start.2 = (f32[3,72,128]{2,1,0:T(8,128)}, f32[3,72,128]{2,1,0:T(8,128)}, u32[]{:S(2)}, u32[]{:S(2)}) collective-permute-start(f32[3,72,128]{2,1,0:T(8,128)} %get-tuple-element.48.own_east.wind_east), channel_id=1, source_target_pairs={{0,1},{1,2},{2,3},{3,4},{4,5},{5,6},{6,7},{7,8},{8,9},{9,10},{10,1... | collective-permute-start | bytes 331784 | tf_op jit(solution)/shard_map/ppermute | solution.py:378
  42.3 6.7 %pack_second.1 = bf16[128,80,128]{2,1,0:T(8,128)(2,1)} custom-call(s32[128]{0:T(128)} %get-tuple-element.52.source_ref.second_ref, bf16[128,72,128]{2,1,0:T(8,128)(2,1)} %kernel_ref.1, s32[128,128]{1,0:T(8,128)} %columns_ref.3, bf16[128,128]{1,0:T(8,128)(2,1)} %observed_ref.3, bf16[128,128]{1,0:T(8,128)(2,1)} %weight_ref.3, ...), custom_call_target="tpu_custom_call" | custom-call | flops 5000000 | bytes 6000000 | tf_op jit(solution)/shard_map/pack_second/pallas_call | solution.py:362
  48.9 15.6 %collective-permute-done.3.from_east.side_east = f32[3,72,128]{2,1,0:T(8,128)} collective-permute-done((f32[3,72,128]{2,1,0:T(8,128)}, f32[3,72,128]{2,1,0:T(8,128)}, u32[]{:S(2)}, u32[]{:S(2)}) %collective-permute-start.3) | collective-permute-done | bytes 110624 | tf_op jit(solution)/shard_map/ppermute | solution.py:378
  64.5 0.0 collective-permute-done.2.from_west.side_west
  64.5 1.6 all-to-all-done.1.block_ref
  66.1 6.7 %all-to-all-start = ((bf16[128,80,128]{2,1,0:T(8,128)(2,1)}), bf16[128,80,128]{2,1,0:T(8,128)(2,1)}, u32[]{:S(2)}, u32[]{:S(2)}) async-start(bf16[128,80,128]{2,1,0:T(8,128)(2,1)} %pack_second.1), calls=%async_computation | async-start | bytes 5242880 | tf_op jit(solution)/shard_map/all_to_all | solution.py:764
  72.8 6.4 %forward.1.field_hbm = bf16[1728,256]{1,0:T(8,128)(2,1)} custom-call(f32[3,8,72,128]{3,2,1,0:T(8,128)} %get-tuple-element.44.state_ref, f32[2,8,72,128]{3,2,1,0:T(8,128)} %get-tuple-element.45.east_ref, f32[2,8,72,128]{3,2,1,0:T(8,128)} %get-tuple-element.46.north_ref, f32[2,8,72,128]{3,2,1,0:T(8,128)} %get-tuple-element.47.mixing_ref, ...), custom_call_target="tpu_custom_call" | custom-call | flops 5000000 | bytes 6000000 | tf_op jit(solution)/shard_map/forward/pallas_call | solution.py:362
  79.2 17.3 %first_soundings.1 = (f32[864,256]{1,0:T(8,128)}, f32[128,128]{1,0:T(8,128)}) custom-call(bf16[1728,256]{1,0:T(8,128)(2,1)} %forward.1.field_hbm, bf16[128,80,128]{2,1,0:T(8,128)(2,1)} %all-to-all-done.1.block_ref), custom_call_target="tpu_custom_call" | custom-call | flops 15000000512 | bytes 6000000 | tf_op jit(solution)/shard_map/first_soundings/pallas_call | solution.py:362
  96.5 11.6 %all-to-all-done.block_ref = bf16[128,80,128]{2,1,0:T(8,128)(2,1)} async-done(((bf16[128,80,128]{2,1,0:T(8,128)(2,1)}), bf16[128,80,128]{2,1,0:T(8,128)(2,1)}, u32[]{:S(2)}, u32[]{:S(2)}) %all-to-all-start) | async-done | bytes 2621472 | tf_op jit(solution)/shard_map/all_to_all | solution.py:764
  108.1 13.0 %second_soundings.1 = (f32[864,256]{1,0:T(8,128)}, f32[256,128]{1,0:T(8,128)}, f32[6,72,128]{2,1,0:T(8,128)}, f32[6,72,128]{2,1,0:T(8,128)}, f32[72,128]{1,0:T(8,128)}, /*index=5*/f32[72,128]{1,0:T(8,128)}) custom-call(bf16[1728,256]{1,0:T(8,128)(2,1)} %forward.1.field_hbm, bf16[128,80,128]{2,1,0:T(8,128)(2,1)} %all-to-all-done.block_ref, ...), custom_call_target="tpu_custom_call" | custom-call | flops 15000000512 | bytes 6000000 | tf_op jit(solution)/shard_map/second_soundings/pallas_call | solution.py:362
  121.1 2.4 %collective-permute-start.4 = (f32[72,128]{1,0:T(8,128)}, f32[72,128]{1,0:T(8,128)S(1)}, u32[]{:S(2)}, u32[]{:S(2)}) collective-permute-start(f32[72,128]{1,0:T(8,128)} %get-tuple-element.63.own_east), channel_id=1, source_target_pairs={{0,1},{1,2},{2,3},{3,4},{4,5},{5,6},{6,7},{7,8},{8,9},{9,10},{10,1... | collective-permute-start | bytes 110600 | tf_op jit(solution)/shard_map/ppermute | solution.py:378
  123.5 0.0 collective-permute-start.5
  123.5 1.4 collective-permute-done.4.from_west
  124.8 0.0 copy-start
  124.8 3.7 %collective-permute-done.5.from_east = f32[72,128]{1,0:T(8,128)S(1)} collective-permute-done((f32[72,128]{1,0:T(8,128)}, f32[72,128]{1,0:T(8,128)S(1)}, u32[]{:S(2)}, u32[]{:S(2)}) %collective-permute-start.5) | collective-permute-done | bytes 36896 | tf_op jit(solution)/shard_map/ppermute | solution.py:378
  128.6 0.0 copy-start.1
  128.6 1.1 pad_maximum_fusion
  129.7 1.3 collective-permute-start.7
  131.0 6.3 %collective-permute-start.6 = (f32[8,72,128]{2,1,0:T(8,128)S(1)}, f32[8,72,128]{2,1,0:T(8,128)}, u32[]{:S(2)}, u32[]{:S(2)}) collective-permute-start(f32[8,72,128]{2,1,0:T(8,128)S(1)} %get-tuple-element.71), channel_id=1, source_target_pairs={{0,16},{16,32},{32,48},{48,64},{64,80},{80,96},{96,112},{1,17},{17... | collective-permute-start | bytes 884744 | tf_op jit(solution)/shard_map/ppermute | solution.py:381
  137.3 0.0 copy-done
  137.3 0.0 copy-done.1
  137.3 11.4 %all-to-all-start.2 = ((f32[128,2,128]{2,1,0:T(2,128)}), f32[128,2,128]{2,1,0:T(2,128)}, u32[]{:S(2)}, u32[]{:S(2)}) async-start(f32[128,2,128]{2,1,0:T(2,128)} %bitcast.8), calls=%async_computation.2 | async-start | bytes 262144 | tf_op jit(solution)/shard_map/all_to_all | solution.py:764
  148.7 0.0 collective-permute-done.7.down_ref
  148.7 0.0 collective-permute-done.6.up_ref
  148.7 6.4 %adjoint.1 = f32[3,72,8,128]{3,2,1,0:T(8,128)} custom-call(f32[864,256]{1,0:T(8,128)} %get-tuple-element.62.adjoint_ref, f32[2,8,72,128]{3,2,1,0:T(8,128)} %get-tuple-element.45.east_ref, f32[2,8,72,128]{3,2,1,0:T(8,128)} %get-tuple-element.46.north_ref, f32[2,8,72,128]{3,2,1,0:T(8,128)} %get-tuple-element.47.mixing_ref, ...), custom_call_target="tpu_custom_call" | custom-call | flops 5000000 | bytes 6000000 | tf_op jit(solution)/shard_map/adjoint/pallas_call | solution.py:362
  155.1 3.5 %all-to-all-done.2 = f32[128,2,128]{2,1,0:T(2,128)} async-done(((f32[128,2,128]{2,1,0:T(2,128)}), f32[128,2,128]{2,1,0:T(2,128)}, u32[]{:S(2)}, u32[]{:S(2)}) %all-to-all-start.2) | async-done | bytes 131104 | tf_op jit(solution)/shard_map/all_to_all | solution.py:764
  158.6 2.1 %innovations.1 = f32[128,128]{1,0:T(8,128)} custom-call(s32[128]{0:T(128)} %get-tuple-element.68.first_ref, s32[128]{0:T(128)} %get-tuple-element.52.source_ref.second_ref, f32[256,128]{1,0:T(8,128)} %bitcast.3.returned_ref, f32[128,128]{1,0:T(8,128)} %get-tuple-element.53.place_ref), custom_call_target="tpu_custom_call" | custom-call | flops 5000000 | bytes 6000000 | tf_op jit(solution)/shard_map/innovations/pallas_call | solution.py:362
Async XLA Ops:
  4.4 14.5 %collective-permute-start = (bf16[19,72,128]{2,1,0:T(8,128)(2,1)}, bf16[19,72,128]{2,1,0:T(8,128)(2,1)}, u32[]{:S(2)}, u32[]{:S(2)}) collective-permute-start(bf16[19,72,128]{2,1,0:T(8,128)(2,1)} %get-tuple-element.40), channel_id=1, source_target_pairs={{0,16},{16,32},{32,48},{48,64},{64,80},{80,96},{96,112},{1,17},{17... | collective-permute-start | bytes 1050632 | tf_op jit(solution)/shard_map/ppermute | solution.py:381
  9.5 9.4 %collective-permute-start.1 = (bf16[15,72,128]{2,1,0:T(8,128)(2,1)}, bf16[15,72,128]{2,1,0:T(8,128)(2,1)}, u32[]{:S(2)}, u32[]{:S(2)}) collective-permute-start(bf16[15,72,128]{2,1,0:T(8,128)(2,1)} %get-tuple-element.41), channel_id=1, source_target_pairs={{16,0},{32,16},{48,32},{64,48},{80,64},{96,80},{112,96},{17,1},{33... | collective-permute-start | bytes 829448 | tf_op jit(solution)/shard_map/ppermute | solution.py:381
  18.9 47.3 %all-to-all-start.1 = ((bf16[128,80,128]{2,1,0:T(8,128)(2,1)}), bf16[128,80,128]{2,1,0:T(8,128)(2,1)}, u32[]{:S(2)}, u32[]{:S(2)}) async-start(bf16[128,80,128]{2,1,0:T(8,128)(2,1)} %get-tuple-element.58), calls=%async_computation.1 | async-start | bytes 5242880 | tf_op jit(solution)/shard_map/all_to_all | solution.py:764
  39.0 25.5 %collective-permute-start.3 = (f32[3,72,128]{2,1,0:T(8,128)}, f32[3,72,128]{2,1,0:T(8,128)}, u32[]{:S(2)}, u32[]{:S(2)}) collective-permute-start(f32[3,72,128]{2,1,0:T(8,128)} %get-tuple-element.49.own_west), channel_id=1, source_target_pairs={{0,15},{1,0},{2,1},{3,2},{4,3},{5,4},{6,5},{7,6},{8,7},{9,8},{10,9... | collective-permute-start | bytes 331784 | tf_op jit(solution)/shard_map/ppermute | solution.py:378
  40.1 24.4 %collective-permute-start.2 = (f32[3,72,128]{2,1,0:T(8,128)}, f32[3,72,128]{2,1,0:T(8,128)}, u32[]{:S(2)}, u32[]{:S(2)}) collective-permute-start(f32[3,72,128]{2,1,0:T(8,128)} %get-tuple-element.48.own_east.wind_east), channel_id=1, source_target_pairs={{0,1},{1,2},{2,3},{3,4},{4,5},{5,6},{6,7},{7,8},{8,9},{9,10},{10,1... | collective-permute-start | bytes 331784 | tf_op jit(solution)/shard_map/ppermute | solution.py:378
  66.1 41.9 %all-to-all-start = ((bf16[128,80,128]{2,1,0:T(8,128)(2,1)}), bf16[128,80,128]{2,1,0:T(8,128)(2,1)}, u32[]{:S(2)}, u32[]{:S(2)}) async-start(bf16[128,80,128]{2,1,0:T(8,128)(2,1)} %pack_second.1), calls=%async_computation | async-start | bytes 5242880 | tf_op jit(solution)/shard_map/all_to_all | solution.py:764
  121.1 3.8 %collective-permute-start.4 = (f32[72,128]{1,0:T(8,128)}, f32[72,128]{1,0:T(8,128)S(1)}, u32[]{:S(2)}, u32[]{:S(2)}) collective-permute-start(f32[72,128]{1,0:T(8,128)} %get-tuple-element.63.own_east), channel_id=1, source_target_pairs={{0,1},{1,2},{2,3},{3,4},{4,5},{5,6},{6,7},{7,8},{8,9},{9,10},{10,1... | collective-permute-start | bytes 110600 | tf_op jit(solution)/shard_map/ppermute | solution.py:378
  123.5 5.1 %collective-permute-start.5 = (f32[72,128]{1,0:T(8,128)}, f32[72,128]{1,0:T(8,128)S(1)}, u32[]{:S(2)}, u32[]{:S(2)}) collective-permute-start(f32[72,128]{1,0:T(8,128)} %get-tuple-element.64.own_west), channel_id=1, source_target_pairs={{0,15},{1,0},{2,1},{3,2},{4,3},{5,4},{6,5},{7,6},{8,7},{9,8},{10,9... | collective-permute-start | bytes 110600 | tf_op jit(solution)/shard_map/ppermute | solution.py:378
  124.8 12.5 %copy-start = (f32[72,128]{1,0:T(8,128)}, f32[72,128]{1,0:T(8,128)S(1)}, u32[]{:S(2)}) copy-start(f32[72,128]{1,0:T(8,128)S(1)} %collective-permute-done.4.from_west) | copy-start | bytes 110596
  128.6 8.7 %copy-start.1 = (f32[72,128]{1,0:T(8,128)}, f32[72,128]{1,0:T(8,128)S(1)}, u32[]{:S(2)}) copy-start(f32[72,128]{1,0:T(8,128)S(1)} %collective-permute-done.5.from_east) | copy-start | bytes 110596
  129.7 19.1 %collective-permute-start.7 = (f32[8,72,128]{2,1,0:T(8,128)S(1)}, f32[8,72,128]{2,1,0:T(8,128)}, u32[]{:S(2)}, u32[]{:S(2)}) collective-permute-start(f32[8,72,128]{2,1,0:T(8,128)S(1)} %get-tuple-element.70), channel_id=1, source_target_pairs={{16,0},{32,16},{48,32},{64,48},{80,64},{96,80},{112,96},{17,1},{33... | collective-permute-start | bytes 884744 | tf_op jit(solution)/shard_map/ppermute | solution.py:381
  131.0 17.8 %collective-permute-start.6 = (f32[8,72,128]{2,1,0:T(8,128)S(1)}, f32[8,72,128]{2,1,0:T(8,128)}, u32[]{:S(2)}, u32[]{:S(2)}) collective-permute-start(f32[8,72,128]{2,1,0:T(8,128)S(1)} %get-tuple-element.71), channel_id=1, source_target_pairs={{0,16},{16,32},{32,48},{48,64},{64,80},{80,96},{96,112},{1,17},{17... | collective-permute-start | bytes 884744 | tf_op jit(solution)/shard_map/ppermute | solution.py:381
  137.3 21.4 %all-to-all-start.2 = ((f32[128,2,128]{2,1,0:T(2,128)}), f32[128,2,128]{2,1,0:T(2,128)}, u32[]{:S(2)}, u32[]{:S(2)}) async-start(f32[128,2,128]{2,1,0:T(2,128)} %bitcast.8), calls=%async_computation.2 | async-start | bytes 262144 | tf_op jit(solution)/shard_map/all_to_all | solution.py:764

commit v11 on v10

--- a/solution.py
+++ b/solution.py
@@ -440,7 +440,7 @@
         tally_ref[pl.ds(eight * 8, 8), :] = tallies
         return carry
 
-    lax.fori_loop(0, targets_ref.shape[0] // 8, rank, 0, unroll=4)
+    lax.fori_loop(0, targets_ref.shape[0] // 8, rank, 0, unroll=8)
 
 
 TOGETHER = 32
@@ -534,7 +534,7 @@
             rows_ref[pl.ds(block, 1), :] = returned_ref[pl.ds(2 * device + rank, 1), :]
         return carry
 
-    lax.fori_loop(0, first_ref.shape[0], one, 0, unroll=8)
+    lax.fori_loop(0, first_ref.shape[0], one, 0, unroll=32)
     place = place_ref[...].astype(jnp.int32)
     live = place < LANES
     found = jnp.take_along_axis(
@@ -564,7 +564,7 @@
         tally_ref[pl.ds(eight * 8, 8), :] = rows.astype(jnp.int32)
         return carry
 
-    lax.fori_loop(0, block_ref.shape[0] // 8, tally, 0, unroll=4)
+    lax.fori_loop(0, block_ref.shape[0] // 8, tally, 0, unroll=8)
     copy = pltpu.make_async_copy(tally_ref, count_ref, sem)
     copy.start()
     copy.wait()

time: 162 us -> 162 us (level)
  waiting for transfers between devices: 37.9 us -> 33.1 us
  starting transfers between devices: 49.8 us -> 53.5 us
    ppermute x4, starting transfers between devices: 5.64 us -> 9.7 us  [shifted(): lax.ppermute(array, 'lon', [(j, (j + lon_by) % lon) for j in range(lon)])]
    ppermute x4, waiting for transfers between devices: 20.7 us -> 16.7 us  [shifted(): lax.ppermute(array, 'lon', [(j, (j + lon_by) % lon) for j in range(lon)])]
where the time goes in v11:
time: 162 us; the launch traced here: 160 us
  Pallas kernels  71.8 us (44%)
  starting transfers between devices  53.5 us (33%)
  waiting for transfers between devices  33.1 us (20%)
    pallas_call x9, Pallas kernels, whole(): pl.pallas_call(body, grid=(steps,), in_specs=[spec(i, array) for i, array...  71.8 us
    all_to_all x3, starting transfers between devices, exchange(): lax.all_to_all(array, ('lat', 'lon'), split_axis=0, concat_axis=0, tiled=...  31.4 us
    ppermute x4, waiting for transfers between devices, shifted(): lax.ppermute(array, 'lon', [(j, (j + lon_by) % lon) for j in range(lon)])  16.7 us
    all_to_all x3, waiting for transfers between devices, exchange(): lax.all_to_all(array, ('lat', 'lon'), split_axis=0, concat_axis=0, tiled=...  15.7 us
    ppermute x4, starting transfers between devices, shifted(): return lax.ppermute(array, 'lat', rows)  12.4 us
    ppermute x4, starting transfers between devices, shifted(): lax.ppermute(array, 'lon', [(j, (j + lon_by) % lon) for j in range(lon)])  9.7 us
  transfers between devices with their start and end apart: 11, of which 7 were waited for; matrix products, arithmetic and copies ran while one was open for 0% of the time, Pallas kernels for 33%

profile of v11, /device:TPU:1, one launch (start us, length us, event | category | flops | bytes accessed | tf_op | source)
XLA Modules:
  0.0 160.3 jit_solution(11828273243536275396)
XLA Ops:
  0.6 3.8 %rows.1 = (bf16[19,72,128]{2,1,0:T(8,128)(2,1)}, bf16[15,72,128]{2,1,0:T(8,128)(2,1)}) custom-call(s32[1]{0:T(128)} %bitcast.last_ref, f32[3,72,8,128]{3,2,1,0:T(8,128)} %initial_ref.3, f32[2,72,8,128]{3,2,1,0:T(8,128)} %east_ref.3, f32[2,72,8,128]{3,2,1,0:T(8,128)} %north_ref.3, f32[2,72,8,128]{3,2,1,0:T(8,128)} %mixing_ref.3), custom_call_target="tpu_custom_call" | custom-call | flops 5000000 | bytes 6000000 | tf_op jit(solution)/shard_map/rows/pallas_call | solution.py:362
  4.4 5.1 %collective-permute-start = (bf16[19,72,128]{2,1,0:T(8,128)(2,1)}, bf16[19,72,128]{2,1,0:T(8,128)(2,1)}, u32[]{:S(2)}, u32[]{:S(2)}) collective-permute-start(bf16[19,72,128]{2,1,0:T(8,128)(2,1)} %get-tuple-element.40), channel_id=1, source_target_pairs={{0,16},{16,32},{32,48},{48,64},{64,80},{80,96},{96,112},{1,17},{17... | collective-permute-start | bytes 1050632 | tf_op jit(solution)/shard_map/ppermute | solution.py:381
  9.5 1.3 collective-permute-start.1
  10.8 7.3 %pack_first.1 = (bf16[128,80,128]{2,1,0:T(8,128)(2,1)}, f32[128,128]{1,0:T(8,128)}, f32[128,128]{1,0:T(8,128)}, s32[128]{0:T(128)}, s32[128]{0:T(128)}) custom-call(s32[128]{0:T(128)} %bitcast.9, s32[128]{0:T(128)} %counts_ref, bf16[128,72,128]{2,1,0:T(8,128)(2,1)} %kernel_ref.1, s32[128,128]{1,0:T(8,128)} %columns_ref.3, bf16[128,128]{1,0:T(8,128)(2,1)} %observed_ref.3, ...), custom_call_target="tpu_custom_call" | custom-call | flops 5000000 | bytes 6000000 | tf_op jit(solution)/shard_map/pack_first/pallas_call | solution.py:362
  18.1 0.7 collective-permute-done.1.down_terms
  18.9 0.0 collective-permute-done.up_terms
  18.9 12.0 %all-to-all-start.1 = ((bf16[128,80,128]{2,1,0:T(8,128)(2,1)}), bf16[128,80,128]{2,1,0:T(8,128)(2,1)}, u32[]{:S(2)}, u32[]{:S(2)}) async-start(bf16[128,80,128]{2,1,0:T(8,128)(2,1)} %get-tuple-element.58), calls=%async_computation.1 | async-start | bytes 5242880 | tf_op jit(solution)/shard_map/all_to_all | solution.py:764
  30.9 8.1 %arrange.1 = (f32[3,8,72,128]{3,2,1,0:T(8,128)}, f32[2,8,72,128]{3,2,1,0:T(8,128)}, f32[2,8,72,128]{3,2,1,0:T(8,128)}, f32[2,8,72,128]{3,2,1,0:T(8,128)}, f32[3,...) custom-call(s32[1]{0:T(128)} %bitcast.last_ref, ...), custom_call_target="tpu_custom_call" | custom-call | flops 5000000 | bytes 6000000 | tf_op jit(solution)/shard_map/arrange/pallas_call | solution.py:362
  39.0 1.1 collective-permute-start.3
  40.1 2.1 %collective-permute-start.2 = (f32[3,72,128]{2,1,0:T(8,128)}, f32[3,72,128]{2,1,0:T(8,128)}, u32[]{:S(2)}, u32[]{:S(2)}) collective-permute-start(f32[3,72,128]{2,1,0:T(8,128)} %get-tuple-element.48.own_east.wind_east), channel_id=1, source_target_pairs={{0,1},{1,2},{2,3},{3,4},{4,5},{5,6},{6,7},{7,8},{8,9},{9,10},{10,1... | collective-permute-start | bytes 331784 | tf_op jit(solution)/shard_map/ppermute | solution.py:378
  42.3 6.7 %pack_second.1 = bf16[128,80,128]{2,1,0:T(8,128)(2,1)} custom-call(s32[128]{0:T(128)} %get-tuple-element.52.source_ref.second_ref, bf16[128,72,128]{2,1,0:T(8,128)(2,1)} %kernel_ref.1, s32[128,128]{1,0:T(8,128)} %columns_ref.3, bf16[128,128]{1,0:T(8,128)(2,1)} %observed_ref.3, bf16[128,128]{1,0:T(8,128)(2,1)} %weight_ref.3, ...), custom_call_target="tpu_custom_call" | custom-call | flops 5000000 | bytes 6000000 | tf_op jit(solution)/shard_map/pack_second/pallas_call | solution.py:362
  48.9 15.6 %collective-permute-done.3.from_east.side_east = f32[3,72,128]{2,1,0:T(8,128)} collective-permute-done((f32[3,72,128]{2,1,0:T(8,128)}, f32[3,72,128]{2,1,0:T(8,128)}, u32[]{:S(2)}, u32[]{:S(2)}) %collective-permute-start.3) | collective-permute-done | bytes 110624 | tf_op jit(solution)/shard_map/ppermute | solution.py:378
  64.5 0.0 collective-permute-done.2.from_west.side_west
  64.5 1.6 %all-to-all-done.1.block_ref = bf16[128,80,128]{2,1,0:T(8,128)(2,1)} async-done(((bf16[128,80,128]{2,1,0:T(8,128)(2,1)}), bf16[128,80,128]{2,1,0:T(8,128)(2,1)}, u32[]{:S(2)}, u32[]{:S(2)}) %all-to-all-start.1) | async-done | bytes 2621472 | tf_op jit(solution)/shard_map/all_to_all | solution.py:764
  66.1 6.7 %all-to-all-start = ((bf16[128,80,128]{2,1,0:T(8,128)(2,1)}), bf16[128,80,128]{2,1,0:T(8,128)(2,1)}, u32[]{:S(2)}, u32[]{:S(2)}) async-start(bf16[128,80,128]{2,1,0:T(8,128)(2,1)} %pack_second.1), calls=%async_computation | async-start | bytes 5242880 | tf_op jit(solution)/shard_map/all_to_all | solution.py:764
  72.8 6.4 %forward.1.field_hbm = bf16[1728,256]{1,0:T(8,128)(2,1)} custom-call(f32[3,8,72,128]{3,2,1,0:T(8,128)} %get-tuple-element.44.state_ref, f32[2,8,72,128]{3,2,1,0:T(8,128)} %get-tuple-element.45.east_ref, f32[2,8,72,128]{3,2,1,0:T(8,128)} %get-tuple-element.46.north_ref, f32[2,8,72,128]{3,2,1,0:T(8,128)} %get-tuple-element.47.mixing_ref, ...), custom_call_target="tpu_custom_call" | custom-call | flops 5000000 | bytes 6000000 | tf_op jit(solution)/shard_map/forward/pallas_call | solution.py:362
  79.2 18.3 %first_soundings.1 = (f32[864,256]{1,0:T(8,128)}, f32[128,128]{1,0:T(8,128)}) custom-call(bf16[1728,256]{1,0:T(8,128)(2,1)} %forward.1.field_hbm, bf16[128,80,128]{2,1,0:T(8,128)(2,1)} %all-to-all-done.1.block_ref), custom_call_target="tpu_custom_call" | custom-call | flops 15000000512 | bytes 6000000 | tf_op jit(solution)/shard_map/first_soundings/pallas_call | solution.py:362
  97.5 10.6 %all-to-all-done.block_ref = bf16[128,80,128]{2,1,0:T(8,128)(2,1)} async-done(((bf16[128,80,128]{2,1,0:T(8,128)(2,1)}), bf16[128,80,128]{2,1,0:T(8,128)(2,1)}, u32[]{:S(2)}, u32[]{:S(2)}) %all-to-all-start) | async-done | bytes 2621472 | tf_op jit(solution)/shard_map/all_to_all | solution.py:764
  108.1 13.0 %second_soundings.1 = (f32[864,256]{1,0:T(8,128)}, f32[256,128]{1,0:T(8,128)}, f32[6,72,128]{2,1,0:T(8,128)}, f32[6,72,128]{2,1,0:T(8,128)}, f32[72,128]{1,0:T(8,128)}, /*index=5*/f32[72,128]{1,0:T(8,128)}) custom-call(bf16[1728,256]{1,0:T(8,128)(2,1)} %forward.1.field_hbm, bf16[128,80,128]{2,1,0:T(8,128)(2,1)} %all-to-all-done.block_ref, ...), custom_call_target="tpu_custom_call" | custom-call | flops 15000000512 | bytes 6000000 | tf_op jit(solution)/shard_map/second_soundings/pallas_call | solution.py:362
  121.0 2.4 %collective-permute-start.4 = (f32[72,128]{1,0:T(8,128)}, f32[72,128]{1,0:T(8,128)S(1)}, u32[]{:S(2)}, u32[]{:S(2)}) collective-permute-start(f32[72,128]{1,0:T(8,128)} %get-tuple-element.63.own_east), channel_id=1, source_target_pairs={{0,1},{1,2},{2,3},{3,4},{4,5},{5,6},{6,7},{7,8},{8,9},{9,10},{10,1... | collective-permute-start | bytes 110600 | tf_op jit(solution)/shard_map/ppermute | solution.py:378
  123.4 4.1 %collective-permute-start.5 = (f32[72,128]{1,0:T(8,128)}, f32[72,128]{1,0:T(8,128)S(1)}, u32[]{:S(2)}, u32[]{:S(2)}) collective-permute-start(f32[72,128]{1,0:T(8,128)} %get-tuple-element.64.own_west), channel_id=1, source_target_pairs={{0,15},{1,0},{2,1},{3,2},{4,3},{5,4},{6,5},{7,6},{8,7},{9,8},{10,9... | collective-permute-start | bytes 110600 | tf_op jit(solution)/shard_map/ppermute | solution.py:378
  127.5 0.8 collective-permute-done.4.from_west
  128.3 0.0 copy-start
  128.3 0.2 collective-permute-done.5.from_east
  128.6 0.0 copy-start.1
  128.6 1.1 pad_maximum_fusion
  129.7 1.3 collective-permute-start.7
  131.0 4.7 %collective-permute-start.6 = (f32[8,72,128]{2,1,0:T(8,128)S(1)}, f32[8,72,128]{2,1,0:T(8,128)}, u32[]{:S(2)}, u32[]{:S(2)}) collective-permute-start(f32[8,72,128]{2,1,0:T(8,128)S(1)} %get-tuple-element.71), channel_id=1, source_target_pairs={{0,16},{16,32},{32,48},{48,64},{64,80},{80,96},{96,112},{1,17},{17... | collective-permute-start | bytes 884744 | tf_op jit(solution)/shard_map/ppermute | solution.py:381
  135.7 0.0 copy-done
  135.7 0.0 copy-done.1
  135.7 12.7 %all-to-all-start.2 = ((f32[128,2,128]{2,1,0:T(2,128)}), f32[128,2,128]{2,1,0:T(2,128)}, u32[]{:S(2)}, u32[]{:S(2)}) async-start(f32[128,2,128]{2,1,0:T(2,128)} %bitcast.8), calls=%async_computation.2 | async-start | bytes 262144 | tf_op jit(solution)/shard_map/all_to_all | solution.py:764
  148.4 0.0 collective-permute-done.7.down_ref
  148.4 0.0 collective-permute-done.6.up_ref
  148.5 6.4 %adjoint.1 = f32[3,72,8,128]{3,2,1,0:T(8,128)} custom-call(f32[864,256]{1,0:T(8,128)} %get-tuple-element.62.adjoint_ref, f32[2,8,72,128]{3,2,1,0:T(8,128)} %get-tuple-element.45.east_ref, f32[2,8,72,128]{3,2,1,0:T(8,128)} %get-tuple-element.46.north_ref, f32[2,8,72,128]{3,2,1,0:T(8,128)} %get-tuple-element.47.mixing_ref, ...), custom_call_target="tpu_custom_call" | custom-call | flops 5000000 | bytes 6000000 | tf_op jit(solution)/shard_map/adjoint/pallas_call | solution.py:362
  154.9 3.5 %all-to-all-done.2 = f32[128,2,128]{2,1,0:T(2,128)} async-done(((f32[128,2,128]{2,1,0:T(2,128)}), f32[128,2,128]{2,1,0:T(2,128)}, u32[]{:S(2)}, u32[]{:S(2)}) %all-to-all-start.2) | async-done | bytes 131104 | tf_op jit(solution)/shard_map/all_to_all | solution.py:764
  158.4 2.0 %innovations.1 = f32[128,128]{1,0:T(8,128)} custom-call(s32[128]{0:T(128)} %get-tuple-element.68.first_ref, s32[128]{0:T(128)} %get-tuple-element.52.source_ref.second_ref, f32[256,128]{1,0:T(8,128)} %bitcast.3.returned_ref, f32[128,128]{1,0:T(8,128)} %get-tuple-element.53.place_ref), custom_call_target="tpu_custom_call" | custom-call | flops 5000000 | bytes 6000000 | tf_op jit(solution)/shard_map/innovations/pallas_call | solution.py:362
Async XLA Ops:
  4.4 14.5 %collective-permute-start = (bf16[19,72,128]{2,1,0:T(8,128)(2,1)}, bf16[19,72,128]{2,1,0:T(8,128)(2,1)}, u32[]{:S(2)}, u32[]{:S(2)}) collective-permute-start(bf16[19,72,128]{2,1,0:T(8,128)(2,1)} %get-tuple-element.40), channel_id=1, source_target_pairs={{0,16},{16,32},{32,48},{48,64},{64,80},{80,96},{96,112},{1,17},{17... | collective-permute-start | bytes 1050632 | tf_op jit(solution)/shard_map/ppermute | solution.py:381
  9.5 9.4 %collective-permute-start.1 = (bf16[15,72,128]{2,1,0:T(8,128)(2,1)}, bf16[15,72,128]{2,1,0:T(8,128)(2,1)}, u32[]{:S(2)}, u32[]{:S(2)}) collective-permute-start(bf16[15,72,128]{2,1,0:T(8,128)(2,1)} %get-tuple-element.41), channel_id=1, source_target_pairs={{16,0},{32,16},{48,32},{64,48},{80,64},{96,80},{112,96},{17,1},{33... | collective-permute-start | bytes 829448 | tf_op jit(solution)/shard_map/ppermute | solution.py:381
  18.9 47.3 %all-to-all-start.1 = ((bf16[128,80,128]{2,1,0:T(8,128)(2,1)}), bf16[128,80,128]{2,1,0:T(8,128)(2,1)}, u32[]{:S(2)}, u32[]{:S(2)}) async-start(bf16[128,80,128]{2,1,0:T(8,128)(2,1)} %get-tuple-element.58), calls=%async_computation.1 | async-start | bytes 5242880 | tf_op jit(solution)/shard_map/all_to_all | solution.py:764
  39.0 25.5 %collective-permute-start.3 = (f32[3,72,128]{2,1,0:T(8,128)}, f32[3,72,128]{2,1,0:T(8,128)}, u32[]{:S(2)}, u32[]{:S(2)}) collective-permute-start(f32[3,72,128]{2,1,0:T(8,128)} %get-tuple-element.49.own_west), channel_id=1, source_target_pairs={{0,15},{1,0},{2,1},{3,2},{4,3},{5,4},{6,5},{7,6},{8,7},{9,8},{10,9... | collective-permute-start | bytes 331784 | tf_op jit(solution)/shard_map/ppermute | solution.py:378
  40.1 24.4 %collective-permute-start.2 = (f32[3,72,128]{2,1,0:T(8,128)}, f32[3,72,128]{2,1,0:T(8,128)}, u32[]{:S(2)}, u32[]{:S(2)}) collective-permute-start(f32[3,72,128]{2,1,0:T(8,128)} %get-tuple-element.48.own_east.wind_east), channel_id=1, source_target_pairs={{0,1},{1,2},{2,3},{3,4},{4,5},{5,6},{6,7},{7,8},{8,9},{9,10},{10,1... | collective-permute-start | bytes 331784 | tf_op jit(solution)/shard_map/ppermute | solution.py:378
  66.1 41.9 %all-to-all-start = ((bf16[128,80,128]{2,1,0:T(8,128)(2,1)}), bf16[128,80,128]{2,1,0:T(8,128)(2,1)}, u32[]{:S(2)}, u32[]{:S(2)}) async-start(bf16[128,80,128]{2,1,0:T(8,128)(2,1)} %pack_second.1), calls=%async_computation | async-start | bytes 5242880 | tf_op jit(solution)/shard_map/all_to_all | solution.py:764
  121.0 7.3 %collective-permute-start.4 = (f32[72,128]{1,0:T(8,128)}, f32[72,128]{1,0:T(8,128)S(1)}, u32[]{:S(2)}, u32[]{:S(2)}) collective-permute-start(f32[72,128]{1,0:T(8,128)} %get-tuple-element.63.own_east), channel_id=1, source_target_pairs={{0,1},{1,2},{2,3},{3,4},{4,5},{5,6},{6,7},{7,8},{8,9},{9,10},{10,1... | collective-permute-start | bytes 110600 | tf_op jit(solution)/shard_map/ppermute | solution.py:378
  123.4 5.1 %collective-permute-start.5 = (f32[72,128]{1,0:T(8,128)}, f32[72,128]{1,0:T(8,128)S(1)}, u32[]{:S(2)}, u32[]{:S(2)}) collective-permute-start(f32[72,128]{1,0:T(8,128)} %get-tuple-element.64.own_west), channel_id=1, source_target_pairs={{0,15},{1,0},{2,1},{3,2},{4,3},{5,4},{6,5},{7,6},{8,7},{9,8},{10,9... | collective-permute-start | bytes 110600 | tf_op jit(solution)/shard_map/ppermute | solution.py:378
  128.3 7.4 %copy-start = (f32[72,128]{1,0:T(8,128)}, f32[72,128]{1,0:T(8,128)S(1)}, u32[]{:S(2)}) copy-start(f32[72,128]{1,0:T(8,128)S(1)} %collective-permute-done.4.from_west) | copy-start | bytes 110596
  128.6 7.1 %copy-start.1 = (f32[72,128]{1,0:T(8,128)}, f32[72,128]{1,0:T(8,128)S(1)}, u32[]{:S(2)}) copy-start(f32[72,128]{1,0:T(8,128)S(1)} %collective-permute-done.5.from_east) | copy-start | bytes 110596
  129.7 18.8 %collective-permute-start.7 = (f32[8,72,128]{2,1,0:T(8,128)S(1)}, f32[8,72,128]{2,1,0:T(8,128)}, u32[]{:S(2)}, u32[]{:S(2)}) collective-permute-start(f32[8,72,128]{2,1,0:T(8,128)S(1)} %get-tuple-element.70), channel_id=1, source_target_pairs={{16,0},{32,16},{48,32},{64,48},{80,64},{96,80},{112,96},{17,1},{33... | collective-permute-start | bytes 884744 | tf_op jit(solution)/shard_map/ppermute | solution.py:381
  131.0 17.5 %collective-permute-start.6 = (f32[8,72,128]{2,1,0:T(8,128)S(1)}, f32[8,72,128]{2,1,0:T(8,128)}, u32[]{:S(2)}, u32[]{:S(2)}) collective-permute-start(f32[8,72,128]{2,1,0:T(8,128)S(1)} %get-tuple-element.71), channel_id=1, source_target_pairs={{0,16},{16,32},{32,48},{48,64},{64,80},{80,96},{96,112},{1,17},{17... | collective-permute-start | bytes 884744 | tf_op jit(solution)/shard_map/ppermute | solution.py:381
  135.7 22.7 %all-to-all-start.2 = ((f32[128,2,128]{2,1,0:T(2,128)}), f32[128,2,128]{2,1,0:T(2,128)}, u32[]{:S(2)}, u32[]{:S(2)}) async-start(f32[128,2,128]{2,1,0:T(2,128)} %bitcast.8), calls=%async_computation.2 | async-start | bytes 262144 | tf_op jit(solution)/shard_map/all_to_all | solution.py:764
